TPU v7x, 32 devices: a whole 2x2x4 slice. The times are simulated.
32 devices in a mesh: dp: 8 (over y, x, core), shard: 4 (over z).
Axes of the slice: x: 2, y: 2, z: 4, core: 2. Of those that a mesh axis runs over, the one named last changes fastest.
Arguments:
- tokens: bfloat16 [32768, 512], P(('dp', 'shard')), may hold values from -6 to 6
- targets: int32 [32768], P(('dp', 'shard')), may hold values from 0 to 255
- gain_one: bfloat16 [512], P('shard'), may hold values from 0.5 to 1.5
- bias_one: bfloat16 [512], P('shard'), may hold values from -3 to 3
- w_query: bfloat16 [512, 512], P('shard'), may hold values from -0.5 to 0.5
- w_key: bfloat16 [512, 512], P('shard'), may hold values from -0.25 to 0.25
- w_value: bfloat16 [512, 512], P('shard'), may hold values from -0.25 to 0.25
- w_control: bfloat16 [512, 512], P('shard'), may hold values from -0.5 to 0.5
- w_mix: bfloat16 [512, 512], P('shard'), may hold values from -1 to 1
- gain_two: bfloat16 [512], P('shard'), may hold values from 0.5 to 1.5
- bias_two: bfloat16 [512], P('shard'), may hold values from -3 to 3
- w_up: bfloat16 [512, 2048], P('shard'), may hold values from -0.25 to 0.25
- bias_up: bfloat16 [2048], P('shard'), may hold values from -3 to 3
- w_down: bfloat16 [2048, 512], P('shard'), may hold values from -0.125 to 0.125
- bias_down: bfloat16 [512], P('shard'), may hold values from -3 to 3
- w_read: bfloat16 [512, 256], P('shard'), may hold values from -0.25 to 0.25
Outputs:
- output: bfloat16 [32768, 512], P(('dp', 'shard'))
- grad_tokens: float32 [32768, 512], P(('dp', 'shard'))
- grad_gain_one: float32 [512], P('shard')
- grad_bias_one: float32 [512], P('shard')
- grad_query: float32 [512, 512], P('shard')
- grad_key: float32 [512, 512], P('shard')
- grad_value: float32 [512, 512], P('shard')
- grad_control: float32 [512, 512], P('shard')
- grad_mix: float32 [512, 512], P('shard')
- grad_gain_two: float32 [512], P('shard')
- grad_bias_two: float32 [512], P('shard')
- grad_up: float32 [512, 2048], P('shard')
- grad_bias_up: float32 [2048], P('shard')
- grad_down: float32 [2048, 512], P('shard')
- grad_bias_down: float32 [512], P('shard')
- grad_read: float32 [512, 256], P('shard')
All inputs are finite; a program needn't handle non-finite values.
Results may differ from a plain program's by a relative error of at most 0.013.
Values may be sent and summed in bfloat16 or wider, within the bound.
No kernel may reach another device: no remote copies, remote signals or barrier semaphores. Data moves between devices by JAX's collectives and lax.ppermute only.
A program may use at most 192 MiB of HBM per device.

v0:
```python
import jax
import jax.numpy as jnp
from jax import lax
from jax.sharding import PartitionSpec as P

H = 8
HEAD = 64
NS = 64
SEQ_LEN = 1024
BLOCK = 512


EPS = 1e-05


def norm_forward(values, gain, shift):
    centre = values - jnp.mean(values, axis=-1, keepdims=True)
    inverse = lax.rsqrt(jnp.mean(centre * centre, axis=-1, keepdims=True) + EPS)
    unit = centre * inverse
    return (unit * gain + shift, unit, inverse)


def norm_backward(grad, unit, inverse, gain):
    d_gain = jnp.sum(grad * unit, axis=0)
    d_shift = jnp.sum(grad, axis=0)
    scaled = grad * gain
    d_values = inverse * (
        scaled
        - jnp.mean(scaled, axis=-1, keepdims=True)
        - unit * jnp.mean(scaled * unit, axis=-1, keepdims=True)
    )
    return (d_values, d_gain, d_shift)


def block_terms(query_block, keyed, weights, start):
    rows = query_block.shape[0]
    length = keyed.shape[0]
    visible = (
        lax.broadcasted_iota(jnp.int32, (rows, length), 1)
        <= lax.broadcasted_iota(jnp.int32, (rows, length), 0) + start
    )
    mask_f = visible.astype(jnp.float32)
    scores = (
        jnp.einsum("thd,shd->hts", query_block, keyed, preferred_element_type=jnp.float32) * mask_f
    ).astype(jnp.bfloat16)
    numer = jnp.einsum("hts,shm->thm", scores, weights, preferred_element_type=jnp.float32)
    total = jnp.einsum(
        "ts,shm->thm", mask_f.astype(jnp.bfloat16), weights, preferred_element_type=jnp.float32
    )
    logits = HEAD ** (-0.5) * numer / total
    probs = jax.nn.softmax(logits, axis=-1)
    ratio = (probs / total).astype(jnp.bfloat16)
    mixing = (
        jnp.einsum("thm,shm->hts", ratio, weights, preferred_element_type=jnp.float32) * mask_f
    ).astype(jnp.bfloat16)
    return (mask_f, scores, total, logits, probs, ratio, mixing)


def sequence_forward(item):
    query, keyed, valued, weights = item

    def step(carry, start):
        query_block = lax.dynamic_slice_in_dim(query, start, BLOCK, 0)
        terms = block_terms(query_block, keyed, weights, start)
        out_block = jnp.einsum("hts,shd->thd", terms[6], valued, preferred_element_type=jnp.float32)
        return (carry, out_block.astype(jnp.bfloat16))

    starts = jnp.arange(SEQ_LEN // BLOCK, dtype=jnp.int32) * BLOCK
    _, blocks = lax.scan(step, 0, starts)
    return blocks.reshape(SEQ_LEN, H, HEAD)


def sequence_backward(item):
    query, keyed, valued, weights, grad_out = item

    def step(carry, start):
        d_keyed, d_valued, d_weights = carry
        query_block = lax.dynamic_slice_in_dim(query, start, BLOCK, 0)
        grad_block = lax.dynamic_slice_in_dim(grad_out, start, BLOCK, 0)
        mask_f, scores, total, logits, probs, ratio, mixing = block_terms(
            query_block, keyed, weights, start
        )
        d_mixing = (
            jnp.einsum("thd,shd->hts", grad_block, valued, preferred_element_type=jnp.float32)
            * mask_f
        ).astype(jnp.bfloat16)
        d_valued = d_valued + jnp.einsum(
            "hts,thd->shd", mixing, grad_block, preferred_element_type=jnp.float32
        )
        d_ratio = jnp.einsum("hts,shm->thm", d_mixing, weights, preferred_element_type=jnp.float32)
        d_weights = d_weights + jnp.einsum(
            "hts,thm->shm", d_mixing, ratio, preferred_element_type=jnp.float32
        )
        d_probs = d_ratio / total
        d_total = -d_ratio * probs / (total * total)
        d_logits = probs * (d_probs - jnp.sum(d_probs * probs, axis=-1, keepdims=True))
        d_numer = (HEAD ** (-0.5) * d_logits / total).astype(jnp.bfloat16)
        d_total = (d_total - d_logits * logits / total).astype(jnp.bfloat16)
        d_scores = (
            jnp.einsum("thm,shm->hts", d_numer, weights, preferred_element_type=jnp.float32)
            * mask_f
        ).astype(jnp.bfloat16)
        d_weights = (
            d_weights
            + jnp.einsum("hts,thm->shm", scores, d_numer, preferred_element_type=jnp.float32)
            + jnp.einsum(
                "ts,thm->shm",
                mask_f.astype(jnp.bfloat16),
                d_total,
                preferred_element_type=jnp.float32,
            )
        )
        d_keyed = d_keyed + jnp.einsum(
            "hts,thd->shd", d_scores, query_block, preferred_element_type=jnp.float32
        )
        d_query = jnp.einsum("hts,shd->thd", d_scores, keyed, preferred_element_type=jnp.float32)
        return ((d_keyed, d_valued, d_weights), d_query.astype(jnp.bfloat16))

    starts = jnp.arange(SEQ_LEN // BLOCK, dtype=jnp.int32) * BLOCK
    zeros_kv = jnp.zeros((SEQ_LEN, H, HEAD), jnp.float32)
    zeros_slot = jnp.zeros((SEQ_LEN, H, NS), jnp.float32)
    (d_keyed, d_valued, d_weights), d_blocks = lax.scan(
        step, (zeros_kv, zeros_kv, zeros_slot), starts
    )
    return (
        d_blocks.reshape(SEQ_LEN, H, HEAD),
        d_keyed.astype(jnp.bfloat16),
        d_valued.astype(jnp.bfloat16),
        d_weights,
    )


def on_device(
    tokens,
    targets,
    gain_one,
    bias_one,
    w_query,
    w_key,
    w_value,
    w_control,
    w_mix,
    gain_two,
    bias_two,
    w_up,
    bias_up,
    w_down,
    bias_down,
    w_read,
):
    full = (
        lax.all_gather(gain_one, "shard", axis=0, tiled=True),
        lax.all_gather(bias_one, "shard", axis=0, tiled=True),
        lax.all_gather(w_query, "shard", axis=0, tiled=True),
        lax.all_gather(w_key, "shard", axis=0, tiled=True),
        lax.all_gather(w_value, "shard", axis=0, tiled=True),
        lax.all_gather(w_control, "shard", axis=0, tiled=True),
        lax.all_gather(w_mix, "shard", axis=0, tiled=True),
        lax.all_gather(gain_two, "shard", axis=0, tiled=True),
        lax.all_gather(bias_two, "shard", axis=0, tiled=True),
        lax.all_gather(w_up, "shard", axis=0, tiled=True),
        lax.all_gather(bias_up, "shard", axis=0, tiled=True),
        lax.all_gather(w_down, "shard", axis=0, tiled=True),
        lax.all_gather(bias_down, "shard", axis=0, tiled=True),
        lax.all_gather(w_read, "shard", axis=0, tiled=True),
    )
    count = tokens.shape[0]
    seqs = count // SEQ_LEN
    width = w_query.shape[1]
    inputs = tokens.astype(jnp.float32)
    normed, unit_one, inverse_one = norm_forward(
        inputs, full[0].astype(jnp.float32), full[1].astype(jnp.float32)
    )
    first_in = normed.astype(jnp.bfloat16)
    w_proj = jnp.concatenate([full[2], full[3], full[4], full[5]], axis=1)
    projected = jnp.dot(first_in, w_proj, preferred_element_type=jnp.float32)
    query = projected[:, :width].astype(jnp.bfloat16).reshape(seqs, SEQ_LEN, H, HEAD)
    keyed = projected[:, width : 2 * width].astype(jnp.bfloat16).reshape(seqs, SEQ_LEN, H, HEAD)
    valued = (
        projected[:, 2 * width : 3 * width].astype(jnp.bfloat16).reshape(seqs, SEQ_LEN, H, HEAD)
    )
    expo = jnp.exp(projected[:, 3 * width :])
    weights = expo.astype(jnp.bfloat16).reshape(seqs, SEQ_LEN, H, NS)
    mixed = lax.map(sequence_forward, (query, keyed, valued, weights)).reshape(count, width)
    attn_out = jnp.dot(mixed, full[6], preferred_element_type=jnp.float32)
    resid = inputs + attn_out
    normed_two, unit_two, inverse_two = norm_forward(
        resid, full[7].astype(jnp.float32), full[8].astype(jnp.float32)
    )
    second_in = normed_two.astype(jnp.bfloat16)
    hidden = jnp.dot(second_in, full[9], preferred_element_type=jnp.float32) + full[10].astype(
        jnp.float32
    )
    active = jax.nn.gelu(hidden, approximate=True).astype(jnp.bfloat16)
    branch = jnp.dot(active, full[11], preferred_element_type=jnp.float32) + full[12].astype(
        jnp.float32
    )
    output = resid + branch
    output_low = output.astype(jnp.bfloat16)
    logits = jnp.dot(output_low, full[13], preferred_element_type=jnp.float32)
    back = (
        lax.all_gather(gain_one, "shard", axis=0, tiled=True),
        lax.all_gather(bias_one, "shard", axis=0, tiled=True),
        lax.all_gather(w_query, "shard", axis=0, tiled=True),
        lax.all_gather(w_key, "shard", axis=0, tiled=True),
        lax.all_gather(w_value, "shard", axis=0, tiled=True),
        lax.all_gather(w_control, "shard", axis=0, tiled=True),
        lax.all_gather(w_mix, "shard", axis=0, tiled=True),
        lax.all_gather(gain_two, "shard", axis=0, tiled=True),
        lax.all_gather(bias_two, "shard", axis=0, tiled=True),
        lax.all_gather(w_up, "shard", axis=0, tiled=True),
        lax.all_gather(bias_up, "shard", axis=0, tiled=True),
        lax.all_gather(w_down, "shard", axis=0, tiled=True),
        lax.all_gather(bias_down, "shard", axis=0, tiled=True),
        lax.all_gather(w_read, "shard", axis=0, tiled=True),
    )
    onehot = (targets[:, None] == jnp.arange(logits.shape[1], dtype=jnp.int32)[None, :]).astype(
        jnp.float32
    )
    d_logits = (jax.nn.softmax(logits, axis=-1) - onehot).astype(jnp.bfloat16)
    g_read = jnp.dot(output_low.T, d_logits, preferred_element_type=jnp.float32)
    d_out = jnp.dot(d_logits, back[13].T, preferred_element_type=jnp.float32)
    d_branch = d_out.astype(jnp.bfloat16)
    g_bias_down = jnp.sum(d_branch.astype(jnp.float32), axis=0)
    g_down = jnp.dot(active.T, d_branch, preferred_element_type=jnp.float32)
    d_active = jnp.dot(d_branch, back[11].T, preferred_element_type=jnp.float32)
    _, gelu_pull = jax.vjp(lambda z: jax.nn.gelu(z, approximate=True), hidden)
    d_hidden = gelu_pull(d_active)[0].astype(jnp.bfloat16)
    g_bias_up = jnp.sum(d_hidden.astype(jnp.float32), axis=0)
    g_up = jnp.dot(second_in.T, d_hidden, preferred_element_type=jnp.float32)
    d_second = jnp.dot(d_hidden, back[9].T, preferred_element_type=jnp.float32)
    d_resid, g_gain_two, g_bias_two = norm_backward(
        d_second, unit_two, inverse_two, back[7].astype(jnp.float32)
    )
    d_resid = d_resid + d_out
    d_attn = d_resid.astype(jnp.bfloat16)
    g_mix = jnp.dot(mixed.T, d_attn, preferred_element_type=jnp.float32)
    d_mixed = jnp.dot(d_attn, back[6].T, preferred_element_type=jnp.float32).astype(jnp.bfloat16)
    d_query, d_keyed, d_valued, d_weights = lax.map(
        sequence_backward, (query, keyed, valued, weights, d_mixed.reshape(seqs, SEQ_LEN, H, HEAD))
    )
    d_control = (d_weights.reshape(count, H * NS) * expo).astype(jnp.bfloat16)
    d_proj = jnp.concatenate(
        [
            d_query.reshape(count, width),
            d_keyed.reshape(count, width),
            d_valued.reshape(count, width),
            d_control,
        ],
        axis=1,
    )
    g_proj = jnp.dot(first_in.T, d_proj, preferred_element_type=jnp.float32)
    back_proj = jnp.concatenate([back[2], back[3], back[4], back[5]], axis=1)
    d_first = jnp.dot(d_proj, back_proj.T, preferred_element_type=jnp.float32)
    d_inputs, g_gain_one, g_bias_one = norm_backward(
        d_first, unit_one, inverse_one, back[0].astype(jnp.float32)
    )
    d_inputs = d_inputs + d_resid
    grads = (
        g_gain_one,
        g_bias_one,
        g_proj[:, :width],
        g_proj[:, width : 2 * width],
        g_proj[:, 2 * width : 3 * width],
        g_proj[:, 3 * width :],
        g_mix,
        g_gain_two,
        g_bias_two,
        g_up,
        g_bias_up,
        g_down,
        g_bias_down,
        g_read,
    )
    pieces = (
        lax.psum_scatter(
            grads[0].astype(jnp.bfloat16), "shard", scatter_dimension=0, tiled=True
        ).astype(jnp.float32),
        lax.psum_scatter(
            grads[1].astype(jnp.bfloat16), "shard", scatter_dimension=0, tiled=True
        ).astype(jnp.float32),
        lax.psum_scatter(
            grads[2].astype(jnp.bfloat16), "shard", scatter_dimension=0, tiled=True
        ).astype(jnp.float32),
        lax.psum_scatter(
            grads[3].astype(jnp.bfloat16), "shard", scatter_dimension=0, tiled=True
        ).astype(jnp.float32),
        lax.psum_scatter(
            grads[4].astype(jnp.bfloat16), "shard", scatter_dimension=0, tiled=True
        ).astype(jnp.float32),
        lax.psum_scatter(
            grads[5].astype(jnp.bfloat16), "shard", scatter_dimension=0, tiled=True
        ).astype(jnp.float32),
        lax.psum_scatter(
            grads[6].astype(jnp.bfloat16), "shard", scatter_dimension=0, tiled=True
        ).astype(jnp.float32),
        lax.psum_scatter(
            grads[7].astype(jnp.bfloat16), "shard", scatter_dimension=0, tiled=True
        ).astype(jnp.float32),
        lax.psum_scatter(
            grads[8].astype(jnp.bfloat16), "shard", scatter_dimension=0, tiled=True
        ).astype(jnp.float32),
        lax.psum_scatter(
            grads[9].astype(jnp.bfloat16), "shard", scatter_dimension=0, tiled=True
        ).astype(jnp.float32),
        lax.psum_scatter(
            grads[10].astype(jnp.bfloat16), "shard", scatter_dimension=0, tiled=True
        ).astype(jnp.float32),
        lax.psum_scatter(
            grads[11].astype(jnp.bfloat16), "shard", scatter_dimension=0, tiled=True
        ).astype(jnp.float32),
        lax.psum_scatter(
            grads[12].astype(jnp.bfloat16), "shard", scatter_dimension=0, tiled=True
        ).astype(jnp.float32),
        lax.psum_scatter(
            grads[13].astype(jnp.bfloat16), "shard", scatter_dimension=0, tiled=True
        ).astype(jnp.float32),
    )
    totals = lax.psum(
        (
            pieces[0],
            pieces[1],
            pieces[2],
            pieces[3],
            pieces[4],
            pieces[5],
            pieces[6],
            pieces[7],
            pieces[8],
            pieces[9],
            pieces[10],
            pieces[11],
            pieces[12],
            pieces[13],
        ),
        "dp",
    )
    return (output_low, d_inputs) + tuple(totals)


def solution(mesh):
    placed = (
        P(("dp", "shard"), None),
        P(("dp", "shard")),
        P("shard"),
        P("shard"),
        P("shard", None),
        P("shard", None),
        P("shard", None),
        P("shard", None),
        P("shard", None),
        P("shard"),
        P("shard"),
        P("shard", None),
        P("shard"),
        P("shard", None),
        P("shard"),
        P("shard", None),
    )
    return jax.shard_map(
        on_device,
        mesh=mesh,
        in_specs=placed,
        out_specs=(
            P(("dp", "shard"), None),
            P(("dp", "shard"), None),
            P("shard"),
            P("shard"),
            P("shard", None),
            P("shard", None),
            P("shard", None),
            P("shard", None),
            P("shard", None),
            P("shard"),
            P("shard"),
            P("shard", None),
            P("shard"),
            P("shard", None),
            P("shard"),
            P("shard", None),
        ),
        check_vma=False,
    )
```

profile of v0, /device:TPU:0, one launch (start us, length us, event | category | flops | bytes accessed | tf_op | source)
XLA Modules:
  0.0 711.2 jit_solution(7792808506296312262)
XLA Ops:
  8.7 12.7 %all-gather = bf16[4,1,128]{2,1,0:T(2,128)(2,1)S(1)} all-gather(bf16[1,1,128]{2,1,0:T(2,128)(2,1)} %bitcast.235), channel_id=1, replica_groups=mesh['dp'=8,'shard'=4] {'shard'}, dimensions={0}, use_global_device_ids=true | all-gather | bytes 1280 | tf_op jit(solution)/shard_map/all_gather | solution.py:152
  21.5 7.9 %all-gather.1 = bf16[4,1,128]{2,1,0:T(2,128)(2,1)S(1)} all-gather(bf16[1,1,128]{2,1,0:T(2,128)(2,1)} %bitcast.236), channel_id=1, replica_groups=mesh['dp'=8,'shard'=4] {'shard'}, dimensions={0}, use_global_device_ids=true | all-gather | bytes 1280 | tf_op jit(solution)/shard_map/all_gather | solution.py:153
  29.3 21.4 %all_gather.54 = bf16[512,512]{1,0:T(8,128)(2,1)S(1)} all-gather(bf16[128,512]{1,0:T(8,128)(2,1)} %param.24), channel_id=1, replica_groups=mesh['dp'=8,'shard'=4] {'shard'}, dimensions={0}, use_global_device_ids=true | all-gather | bytes 655360 | tf_op jit(solution)/shard_map/all_gather | solution.py:154
  50.7 21.5 %all_gather.55 = bf16[512,512]{1,0:T(8,128)(2,1)S(1)} all-gather(bf16[128,512]{1,0:T(8,128)(2,1)} %param.25), channel_id=1, replica_groups=mesh['dp'=8,'shard'=4] {'shard'}, dimensions={0}, use_global_device_ids=true | all-gather | bytes 655360 | tf_op jit(solution)/shard_map/all_gather | solution.py:155
  72.2 16.0 %all_gather.56 = bf16[512,512]{1,0:T(8,128)(2,1)S(1)} all-gather(bf16[128,512]{1,0:T(8,128)(2,1)S(1)} %copy-done.33), channel_id=1, replica_groups=mesh['dp'=8,'shard'=4] {'shard'}, dimensions={0}, use_global_device_ids=true | all-gather | bytes 655360 | tf_op jit(solution)/shard_map/all_gather | solution.py:156
  88.2 19.9 %all_gather.57 = bf16[512,512]{1,0:T(8,128)(2,1)S(1)} all-gather(bf16[128,512]{1,0:T(8,128)(2,1)S(1)} %copy-done.34), channel_id=1, replica_groups=mesh['dp'=8,'shard'=4] {'shard'}, dimensions={0}, use_global_device_ids=true | all-gather | bytes 655360 | tf_op jit(solution)/shard_map/all_gather | solution.py:157
  110.8 5.8 fusion.90
  128.6 50.1 %while.47 = (s32[]{:T(128)}, bf16[2,512,8,64]{1,3,2,0:T(8,128)(2,1)}, s32[2]{0:T(128)S(1)}, bf16[1024,8,64]{0,2,1:T(8,128)(2,1)}, bf16[1024,8,64]{0,2,1:T(8,128)...) while((s32[]{:T(128)}, ...), condition=%wide.region_5.0_spmd, body=%wide.region_2.5_spmd.sunk | while | flops 2706117120 | bytes 19962024 | solution.py:69
  135.7 8.3 %fusion.199 = f32[512,8,64]{0,2,1:T(8,128)} fusion(f32[512,8,64]{0,2,1:T(8,128)} %bitcast.242, bf16[1024,8,64]{0,2,1:T(8,128)(2,1)S(1)} %get-tuple-element.510, bf16[1024,8,64]{0,2,1:T(8,128)(2,1)} %get-tuple-element.509, f32[512,1024]{1,0:T(8,128)} %fusion.197, bf16[1024,8,64]{0,2,1:T(8,128)(2,1)} %get-tuple-element.508, s32[]{:T(128)S(6)} %select_n.10), kind=kOutput, calls=%fused_computation.17.clone.1 | convolution fusion | flops 1082654720 | bytes 6815748 | tf_op jit(solution)/shard_map/while/body/eval_jaxpr/while/body/eval_jaxpr/hts,shm->thm/dot_general | solution.py:46
  145.8 8.2 %fusion.201 = bf16[2,512,8,64]{1,3,2,0:T(8,128)(2,1)} fusion(bf16[2,512,8,64]{1,3,2,0:T(8,128)(2,1)} %get-tuple-element.496, s32[]{:T(128)S(6)} %copy.102, bf16[1024,8,64]{0,2,1:T(8,128)(2,1)S(1)} %get-tuple-element.511, bf16[1024,8,64]{0,2,1:T(8,128)(2,1)S(1)} %get-tuple-element.510, f32[512,1024]{1,0:T(8,128)} %fusion.197, ...), kind=kOutput, calls=%fused_computation.13.clone.1 | convolution fusion | flops 1083445248 | bytes 7880708 | tf_op jit(solution)/shard_map/while/body/eval_jaxpr/while/body/eval_jaxpr/hts,shd->thd/dot_general | solution.py:65
  160.5 8.3 %fusion.199 = f32[512,8,64]{0,2,1:T(8,128)} fusion(f32[512,8,64]{0,2,1:T(8,128)} %bitcast.242, bf16[1024,8,64]{0,2,1:T(8,128)(2,1)S(1)} %get-tuple-element.510, bf16[1024,8,64]{0,2,1:T(8,128)(2,1)} %get-tuple-element.509, f32[512,1024]{1,0:T(8,128)} %fusion.197, bf16[1024,8,64]{0,2,1:T(8,128)(2,1)} %get-tuple-element.508, s32[]{:T(128)S(6)} %select_n.10), kind=kOutput, calls=%fused_computation.17.clone.1 | convolution fusion | flops 1082654720 | bytes 6815748 | tf_op jit(solution)/shard_map/while/body/eval_jaxpr/while/body/eval_jaxpr/hts,shm->thm/dot_general | solution.py:46
  170.5 8.2 %fusion.201 = bf16[2,512,8,64]{1,3,2,0:T(8,128)(2,1)} fusion(bf16[2,512,8,64]{1,3,2,0:T(8,128)(2,1)} %get-tuple-element.496, s32[]{:T(128)S(6)} %copy.102, bf16[1024,8,64]{0,2,1:T(8,128)(2,1)S(1)} %get-tuple-element.511, bf16[1024,8,64]{0,2,1:T(8,128)(2,1)S(1)} %get-tuple-element.510, f32[512,1024]{1,0:T(8,128)} %fusion.197, ...), kind=kOutput, calls=%fused_computation.13.clone.1 | convolution fusion | flops 1083445248 | bytes 7880708 | tf_op jit(solution)/shard_map/while/body/eval_jaxpr/while/body/eval_jaxpr/hts,shd->thd/dot_general | solution.py:65
  178.7 9.6 %all-gather.2 = bf16[4,1,128]{2,1,0:T(2,128)(2,1)S(1)} all-gather(bf16[1,1,128]{2,1,0:T(2,128)(2,1)S(1)} %bitcast.237), channel_id=1, replica_groups=mesh['dp'=8,'shard'=4] {'shard'}, dimensions={0}, use_global_device_ids=true | all-gather | bytes 1280 | tf_op jit(solution)/shard_map/all_gather | solution.py:159
  188.3 7.5 %all-gather.3 = bf16[4,1,128]{2,1,0:T(2,128)(2,1)S(1)} all-gather(bf16[1,1,128]{2,1,0:T(2,128)(2,1)S(1)} %bitcast.238), channel_id=1, replica_groups=mesh['dp'=8,'shard'=4] {'shard'}, dimensions={0}, use_global_device_ids=true | all-gather | bytes 1280 | tf_op jit(solution)/shard_map/all_gather | solution.py:160
  195.9 9.5 %all-gather.5 = bf16[4,1,128]{2,1,0:T(2,128)(2,1)S(1)} all-gather(bf16[1,1,128]{2,1,0:T(2,128)(2,1)S(1)} %bitcast.239), channel_id=1, replica_groups=mesh['dp'=8,'shard'=4] {'shard'}, dimensions={0}, use_global_device_ids=true | all-gather | bytes 1280 | tf_op jit(solution)/shard_map/all_gather | solution.py:164
  205.4 11.9 %all-gather.4 = bf16[4,1,512]{2,1,0:T(2,128)(2,1)S(1)} all-gather(bf16[1,1,512]{2,1,0:T(2,128)(2,1)S(1)} %reshape.163), channel_id=1, replica_groups=mesh['dp'=8,'shard'=4] {'shard'}, dimensions={0}, use_global_device_ids=true | all-gather | bytes 5120 | tf_op jit(solution)/shard_map/all_gather | solution.py:162
  219.9 13.8 %all_gather.65 = bf16[512,256]{1,0:T(8,128)(2,1)S(1)} all-gather(bf16[128,256]{1,0:T(8,128)(2,1)S(1)} %copy-done.36), channel_id=1, replica_groups=mesh['dp'=8,'shard'=4] {'shard'}, dimensions={0}, use_global_device_ids=true | all-gather | bytes 327680 | tf_op jit(solution)/shard_map/all_gather | solution.py:165
  233.7 14.9 %all_gather.58 = bf16[512,512]{1,0:T(8,128)(2,1)S(1)} all-gather(bf16[128,512]{1,0:T(8,128)(2,1)S(1)} %copy-done.35), channel_id=1, replica_groups=mesh['dp'=8,'shard'=4] {'shard'}, dimensions={0}, use_global_device_ids=true | all-gather | bytes 655360 | tf_op jit(solution)/shard_map/all_gather | solution.py:158
  251.2 8.0 %fusion.85 = f32[1024,2048]{1,0:T(8,128)} fusion(bf16[512,2048]{1,0:T(8,128)(2,1)} %all-gather.9.cloned.1.call-done, f32[1024,512]{0,1:T(8,128)} %copy-done.11, f32[512]{0:T(512)S(1)} %bitcast.232, f32[512]{0:T(512)S(1)} %bitcast.225, f32[1024]{0:T(1024)S(1)} %add_rsqrt_fusion, f32[1024]{0:T(1024)S(1)} %broadcast_multiply_fusion.4), kind=kOutput, calls=%fused_computation.146 | convolution fusion | flops 2150105088 | bytes 12595200 | tf_op jit(solution)/shard_map/dot_general | solution.py:191
  259.2 8.4 %add_convert_fusion = bf16[1024,512]{0,1:T(8,128)(2,1)S(1)} fusion(f32[1024,512]{0,1:T(8,128)} %copy-done.11, bf16[2048,512]{1,0:T(8,128)(2,1)} %all-gather.11.cloned.1.call-done, f32[512]{0:T(512)S(1)} %bitcast.234, f32[1024,2048]{1,0:T(8,128)} %fusion.85, f32[2048]{0:T(1024)S(1)} %bitcast.229), kind=kOutput, calls=%fused_computation.103 | convolution fusion | flops 2170028032 | bytes 13641728 | tf_op jit(solution)/shard_map/dot_general | solution.py:195
  270.3 3.7 convert_reduce_fusion.1
  277.4 11.3 %fusion.95 = (bf16[2048]{0:T(1024)(128)(2,1)}, bf16[1024,2048]{1,0:T(8,128)(2,1)S(1)}) fusion(f32[1024,2048]{1,0:T(8,128)} %fusion.85, f32[2048]{0:T(1024)S(1)} %bitcast.230, bf16[2048,512]{1,0:T(8,128)(2,1)} %all-gather.11.cloned.1.call-done, f32[1024,512]{1,0:T(8,128)} %get-tuple-element.362), kind=kOutput, calls=%fused_computation.156 | convolution fusion | flops 2194143232 | bytes 16789504 | tf_op jit(solution)/shard_map/dot_general | solution.py:226
  288.7 4.3 fusion.94
  304.8 105.3 %while.48 = (s32[]{:T(128)}, f32[1024,8,64]{0,2,1:T(8,128)}, f32[1024,8,64]{0,2,1:T(8,128)}, f32[1024,8,64]{0,2,1:T(8,128)}, bf16[2,512,8,64]{1,3,2,0:T(8,128)(2...) while((s32[]{:T(128)}, f32[1024,8,64]{0,2,1:T(8,128)}, ...), condition=%wide.region_16.17_spmd.clone, body=%wide.region_12.16_spmd.clone.sunk | while | flops 7028085248 | bytes 186163808 | solution.py:122
  310.3 3.8 multiply_convert_fusion.14
  314.1 5.0 convolution_bitcast_fusion.2
  322.7 5.2 fusion.230
  338.8 6.9 bitcast_add_fusion.7
  345.7 3.8 multiply_convert_fusion.15
  360.6 3.8 multiply_convert_fusion.14
  364.4 5.0 convolution_bitcast_fusion.2
  372.9 5.2 fusion.230
  385.9 4.7 fusion.234
  390.6 7.5 %bitcast_add_fusion.7 = f32[1024,8,64]{0,2,1:T(8,128)} fusion(f32[1024,8,64]{0,2,1:T(8,128)} %get-tuple-element.531, bf16[512,8,64]{0,2,1:T(8,128)(2,1)} %copy-done.15, bf16[1024,8,64]{0,2,1:T(8,128)(2,1)} %copy-done, f32[512,1024]{1,0:T(8,128)S(1)} %fusion.229, pred[]{:T(512)S(6)} %compare.3, bf16[1024,8,64]{0,2,1:T(8,128)(2,1)} %get-tuple-element.552, ...), kind=kOutput, calls=%fused_computation.33.clone.1 | convolution fusion | flops 1083179008 | bytes 8388613 | tf_op jit(solution)/shard_map/while/body/eval_jaxpr/while/body/eval_jaxpr/hts,thd->shd/dot_general | solution.py:87
  398.1 3.8 multiply_convert_fusion.15
  404.7 5.0 bitcast_add_fusion.6
  424.2 3.8 multiply_convert_fusion.7
  428.1 4.6 convolution_convert_fusion.3
  436.3 9.7 %convolution_convert_fusion.1 = bf16[2048,512]{1,0:T(8,128)(2,1)} fusion(f32[1024,512]{1,0:T(8,128)} %get-tuple-element.362, f32[1024,2048]{1,0:T(8,128)} %fusion.85, f32[2048]{0:T(1024)S(1)} %bitcast.231), kind=kOutput, calls=%fused_computation.81 | convolution fusion | flops 2170028032 | bytes 12591104 | tf_op jit(solution)/shard_map/dot_general | solution.py:225
  446.7 6.6 convolution_convert_fusion.2
  458.3 6.6 fusion.93
  475.2 9.9 %all-reduce.7 = (bf16[512]{0:T(512)(128)(2,1)S(1)}, bf16[512]{0:T(512)(128)(2,1)S(1)}, bf16[512]{0:T(512)(128)(2,1)S(1)}, bf16[512]{0:T(512)(128)(2,1)S(1)}, bf1...) all-reduce(bf16[512]{0:T(512)(128)(2,1)S(1)} %get-tuple-element.277, ...), channel_id=2, replica_groups=mesh['dp'=8,'shard'=4] {'shard'}, use_global_device_ids=true, to_apply=%region_20.21.clone | all-reduce | flops 4608 | bytes 18432
  485.6 7.0 reduce-scatter.13.cloned.1.call-done
  492.6 22.3 %reduce-scatter.11.cloned.1.call-done = bf16[128,512]{1,0:T(8,128)(2,1)} async-done(((bf16[512,512]{1,0:T(8,128)(2,1)}), bf16[128,512]{1,0:T(8,128)(2,1)}) %reduce-scatter.11.cloned.1.call-update) | async-done | bytes 131088 | tf_op jit(solution)/shard_map/reduce_scatter | solution.py:285
  514.9 22.3 %reduce-scatter.9.cloned.1.call-done = bf16[128,512]{1,0:T(8,128)(2,1)} async-done(((bf16[512,512]{1,0:T(8,128)(2,1)}), bf16[128,512]{1,0:T(8,128)(2,1)}) %reduce-scatter.9.cloned.1.call-update) | async-done | bytes 131088 | tf_op jit(solution)/shard_map/reduce_scatter | solution.py:282
  537.2 44.6 %reduce-scatter.21.cloned.1.call-done = bf16[512,512]{1,0:T(8,128)(2,1)} async-done(((bf16[2048,512]{1,0:T(8,128)(2,1)}), bf16[512,512]{1,0:T(8,128)(2,1)}) %reduce-scatter.21.cloned.1.call-update) | async-done | bytes 524304 | tf_op jit(solution)/shard_map/reduce_scatter | solution.py:309
  581.8 45.4 %reduce-scatter.19.cloned.1.call-done = bf16[128,2048]{1,0:T(8,128)(2,1)} async-done(((bf16[512,2048]{1,0:T(8,128)(2,1)}), bf16[128,2048]{1,0:T(8,128)(2,1)}) %reduce-scatter.19.cloned.1.call-update) | async-done | bytes 524304 | tf_op jit(solution)/shard_map/reduce_scatter | solution.py:303
  627.1 77.0 %all-reduce.9 = (f32[128]{0:T(128)}, f32[128]{0:T(128)}, f32[128,512]{1,0:T(8,128)}, f32[128,512]{1,0:T(8,128)}, f32[128,512]{1,0:T(8,128)}, /*index=5*/f32[128,...) all-reduce(f32[128]{0:T(128)S(1)} %dynamic-slice_convert_fusion.5, ...), channel_id=1, replica_groups=mesh['dp'=8,'shard'=4] {'dp'}, use_global_device_ids=true, to_apply=%region_21.22 | all-reduce | flops 885888 | bytes 5317632 | tf_op jit(solution)/shard_map/psum | solution.py:319
  (275 shorter events, 125.2 us)
Async XLA Ops:
  7.2 65.1 %copy-start.33 = (bf16[128,512]{1,0:T(8,128)(2,1)S(1)}, bf16[128,512]{1,0:T(8,128)(2,1)}, u32[]{:S(2)}) copy-start(bf16[128,512]{1,0:T(8,128)(2,1)} %param.26) | copy-start | bytes 393220
  7.2 81.0 %copy-start.34 = (bf16[128,512]{1,0:T(8,128)(2,1)S(1)}, bf16[128,512]{1,0:T(8,128)(2,1)}, u32[]{:S(2)}) copy-start(bf16[128,512]{1,0:T(8,128)(2,1)} %param.27) | copy-start | bytes 393220
  7.2 244.0 %all-gather.9.cloned.1.call-start = ((), (), s32[]{:S(2)}) async-start(), calls=%async_computation.8 | async-start | bytes 2621440 | tf_op jit(solution)/shard_map/all_gather | solution.py:161
  7.9 251.3 %all-gather.11.cloned.1.call-start = ((), (), s32[]{:S(2)}) async-start(), calls=%async_computation.9 | async-start | bytes 2621440 | tf_op jit(solution)/shard_map/all_gather | solution.py:163
  8.7 476.9 %reduce-scatter.23.cloned.1.call-start = ((), (), s32[]{:S(2)}) async-start(), calls=%async_computation.17 | async-start | bytes 327680 | tf_op jit(solution)/shard_map/reduce_scatter | solution.py:315
  21.5 89.0 %copy-start.39 = (f32[4,1,128]{2,1,0:T(1,128)}, f32[4,1,128]{2,1,0:T(1,128)S(1)}, u32[]{:S(2)}) copy-start(f32[4,1,128]{2,1,0:T(1,128)S(1)} %convert_element_type.250) | copy-start | bytes 6148
  29.3 81.2 %copy-start.43 = (f32[4,1,128]{2,1,0:T(1,128)}, f32[4,1,128]{2,1,0:T(1,128)S(1)}, u32[]{:S(2)}) copy-start(f32[4,1,128]{2,1,0:T(1,128)S(1)} %convert_element_type.251) | copy-start | bytes 6148
  109.6 139.1 %copy-start.2 = (bf16[1024,512]{0,1:T(8,128)(2,1)}, bf16[1024,512]{0,1:T(8,128)(2,1)S(1)}, u32[]{:S(2)}) copy-start(bf16[1024,512]{0,1:T(8,128)(2,1)S(1)} %copy.72) | copy-start | bytes 3145732
  110.5 6.1 copy-start.27
  128.6 50.1 %copy-start.56 = (bf16[128]{0:T(256)(128)(2,1)S(1)}, bf16[128]{0:T(256)(128)(2,1)}, u32[]{:S(2)}) copy-start(bf16[128]{0:T(256)(128)(2,1)} %param.29) | copy-start | bytes 772
  128.6 59.7 %copy-start.57 = (bf16[128]{0:T(256)(128)(2,1)S(1)}, bf16[128]{0:T(256)(128)(2,1)}, u32[]{:S(2)}) copy-start(bf16[128]{0:T(256)(128)(2,1)} %param.30) | copy-start | bytes 772
  128.6 67.2 %copy-start.53 = (bf16[512]{0:T(512)(128)(2,1)S(1)}, bf16[512]{0:T(512)(128)(2,1)}, u32[]{:S(2)}) copy-start(bf16[512]{0:T(512)(128)(2,1)} %param.32) | copy-start | bytes 3076
  128.6 67.2 %copy-start.58 = (bf16[128]{0:T(256)(128)(2,1)S(1)}, bf16[128]{0:T(256)(128)(2,1)}, u32[]{:S(2)}) copy-start(bf16[128]{0:T(256)(128)(2,1)} %param.34) | copy-start | bytes 772
  188.3 111.3 %copy-start.45 = (f32[4,1,128]{2,1,0:T(1,128)}, f32[4,1,128]{2,1,0:T(1,128)S(1)}, u32[]{:S(2)}) copy-start(f32[4,1,128]{2,1,0:T(1,128)S(1)} %convert_element_type.252) | copy-start | bytes 6148
  195.9 55.3 %copy-start.51 = (f32[4,1,128]{2,1,0:T(1,128)}, f32[4,1,128]{2,1,0:T(1,128)S(1)}, u32[]{:S(2)}) copy-start(f32[4,1,128]{2,1,0:T(1,128)S(1)} %convert_element_type.253) | copy-start | bytes 6148
  217.3 60.1 %copy-start.47 = (f32[4,1,512]{2,1,0:T(1,128)}, f32[4,1,512]{2,1,0:T(1,128)S(1)}, u32[]{:S(2)}) copy-start(f32[4,1,512]{2,1,0:T(1,128)S(1)} %convert_element_type.254) | copy-start | bytes 24580
  217.3 16.4 %copy-start.35 = (bf16[128,512]{1,0:T(8,128)(2,1)S(1)}, bf16[128,512]{1,0:T(8,128)(2,1)}, u32[]{:S(2)}) copy-start(bf16[128,512]{1,0:T(8,128)(2,1)} %param.28) | copy-start | bytes 393220
  219.9 29.5 %copy-start.19 = (bf16[64,8,2,512]{3,1,2,0:T(8,128)(2,1)}, bf16[64,8,2,512]{3,1,2,0:T(8,128)(2,1)S(1)}, u32[]{:S(2)}) copy-start(bf16[64,8,2,512]{3,1,2,0:T(8,128)(2,1)S(1)} %copy.94) | copy-start | bytes 3145732
  249.5 50.1 %copy-start.37 = (f32[1024]{0:T(1024)}, f32[1024]{0:T(1024)S(1)}, u32[]{:S(2)}) copy-start(f32[1024]{0:T(1024)S(1)} %broadcast_multiply_fusion.4) | copy-start | bytes 12292
  251.1 48.5 %copy-start.41 = (f32[1024]{0:T(1024)}, f32[1024]{0:T(1024)S(1)}, u32[]{:S(2)}) copy-start(f32[1024]{0:T(1024)S(1)} %add_rsqrt_fusion) | copy-start | bytes 12292
  274.0 211.6 %reduce-scatter.17.cloned.1.call-start = ((), (), s32[]{:S(2)}) async-start(), calls=%async_computation.14 | async-start | bytes 655360 | tf_op jit(solution)/shard_map/reduce_scatter | solution.py:294
  277.4 11.3 %copy-start.59 = (bf16[512,2048]{1,0:T(8,128)(2,1)S(1)}, bf16[512,2048]{1,0:T(8,128)(2,1)}, u32[]{:S(2)}) copy-start(bf16[512,2048]{1,0:T(8,128)(2,1)} %all-gather.9.cloned.1.call-done) | copy-start | bytes 6291460
  288.7 4.3 copy-start.62
  296.0 3.7 copy-start.16
  305.0 5.1 copy-start
  305.0 5.1 copy-start.4
  314.1 5.0 copy-start.6
  345.7 3.8 copy-start.7
  345.7 3.8 copy-start.23
  355.3 5.1 copy-start
  355.3 5.1 copy-start.4
  364.4 5.0 copy-start.6
  398.1 3.8 copy-start.7
  398.1 3.8 copy-start.23
  404.6 5.0 copy-start.24
  404.7 5.0 copy-start.1
  404.7 5.0 copy-start.5
  424.2 3.9 copy-start.3
  424.2 3.9 copy-start.30
  424.2 3.9 copy-start.32
  424.2 3.9 copy-start.40
  424.2 3.9 copy-start.44
  428.0 57.6 %reduce-scatter.15.cloned.1.call-start = ((), (), s32[]{:S(2)}) async-start(), calls=%async_computation.13 | async-start | bytes 655360 | tf_op jit(solution)/shard_map/reduce_scatter | solution.py:291
  434.2 58.4 %reduce-scatter.13.cloned.1.call-start = ((), (), s32[]{:S(2)}) async-start(), calls=%async_computation.12 | async-start | bytes 655360 | tf_op jit(solution)/shard_map/reduce_scatter | solution.py:288
  434.7 80.2 %reduce-scatter.11.cloned.1.call-start = ((), (), s32[]{:S(2)}) async-start(), calls=%async_computation.11 | async-start | bytes 655360 | tf_op jit(solution)/shard_map/reduce_scatter | solution.py:285
  435.5 101.7 %reduce-scatter.9.cloned.1.call-start = ((), (), s32[]{:S(2)}) async-start(), calls=%async_computation.10 | async-start | bytes 655360 | tf_op jit(solution)/shard_map/reduce_scatter | solution.py:282
  436.2 145.6 %reduce-scatter.21.cloned.1.call-start = ((), (), s32[]{:S(2)}) async-start(), calls=%async_computation.16 | async-start | bytes 2621440 | tf_op jit(solution)/shard_map/reduce_scatter | solution.py:309
  446.0 181.1 %reduce-scatter.19.cloned.1.call-start = ((), (), s32[]{:S(2)}) async-start(), calls=%async_computation.15 | async-start | bytes 2621440 | tf_op jit(solution)/shard_map/reduce_scatter | solution.py:303
  (38 other events, 79.3 us)
Sparse Core Ops, SparseCore 0:
  9.6 67.3 all-gather.8
  78.5 51.3 all-gather.10
  274.1 17.9 reduce-scatter.22
  428.1 19.8 reduce-scatter.16
  450.3 19.7 reduce-scatter.14
  472.3 20.2 reduce-scatter.12
  495.0 19.9 reduce-scatter.10
  517.3 19.8 reduce-scatter.8
  539.6 42.1 reduce-scatter.20
  583.9 43.1 reduce-scatter.18
where the time goes:
time: 717 us; the launch traced here: 711 us
  blocking collectives  254 us (35%)
  matrix products  198 us (28%)
  waiting for transfers between devices  145 us (20%)
  local copies, waits for them, and re-layouts  48.1 us (7%)
  other arithmetic  40.1 us (6%)
  between operations  16.2 us (2%)
  loops' own time  9.29 us (1%)
    psum x1, blocking collectives, on_device(): lax.psum((pieces[0], pieces[1], pieces[2], pieces[3], pieces[4], pieces[5...  77 us
    reduce_scatter x1, waiting for transfers between devices, on_device(): lax.psum_scatter(grads[9].astype(jnp.bfloat16), 'shard', scatter_dimensio...  45.4 us
    reduce_scatter x1, waiting for transfers between devices, on_device(): lax.psum_scatter(grads[11].astype(jnp.bfloat16), 'shard', scatter_dimensi...  44.6 us
    dot_general x4, matrix products, block_terms(): jnp.einsum('hts,shm->thm', scores, weights, preferred_element_type=jnp.fl...  27.1 us
    reduce_scatter x1, waiting for transfers between devices, on_device(): lax.psum_scatter(grads[3].astype(jnp.bfloat16), 'shard', scatter_dimensio...  22.3 us
    reduce_scatter x1, waiting for transfers between devices, on_device(): lax.psum_scatter(grads[2].astype(jnp.bfloat16), 'shard', scatter_dimensio...  22.3 us
    all_gather x1, blocking collectives, on_device(): lax.all_gather(w_key, 'shard', axis=0, tiled=True)  21.5 us
    all_gather x1, blocking collectives, on_device(): lax.all_gather(w_query, 'shard', axis=0, tiled=True)  21.4 us
  transfers between devices with their start and end apart: 10, of which 5 were waited for; matrix products, arithmetic and copies ran while one was open for 38% of the time, Pallas kernels for 0%

commit v1 on v0

v1 whole, which is shorter than its diff:
```python
import jax
import jax.numpy as jnp
from jax import lax
from jax.experimental import pallas as pl
from jax.experimental.pallas import tpu as pltpu
from jax.sharding import PartitionSpec as P

EPS = 1e-05
WIDTH = 512
HEAD = 64
FF = 2048
VOCAB = 256
SEQ_LEN = 1024
CHUNK = 256
HALF = 256
PIECE = 16
COLS_PROJ = 4 * HALF
COLS_UP = WIDTH + FF
COLS_DOWN = 4 * WIDTH + VOCAB
F32 = jnp.float32
BF16 = jnp.bfloat16
MIB = 1024 * 1024


def nn(a, b):
    return lax.dot_general(a, b, (((1,), (0,)), ((), ())), preferred_element_type=F32)


def nt(a, b):
    return lax.dot_general(a, b, (((1,), (1,)), ((), ())), preferred_element_type=F32)


def tn(a, b):
    return lax.dot_general(a, b, (((0,), (0,)), ((), ())), preferred_element_type=F32)


def norm_parts(values):
    centre = values - jnp.mean(values, axis=-1, keepdims=True)
    inverse = lax.rsqrt(jnp.mean(centre * centre, axis=-1, keepdims=True) + EPS)
    return centre * inverse, inverse


def norm_pull(grad, unit, inverse, gain):
    scaled = grad * gain
    return inverse * (
        scaled
        - jnp.mean(scaled, axis=-1, keepdims=True)
        - unit * jnp.mean(scaled * unit, axis=-1, keepdims=True)
    )


def vector_of(vec_ref, idx, row):
    return jnp.concatenate(
        [vec_ref[s ^ idx[2], row : row + 1, :].astype(F32) for s in range(4)], axis=1
    )


def bias_up_of(vec_ref, idx):
    return jnp.concatenate(
        [
            vec_ref[s ^ idx[2], row : row + 1, :].astype(F32)
            for s in range(4)
            for row in range(5, 9)
        ],
        axis=1,
    )


def each_piece(idx, near, far):
    for c, buf in ((0, near), (1, far)):
        for xy in range(4):
            member = ((xy ^ idx[1]) * 2) + (c ^ idx[0])
            for s in range(4):
                yield s ^ idx[2], member, buf.at[xy, s]


def rows_at(start, size):
    return pl.ds(pl.multiple_of(start, PIECE), size)


def put_parts(idx, keep, send, tile, shard, columns):
    for xy in range(4):
        first = tile[32 * xy : 32 * xy + 16]
        second = tile[32 * xy + 16 : 32 * xy + 32]
        own_first = idx[0] == 0
        keep[xy ^ idx[1], shard ^ idx[2], :, columns] = jnp.where(own_first, first, second)
        send[xy ^ idx[1], shard ^ idx[2], :, columns] = jnp.where(own_first, second, first)


def pack_kernel(idx, wq, wk, wv, wc, wm, wu, wd, wr, pa, pb, pc, pd):
    member = idx[1] * 2 + idx[0]
    rows = rows_at(member * PIECE, PIECE)
    for j, w in enumerate((wq, wk, wv, wc)):
        pa[:, j * HALF : (j + 1) * HALF] = w[rows, :HALF]
        pb[:, j * HALF : (j + 1) * HALF] = w[rows, HALF:]
    pc[:, :WIDTH] = wm[rows, :]
    pc[:, WIDTH:] = wu[rows, :]
    for i in range(4):
        pd[:, i * WIDTH : (i + 1) * WIDTH] = wd[rows_at(member * 64 + 16 * i, PIECE), :]
    pd[:, 4 * WIDTH :] = wr[rows, :]


def first_norm_kernel(idx, vec, x, a1, a1t):
    unit, _ = norm_parts(x[...].astype(F32))
    low = (unit * vector_of(vec, idx, 0) + vector_of(vec, idx, 1)).astype(BF16)
    a1[...] = low
    a1t[...] = low.T


def lanes_low():
    return lax.broadcasted_iota(jnp.int32, (1, 128), 1) < HEAD


def spread(value):
    low = lanes_low().astype(F32).astype(BF16)
    high = (1.0 - lanes_low().astype(F32)).astype(BF16)
    return jnp.concatenate([value * low, value * high], axis=0)


def join(value):
    return jnp.where(lanes_low(), value[:CHUNK], value[CHUNK:])


def head_sum(value):
    low = lanes_low()
    first = jnp.sum(jnp.where(low, value, 0.0), axis=-1, keepdims=True)
    second = jnp.sum(jnp.where(low, 0.0, value), axis=-1, keepdims=True)
    return jnp.where(low, first, second)


def head_max(value):
    low = lanes_low()
    first = jnp.max(jnp.where(low, value, -jnp.inf), axis=-1, keepdims=True)
    second = jnp.max(jnp.where(low, -jnp.inf, value), axis=-1, keepdims=True)
    return jnp.where(low, first, second)


def same_head():
    row = lax.broadcasted_iota(jnp.int32, (128, 128), 0) < HEAD
    col = lax.broadcasted_iota(jnp.int32, (128, 128), 1) < HEAD
    return row == col


def causal_mask(rows, transposed=False):
    row = lax.broadcasted_iota(jnp.int32, (rows, CHUNK), 0) & (CHUNK - 1)
    col = lax.broadcasted_iota(jnp.int32, (rows, CHUNK), 1)
    return (row <= col) if transposed else (col <= row)


def attend_kernel(
    idx, a1, near, far,
    q_o, k_o, v_o, e_o, x_o, p_o, s_o, z_o, r_o, o_o, kept_s, kept_u, w_o,
    state_s, state_u, count_z,
):
    step = pl.program_id(0)

    @pl.when(step == 0)
    def _():
        for shard, member, piece in each_piece(idx, near, far):
            w_o[rows_at(shard * 128 + member * PIECE, PIECE), :] = piece[...]
        state_s[...] = jnp.zeros_like(state_s)
        state_u[...] = jnp.zeros_like(state_u)
        count_z[...] = jnp.zeros_like(count_z)

    a = a1[...]
    q_o[...] = nn(a, w_o[:, :HALF]).astype(BF16)
    k_o[...] = nn(a, w_o[:, HALF : 2 * HALF]).astype(BF16)
    v_o[...] = nn(a, w_o[:, 2 * HALF : 3 * HALF]).astype(BF16)
    expo = jnp.exp(nn(a, w_o[:, 3 * HALF :]))
    x_o[...] = expo
    e_o[...] = expo.astype(BF16)
    tri = causal_mask(2 * CHUNK)
    total = nn(tri[:CHUNK].astype(F32).astype(BF16), e_o[...]) + count_z[...]
    count_z[...] = total[CHUNK - 1 :, :]
    inverse = 1.0 / total
    z_o[...] = inverse
    for pair in range(2):
        at = slice(128 * pair, 128 * pair + 128)
        q, k, v, e = q_o[:, at], k_o[:, at], v_o[:, at], e_o[:, at]
        inv = inverse[:, at]
        low_s = state_s[pair].astype(BF16)
        low_u = state_u[pair].astype(BF16)
        kept_s[0, pair] = low_s
        kept_u[0, pair] = low_u
        scores = jnp.where(tri, nt(spread(q), k), 0.0).astype(BF16)
        numer = join(nn(scores, e)) + nn(q, low_s)
        logits = (HEAD ** -0.5) * numer * inv
        expd = jnp.exp(logits - head_max(logits))
        probs = expd / head_sum(expd)
        ratio = (probs * inv).astype(BF16)
        mixing = jnp.where(tri, nt(spread(ratio), e), 0.0).astype(BF16)
        o_o[:, at] = (join(nn(mixing, v)) + nn(ratio, low_u)).astype(BF16)
        s_o[:, at] = logits
        p_o[:, at] = probs
        r_o[:, at] = ratio
        block = same_head()
        state_s[pair] += jnp.where(block, tn(k, e), 0.0)
        state_u[pair] += jnp.where(block, tn(e, v), 0.0)


def feed_kernel(
    idx, vec, x, o0, o1, target, up_near, up_far, down_near, down_far,
    out_o, h_o, slope_o, dy_o, bias_o, keep, send,
    w_mix, w_up, w_down, w_read, act_s, out_s, dl_s, df_s,
):
    step = pl.program_id(0)

    @pl.when(step == 0)
    def _():
        for shard, member, piece in each_piece(idx, up_near, up_far):
            rows = rows_at(shard * 128 + member * PIECE, PIECE)
            w_mix[rows, :] = piece[:, :WIDTH]
            w_up[rows, :] = piece[:, WIDTH:]
        for shard, member, piece in each_piece(idx, down_near, down_far):
            for i in range(4):
                rows = rows_at(shard * 512 + member * 64 + 16 * i, PIECE)
                w_down[rows, :] = piece[:, i * WIDTH : (i + 1) * WIDTH]
            w_read[rows_at(shard * 128 + member * PIECE, PIECE), :] = piece[:, 4 * WIDTH :]
        bias_o[...] = jnp.zeros_like(bias_o)

    rows = pl.ds(pl.multiple_of(step * CHUNK, CHUNK), CHUNK)
    attn = nn(o0[...], w_mix[:HALF, :]) + nn(o1[...], w_mix[HALF:, :])
    resid = x[...].astype(F32) + attn
    h_o[...] = resid
    unit, _ = norm_parts(resid)
    second = (unit * vector_of(vec, idx, 2) + vector_of(vec, idx, 3)).astype(BF16)
    bias = bias_up_of(vec, idx)
    branch = jnp.zeros((CHUNK, WIDTH), F32)
    scale = (2.0 / jnp.pi) ** 0.5
    for j in range(4):
        at = slice(512 * j, 512 * j + 512)
        z = nn(second, w_up[:, at]) + bias[:, at]
        zz = z * z
        t = jnp.tanh(scale * z * (1.0 + 0.044715 * zz))
        cdf = 0.5 * (1.0 + t)
        act = (z * cdf).astype(BF16)
        slope_o[:, at] = cdf + 0.5 * z * (1.0 - t * t) * (scale * (1.0 + 3 * 0.044715 * zz))
        act_s[rows, at] = act
        branch += nn(act, w_down[at, :])
    out = (resid + (branch + vector_of(vec, idx, 4))).astype(BF16)
    out_o[...] = out
    out_s[rows, :] = out
    logits = nn(out, w_read[...])
    expd = jnp.exp(logits - jnp.max(logits, axis=-1, keepdims=True))
    soft = expd / jnp.sum(expd, axis=-1, keepdims=True)
    classes = lax.broadcasted_iota(jnp.int32, (CHUNK, VOCAB), 1)
    dl = (soft - jnp.where(classes == target[...], 1.0, 0.0)).astype(BF16)
    dl_s[rows, :] = dl
    dy = nt(dl, w_read[...])
    dy_o[...] = dy
    df = dy.astype(BF16)
    df_s[rows, :] = df
    bias_o[...] += jnp.sum(df.astype(F32), axis=0, keepdims=True)

    @pl.when(step == pl.num_programs(0) - 1)
    def _():
        for shard in range(4):
            tile = tn(out_s[:, shard * 128 : shard * 128 + 128], dl_s[...]).astype(BF16)
            put_parts(idx, keep, send, tile, shard, slice(4 * WIDTH, None))
            for xy in range(4):
                start = shard * 512 + xy * 128
                tile = tn(act_s[:, start : start + 128], df_s[...]).astype(BF16)
                own_first = idx[0] == 0
                for i in range(4):
                    first = tile[16 * i : 16 * i + 16]
                    later = tile[64 + 16 * i : 64 + 16 * i + 16]
                    at = slice(i * WIDTH, (i + 1) * WIDTH)
                    keep[xy ^ idx[1], shard ^ idx[2], :, at] = jnp.where(own_first, first, later)
                    send[xy ^ idx[1], shard ^ idx[2], :, at] = jnp.where(own_first, later, first)


def feed_back_kernel(
    idx, vec, h, slope, dy, o0, o1, up_near, up_far, down_near, down_far,
    dh_o, do_o, gain_o, shift_o, bias_o, keep, send,
    w_mix, w_up, w_down, dz_s, a2_s, da_s,
):
    step = pl.program_id(0)

    @pl.when(step == 0)
    def _():
        for shard, member, piece in each_piece(idx, up_near, up_far):
            rows = rows_at(shard * 128 + member * PIECE, PIECE)
            w_mix[rows, :] = piece[:, :WIDTH]
            w_up[rows, :] = piece[:, WIDTH:]
        for shard, member, piece in each_piece(idx, down_near, down_far):
            for i in range(4):
                rows = rows_at(shard * 512 + member * 64 + 16 * i, PIECE)
                w_down[rows, :] = piece[:, i * WIDTH : (i + 1) * WIDTH]
        gain_o[...] = jnp.zeros_like(gain_o)
        shift_o[...] = jnp.zeros_like(shift_o)
        bias_o[...] = jnp.zeros_like(bias_o)

    rows = pl.ds(pl.multiple_of(step * CHUNK, CHUNK), CHUNK)
    gain = vector_of(vec, idx, 2)
    unit, inverse = norm_parts(h[...])
    a2_s[rows, :] = (unit * gain + vector_of(vec, idx, 3)).astype(BF16)
    d_out = dy[...]
    df = d_out.astype(BF16)
    d_second = jnp.zeros((CHUNK, WIDTH), F32)
    for j in range(4):
        at = slice(512 * j, 512 * j + 512)
        dz = (nt(df, w_down[at, :]) * slope[:, at]).astype(BF16)
        dz_s[rows, at] = dz
        bias_o[:, at] += jnp.sum(dz.astype(F32), axis=0, keepdims=True)
        d_second += nt(dz, w_up[:, at])
    gain_o[...] += jnp.sum(d_second * unit, axis=0, keepdims=True)
    shift_o[...] += jnp.sum(d_second, axis=0, keepdims=True)
    dh = d_out + norm_pull(d_second, unit, inverse, gain)
    dh_o[...] = dh
    da = dh.astype(BF16)
    da_s[rows, :] = da
    do_o[...] = nt(da, w_mix[...]).astype(BF16)

    @pl.when(step == pl.num_programs(0) - 1)
    def _():
        for shard in range(4):
            half = (o0, o1)[shard // 2]
            start = (shard % 2) * 128
            tile = tn(half[:, start : start + 128], da_s[...]).astype(BF16)
            put_parts(idx, keep, send, tile, shard, slice(0, WIDTH))
            for j in range(4):
                tile = tn(
                    a2_s[:, shard * 128 : shard * 128 + 128], dz_s[:, 512 * j : 512 * j + 512]
                ).astype(BF16)
                at = slice(WIDTH + 512 * j, WIDTH + 512 * j + 512)
                put_parts(idx, keep, send, tile, shard, at)


def attend_back_kernel(
    idx, a1t, q_i, k_i, v_i, e_i, x_i, p_i, s_i, z_i, r_i, do_i, kept_s, kept_u,
    dx_o, keep, send,
    state_r, state_t, count_z, dx_s,
):
    step = pl.program_id(0)
    chunk = pl.num_programs(0) - 1 - step

    @pl.when(step == 0)
    def _():
        state_r[...] = jnp.zeros_like(state_r)
        state_t[...] = jnp.zeros_like(state_t)
        count_z[...] = jnp.zeros_like(count_z)

    rows = pl.ds(pl.multiple_of(chunk * CHUNK, CHUNK), CHUNK)
    tri = causal_mask(2 * CHUNK)
    trt = causal_mask(2 * CHUNK, True)
    later = trt[:CHUNK].astype(F32).astype(BF16)
    for pair in range(2):
        at = slice(128 * pair, 128 * pair + 128)
        q, k, v, e = q_i[:, at], k_i[:, at], v_i[:, at], e_i[:, at]
        ratio, do = r_i[:, at], do_i[:, at]
        probs, logits, inv = p_i[:, at], s_i[:, at], z_i[:, at]
        low_s, low_u = kept_s[0, pair], kept_u[0, pair]
        low_r = state_r[pair].astype(BF16)
        low_t = state_t[pair].astype(BF16)
        d_mix = jnp.where(tri, nt(spread(do), v), 0.0).astype(BF16)
        d_ratio = (join(nn(d_mix, e)) + nt(do, low_u)) * inv
        d_logits = probs * (d_ratio - head_sum(d_ratio * probs))
        d_numer = ((HEAD ** -0.5) * d_logits * inv).astype(BF16)
        d_total = (-d_ratio * (probs * inv) - d_logits * logits * inv).astype(BF16)
        d_scores = jnp.where(tri, nt(spread(d_numer), e), 0.0).astype(BF16)
        dq = join(nn(d_scores, k)) + nt(d_numer, low_s)
        scores = jnp.where(trt, nt(spread(k), q), 0.0).astype(BF16)
        wide_e = spread(e)
        mixing = jnp.where(trt, nt(wide_e, ratio), 0.0).astype(BF16)
        d_mix_t = jnp.where(trt, nt(spread(v), do), 0.0).astype(BF16)
        d_scores_t = jnp.where(trt, nt(wide_e, d_numer), 0.0).astype(BF16)
        dv = join(nn(mixing, do)) + nn(e, low_r)
        dk = join(nn(d_scores_t, q)) + nt(e, low_t)
        total_z = nn(later, d_total) + count_z[:, at]
        count_z[:, at] = total_z[:1, :]
        de = join(nn(d_mix_t, ratio) + nn(scores, d_numer)) + nt(v, low_r) + nn(k, low_t) + total_z
        dc = de * x_i[:, at]
        for j, value in enumerate((dq, dk, dv, dc)):
            dx_o[:, j * HALF + 128 * pair : j * HALF + 128 * pair + 128] = value.astype(BF16)
        block = same_head()
        state_r[pair] += jnp.where(block, tn(ratio, do), 0.0)
        state_t[pair] += jnp.where(block, tn(q, d_numer), 0.0)
    dx_s[rows, :] = dx_o[...]

    @pl.when(step == pl.num_programs(0) - 1)
    def _():
        for shard in range(4):
            for j in range(4):
                at = slice(j * HALF, (j + 1) * HALF)
                tile = nn(a1t[shard * 128 : shard * 128 + 128, :], dx_s[:, at]).astype(BF16)
                put_parts(idx, keep, send, tile, shard, at)


def inputs_kernel(idx, vec, x, dh, dx0, dx1, w0, w1, g_bd, g_g2, g_b2, g_bu, dx_o, vec_o, gain, shift):
    step = pl.program_id(0)

    @pl.when(step == 0)
    def _():
        gain[...] = jnp.zeros_like(gain)
        shift[...] = jnp.zeros_like(shift)

    unit, inverse = norm_parts(x[...].astype(F32))
    d_first = nt(dx0[...], w0[...]) + nt(dx1[...], w1[...])
    gain[...] += jnp.sum(d_first * unit, axis=0, keepdims=True)
    shift[...] += jnp.sum(d_first, axis=0, keepdims=True)
    dx_o[...] = dh[...] + norm_pull(d_first, unit, inverse, vector_of(vec, idx, 0))

    @pl.when(step == pl.num_programs(0) - 1)
    def _():
        for s in range(4):
            at = slice(128 * s, 128 * s + 128)
            rows = [gain[:, at], shift[:, at], g_g2[:, at], g_b2[:, at], g_bd[:, at]]
            rows += [g_bu[:, 512 * s + 128 * j : 512 * s + 128 * j + 128] for j in range(4)]
            rows.append(jnp.zeros((7, 128), F32))
            vec_o[s ^ idx[2]] = jnp.concatenate(rows, axis=0)


def unpack_proj_kernel(idx, *refs):
    first, second, outs = refs[:8], refs[8:16], refs[16:]
    member = idx[1] * 2 + idx[0]
    for k in range(8):
        rows = rows_at((member ^ k) * PIECE, PIECE)
        for j, out in enumerate(outs):
            at = slice(j * HALF, (j + 1) * HALF)
            out[rows, :HALF] = first[k][:, at].astype(F32)
            out[rows, HALF:] = second[k][:, at].astype(F32)


def unpack_up_kernel(idx, *refs):
    pieces, (mix, up) = refs[:8], refs[8:]
    member = idx[1] * 2 + idx[0]
    for k in range(8):
        rows = rows_at((member ^ k) * PIECE, PIECE)
        mix[rows, :] = pieces[k][:, :WIDTH].astype(F32)
        up[rows, :] = pieces[k][:, WIDTH:].astype(F32)


def unpack_down_kernel(idx, *refs):
    pieces, (down, read) = refs[:8], refs[8:]
    member = idx[1] * 2 + idx[0]
    for k in range(8):
        other = member ^ k
        for i in range(4):
            at = slice(i * WIDTH, (i + 1) * WIDTH)
            down[rows_at(other * 64 + 16 * i, PIECE), :] = pieces[k][:, at].astype(F32)
        read[rows_at(other * PIECE, PIECE), :] = pieces[k][:, 4 * WIDTH :].astype(F32)


def shaped(shape, dtype):
    return jax.ShapeDtypeStruct(shape, dtype)


def call(kernel, name, args, outs, steps=None, scratch=(), flops=0, limit=56):
    grid = (steps,) if steps else ()

    def spec(shape, block):
        if block is None:
            return pl.BlockSpec(tuple(shape), lambda *_: (0,) * len(shape))
        return pl.BlockSpec(*block)

    in_specs = []
    for array, block in args:
        if array.dtype == jnp.int32 and array.shape == (3,):
            in_specs.append(pl.BlockSpec(memory_space=pltpu.SMEM))
        else:
            in_specs.append(spec(array.shape, block))
    moved = sum(a.size * a.dtype.itemsize for a, _ in args)
    return pl.pallas_call(
        kernel,
        grid=grid,
        in_specs=in_specs,
        out_specs=[spec(shape, block) for shape, _, block in outs],
        out_shape=[shaped(shape, dtype) for shape, dtype, _ in outs],
        scratch_shapes=list(scratch),
        compiler_params=pltpu.CompilerParams(
            vmem_limit_bytes=limit * MIB,
            dimension_semantics=("arbitrary",) * len(grid) if grid else None,
        ),
        cost_estimate=pl.CostEstimate(flops=int(flops), bytes_accessed=int(moved), transcendentals=0),
        name=name,
    )(*[array for array, _ in args])


def swap(value, axis, size, distance):
    return lax.ppermute(value, axis, [(i, i ^ distance) for i in range(size)])


def gather_pieces(piece, dp, shards):
    rows = jnp.stack([piece] + [swap(piece, "shard", shards, k) for k in range(1, 4)])
    near = jnp.stack([rows] + [swap(rows, "dp", dp, 2 * k) for k in range(1, 4)])
    return near, swap(near, "dp", dp, 1)


def reduce_pieces(keep, send, dp, shards):
    got = swap(send, "dp", dp, 1)
    part = [(keep[k].astype(F32) + got[k].astype(F32)).astype(BF16) for k in range(4)]
    got = [swap(part[k], "dp", dp, 2 * k) for k in range(1, 4)]
    rows = [
        (
            (part[0][k].astype(F32) + got[0][k].astype(F32))
            + (got[1][k].astype(F32) + got[2][k].astype(F32))
        ).astype(BF16)
        for k in range(4)
    ]
    got = [swap(rows[k], "shard", shards, k) for k in range(1, 4)]
    total = (
        (rows[0].astype(F32) + got[0].astype(F32)) + (got[1].astype(F32) + got[2].astype(F32))
    ).astype(BF16)
    distance = 8
    while distance < dp:
        total = (total.astype(F32) + swap(total, "dp", dp, distance).astype(F32)).astype(BF16)
        distance *= 2
    return [total] + [swap(total, "dp", dp, k) for k in range(1, 8)]


def reduce_vectors(block, dp, shards):
    got = [swap(block[k], "shard", shards, k) for k in range(1, 4)]
    total = (block[0] + got[0]) + (got[1] + got[2])
    got = [total] + [swap(total, "dp", dp, k) for k in range(1, 8)]
    total = ((got[0] + got[1]) + (got[2] + got[3])) + ((got[4] + got[5]) + (got[6] + got[7]))
    distance = 8
    while distance < dp:
        total = total + swap(total, "dp", dp, distance)
        distance *= 2
    return total


def body(dp, shards):
    def on_device(
        tokens, targets, gain_one, bias_one, w_query, w_key, w_value, w_control, w_mix,
        gain_two, bias_two, w_up, bias_up, w_down, bias_down, w_read,
    ):
        count = tokens.shape[0]
        steps = count // CHUNK
        member = lax.axis_index("dp") % 8
        idx = jnp.stack([member % 2, member // 2, lax.axis_index("shard")]).astype(jnp.int32)

        own = jnp.concatenate(
            [
                jnp.stack([gain_one, bias_one, gain_two, bias_two, bias_down]),
                bias_up.reshape(4, 128),
                jnp.zeros((7, 128), BF16),
            ]
        )
        vec = jnp.stack([own] + [swap(own, "shard", shards, k) for k in range(1, 4)])
        weights = (w_query, w_key, w_value, w_control, w_mix, w_up, w_down, w_read)
        packed = call(
            pack_kernel,
            "pack_weights",
            [(idx, None)] + [(w, None) for w in weights],
            [((PIECE, n), BF16, None) for n in (COLS_PROJ, COLS_PROJ, COLS_UP, COLS_DOWN)],
            limit=16,
        )
        proj0, proj1, up, down = [gather_pieces(p, dp, shards) for p in packed]

        a1, a1t = call(
            first_norm_kernel,
            "first_norm",
            [(idx, None), (vec, None), (tokens, None)],
            [((count, WIDTH), BF16, None), ((WIDTH, count), BF16, None)],
            limit=24,
        )

        forward = lambda i: (i, 0)
        tok = lambda n: ((CHUNK, n), forward)
        kept = ((1, 2, 128, 128), lambda i: (i, 0, 0, 0))
        halves = []
        for bufs in (proj0, proj1):
            names = [((count, HALF), t, tok(HALF)) for t in (BF16,) * 4 + (F32,) * 4 + (BF16,) * 2]
            states = [((steps, 2, 128, 128), BF16, kept)] * 2
            halves.append(
                call(
                    attend_kernel,
                    "attend",
                    [(idx, None), (a1, tok(WIDTH)), (bufs[0], None), (bufs[1], None)],
                    names + states + [((WIDTH, COLS_PROJ), BF16, None)],
                    steps,
                    [
                        pltpu.VMEM((2, 128, 128), F32),
                        pltpu.VMEM((2, 128, 128), F32),
                        pltpu.VMEM((1, HALF), F32),
                    ],
                    flops=6e9,
                )
            )
        o0, o1 = halves[0][9], halves[1][9]

        parts = (4, 4, PIECE)
        out, h, slope, dy, g_bias_down, keep_down, send_down = call(
            feed_kernel,
            "feed_forward",
            [
                (idx, None), (vec, None), (tokens, tok(WIDTH)), (o0, tok(HALF)), (o1, tok(HALF)),
                (targets.reshape(count, 1), tok(1)),
                (up[0], None), (up[1], None), (down[0], None), (down[1], None),
            ],
            [
                ((count, WIDTH), BF16, tok(WIDTH)),
                ((count, WIDTH), F32, tok(WIDTH)),
                ((count, FF), F32, tok(FF)),
                ((count, WIDTH), F32, tok(WIDTH)),
                ((1, WIDTH), F32, None),
                (parts + (COLS_DOWN,), BF16, None),
                (parts + (COLS_DOWN,), BF16, None),
            ],
            steps,
            [
                pltpu.VMEM((WIDTH, WIDTH), BF16),
                pltpu.VMEM((WIDTH, FF), BF16),
                pltpu.VMEM((FF, WIDTH), BF16),
                pltpu.VMEM((WIDTH, VOCAB), BF16),
                pltpu.VMEM((count, FF), BF16),
                pltpu.VMEM((count, WIDTH), BF16),
                pltpu.VMEM((count, VOCAB), BF16),
                pltpu.VMEM((count, WIDTH), BF16),
            ],
            flops=8e9,
        )
        pieces_down = reduce_pieces(keep_down, send_down, dp, shards)

        dh, d_mixed, g_gain_two, g_bias_two, g_bias_up, keep_up, send_up = call(
            feed_back_kernel,
            "feed_backward",
            [
                (idx, None), (vec, None), (h, tok(WIDTH)), (slope, tok(FF)), (dy, tok(WIDTH)),
                (o0, None), (o1, None),
                (up[0], None), (up[1], None), (down[0], None), (down[1], None),
            ],
            [
                ((count, WIDTH), F32, tok(WIDTH)),
                ((count, WIDTH), BF16, tok(WIDTH)),
                ((1, WIDTH), F32, None),
                ((1, WIDTH), F32, None),
                ((1, FF), F32, None),
                (parts + (COLS_UP,), BF16, None),
                (parts + (COLS_UP,), BF16, None),
            ],
            steps,
            [
                pltpu.VMEM((WIDTH, WIDTH), BF16),
                pltpu.VMEM((WIDTH, FF), BF16),
                pltpu.VMEM((FF, WIDTH), BF16),
                pltpu.VMEM((count, FF), BF16),
                pltpu.VMEM((count, WIDTH), BF16),
                pltpu.VMEM((count, WIDTH), BF16),
            ],
            flops=8e9,
        )
        pieces_up = reduce_pieces(keep_up, send_up, dp, shards)

        back = lambda i: (steps - 1 - i, 0)
        kept_back = ((1, 2, 128, 128), lambda i: (steps - 1 - i, 0, 0, 0))
        d_proj, pieces_proj = [], []
        for half in range(2):
            q, k, v, e, x, p, s, z, r, _, ks, ku, w = halves[half]
            tb = ((CHUNK, HALF), back)
            column = ((CHUNK, HALF), lambda i, half=half: (steps - 1 - i, half))
            dx, keep, send = call(
                attend_back_kernel,
                "attend_backward",
                [(idx, None), (a1t, None)]
                + [(t, tb) for t in (q, k, v, e, x, p, s, z, r)]
                + [(d_mixed, column), (ks, kept_back), (ku, kept_back)],
                [
                    ((count, COLS_PROJ), BF16, ((CHUNK, COLS_PROJ), back)),
                    (parts + (COLS_PROJ,), BF16, None),
                    (parts + (COLS_PROJ,), BF16, None),
                ],
                steps,
                [
                    pltpu.VMEM((2, 128, 128), F32),
                    pltpu.VMEM((2, 128, 128), F32),
                    pltpu.VMEM((1, HALF), F32),
                    pltpu.VMEM((count, COLS_PROJ), BF16),
                ],
                flops=10e9,
            )
            d_proj.append(dx)
            pieces_proj.append(reduce_pieces(keep, send, dp, shards))

        d_tokens, block = call(
            inputs_kernel,
            "input_gradient",
            [
                (idx, None), (vec, None), (tokens, tok(WIDTH)), (dh, tok(WIDTH)),
                (d_proj[0], tok(COLS_PROJ)), (d_proj[1], tok(COLS_PROJ)),
                (halves[0][12], None), (halves[1][12], None),
                (g_bias_down, None), (g_gain_two, None), (g_bias_two, None), (g_bias_up, None),
            ],
            [((count, WIDTH), F32, tok(WIDTH)), ((4, 16, 128), F32, None)],
            steps,
            [pltpu.VMEM((1, WIDTH), F32), pltpu.VMEM((1, WIDTH), F32)],
            flops=3e9,
            limit=32,
        )
        vectors = reduce_vectors(block, dp, shards)

        rows = WIDTH // shards
        g_down, g_read = call(
            unpack_down_kernel,
            "unpack_down",
            [(idx, None)] + [(p, None) for p in pieces_down],
            [((4 * rows, WIDTH), F32, None), ((rows, VOCAB), F32, None)],
            limit=16,
        )
        g_mix, g_up = call(
            unpack_up_kernel,
            "unpack_up",
            [(idx, None)] + [(p, None) for p in pieces_up],
            [((rows, WIDTH), F32, None), ((rows, FF), F32, None)],
            limit=16,
        )
        g_query, g_key, g_value, g_control = call(
            unpack_proj_kernel,
            "unpack_proj",
            [(idx, None)] + [(p, None) for p in pieces_proj[0] + pieces_proj[1]],
            [((rows, WIDTH), F32, None)] * 4,
            limit=16,
        )
        return (
            out, d_tokens, vectors[0], vectors[1], g_query, g_key, g_value, g_control, g_mix,
            vectors[2], vectors[3], g_up, vectors[5:9].reshape(512), g_down, vectors[4], g_read,
        )

    return on_device


def solution(mesh):
    dp, shards = mesh.shape["dp"], mesh.shape["shard"]
    vector, matrix = P("shard"), P("shard", None)
    rows = P(("dp", "shard"), None)
    params = (
        vector, vector, matrix, matrix, matrix, matrix, matrix,
        vector, vector, matrix, vector, matrix, vector, matrix,
    )
    return jax.shard_map(
        body(dp, shards),
        mesh=mesh,
        in_specs=(rows, P(("dp", "shard"))) + params,
        out_specs=(rows, rows) + params,
        check_vma=False,
    )
```

time: 717 us -> 310 us (0.43)
  blocking collectives: 254 us -> 0 us
  matrix products: 198 us -> 0 us
  starting transfers between devices: 0.8 us -> 122 us
  Pallas kernels: 0 us -> 108 us
  waiting for transfers between devices: 145 us -> 60.5 us
  other arithmetic: 40.1 us -> 2.32 us
  local copies, waits for them, and re-layouts: 48.1 us -> 16 us
  between operations: 16.2 us -> 1.43 us
  loops' own time: 9.29 us -> 0 us
    dot_general x39 -> x0, matrix products: 189 us -> none  [the longest x4 27.1 us: block_terms(): jnp.einsum('hts,shm->thm', scores, weights, preferred_element_type=jnp.fl...]
    all_gather x12 -> x0, blocking collectives: 167 us -> none  [the longest x1 21.5 us: on_device(): lax.all_gather(w_key, 'shard', axis=0, tiled=True)]
    reduce_scatter x8 -> x0, waiting for transfers between devices: 142 us -> none  [the longest x1 45.4 us: on_device(): lax.psum_scatter(grads[9].astype(jnp.bfloat16), 'shard', scatter_dimensio...]
    ppermute x0 -> x97, starting transfers between devices: none -> 122 us  [swap(): return lax.ppermute(value, axis, [(i, i ^ distance) for i in range(size)])]
    pallas_call x0 -> x12, Pallas kernels: none -> 108 us  [call(): pl.pallas_call(kernel, grid=grid, in_specs=in_specs, out_specs=[spec(shap...]
    psum x1 -> x0, blocking collectives: 77 us -> none  [on_device(): lax.psum((pieces[0], pieces[1], pieces[2], pieces[3], pieces[4], pieces[5...]
    ppermute x0 -> x97, waiting for transfers between devices: none -> 60.5 us  [swap(): return lax.ppermute(value, axis, [(i, i ^ distance) for i in range(size)])]
    sub x6 -> x0, other arithmetic: 13.6 us -> none  [the longest x4 7.37 us: block_terms(): probs = jax.nn.softmax(logits, axis=-1)]
  transfers between devices with their start and end apart: 10 -> 97, of which waited for: 5 -> 30; matrix products, arithmetic and copies ran while one was open for 38% -> 1% of each run, Pallas kernels for 0% -> 16%
where the time goes in v1:
time: 310 us
  starting transfers between devices  122 us (39%)
  Pallas kernels  108 us (35%)
  waiting for transfers between devices  60.5 us (20%)
  local copies, waits for them, and re-layouts  16 us (5%)
    ppermute x97, starting transfers between devices, swap(): return lax.ppermute(value, axis, [(i, i ^ distance) for i in range(size)])  122 us
    pallas_call x12, Pallas kernels, call(): pl.pallas_call(kernel, grid=grid, in_specs=in_specs, out_specs=[spec(shap...  108 us
    ppermute x97, waiting for transfers between devices, swap(): return lax.ppermute(value, axis, [(i, i ^ distance) for i in range(size)])  60.5 us
    unnamed x82, local copies, waits for them, and re-layouts  12.3 us
  transfers between devices with their start and end apart: 97, of which 30 were waited for; matrix products, arithmetic and copies ran while one was open for 1% of the time, Pallas kernels for 16%

profile of v1, /device:TPU:0, one launch (start us, length us, event | category | flops | bytes accessed | tf_op | source)
XLA Modules:
  0.0 309.7 jit_solution(6033235534157038126)
XLA Ops:
  2.3 3.1 collective-permute-start
  5.4 2.6 collective-permute-start.1
  17.0 3.5 %collective-permute-start.11 = (bf16[16,1024]{1,0:T(8,128)(2,1)S(1)}, bf16[16,1024]{1,0:T(8,128)(2,1)S(1)}, u32[]{:S(2)}, u32[]{:S(2)}) collective-permute-start(bf16[16,1024]{1,0:T(8,128)(2,1)S(1)} %get-tuple-element.81), channel_id=1, source_target_pairs={{0,2},{1,3},{2,0},{3,1},{4,6},{5,7},{6,4},{7,5},{8,10},{9,11},{10,... | collective-permute-start | bytes 98312 | tf_op jit(solution)/shard_map/ppermute | solution.py:480
  22.1 3.8 %collective-permute-start.4 = (bf16[16,1024]{1,0:T(8,128)(2,1)S(1)}, bf16[16,1024]{1,0:T(8,128)(2,1)S(1)}, u32[]{:S(2)}, u32[]{:S(2)}) collective-permute-start(bf16[16,1024]{1,0:T(8,128)(2,1)S(1)} %get-tuple-element.79), channel_id=1, source_target_pairs={{0,2},{1,3},{2,0},{3,1},{4,6},{5,7},{6,4},{7,5},{8,10},{9,11},{10,... | collective-permute-start | bytes 98312 | tf_op jit(solution)/shard_map/ppermute | solution.py:480
  28.2 3.8 %collective-permute-start.18 = (bf16[16,2560]{1,0:T(8,128)(2,1)S(1)}, bf16[16,2560]{1,0:T(8,128)(2,1)S(1)}, u32[]{:S(2)}, u32[]{:S(2)}) collective-permute-start(bf16[16,2560]{1,0:T(8,128)(2,1)S(1)} %get-tuple-element.83), channel_id=1, source_target_pairs={{0,2},{1,3},{2,0},{3,1},{4,6},{5,7},{6,4},{7,5},{8,10},{9,11},{10,... | collective-permute-start | bytes 245768 | tf_op jit(solution)/shard_map/ppermute | solution.py:480
  33.4 3.1 %collective-permute-start.25 = (bf16[16,2304]{1,0:T(8,128)(2,1)S(1)}, bf16[16,2304]{1,0:T(8,128)(2,1)S(1)}, u32[]{:S(2)}, u32[]{:S(2)}) collective-permute-start(bf16[16,2304]{1,0:T(8,128)(2,1)S(1)} %get-tuple-element.84), channel_id=1, source_target_pairs={{0,2},{1,3},{2,0},{3,1},{4,6},{5,7},{6,4},{7,5},{8,10},{9,11},{10,... | collective-permute-start | bytes 221192 | tf_op jit(solution)/shard_map/ppermute | solution.py:480
  36.5 1.9 collective-permute-start.26
  46.3 1.9 collective-permute-start.22
  48.3 3.9 %collective-permute-done.14 = bf16[4,16,1024]{2,1,0:T(8,128)(2,1)S(1)} collective-permute-done((bf16[4,16,1024]{2,1,0:T(8,128)(2,1)S(1)}, bf16[4,16,1024]{2,1,0:T(8,128)(2,1)S(1)}, u32[]{:S(2)}, u32[]{:S(2)}) %collective-permute-start.14) | collective-permute-done | bytes 131104 | tf_op jit(solution)/shard_map/ppermute | solution.py:480
  52.2 2.0 collective-permute-start.27
  57.5 2.3 collective-permute-done.21
  59.8 3.5 %collective-permute-start.29 = (bf16[4,16,2304]{2,1,0:T(8,128)(2,1)S(1)}, bf16[4,16,2304]{2,1,0:T(8,128)(2,1)S(1)}, u32[]{:S(2)}, u32[]{:S(2)}) collective-permute-start(bf16[4,16,2304]{2,1,0:T(8,128)(2,1)S(1)} %get-tuple-element.171), channel_id=1, source_target_pairs={{0,24},{4,28},{8,16},{12,20},{16,8},{20,12},{24,0},{28,4},{1,25},{... | collective-permute-start | bytes 884744 | tf_op jit(solution)/shard_map/ppermute | solution.py:480
  64.2 6.1 %collective-permute-done.27 = bf16[4,16,2304]{2,1,0:T(8,128)(2,1)S(1)} collective-permute-done((bf16[4,16,2304]{2,1,0:T(8,128)(2,1)S(1)}, bf16[4,16,2304]{2,1,0:T(8,128)(2,1)S(1)}, u32[]{:S(2)}, u32[]{:S(2)}) %collective-permute-start.27) | collective-permute-done | bytes 294944 | tf_op jit(solution)/shard_map/ppermute | solution.py:480
  70.3 1.9 collective-permute-start.7
  73.1 2.0 collective-permute-done.29
  79.1 11.2 %attend.3 = (bf16[1024,256]{1,0:T(8,128)(2,1)}, bf16[1024,256]{1,0:T(8,128)(2,1)}, bf16[1024,256]{1,0:T(8,128)(2,1)}, bf16[1024,256]{1,0:T(8,128)(2,1)}, f32[102...) custom-call(s32[3]{0:T(128)} %copy-done.12, ...), custom_call_target="tpu_custom_call" | custom-call | flops 6000000000 | bytes 2097164 | tf_op jit(solution)/shard_map/attend/pallas_call | solution.py:463
  91.1 11.2 %attend.2 = (bf16[1024,256]{1,0:T(8,128)(2,1)}, bf16[1024,256]{1,0:T(8,128)(2,1)}, bf16[1024,256]{1,0:T(8,128)(2,1)}, bf16[1024,256]{1,0:T(8,128)(2,1)}, f32[102...) custom-call(s32[3]{0:T(128)} %copy-done.12, ...), custom_call_target="tpu_custom_call" | custom-call | flops 6000000000 | bytes 2097164 | tf_op jit(solution)/shard_map/attend/pallas_call | solution.py:463
  103.8 22.0 %feed_forward.1 = (bf16[1024,512]{1,0:T(8,128)(2,1)}, f32[1024,512]{1,0:T(8,128)}, f32[1024,2048]{1,0:T(8,128)}, f32[1024,512]{1,0:T(8,128)}, f32[1,512]{1,0:T(1...) custom-call(s32[3]{0:T(128)} %copy-done.12, bf16[4,16,128]{2,1,0:T(8,128)(2,1)} %copy-done.9, ...), custom_call_target="tpu_custom_call" | custom-call | flops 8000000000 | bytes 7098380 | tf_op jit(solution)/shard_map/feed_forward/pallas_call | solution.py:463
  125.8 17.4 %feed_backward.1 = (f32[1024,512]{1,0:T(8,128)}, bf16[1024,512]{1,0:T(8,128)(2,1)}, f32[1,512]{1,0:T(1,128)}, f32[1,512]{1,0:T(1,128)}, f32[1,2048]{1,0:T(1,128)...) custom-call(s32[3]{0:T(128)} %copy-done.12, bf16[4,16,128]{2,1,0:T(8,128)(2,1)} %copy-done.9, ...), custom_call_target="tpu_custom_call" | custom-call | flops 8000000000 | bytes 18628620 | tf_op jit(solution)/shard_map/feed_backward/pallas_call | solution.py:463
  143.1 17.0 %attend_backward.3 = (bf16[1024,1024]{1,0:T(8,128)(2,1)}, bf16[4,4,16,1024]{3,2,1,0:T(8,128)(2,1)}, bf16[4,4,16,1024]{3,2,1,0:T(8,128)(2,1)}) custom-call(s32[3]{0:T(128)} %copy-done.12, bf16[512,1024]{1,0:T(8,128)(2,1)} %copy-done.14, bf16[1024,256]{1,0:T(8,128)(2,1)} %get-tuple-element.104.q_i, bf16[1024,256]{1,0:T(8,128)(2,1)} %get-tuple-element.105.k_i, ...), custom_call_target="tpu_custom_call" | custom-call | flops 10000000000 | bytes 9437196 | tf_op jit(solution)/shard_map/attend_backward/pallas_call | solution.py:463
  160.7 16.9 %attend_backward.2 = (bf16[1024,1024]{1,0:T(8,128)(2,1)}, bf16[4,4,16,1024]{3,2,1,0:T(8,128)(2,1)}, bf16[4,4,16,1024]{3,2,1,0:T(8,128)(2,1)}) custom-call(s32[3]{0:T(128)} %copy-done.12, bf16[512,1024]{1,0:T(8,128)(2,1)} %copy-done.14, bf16[1024,256]{1,0:T(8,128)(2,1)} %get-tuple-element.91.q_i, bf16[1024,256]{1,0:T(8,128)(2,1)} %get-tuple-element.92.k_i, ...), custom_call_target="tpu_custom_call" | custom-call | flops 10000000000 | bytes 9437196 | tf_op jit(solution)/shard_map/attend_backward/pallas_call | solution.py:463
  179.3 5.3 %input_gradient.1 = (f32[1024,512]{1,0:T(8,128)}, f32[4,16,128]{2,1,0:T(8,128)S(1)}) custom-call(s32[3]{0:T(128)S(1)} %copy-done.13, bf16[4,16,128]{2,1,0:T(8,128)(2,1)S(1)} %copy-done.10, bf16[1024,512]{1,0:T(8,128)(2,1)S(1)} %copy-done.1, f32[1024,512]{1,0:T(8,128)S(1)} %copy-done.16, bf16[1024,1024]{1,0:T(8,128)(2,1)S(1)} %copy-done.18, ...), custom_call_target="tpu_custom_call" | custom-call | flops 3000000000 | bytes 9467916 | tf_op jit(solution)/shard_map/input_gradient/pallas_call | solution.py:463
  184.6 2.0 collective-permute-start.31
  186.6 2.5 collective-permute-start.32
  191.2 3.4 %collective-permute-done.33 = f32[16,128]{1,0:T(8,128)S(1)} collective-permute-done((f32[16,128]{1,0:T(8,128)S(1)}, f32[16,128]{1,0:T(8,128)S(1)}, u32[]{:S(2)}, u32[]{:S(2)}) %collective-permute-start.33) | collective-permute-done | bytes 8224 | tf_op jit(solution)/shard_map/ppermute | solution.py:480
  198.9 2.3 collective-permute-start.39
  209.2 2.2 collective-permute-done.56
  211.4 1.9 collective-permute-start.42
  215.1 2.0 collective-permute-start.44
  217.3 2.9 collective-permute-done.43
  223.9 2.2 collective-permute-done.60
  228.7 2.1 collective-permute-done.46
  230.9 2.4 collective-permute-start.63
  234.7 1.8 collective-permute-start.66
  243.8 4.6 %collective-permute-done.84 = bf16[4,16,2304]{2,1,0:T(8,128)(2,1)S(1)} collective-permute-done((bf16[4,16,2304]{2,1,0:T(8,128)(2,1)S(1)}, bf16[4,16,2304]{2,1,0:T(8,128)(2,1)S(1)}, u32[]{:S(2)}, u32[]{:S(2)}) %collective-permute-start.84) | collective-permute-done | bytes 294944 | tf_op jit(solution)/shard_map/ppermute | solution.py:480
  249.6 5.2 %collective-permute-done.85 = bf16[4,16,2304]{2,1,0:T(8,128)(2,1)S(1)} collective-permute-done((bf16[4,16,2304]{2,1,0:T(8,128)(2,1)S(1)}, bf16[4,16,2304]{2,1,0:T(8,128)(2,1)S(1)}, u32[]{:S(2)}, u32[]{:S(2)}) %collective-permute-start.85) | collective-permute-done | bytes 294944 | tf_op jit(solution)/shard_map/ppermute | solution.py:480
  256.4 1.9 collective-permute-start.72
  259.2 3.2 %collective-permute-done.70 = bf16[4,16,2560]{2,1,0:T(8,128)(2,1)S(1)} collective-permute-done((bf16[4,16,2560]{2,1,0:T(8,128)(2,1)S(1)}, bf16[4,16,2560]{2,1,0:T(8,128)(2,1)S(1)}, u32[]{:S(2)}, u32[]{:S(2)}) %collective-permute-start.70) | collective-permute-done | bytes 327712 | tf_op jit(solution)/shard_map/ppermute | solution.py:480
  263.0 2.5 collective-permute-start.88
  265.5 3.9 %collective-permute-done.72 = bf16[4,16,2560]{2,1,0:T(8,128)(2,1)S(1)} collective-permute-done((bf16[4,16,2560]{2,1,0:T(8,128)(2,1)S(1)}, bf16[4,16,2560]{2,1,0:T(8,128)(2,1)S(1)}, u32[]{:S(2)}, u32[]{:S(2)}) %collective-permute-start.72) | collective-permute-done | bytes 327712 | tf_op jit(solution)/shard_map/ppermute | solution.py:480
  269.4 4.9 %collective-permute-start.89 = (bf16[16,2304]{1,0:T(8,128)(2,1)S(1)}, bf16[16,2304]{1,0:T(8,128)(2,1)S(1)}, u32[]{:S(2)}, u32[]{:S(2)}) collective-permute-start(bf16[16,2304]{1,0:T(8,128)(2,1)S(1)} %get-tuple-element.152), channel_id=1, source_target_pairs={{0,3},{1,2},{2,1},{3,0},{4,7},{5,6},{6,5},{7,4},{8,11},{9,10},{10,... | collective-permute-start | bytes 221192 | tf_op jit(solution)/shard_map/ppermute | solution.py:480
  274.6 2.5 collective-permute-start.53
  279.4 2.1 collective-permute-start.75
  282.4 2.1 collective-permute-start.90
  284.5 3.3 %collective-permute-done.74 = bf16[16,2560]{1,0:T(8,128)(2,1)S(1)} collective-permute-done((bf16[16,2560]{1,0:T(8,128)(2,1)S(1)}, bf16[16,2560]{1,0:T(8,128)(2,1)S(1)}, u32[]{:S(2)}, u32[]{:S(2)}) %collective-permute-start.74) | collective-permute-done | bytes 81952 | tf_op jit(solution)/shard_map/ppermute | solution.py:480
  288.9 1.8 collective-permute-start.94
  295.0 3.5 %collective-permute-start.78 = (bf16[16,2560]{1,0:T(8,128)(2,1)S(1)}, bf16[16,2560]{1,0:T(8,128)(2,1)S(1)}, u32[]{:S(2)}, u32[]{:S(2)}) collective-permute-start(bf16[16,2560]{1,0:T(8,128)(2,1)S(1)} %fusion.13.refs_0_), channel_id=1, source_target_pairs={{0,12},{4,8},{8,4},{12,0},{16,28},{20,24},{24,20},{28,16},{1,13},{... | collective-permute-start | bytes 245768 | tf_op jit(solution)/shard_map/ppermute | solution.py:480
  301.0 2.0 collective-permute-start.82
  (270 shorter events, 90.8 us)
Async XLA Ops:
  2.3 19.2 %collective-permute-start = (bf16[16,128]{1,0:T(8,128)(2,1)S(1)}, bf16[16,128]{1,0:T(8,128)(2,1)S(1)}, u32[]{:S(2)}, u32[]{:S(2)}) collective-permute-start(bf16[16,128]{1,0:T(8,128)(2,1)S(1)} %concatenate.3), channel_id=1, source_target_pairs={{0,1},{1,0},{2,3},{3,2},{4,5},{5,4},{6,7},{7,6},{8,9},{9,8},{10,11... | collective-permute-start | bytes 12296 | tf_op jit(solution)/shard_map/ppermute | solution.py:480
  5.4 16.2 %collective-permute-start.1 = (bf16[16,128]{1,0:T(8,128)(2,1)S(1)}, bf16[16,128]{1,0:T(8,128)(2,1)S(1)}, u32[]{:S(2)}, u32[]{:S(2)}) collective-permute-start(bf16[16,128]{1,0:T(8,128)(2,1)S(1)} %concatenate.3), channel_id=1, source_target_pairs={{0,2},{1,3},{2,0},{3,1},{4,6},{5,7},{6,4},{7,5},{8,10},{9,11},{10,... | collective-permute-start | bytes 12296 | tf_op jit(solution)/shard_map/ppermute | solution.py:480
  8.0 14.2 %collective-permute-start.2 = (bf16[16,128]{1,0:T(8,128)(2,1)S(1)}, bf16[16,128]{1,0:T(8,128)(2,1)S(1)}, u32[]{:S(2)}, u32[]{:S(2)}) collective-permute-start(bf16[16,128]{1,0:T(8,128)(2,1)S(1)} %concatenate.3), channel_id=1, source_target_pairs={{0,3},{1,2},{2,1},{3,0},{4,7},{5,6},{6,5},{7,4},{8,11},{9,10},{10,... | collective-permute-start | bytes 12296 | tf_op jit(solution)/shard_map/ppermute | solution.py:480
  16.1 11.4 %collective-permute-start.10 = (bf16[16,1024]{1,0:T(8,128)(2,1)S(1)}, bf16[16,1024]{1,0:T(8,128)(2,1)S(1)}, u32[]{:S(2)}, u32[]{:S(2)}) collective-permute-start(bf16[16,1024]{1,0:T(8,128)(2,1)S(1)} %get-tuple-element.81), channel_id=1, source_target_pairs={{0,1},{1,0},{2,3},{3,2},{4,5},{5,4},{6,7},{7,6},{8,9},{9,8},{10,11... | collective-permute-start | bytes 98312 | tf_op jit(solution)/shard_map/ppermute | solution.py:480
  17.0 10.6 %collective-permute-start.11 = (bf16[16,1024]{1,0:T(8,128)(2,1)S(1)}, bf16[16,1024]{1,0:T(8,128)(2,1)S(1)}, u32[]{:S(2)}, u32[]{:S(2)}) collective-permute-start(bf16[16,1024]{1,0:T(8,128)(2,1)S(1)} %get-tuple-element.81), channel_id=1, source_target_pairs={{0,2},{1,3},{2,0},{3,1},{4,6},{5,7},{6,4},{7,5},{8,10},{9,11},{10,... | collective-permute-start | bytes 98312 | tf_op jit(solution)/shard_map/ppermute | solution.py:480
  21.6 10.4 %collective-permute-start.3 = (bf16[16,1024]{1,0:T(8,128)(2,1)S(1)}, bf16[16,1024]{1,0:T(8,128)(2,1)S(1)}, u32[]{:S(2)}, u32[]{:S(2)}) collective-permute-start(bf16[16,1024]{1,0:T(8,128)(2,1)S(1)} %get-tuple-element.79), channel_id=1, source_target_pairs={{0,1},{1,0},{2,3},{3,2},{4,5},{5,4},{6,7},{7,6},{8,9},{9,8},{10,11... | collective-permute-start | bytes 98312 | tf_op jit(solution)/shard_map/ppermute | solution.py:480
  22.1 10.0 %collective-permute-start.4 = (bf16[16,1024]{1,0:T(8,128)(2,1)S(1)}, bf16[16,1024]{1,0:T(8,128)(2,1)S(1)}, u32[]{:S(2)}, u32[]{:S(2)}) collective-permute-start(bf16[16,1024]{1,0:T(8,128)(2,1)S(1)} %get-tuple-element.79), channel_id=1, source_target_pairs={{0,2},{1,3},{2,0},{3,1},{4,6},{5,7},{6,4},{7,5},{8,10},{9,11},{10,... | collective-permute-start | bytes 98312 | tf_op jit(solution)/shard_map/ppermute | solution.py:480
  27.7 8.9 %collective-permute-start.17 = (bf16[16,2560]{1,0:T(8,128)(2,1)S(1)}, bf16[16,2560]{1,0:T(8,128)(2,1)S(1)}, u32[]{:S(2)}, u32[]{:S(2)}) collective-permute-start(bf16[16,2560]{1,0:T(8,128)(2,1)S(1)} %get-tuple-element.83), channel_id=1, source_target_pairs={{0,1},{1,0},{2,3},{3,2},{4,5},{5,4},{6,7},{7,6},{8,9},{9,8},{10,11... | collective-permute-start | bytes 245768 | tf_op jit(solution)/shard_map/ppermute | solution.py:480
  28.2 11.2 %collective-permute-start.18 = (bf16[16,2560]{1,0:T(8,128)(2,1)S(1)}, bf16[16,2560]{1,0:T(8,128)(2,1)S(1)}, u32[]{:S(2)}, u32[]{:S(2)}) collective-permute-start(bf16[16,2560]{1,0:T(8,128)(2,1)S(1)} %get-tuple-element.83), channel_id=1, source_target_pairs={{0,2},{1,3},{2,0},{3,1},{4,6},{5,7},{6,4},{7,5},{8,10},{9,11},{10,... | collective-permute-start | bytes 245768 | tf_op jit(solution)/shard_map/ppermute | solution.py:480
  32.0 8.8 %collective-permute-start.19 = (bf16[16,2560]{1,0:T(8,128)(2,1)S(1)}, bf16[16,2560]{1,0:T(8,128)(2,1)S(1)}, u32[]{:S(2)}, u32[]{:S(2)}) collective-permute-start(bf16[16,2560]{1,0:T(8,128)(2,1)S(1)} %get-tuple-element.83), channel_id=1, source_target_pairs={{0,3},{1,2},{2,1},{3,0},{4,7},{5,6},{6,5},{7,4},{8,11},{9,10},{10,... | collective-permute-start | bytes 245768 | tf_op jit(solution)/shard_map/ppermute | solution.py:480
  32.2 10.3 %collective-permute-start.24 = (bf16[16,2304]{1,0:T(8,128)(2,1)S(1)}, bf16[16,2304]{1,0:T(8,128)(2,1)S(1)}, u32[]{:S(2)}, u32[]{:S(2)}) collective-permute-start(bf16[16,2304]{1,0:T(8,128)(2,1)S(1)} %get-tuple-element.84), channel_id=1, source_target_pairs={{0,1},{1,0},{2,3},{3,2},{4,5},{5,4},{6,7},{7,6},{8,9},{9,8},{10,11... | collective-permute-start | bytes 221192 | tf_op jit(solution)/shard_map/ppermute | solution.py:480
  33.4 9.9 %collective-permute-start.25 = (bf16[16,2304]{1,0:T(8,128)(2,1)S(1)}, bf16[16,2304]{1,0:T(8,128)(2,1)S(1)}, u32[]{:S(2)}, u32[]{:S(2)}) collective-permute-start(bf16[16,2304]{1,0:T(8,128)(2,1)S(1)} %get-tuple-element.84), channel_id=1, source_target_pairs={{0,2},{1,3},{2,0},{3,1},{4,6},{5,7},{6,4},{7,5},{8,10},{9,11},{10,... | collective-permute-start | bytes 221192 | tf_op jit(solution)/shard_map/ppermute | solution.py:480
  36.5 8.3 %collective-permute-start.26 = (bf16[16,2304]{1,0:T(8,128)(2,1)S(1)}, bf16[16,2304]{1,0:T(8,128)(2,1)S(1)}, u32[]{:S(2)}, u32[]{:S(2)}) collective-permute-start(bf16[16,2304]{1,0:T(8,128)(2,1)S(1)} %get-tuple-element.84), channel_id=1, source_target_pairs={{0,3},{1,2},{2,1},{3,0},{4,7},{5,6},{6,5},{7,4},{8,11},{9,10},{10,... | collective-permute-start | bytes 221192 | tf_op jit(solution)/shard_map/ppermute | solution.py:480
  40.8 11.4 %collective-permute-start.14 = (bf16[4,16,1024]{2,1,0:T(8,128)(2,1)S(1)}, bf16[4,16,1024]{2,1,0:T(8,128)(2,1)S(1)}, u32[]{:S(2)}, u32[]{:S(2)}) collective-permute-start(bf16[4,16,1024]{2,1,0:T(8,128)(2,1)S(1)} %get-tuple-element.173), channel_id=1, source_target_pairs={{0,16},{4,20},{8,24},{12,28},{16,0},{20,4},{24,8},{28,12},{1,17},{... | collective-permute-start | bytes 393224 | tf_op jit(solution)/shard_map/ppermute | solution.py:480
  42.4 9.8 %collective-permute-start.15 = (bf16[4,16,1024]{2,1,0:T(8,128)(2,1)S(1)}, bf16[4,16,1024]{2,1,0:T(8,128)(2,1)S(1)}, u32[]{:S(2)}, u32[]{:S(2)}) collective-permute-start(bf16[4,16,1024]{2,1,0:T(8,128)(2,1)S(1)} %get-tuple-element.173), channel_id=1, source_target_pairs={{0,24},{4,28},{8,16},{12,20},{16,8},{20,12},{24,0},{28,4},{1,25},{... | collective-permute-start | bytes 393224 | tf_op jit(solution)/shard_map/ppermute | solution.py:480
  43.3 12.7 %collective-permute-start.20 = (bf16[4,16,2560]{2,1,0:T(8,128)(2,1)S(1)}, bf16[4,16,2560]{2,1,0:T(8,128)(2,1)S(1)}, u32[]{:S(2)}, u32[]{:S(2)}) collective-permute-start(bf16[4,16,2560]{2,1,0:T(8,128)(2,1)S(1)} %get-tuple-element.169), channel_id=1, source_target_pairs={{0,8},{4,12},{8,0},{12,4},{16,24},{20,28},{24,16},{28,20},{1,9},{5... | collective-permute-start | bytes 983048 | tf_op jit(solution)/shard_map/ppermute | solution.py:480
  44.8 15.0 %collective-permute-start.21 = (bf16[4,16,2560]{2,1,0:T(8,128)(2,1)S(1)}, bf16[4,16,2560]{2,1,0:T(8,128)(2,1)S(1)}, u32[]{:S(2)}, u32[]{:S(2)}) collective-permute-start(bf16[4,16,2560]{2,1,0:T(8,128)(2,1)S(1)} %get-tuple-element.169), channel_id=1, source_target_pairs={{0,16},{4,20},{8,24},{12,28},{16,0},{20,4},{24,8},{28,12},{1,17},{... | collective-permute-start | bytes 983048 | tf_op jit(solution)/shard_map/ppermute | solution.py:480
  46.3 17.7 %collective-permute-start.22 = (bf16[4,16,2560]{2,1,0:T(8,128)(2,1)S(1)}, bf16[4,16,2560]{2,1,0:T(8,128)(2,1)S(1)}, u32[]{:S(2)}, u32[]{:S(2)}) collective-permute-start(bf16[4,16,2560]{2,1,0:T(8,128)(2,1)S(1)} %get-tuple-element.169), channel_id=1, source_target_pairs={{0,24},{4,28},{8,16},{12,20},{16,8},{20,12},{24,0},{28,4},{1,25},{... | collective-permute-start | bytes 983048 | tf_op jit(solution)/shard_map/ppermute | solution.py:480
  52.2 23.0 %collective-permute-start.6 = (bf16[4,16,1024]{2,1,0:T(8,128)(2,1)S(1)}, bf16[4,16,1024]{2,1,0:T(8,128)(2,1)S(1)}, u32[]{:S(2)}, u32[]{:S(2)}) collective-permute-start(bf16[4,16,1024]{2,1,0:T(8,128)(2,1)S(1)} %get-tuple-element.175), channel_id=1, source_target_pairs={{0,8},{4,12},{8,0},{12,4},{16,24},{20,28},{24,16},{28,20},{1,9},{5... | collective-permute-start | bytes 393224 | tf_op jit(solution)/shard_map/ppermute | solution.py:480
  52.2 18.1 %collective-permute-start.27 = (bf16[4,16,2304]{2,1,0:T(8,128)(2,1)S(1)}, bf16[4,16,2304]{2,1,0:T(8,128)(2,1)S(1)}, u32[]{:S(2)}, u32[]{:S(2)}) collective-permute-start(bf16[4,16,2304]{2,1,0:T(8,128)(2,1)S(1)} %get-tuple-element.171), channel_id=1, source_target_pairs={{0,8},{4,12},{8,0},{12,4},{16,24},{20,28},{24,16},{28,20},{1,9},{5... | collective-permute-start | bytes 884744 | tf_op jit(solution)/shard_map/ppermute | solution.py:480
  55.9 16.2 %collective-permute-start.28 = (bf16[4,16,2304]{2,1,0:T(8,128)(2,1)S(1)}, bf16[4,16,2304]{2,1,0:T(8,128)(2,1)S(1)}, u32[]{:S(2)}, u32[]{:S(2)}) collective-permute-start(bf16[4,16,2304]{2,1,0:T(8,128)(2,1)S(1)} %get-tuple-element.171), channel_id=1, source_target_pairs={{0,16},{4,20},{8,24},{12,28},{16,0},{20,4},{24,8},{28,12},{1,17},{... | collective-permute-start | bytes 884744 | tf_op jit(solution)/shard_map/ppermute | solution.py:480
  59.8 15.3 %collective-permute-start.29 = (bf16[4,16,2304]{2,1,0:T(8,128)(2,1)S(1)}, bf16[4,16,2304]{2,1,0:T(8,128)(2,1)S(1)}, u32[]{:S(2)}, u32[]{:S(2)}) collective-permute-start(bf16[4,16,2304]{2,1,0:T(8,128)(2,1)S(1)} %get-tuple-element.171), channel_id=1, source_target_pairs={{0,24},{4,28},{8,16},{12,20},{16,8},{20,12},{24,0},{28,4},{1,25},{... | collective-permute-start | bytes 884744 | tf_op jit(solution)/shard_map/ppermute | solution.py:480
  64.0 14.2 %collective-permute-start.16 = (bf16[4,4,16,1024]{3,2,1,0:T(8,128)(2,1)S(1)}, bf16[4,4,16,1024]{3,2,1,0:T(8,128)(2,1)S(1)}, u32[]{:S(2)}, u32[]{:S(2)}) collective-permute-start(bf16[4,4,16,1024]{3,2,1,0:T(8,128)(2,1)S(1)} %pad_maximum_fusion.3.near), channel_id=1, source_target_pairs={{0,4},{4,0},{8,12},{12,8},{16,20},{20,16},{24,28},{28,24},{1,5},{5... | collective-permute-start | bytes 1572872 | tf_op jit(solution)/shard_map/ppermute | solution.py:480
  75.0 27.3 %collective-permute-start.23 = (bf16[4,4,16,2560]{3,2,1,0:T(8,128)(2,1)S(1)}, bf16[4,4,16,2560]{3,2,1,0:T(8,128)(2,1)S(1)}, u32[]{:S(2)}, u32[]{:S(2)}) collective-permute-start(bf16[4,4,16,2560]{3,2,1,0:T(8,128)(2,1)S(1)} %pad_maximum_fusion.up_near), channel_id=1, source_target_pairs={{0,4},{4,0},{8,12},{12,8},{16,20},{20,16},{24,28},{28,24},{1,5},{5... | collective-permute-start | bytes 3932168 | tf_op jit(solution)/shard_map/ppermute | solution.py:480
  75.2 27.1 %collective-permute-start.30 = (bf16[4,4,16,2304]{3,2,1,0:T(8,128)(2,1)S(1)}, bf16[4,4,16,2304]{3,2,1,0:T(8,128)(2,1)S(1)}, u32[]{:S(2)}, u32[]{:S(2)}) collective-permute-start(bf16[4,4,16,2304]{3,2,1,0:T(8,128)(2,1)S(1)} %pad_maximum_fusion.1.down_near), channel_id=1, source_target_pairs={{0,4},{4,0},{8,12},{12,8},{16,20},{20,16},{24,28},{28,24},{1,5},{5... | collective-permute-start | bytes 3538952 | tf_op jit(solution)/shard_map/ppermute | solution.py:480
  78.1 12.1 %collective-permute-start.9 = (bf16[4,4,16,1024]{3,2,1,0:T(8,128)(2,1)S(1)}, bf16[4,4,16,1024]{3,2,1,0:T(8,128)(2,1)S(1)}, u32[]{:S(2)}, u32[]{:S(2)}) collective-permute-start(bf16[4,4,16,1024]{3,2,1,0:T(8,128)(2,1)S(1)} %pad_maximum_fusion.2.near), channel_id=1, source_target_pairs={{0,4},{4,0},{8,12},{12,8},{16,20},{20,16},{24,28},{28,24},{1,5},{5... | collective-permute-start | bytes 1572872 | tf_op jit(solution)/shard_map/ppermute | solution.py:480
  160.1 45.1 %collective-permute-start.55 = (bf16[4,4,16,1024]{3,2,1,0:T(8,128)(2,1)}, bf16[4,4,16,1024]{3,2,1,0:T(8,128)(2,1)S(1)}, u32[]{:S(2)}, u32[]{:S(2)}) collective-permute-start(bf16[4,4,16,1024]{3,2,1,0:T(8,128)(2,1)} %get-tuple-element.127), channel_id=1, source_target_pairs={{0,4},{4,0},{8,12},{12,8},{16,20},{20,16},{24,28},{28,24},{1,5},{5... | collective-permute-start | bytes 1572872 | tf_op jit(solution)/shard_map/ppermute | solution.py:480
  190.5 17.3 %collective-permute-start.41 = (bf16[4,4,16,1024]{3,2,1,0:T(8,128)(2,1)S(1)}, bf16[4,4,16,1024]{3,2,1,0:T(8,128)(2,1)S(1)}, u32[]{:S(2)}, u32[]{:S(2)}) collective-permute-start(bf16[4,4,16,1024]{3,2,1,0:T(8,128)(2,1)S(1)} %copy-done.38), channel_id=1, source_target_pairs={{0,4},{4,0},{8,12},{12,8},{16,20},{20,16},{24,28},{28,24},{1,5},{5... | collective-permute-start | bytes 1572872 | tf_op jit(solution)/shard_map/ppermute | solution.py:480
  202.1 32.5 %collective-permute-start.83 = (bf16[4,4,16,2304]{3,2,1,0:T(8,128)(2,1)S(1)}, bf16[4,4,16,2304]{3,2,1,0:T(8,128)(2,1)S(1)}, u32[]{:S(2)}, u32[]{:S(2)}) collective-permute-start(bf16[4,4,16,2304]{3,2,1,0:T(8,128)(2,1)S(1)} %copy-done.36), channel_id=1, source_target_pairs={{0,4},{4,0},{8,12},{12,8},{16,20},{20,16},{24,28},{28,24},{1,5},{5... | collective-permute-start | bytes 3538952 | tf_op jit(solution)/shard_map/ppermute | solution.py:480
  203.5 37.5 %collective-permute-start.69 = (bf16[4,4,16,2560]{3,2,1,0:T(8,128)(2,1)S(1)}, bf16[4,4,16,2560]{3,2,1,0:T(8,128)(2,1)S(1)}, u32[]{:S(2)}, u32[]{:S(2)}) collective-permute-start(bf16[4,4,16,2560]{3,2,1,0:T(8,128)(2,1)S(1)} %copy-done.34), channel_id=1, source_target_pairs={{0,4},{4,0},{8,12},{12,8},{16,20},{20,16},{24,28},{28,24},{1,5},{5... | collective-permute-start | bytes 3932168 | tf_op jit(solution)/shard_map/ppermute | solution.py:480
  238.7 9.7 %collective-permute-start.84 = (bf16[4,16,2304]{2,1,0:T(8,128)(2,1)S(1)}, bf16[4,16,2304]{2,1,0:T(8,128)(2,1)S(1)}, u32[]{:S(2)}, u32[]{:S(2)}) collective-permute-start(bf16[4,16,2304]{2,1,0:T(8,128)(2,1)S(1)} %get-tuple-element.147), channel_id=1, source_target_pairs={{0,8},{4,12},{8,0},{12,4},{16,24},{20,28},{24,16},{28,20},{1,9},{5... | collective-permute-start | bytes 884744 | tf_op jit(solution)/shard_map/ppermute | solution.py:480
  239.8 15.0 %collective-permute-start.85 = (bf16[4,16,2304]{2,1,0:T(8,128)(2,1)S(1)}, bf16[4,16,2304]{2,1,0:T(8,128)(2,1)S(1)}, u32[]{:S(2)}, u32[]{:S(2)}) collective-permute-start(bf16[4,16,2304]{2,1,0:T(8,128)(2,1)S(1)} %get-tuple-element.146), channel_id=1, source_target_pairs={{0,16},{4,20},{8,24},{12,28},{16,0},{20,4},{24,8},{28,12},{1,17},{... | collective-permute-start | bytes 884744 | tf_op jit(solution)/shard_map/ppermute | solution.py:480
  241.0 15.4 %collective-permute-start.86 = (bf16[4,16,2304]{2,1,0:T(8,128)(2,1)S(1)}, bf16[4,16,2304]{2,1,0:T(8,128)(2,1)S(1)}, u32[]{:S(2)}, u32[]{:S(2)}) collective-permute-start(bf16[4,16,2304]{2,1,0:T(8,128)(2,1)S(1)} %get-tuple-element.145), channel_id=1, source_target_pairs={{0,24},{4,28},{8,16},{12,20},{16,8},{20,12},{24,0},{28,4},{1,25},{... | collective-permute-start | bytes 884744 | tf_op jit(solution)/shard_map/ppermute | solution.py:480
  242.6 15.8 %collective-permute-start.48 = (bf16[16,1024]{1,0:T(8,128)(2,1)S(1)}, bf16[16,1024]{1,0:T(8,128)(2,1)S(1)}, u32[]{:S(2)}, u32[]{:S(2)}) collective-permute-start(bf16[16,1024]{1,0:T(8,128)(2,1)S(1)} %fusion.57.refs_0_), channel_id=1, source_target_pairs={{0,4},{4,0},{8,12},{12,8},{16,20},{20,16},{24,28},{28,24},{1,5},{5... | collective-permute-start | bytes 98312 | tf_op jit(solution)/shard_map/ppermute | solution.py:480
  243.0 15.5 %collective-permute-start.49 = (bf16[16,1024]{1,0:T(8,128)(2,1)S(1)}, bf16[16,1024]{1,0:T(8,128)(2,1)S(1)}, u32[]{:S(2)}, u32[]{:S(2)}) collective-permute-start(bf16[16,1024]{1,0:T(8,128)(2,1)S(1)} %fusion.57.refs_0_), channel_id=1, source_target_pairs={{0,8},{4,12},{8,0},{12,4},{16,24},{20,28},{24,16},{28,20},{1,9},{5... | collective-permute-start | bytes 98312 | tf_op jit(solution)/shard_map/ppermute | solution.py:480
  248.4 14.1 %collective-permute-start.70 = (bf16[4,16,2560]{2,1,0:T(8,128)(2,1)S(1)}, bf16[4,16,2560]{2,1,0:T(8,128)(2,1)S(1)}, u32[]{:S(2)}, u32[]{:S(2)}) collective-permute-start(bf16[4,16,2560]{2,1,0:T(8,128)(2,1)S(1)} %get-tuple-element.143), channel_id=1, source_target_pairs={{0,8},{4,12},{8,0},{12,4},{16,24},{20,28},{24,16},{28,20},{1,9},{5... | collective-permute-start | bytes 983048 | tf_op jit(solution)/shard_map/ppermute | solution.py:480
  254.7 8.3 %collective-permute-start.71 = (bf16[4,16,2560]{2,1,0:T(8,128)(2,1)S(1)}, bf16[4,16,2560]{2,1,0:T(8,128)(2,1)S(1)}, u32[]{:S(2)}, u32[]{:S(2)}) collective-permute-start(bf16[4,16,2560]{2,1,0:T(8,128)(2,1)S(1)} %get-tuple-element.142), channel_id=1, source_target_pairs={{0,16},{4,20},{8,24},{12,28},{16,0},{20,4},{24,8},{28,12},{1,17},{... | collective-permute-start | bytes 983048 | tf_op jit(solution)/shard_map/ppermute | solution.py:480
  256.4 13.0 %collective-permute-start.72 = (bf16[4,16,2560]{2,1,0:T(8,128)(2,1)S(1)}, bf16[4,16,2560]{2,1,0:T(8,128)(2,1)S(1)}, u32[]{:S(2)}, u32[]{:S(2)}) collective-permute-start(bf16[4,16,2560]{2,1,0:T(8,128)(2,1)S(1)} %get-tuple-element.141), channel_id=1, source_target_pairs={{0,24},{4,28},{8,16},{12,20},{16,8},{20,12},{24,0},{28,4},{1,25},{... | collective-permute-start | bytes 983048 | tf_op jit(solution)/shard_map/ppermute | solution.py:480
  258.4 16.1 %collective-permute-start.50 = (bf16[16,1024]{1,0:T(8,128)(2,1)S(1)}, bf16[16,1024]{1,0:T(8,128)(2,1)S(1)}, u32[]{:S(2)}, u32[]{:S(2)}) collective-permute-start(bf16[16,1024]{1,0:T(8,128)(2,1)S(1)} %fusion.57.refs_0_), channel_id=1, source_target_pairs={{0,12},{4,8},{8,4},{12,0},{16,28},{20,24},{24,20},{28,16},{1,13},{... | collective-permute-start | bytes 98312 | tf_op jit(solution)/shard_map/ppermute | solution.py:480
  258.5 16.1 %collective-permute-start.51 = (bf16[16,1024]{1,0:T(8,128)(2,1)S(1)}, bf16[16,1024]{1,0:T(8,128)(2,1)S(1)}, u32[]{:S(2)}, u32[]{:S(2)}) collective-permute-start(bf16[16,1024]{1,0:T(8,128)(2,1)S(1)} %fusion.57.refs_0_), channel_id=1, source_target_pairs={{0,16},{4,20},{8,24},{12,28},{16,0},{20,4},{24,8},{28,12},{1,17},{... | collective-permute-start | bytes 98312 | tf_op jit(solution)/shard_map/ppermute | solution.py:480
  262.5 14.7 %collective-permute-start.87 = (bf16[16,2304]{1,0:T(8,128)(2,1)S(1)}, bf16[16,2304]{1,0:T(8,128)(2,1)S(1)}, u32[]{:S(2)}, u32[]{:S(2)}) collective-permute-start(bf16[16,2304]{1,0:T(8,128)(2,1)S(1)} %get-tuple-element.151), channel_id=1, source_target_pairs={{0,1},{1,0},{2,3},{3,2},{4,5},{5,4},{6,7},{7,6},{8,9},{9,8},{10,11... | collective-permute-start | bytes 221192 | tf_op jit(solution)/shard_map/ppermute | solution.py:480
  263.0 15.1 %collective-permute-start.88 = (bf16[16,2304]{1,0:T(8,128)(2,1)S(1)}, bf16[16,2304]{1,0:T(8,128)(2,1)S(1)}, u32[]{:S(2)}, u32[]{:S(2)}) collective-permute-start(bf16[16,2304]{1,0:T(8,128)(2,1)S(1)} %get-tuple-element.153), channel_id=1, source_target_pairs={{0,2},{1,3},{2,0},{3,1},{4,6},{5,7},{6,4},{7,5},{8,10},{9,11},{10,... | collective-permute-start | bytes 221192 | tf_op jit(solution)/shard_map/ppermute | solution.py:480
  269.4 10.0 %collective-permute-start.89 = (bf16[16,2304]{1,0:T(8,128)(2,1)S(1)}, bf16[16,2304]{1,0:T(8,128)(2,1)S(1)}, u32[]{:S(2)}, u32[]{:S(2)}) collective-permute-start(bf16[16,2304]{1,0:T(8,128)(2,1)S(1)} %get-tuple-element.152), channel_id=1, source_target_pairs={{0,3},{1,2},{2,1},{3,0},{4,7},{5,6},{6,5},{7,4},{8,11},{9,10},{10,... | collective-permute-start | bytes 221192 | tf_op jit(solution)/shard_map/ppermute | solution.py:480
  278.1 9.7 %collective-permute-start.74 = (bf16[16,2560]{1,0:T(8,128)(2,1)S(1)}, bf16[16,2560]{1,0:T(8,128)(2,1)S(1)}, u32[]{:S(2)}, u32[]{:S(2)}) collective-permute-start(bf16[16,2560]{1,0:T(8,128)(2,1)S(1)} %get-tuple-element.150), channel_id=1, source_target_pairs={{0,2},{1,3},{2,0},{3,1},{4,6},{5,7},{6,4},{7,5},{8,10},{9,11},{10,... | collective-permute-start | bytes 245768 | tf_op jit(solution)/shard_map/ppermute | solution.py:480
  279.4 8.3 %collective-permute-start.75 = (bf16[16,2560]{1,0:T(8,128)(2,1)S(1)}, bf16[16,2560]{1,0:T(8,128)(2,1)S(1)}, u32[]{:S(2)}, u32[]{:S(2)}) collective-permute-start(bf16[16,2560]{1,0:T(8,128)(2,1)S(1)} %get-tuple-element.149), channel_id=1, source_target_pairs={{0,3},{1,2},{2,1},{3,0},{4,7},{5,6},{6,5},{7,4},{8,11},{9,10},{10,... | collective-permute-start | bytes 245768 | tf_op jit(solution)/shard_map/ppermute | solution.py:480
  282.4 8.3 %collective-permute-start.90 = (bf16[16,2304]{1,0:T(8,128)(2,1)S(1)}, bf16[16,2304]{1,0:T(8,128)(2,1)S(1)}, u32[]{:S(2)}, u32[]{:S(2)}) collective-permute-start(bf16[16,2304]{1,0:T(8,128)(2,1)S(1)} %fusion.23.refs_0_), channel_id=1, source_target_pairs={{0,4},{4,0},{8,12},{12,8},{16,20},{20,16},{24,28},{28,24},{1,5},{5... | collective-permute-start | bytes 221192 | tf_op jit(solution)/shard_map/ppermute | solution.py:480
  295.0 11.8 %collective-permute-start.78 = (bf16[16,2560]{1,0:T(8,128)(2,1)S(1)}, bf16[16,2560]{1,0:T(8,128)(2,1)S(1)}, u32[]{:S(2)}, u32[]{:S(2)}) collective-permute-start(bf16[16,2560]{1,0:T(8,128)(2,1)S(1)} %fusion.13.refs_0_), channel_id=1, source_target_pairs={{0,12},{4,8},{8,4},{12,0},{16,28},{20,24},{24,20},{28,16},{1,13},{... | collective-permute-start | bytes 245768 | tf_op jit(solution)/shard_map/ppermute | solution.py:480
  298.5 9.4 %collective-permute-start.80 = (bf16[16,2560]{1,0:T(8,128)(2,1)S(1)}, bf16[16,2560]{1,0:T(8,128)(2,1)S(1)}, u32[]{:S(2)}, u32[]{:S(2)}) collective-permute-start(bf16[16,2560]{1,0:T(8,128)(2,1)S(1)} %fusion.13.refs_0_), channel_id=1, source_target_pairs={{0,20},{4,16},{8,28},{12,24},{16,4},{20,0},{24,12},{28,8},{1,21},{... | collective-permute-start | bytes 245768 | tf_op jit(solution)/shard_map/ppermute | solution.py:480
  (90 other events, 782.1 us)

commit v2 on v1

--- a/solution.py
+++ b/solution.py
@@ -15,6 +15,8 @@
 HALF = 256
 PIECE = 16
 COLS_PROJ = 4 * HALF
+COLS_BOTH = 2 * COLS_PROJ
+COLS_LAST = COLS_PROJ + 128
 COLS_UP = WIDTH + FF
 COLS_DOWN = 4 * WIDTH + VOCAB
 F32 = jnp.float32
@@ -74,6 +76,12 @@
                 yield s ^ idx[2], member, buf.at[xy, s]
 
 
+def each_member(idx, near, far):
+    for c, buf in ((0, near), (1, far)):
+        for xy in range(4):
+            yield None, ((xy ^ idx[1]) * 2) + (c ^ idx[0]), buf.at[xy]
+
+
 def rows_at(start, size):
     return pl.ds(pl.multiple_of(start, PIECE), size)
 
@@ -87,31 +95,49 @@
         send[xy ^ idx[1], shard ^ idx[2], :, columns] = jnp.where(own_first, second, first)
 
 
-def pack_kernel(idx, wq, wk, wv, wc, wm, wu, wd, wr, pa, pb, pc, pd):
+def pack_kernel(
+    idx, g1, b1, g2, b2, bd, bu, wq, wk, wv, wc, wm, wu, wd, wr, pa, pc, pd, sems
+):
     member = idx[1] * 2 + idx[0]
+    across = (idx[1] ^ 3) * 2 + idx[0]
     rows = rows_at(member * PIECE, PIECE)
+    moves = []
     for j, w in enumerate((wq, wk, wv, wc)):
-        pa[:, j * HALF : (j + 1) * HALF] = w[rows, :HALF]
-        pb[:, j * HALF : (j + 1) * HALF] = w[rows, HALF:]
-    pc[:, :WIDTH] = wm[rows, :]
-    pc[:, WIDTH:] = wu[rows, :]
-    for i in range(4):
-        pd[:, i * WIDTH : (i + 1) * WIDTH] = wd[rows_at(member * 64 + 16 * i, PIECE), :]
-    pd[:, 4 * WIDTH :] = wr[rows, :]
-
-
-def first_norm_kernel(idx, vec, x, a1, a1t):
+        for half in range(2):
+            start = half * COLS_PROJ + j * HALF
+            part = w.at[rows, half * HALF : (half + 1) * HALF]
+            moves.append((part, pa.at[:, start : start + HALF]))
+    moves.append((wm.at[rows, :], pc.at[:, :WIDTH]))
+    moves.append((wu.at[rows, :], pc.at[:, WIDTH:]))
+    for place, who in enumerate((member, across)):
+        for i in range(4):
+            part = wd.at[rows_at(who * 64 + 16 * i, PIECE), :]
+            moves.append((part, pd.at[place, :, i * WIDTH : (i + 1) * WIDTH]))
+        moves.append((wr.at[rows_at(who * PIECE, PIECE), :], pd.at[place, :, 4 * WIDTH :]))
+    copies = [pltpu.make_async_copy(src, dst, sems.at[i]) for i, (src, dst) in enumerate(moves)]
+    for copy in copies:
+        copy.start()
+    lines = [v[...].astype(F32).reshape(1, 128) for v in (g1, b1, g2, b2, bd)]
+    lines += [bu[128 * j : 128 * j + 128].astype(F32).reshape(1, 128) for j in range(4)]
+    lines.append(jnp.zeros((7, 128), F32))
+    pa[:, COLS_BOTH:] = jnp.concatenate(lines, axis=0).astype(BF16)
+    for copy in copies:
+        copy.wait()
+
+
+def first_norm_kernel(idx, vec, x, a1, unit_t, columns):
     unit, _ = norm_parts(x[...].astype(F32))
-    low = (unit * vector_of(vec, idx, 0) + vector_of(vec, idx, 1)).astype(BF16)
-    a1[...] = low
-    a1t[...] = low.T
+    gain, shift = vector_of(vec, idx, 0), vector_of(vec, idx, 1)
+    a1[...] = (unit * gain + shift).astype(BF16)
+    unit_t[...] = unit.astype(BF16).T
+    columns[...] = jnp.concatenate([gain, shift, jnp.zeros((6, WIDTH), F32)], axis=0).T
 
 
 def lanes_low():
     return lax.broadcasted_iota(jnp.int32, (1, 128), 1) < HEAD
 
 
-def spread(value):
+def stacked(value):
     low = lanes_low().astype(F32).astype(BF16)
     high = (1.0 - lanes_low().astype(F32)).astype(BF16)
     return jnp.concatenate([value * low, value * high], axis=0)
@@ -182,13 +208,13 @@
         low_u = state_u[pair].astype(BF16)
         kept_s[0, pair] = low_s
         kept_u[0, pair] = low_u
-        scores = jnp.where(tri, nt(spread(q), k), 0.0).astype(BF16)
+        scores = jnp.where(tri, nt(stacked(q), k), 0.0).astype(BF16)
         numer = join(nn(scores, e)) + nn(q, low_s)
         logits = (HEAD ** -0.5) * numer * inv
         expd = jnp.exp(logits - head_max(logits))
         probs = expd / head_sum(expd)
         ratio = (probs * inv).astype(BF16)
-        mixing = jnp.where(tri, nt(spread(ratio), e), 0.0).astype(BF16)
+        mixing = jnp.where(tri, nt(stacked(ratio), e), 0.0).astype(BF16)
         o_o[:, at] = (join(nn(mixing, v)) + nn(ratio, low_u)).astype(BF16)
         s_o[:, at] = logits
         p_o[:, at] = probs
@@ -326,10 +352,70 @@
                 put_parts(idx, keep, send, tile, shard, at)
 
 
+def proj_gradient(idx, unit_t, columns, w, dx, keep, send):
+    ones = jnp.ones((PIECE, dx.shape[0]), BF16)
+    sums = nn(ones, dx[...])[:1]
+    shares = []
+    for shard in range(4):
+        rows = slice(shard * 128, shard * 128 + 128)
+        gain, shift = columns[rows, 0:1], columns[rows, 1:2]
+        on_gain = jnp.zeros((128, HALF), F32)
+        on_shift = jnp.zeros((128, HALF), F32)
+        for j in range(4):
+            at = slice(j * HALF, (j + 1) * HALF)
+            tile = nn(unit_t[rows, :], dx[:, at])
+            weight = w[rows, at].astype(F32)
+            on_gain += tile * weight
+            on_shift += weight * sums[:, at]
+            put_parts(idx, keep, send, (tile * gain + shift * sums[:, at]).astype(BF16), shard, at)
+        both = [jnp.sum(v, axis=1, keepdims=True) for v in (on_gain, on_shift)]
+        shares.append(jnp.concatenate(both + [jnp.zeros((128, 6), F32)], axis=1))
+    return jnp.concatenate(shares, axis=0).T
+
+
 def attend_back_kernel(
-    idx, a1t, q_i, k_i, v_i, e_i, x_i, p_i, s_i, z_i, r_i, do_i, kept_s, kept_u,
+    idx, unit_t, columns, w, q_i, k_i, v_i, e_i, x_i, p_i, s_i, z_i, r_i, do_i, kept_s, kept_u,
+    dx_o, keep, send, share_o,
+    state_r, state_t, count_z, dx_s,
+):
+    attend_back_step(
+        q_i, k_i, v_i, e_i, x_i, p_i, s_i, z_i, r_i, do_i, kept_s, kept_u,
+        dx_o, state_r, state_t, count_z, dx_s,
+    )
+
+    @pl.when(pl.program_id(0) == pl.num_programs(0) - 1)
+    def _():
+        share_o[...] = proj_gradient(idx, unit_t, columns, w, dx_s, keep, send)
+
+
+def attend_back_last_kernel(
+    idx, unit_t, columns, w, q_i, k_i, v_i, e_i, x_i, p_i, s_i, z_i, r_i, do_i, kept_s, kept_u,
+    share, g_g2, g_b2, g_bd, g_bu,
     dx_o, keep, send,
     state_r, state_t, count_z, dx_s,
+):
+    attend_back_step(
+        q_i, k_i, v_i, e_i, x_i, p_i, s_i, z_i, r_i, do_i, kept_s, kept_u,
+        dx_o, state_r, state_t, count_z, dx_s,
+    )
+
+    @pl.when(pl.program_id(0) == pl.num_programs(0) - 1)
+    def _():
+        total = proj_gradient(idx, unit_t, columns, w, dx_s, keep, send) + share[...]
+        for s in range(4):
+            at = slice(128 * s, 128 * s + 128)
+            lines = [total[:2, at], g_g2[:, at], g_b2[:, at], g_bd[:, at]]
+            lines += [g_bu[:, 512 * s + 128 * j : 512 * s + 128 * j + 128] for j in range(4)]
+            lines.append(jnp.zeros((7, 128), F32))
+            block = jnp.concatenate(lines, axis=0).astype(BF16)
+            for xy in range(4):
+                keep[xy, s ^ idx[2], :, COLS_PROJ:] = block
+                send[xy, s ^ idx[2], :, COLS_PROJ:] = block
+
+
+def attend_back_step(
+    q_i, k_i, v_i, e_i, x_i, p_i, s_i, z_i, r_i, do_i, kept_s, kept_u,
+    dx_o, state_r, state_t, count_z, dx_s,
 ):
     step = pl.program_id(0)
     chunk = pl.num_programs(0) - 1 - step
@@ -352,17 +438,17 @@
         low_s, low_u = kept_s[0, pair], kept_u[0, pair]
         low_r = state_r[pair].astype(BF16)
         low_t = state_t[pair].astype(BF16)
-        d_mix = jnp.where(tri, nt(spread(do), v), 0.0).astype(BF16)
+        d_mix = jnp.where(tri, nt(stacked(do), v), 0.0).astype(BF16)
         d_ratio = (join(nn(d_mix, e)) + nt(do, low_u)) * inv
         d_logits = probs * (d_ratio - head_sum(d_ratio * probs))
         d_numer = ((HEAD ** -0.5) * d_logits * inv).astype(BF16)
         d_total = (-d_ratio * (probs * inv) - d_logits * logits * inv).astype(BF16)
-        d_scores = jnp.where(tri, nt(spread(d_numer), e), 0.0).astype(BF16)
+        d_scores = jnp.where(tri, nt(stacked(d_numer), e), 0.0).astype(BF16)
         dq = join(nn(d_scores, k)) + nt(d_numer, low_s)
-        scores = jnp.where(trt, nt(spread(k), q), 0.0).astype(BF16)
-        wide_e = spread(e)
+        scores = jnp.where(trt, nt(stacked(k), q), 0.0).astype(BF16)
+        wide_e = stacked(e)
         mixing = jnp.where(trt, nt(wide_e, ratio), 0.0).astype(BF16)
-        d_mix_t = jnp.where(trt, nt(spread(v), do), 0.0).astype(BF16)
+        d_mix_t = jnp.where(trt, nt(stacked(v), do), 0.0).astype(BF16)
         d_scores_t = jnp.where(trt, nt(wide_e, d_numer), 0.0).astype(BF16)
         dv = join(nn(mixing, do)) + nn(e, low_r)
         dk = join(nn(d_scores_t, q)) + nt(e, low_t)
@@ -377,68 +463,39 @@
         state_t[pair] += jnp.where(block, tn(q, d_numer), 0.0)
     dx_s[rows, :] = dx_o[...]
 
-    @pl.when(step == pl.num_programs(0) - 1)
-    def _():
-        for shard in range(4):
-            for j in range(4):
-                at = slice(j * HALF, (j + 1) * HALF)
-                tile = nn(a1t[shard * 128 : shard * 128 + 128, :], dx_s[:, at]).astype(BF16)
-                put_parts(idx, keep, send, tile, shard, at)
-
-
-def inputs_kernel(idx, vec, x, dh, dx0, dx1, w0, w1, g_bd, g_g2, g_b2, g_bu, dx_o, vec_o, gain, shift):
-    step = pl.program_id(0)
-
-    @pl.when(step == 0)
-    def _():
-        gain[...] = jnp.zeros_like(gain)
-        shift[...] = jnp.zeros_like(shift)
-
+
+def inputs_kernel(idx, vec, x, dh, dx0, dx1, w0, w1, dx_o):
     unit, inverse = norm_parts(x[...].astype(F32))
     d_first = nt(dx0[...], w0[...]) + nt(dx1[...], w1[...])
-    gain[...] += jnp.sum(d_first * unit, axis=0, keepdims=True)
-    shift[...] += jnp.sum(d_first, axis=0, keepdims=True)
     dx_o[...] = dh[...] + norm_pull(d_first, unit, inverse, vector_of(vec, idx, 0))
 
-    @pl.when(step == pl.num_programs(0) - 1)
-    def _():
-        for s in range(4):
-            at = slice(128 * s, 128 * s + 128)
-            rows = [gain[:, at], shift[:, at], g_g2[:, at], g_b2[:, at], g_bd[:, at]]
-            rows += [g_bu[:, 512 * s + 128 * j : 512 * s + 128 * j + 128] for j in range(4)]
-            rows.append(jnp.zeros((7, 128), F32))
-            vec_o[s ^ idx[2]] = jnp.concatenate(rows, axis=0)
-
-
-def unpack_proj_kernel(idx, *refs):
-    first, second, outs = refs[:8], refs[8:16], refs[16:]
-    member = idx[1] * 2 + idx[0]
-    for k in range(8):
-        rows = rows_at((member ^ k) * PIECE, PIECE)
-        for j, out in enumerate(outs):
-            at = slice(j * HALF, (j + 1) * HALF)
-            out[rows, :HALF] = first[k][:, at].astype(F32)
-            out[rows, HALF:] = second[k][:, at].astype(F32)
-
-
-def unpack_up_kernel(idx, *refs):
-    pieces, (mix, up) = refs[:8], refs[8:]
-    member = idx[1] * 2 + idx[0]
-    for k in range(8):
-        rows = rows_at((member ^ k) * PIECE, PIECE)
-        mix[rows, :] = pieces[k][:, :WIDTH].astype(F32)
-        up[rows, :] = pieces[k][:, WIDTH:].astype(F32)
-
-
-def unpack_down_kernel(idx, *refs):
-    pieces, (down, read) = refs[:8], refs[8:]
-    member = idx[1] * 2 + idx[0]
-    for k in range(8):
-        other = member ^ k
+
+def unpack_proj_kernel(idx, near, far, query, key, value, control, g1, b1, g2, b2, bd, bu):
+    for shard, member, piece in each_member(idx, near, far):
+        rows = rows_at(member * PIECE, PIECE)
+        for j, out in enumerate((query, key, value, control)):
+            for half in range(2):
+                start = half * COLS_PROJ + j * HALF
+                out[rows, half * HALF : (half + 1) * HALF] = piece[:, start : start + HALF].astype(F32)
+
+        @pl.when(member == 0)
+        def _():
+            lines = piece[:, COLS_BOTH:].astype(F32)
+            for i, out in enumerate((g1, b1, g2, b2, bd)):
+                out[...] = lines[i]
+            for i in range(4):
+                bu[128 * i : 128 * i + 128] = lines[5 + i]
+
+
+def unpack_feed_kernel(idx, near, far, mix, up, down, read):
+    for shard, member, piece in each_member(idx, near, far):
+        rows = rows_at(member * PIECE, PIECE)
+        mix[rows, :] = piece[:, :WIDTH].astype(F32)
+        up[rows, :] = piece[:, WIDTH:COLS_UP].astype(F32)
         for i in range(4):
-            at = slice(i * WIDTH, (i + 1) * WIDTH)
-            down[rows_at(other * 64 + 16 * i, PIECE), :] = pieces[k][:, at].astype(F32)
-        read[rows_at(other * PIECE, PIECE), :] = pieces[k][:, 4 * WIDTH :].astype(F32)
+            start = COLS_UP + i * WIDTH
+            down[rows_at(member * 64 + 16 * i, PIECE), :] = piece[:, start : start + WIDTH].astype(F32)
+        read[rows, :] = piece[:, COLS_UP + 4 * WIDTH :].astype(F32)
 
 
 def shaped(shape, dtype):
@@ -457,6 +514,8 @@
     for array, block in args:
         if array.dtype == jnp.int32 and array.shape == (3,):
             in_specs.append(pl.BlockSpec(memory_space=pltpu.SMEM))
+        elif block == "hbm":
+            in_specs.append(pl.BlockSpec(memory_space=pl.ANY))
         else:
             in_specs.append(spec(array.shape, block))
     moved = sum(a.size * a.dtype.itemsize for a, _ in args)
@@ -480,44 +539,48 @@
     return lax.ppermute(value, axis, [(i, i ^ distance) for i in range(size)])
 
 
-def gather_pieces(piece, dp, shards):
-    rows = jnp.stack([piece] + [swap(piece, "shard", shards, k) for k in range(1, 4)])
-    near = jnp.stack([rows] + [swap(rows, "dp", dp, 2 * k) for k in range(1, 4)])
-    return near, swap(near, "dp", dp, 1)
-
-
-def reduce_pieces(keep, send, dp, shards):
-    got = swap(send, "dp", dp, 1)
-    part = [(keep[k].astype(F32) + got[k].astype(F32)).astype(BF16) for k in range(4)]
-    got = [swap(part[k], "dp", dp, 2 * k) for k in range(1, 4)]
-    rows = [
-        (
-            (part[0][k].astype(F32) + got[0][k].astype(F32))
-            + (got[1][k].astype(F32) + got[2][k].astype(F32))
-        ).astype(BF16)
-        for k in range(4)
-    ]
-    got = [swap(rows[k], "shard", shards, k) for k in range(1, 4)]
-    total = (
-        (rows[0].astype(F32) + got[0].astype(F32)) + (got[1].astype(F32) + got[2].astype(F32))
-    ).astype(BF16)
+def pin(*values):
+    return lax.optimization_barrier(values)
+
+
+def near_rows(piece, shards):
+    return [swap(piece, "shard", shards, k) for k in range(1, 4)]
+
+
+def sum_of(values):
+    values = [v.astype(F32) for v in values]
+    return ((values[0] + values[1]) + (values[2] + values[3])).astype(BF16)
+
+
+def core_sum(keep, got):
+    return [(keep[k].astype(F32) + got[k].astype(F32)).astype(BF16) for k in range(4)]
+
+
+def plane_start(parts, dp):
+    return [swap(parts[k], "dp", dp, 2 * k) for k in range(1, 4)]
+
+
+def plane_sum(parts, got):
+    return [sum_of([parts[0][k], got[0][k], got[1][k], got[2][k]]) for k in range(4)]
+
+
+def shard_start(rows, shards):
+    return [swap(rows[k], "shard", shards, k) for k in range(1, 4)]
+
+
+def shard_sum(rows, got, dp):
+    total = sum_of([rows[0]] + got)
     distance = 8
     while distance < dp:
         total = (total.astype(F32) + swap(total, "dp", dp, distance).astype(F32)).astype(BF16)
         distance *= 2
-    return [total] + [swap(total, "dp", dp, k) for k in range(1, 8)]
-
-
-def reduce_vectors(block, dp, shards):
-    got = [swap(block[k], "shard", shards, k) for k in range(1, 4)]
-    total = (block[0] + got[0]) + (got[1] + got[2])
-    got = [total] + [swap(total, "dp", dp, k) for k in range(1, 8)]
-    total = ((got[0] + got[1]) + (got[2] + got[3])) + ((got[4] + got[5]) + (got[6] + got[7]))
-    distance = 8
-    while distance < dp:
-        total = total + swap(total, "dp", dp, distance)
-        distance *= 2
     return total
+
+
+def spread(total, dp):
+    pair = jnp.stack([total, swap(total, "dp", dp, 2)])
+    near = jnp.concatenate([pair, swap(pair, "dp", dp, 4)])
+    return near, swap(near, "dp", dp, 1)
 
 
 def body(dp, shards):
@@ -527,67 +590,90 @@
     ):
         count = tokens.shape[0]
         steps = count // CHUNK
+        rows = WIDTH // shards
         member = lax.axis_index("dp") % 8
         idx = jnp.stack([member % 2, member // 2, lax.axis_index("shard")]).astype(jnp.int32)
-
-        own = jnp.concatenate(
-            [
-                jnp.stack([gain_one, bias_one, gain_two, bias_two, bias_down]),
-                bias_up.reshape(4, 128),
-                jnp.zeros((7, 128), BF16),
-            ]
-        )
-        vec = jnp.stack([own] + [swap(own, "shard", shards, k) for k in range(1, 4)])
+        forward = lambda i: (i, 0)
+        back = lambda i: (steps - 1 - i, 0)
+        tok = lambda n: ((CHUNK, n), forward)
+        parts = (4, 4, PIECE)
+
         weights = (w_query, w_key, w_value, w_control, w_mix, w_up, w_down, w_read)
-        packed = call(
+        sizes = [(PIECE, COLS_BOTH + 128), (PIECE, COLS_UP), (2, PIECE, COLS_DOWN)]
+        vectors = (gain_one, bias_one, gain_two, bias_two, bias_down, bias_up)
+        pa, pu, pd = call(
             pack_kernel,
             "pack_weights",
-            [(idx, None)] + [(w, None) for w in weights],
-            [((PIECE, n), BF16, None) for n in (COLS_PROJ, COLS_PROJ, COLS_UP, COLS_DOWN)],
-            limit=16,
+            [(idx, None)] + [(v, None) for v in vectors] + [(w, "hbm") for w in weights],
+            [(size, BF16, None) for size in sizes],
+            scratch=[pltpu.SemaphoreType.DMA((20,))],
         )
-        proj0, proj1, up, down = [gather_pieces(p, dp, shards) for p in packed]
-
-        a1, a1t = call(
+        pa, pu, pd = pin(pa, pu, pd)
+        got_a = near_rows(pa, shards)
+        rows_a = jnp.stack([pa[:, :COLS_BOTH]] + [g[:, :COLS_BOTH] for g in got_a])
+        vec = jnp.stack([pa[:, COLS_BOTH:]] + [g[:, COLS_BOTH:] for g in got_a])
+        rows_a, vec, pu, pd, tokens_a = pin(rows_a, vec, pu, pd, tokens)
+        plane_a = [swap(rows_a, "dp", dp, 2 * k) for k in range(1, 4)]
+        got_u = near_rows(pu, shards)
+        got_d = near_rows(pd, shards)
+        a1, unit_t, columns = call(
             first_norm_kernel,
             "first_norm",
-            [(idx, None), (vec, None), (tokens, None)],
-            [((count, WIDTH), BF16, None), ((WIDTH, count), BF16, None)],
-            limit=24,
+            [(idx, None), (vec, None), (tokens_a, None)],
+            [
+                ((count, WIDTH), BF16, None),
+                ((WIDTH, count), BF16, None),
+                ((WIDTH, 8), F32, None),
+            ],
         )
-
-        forward = lambda i: (i, 0)
-        tok = lambda n: ((CHUNK, n), forward)
+        target = targets.reshape(count, 1)
+        plane_a, a1, unit_t, columns, target = pin(plane_a, a1, unit_t, columns, target)
+        near_a = jnp.stack([rows_a] + plane_a)
+        far_a = swap(near_a, "dp", dp, 1)
+        near_a, got_u, got_d, a1 = pin(near_a, got_u, got_d, a1)
+        rows_u = jnp.stack([pu] + got_u)
+        plane_u = [swap(rows_u, "dp", dp, 2 * k) for k in range(1, 4)]
+        rows_d = jnp.stack([pd] + got_d)
+        plane_d = [swap(rows_d[:, 0], "dp", dp, 2 * k) for k in range(1, 3)]
+        far_a, a1 = pin(far_a, a1)
+
         kept = ((1, 2, 128, 128), lambda i: (i, 0, 0, 0))
-        halves = []
-        for bufs in (proj0, proj1):
+
+        def attend(a1, half):
+            at = ((4, 4, PIECE, COLS_PROJ), lambda i: (0, 0, 0, half))
             names = [((count, HALF), t, tok(HALF)) for t in (BF16,) * 4 + (F32,) * 4 + (BF16,) * 2]
             states = [((steps, 2, 128, 128), BF16, kept)] * 2
-            halves.append(
-                call(
-                    attend_kernel,
-                    "attend",
-                    [(idx, None), (a1, tok(WIDTH)), (bufs[0], None), (bufs[1], None)],
-                    names + states + [((WIDTH, COLS_PROJ), BF16, None)],
-                    steps,
-                    [
-                        pltpu.VMEM((2, 128, 128), F32),
-                        pltpu.VMEM((2, 128, 128), F32),
-                        pltpu.VMEM((1, HALF), F32),
-                    ],
-                    flops=6e9,
-                )
+            return call(
+                attend_kernel,
+                "attend",
+                [(idx, None), (a1, tok(WIDTH)), (near_a, at), (far_a, at)],
+                names + states + [((WIDTH, COLS_PROJ), BF16, None)],
+                steps,
+                [
+                    pltpu.VMEM((2, 128, 128), F32),
+                    pltpu.VMEM((2, 128, 128), F32),
+                    pltpu.VMEM((1, HALF), F32),
+                ],
+                flops=6e9,
             )
-        o0, o1 = halves[0][9], halves[1][9]
-
-        parts = (4, 4, PIECE)
-        out, h, slope, dy, g_bias_down, keep_down, send_down = call(
+
+        first = attend(a1, 0)
+        first, plane_u, plane_d, a1 = pin(first, plane_u, plane_d, a1)
+        near_u = jnp.stack([rows_u] + plane_u)
+        far_u = swap(near_u, "dp", dp, 1)
+        near_d = jnp.stack([rows_d[:, 0]] + plane_d + [rows_d[:, 1]])
+        far_d = swap(near_d, "dp", dp, 1)
+        second = attend(a1, 1)
+        second, far_u, far_d = pin(second, far_u, far_d)
+        halves = (first, second)
+        o0, o1 = first[9], second[9]
+
+        out, h, slope, dy, g_bias_down, keep_d, send_d = call(
             feed_kernel,
             "feed_forward",
             [
                 (idx, None), (vec, None), (tokens, tok(WIDTH)), (o0, tok(HALF)), (o1, tok(HALF)),
-                (targets.reshape(count, 1), tok(1)),
-                (up[0], None), (up[1], None), (down[0], None), (down[1], None),
+                (target, tok(1)), (near_u, None), (far_u, None), (near_d, None), (far_d, None),
             ],
             [
                 ((count, WIDTH), BF16, tok(WIDTH)),
@@ -611,15 +697,15 @@
             ],
             flops=8e9,
         )
-        pieces_down = reduce_pieces(keep_down, send_down, dp, shards)
-
-        dh, d_mixed, g_gain_two, g_bias_two, g_bias_up, keep_up, send_up = call(
+        got_d = swap(send_d, "dp", dp, 1)
+
+        dh, d_mixed, g_gain_two, g_bias_two, g_bias_up, keep_u, send_u = call(
             feed_back_kernel,
             "feed_backward",
             [
                 (idx, None), (vec, None), (h, tok(WIDTH)), (slope, tok(FF)), (dy, tok(WIDTH)),
                 (o0, None), (o1, None),
-                (up[0], None), (up[1], None), (down[0], None), (down[1], None),
+                (near_u, None), (far_u, None), (near_d, None), (far_d, None),
             ],
             [
                 ((count, WIDTH), F32, tok(WIDTH)),
@@ -641,26 +727,33 @@
             ],
             flops=8e9,
         )
-        pieces_up = reduce_pieces(keep_up, send_up, dp, shards)
-
-        back = lambda i: (steps - 1 - i, 0)
+        got_d, d_mixed, send_u = pin(got_d, d_mixed, send_u)
+        got_u = swap(send_u, "dp", dp, 1)
+        sum_d = core_sum(keep_d, got_d)
+        sum_d, d_mixed = pin(sum_d, d_mixed)
+        got_d = plane_start(sum_d, dp)
+
         kept_back = ((1, 2, 128, 128), lambda i: (steps - 1 - i, 0, 0, 0))
-        d_proj, pieces_proj = [], []
-        for half in range(2):
+
+        def attend_back(half, d_mixed, extra=()):
             q, k, v, e, x, p, s, z, r, _, ks, ku, w = halves[half]
             tb = ((CHUNK, HALF), back)
-            column = ((CHUNK, HALF), lambda i, half=half: (steps - 1 - i, half))
-            dx, keep, send = call(
-                attend_back_kernel,
+            column = ((CHUNK, HALF), lambda i: (steps - 1 - i, half))
+            last = half == 1
+            cols = COLS_LAST if last else COLS_PROJ
+            return call(
+                attend_back_last_kernel if last else attend_back_kernel,
                 "attend_backward",
-                [(idx, None), (a1t, None)]
+                [(idx, None), (unit_t, None), (columns, None), (w, None)]
                 + [(t, tb) for t in (q, k, v, e, x, p, s, z, r)]
-                + [(d_mixed, column), (ks, kept_back), (ku, kept_back)],
+                + [(d_mixed, column), (ks, kept_back), (ku, kept_back)]
+                + [(t, None) for t in extra],
                 [
                     ((count, COLS_PROJ), BF16, ((CHUNK, COLS_PROJ), back)),
-                    (parts + (COLS_PROJ,), BF16, None),
-                    (parts + (COLS_PROJ,), BF16, None),
-                ],
+                    (parts + (cols,), BF16, None),
+                    (parts + (cols,), BF16, None),
+                ]
+                + ([] if last else [((8, WIDTH), F32, None)]),
                 steps,
                 [
                     pltpu.VMEM((2, 128, 128), F32),
@@ -670,51 +763,67 @@
                 ],
                 flops=10e9,
             )
-            d_proj.append(dx)
-            pieces_proj.append(reduce_pieces(keep, send, dp, shards))
-
-        d_tokens, block = call(
+
+        dx0, keep_a, send_a, share = attend_back(0, d_mixed)
+        got_d, got_u, send_a, d_mixed = pin(got_d, got_u, send_a, d_mixed)
+        got_a = swap(send_a, "dp", dp, 1)
+        sum_u = core_sum(keep_u, got_u)
+        rows_d = plane_sum(sum_d, got_d)
+        sum_u, rows_d, d_mixed = pin(sum_u, rows_d, d_mixed)
+        got_u = plane_start(sum_u, dp)
+        got_d = shard_start(rows_d, shards)
+
+        extra = (share, g_gain_two, g_bias_two, g_bias_down, g_bias_up)
+        dx1, keep_b, send_b = attend_back(1, d_mixed, extra)
+        got_d, got_u, got_a, send_b, dx1 = pin(got_d, got_u, got_a, send_b, dx1)
+        got_b = swap(send_b, "dp", dp, 1)
+        sum_p = [
+            jnp.concatenate(both, axis=-1)
+            for both in zip(core_sum(keep_a, got_a), core_sum(keep_b, got_b))
+        ]
+        sum_p, got_u, dx1 = pin(sum_p, got_u, dx1)
+        got_p = plane_start(sum_p, dp)
+        rows_u = plane_sum(sum_u, got_u)
+        got_u = shard_start(rows_u, shards)
+        d_tokens = call(
             inputs_kernel,
             "input_gradient",
             [
                 (idx, None), (vec, None), (tokens, tok(WIDTH)), (dh, tok(WIDTH)),
-                (d_proj[0], tok(COLS_PROJ)), (d_proj[1], tok(COLS_PROJ)),
-                (halves[0][12], None), (halves[1][12], None),
-                (g_bias_down, None), (g_gain_two, None), (g_bias_two, None), (g_bias_up, None),
+                (dx0, tok(COLS_PROJ)), (dx1, tok(COLS_PROJ)),
+                (first[12], None), (second[12], None),
             ],
-            [((count, WIDTH), F32, tok(WIDTH)), ((4, 16, 128), F32, None)],
+            [((count, WIDTH), F32, tok(WIDTH))],
             steps,
-            [pltpu.VMEM((1, WIDTH), F32), pltpu.VMEM((1, WIDTH), F32)],
             flops=3e9,
-            limit=32,
+        )[0]
+        got_p, got_u, got_d, d_tokens = pin(got_p, got_u, got_d, d_tokens)
+        rows_p = plane_sum(sum_p, got_p)
+        got_p = shard_start(rows_p, shards)
+        total_u = shard_sum(rows_u, got_u, dp)
+        total_d = shard_sum(rows_d, got_d, dp)
+        near_f, far_f = spread(jnp.concatenate([total_u, total_d], axis=-1), dp)
+        near_p, far_p = spread(shard_sum(rows_p, got_p, dp), dp)
+        g_mix, g_up, g_down, g_read = call(
+            unpack_feed_kernel,
+            "unpack_feed",
+            [(idx, None), (near_f, None), (far_f, None)],
+            [
+                ((rows, WIDTH), F32, None),
+                ((rows, FF), F32, None),
+                ((4 * rows, WIDTH), F32, None),
+                ((rows, VOCAB), F32, None),
+            ],
         )
-        vectors = reduce_vectors(block, dp, shards)
-
-        rows = WIDTH // shards
-        g_down, g_read = call(
-            unpack_down_kernel,
-            "unpack_down",
-            [(idx, None)] + [(p, None) for p in pieces_down],
-            [((4 * rows, WIDTH), F32, None), ((rows, VOCAB), F32, None)],
-            limit=16,
-        )
-        g_mix, g_up = call(
-            unpack_up_kernel,
-            "unpack_up",
-            [(idx, None)] + [(p, None) for p in pieces_up],
-            [((rows, WIDTH), F32, None), ((rows, FF), F32, None)],
-            limit=16,
-        )
-        g_query, g_key, g_value, g_control = call(
+        g_query, g_key, g_value, g_control, g1, b1, g2, b2, bd, bu = call(
             unpack_proj_kernel,
             "unpack_proj",
-            [(idx, None)] + [(p, None) for p in pieces_proj[0] + pieces_proj[1]],
-            [((rows, WIDTH), F32, None)] * 4,
-            limit=16,
+            [(idx, None), (near_p, None), (far_p, None)],
+            [((rows, WIDTH), F32, None)] * 4 + [((128,), F32, None)] * 5 + [((512,), F32, None)],
         )
         return (
-            out, d_tokens, vectors[0], vectors[1], g_query, g_key, g_value, g_control, g_mix,
-            vectors[2], vectors[3], g_up, vectors[5:9].reshape(512), g_down, vectors[4], g_read,
+            out, d_tokens, g1, b1, g_query, g_key, g_value, g_control, g_mix,
+            g2, b2, g_up, bu, g_down, bd, g_read,
         )
 
     return on_device

time: 310 us -> 221 us (0.71)
  starting transfers between devices: 122 us -> 52.2 us
  waiting for transfers between devices: 60.5 us -> 42.1 us
  local copies, waits for them, and re-layouts: 16 us -> 4.28 us
  Pallas kernels: 108 us -> 117 us
    ppermute x97 -> x48, starting transfers between devices: 122 us -> 52.2 us  [swap(): return lax.ppermute(value, axis, [(i, i ^ distance) for i in range(size)])]
    ppermute x97 -> x48, waiting for transfers between devices: 60.5 us -> 42.1 us  [swap(): return lax.ppermute(value, axis, [(i, i ^ distance) for i in range(size)])]
    unnamed x82 -> x32, local copies, waits for them, and re-layouts: 12.3 us -> 1.6 us
    pallas_call x12 -> x11, Pallas kernels: 108 us -> 117 us  [call(): pl.pallas_call(kernel, grid=grid, in_specs=in_specs, out_specs=[spec(shap...]
  transfers between devices with their start and end apart: 97 -> 48, of which waited for: 30 -> 21; matrix products, arithmetic and copies ran while one was open for 1% -> 2% of each run, Pallas kernels for 16% -> 41%
where the time goes in v2:
time: 221 us; the launch traced here: 220 us
  Pallas kernels  117 us (53%)
  starting transfers between devices  52.2 us (24%)
  waiting for transfers between devices  42.1 us (19%)
  local copies, waits for them, and re-layouts  4.28 us (2%)
  other arithmetic  3.69 us (2%)
    pallas_call x11, Pallas kernels, call(): pl.pallas_call(kernel, grid=grid, in_specs=in_specs, out_specs=[spec(shap...  117 us
    ppermute x48, starting transfers between devices, swap(): return lax.ppermute(value, axis, [(i, i ^ distance) for i in range(size)])  52.2 us
    ppermute x48, waiting for transfers between devices, swap(): return lax.ppermute(value, axis, [(i, i ^ distance) for i in range(size)])  42.1 us
  transfers between devices with their start and end apart: 48, of which 21 were waited for; matrix products, arithmetic and copies ran while one was open for 2% of the time, Pallas kernels for 41%

profile of v2, /device:TPU:0, one launch (start us, length us, event | category | flops | bytes accessed | tf_op | source)
XLA Modules:
  0.0 220.3 jit_solution(17635554711187238809)
XLA Ops:
  1.3 2.7 %pack_weights.1 = (bf16[16,2176]{1,0:T(8,128)(2,1)}, bf16[16,2560]{1,0:T(8,128)(2,1)}, bf16[2,16,2304]{2,1,0:T(8,128)(2,1)}) custom-call(s32[3]{0:T(128)} %pad_add_fusion.idx, bf16[128]{0:T(256)(128)(2,1)} %g1.1, bf16[128]{0:T(256)(128)(2,1)} %b1.1, bf16[128]{0:T(256)(128)(2,1)} %g2.1, bf16[128]{0:T(256)(128)(2,1)} %b2.1, bf16[128]{0:T(256)(128)(2,1)} %bd.1, ...), custom_call_target="tpu_custom_call" | custom-call | bytes 1771788 | tf_op jit(solution)/shard_map/pack_weights/pallas_call | solution.py:522
  4.0 5.1 %collective-permute-start.2 = (bf16[16,2176]{1,0:T(8,128)(2,1)}, bf16[16,2176]{1,0:T(8,128)(2,1)S(1)}, u32[]{:S(2)}, u32[]{:S(2)}) collective-permute-start(bf16[16,2176]{1,0:T(8,128)(2,1)} %get-tuple-element.189), channel_id=1, source_target_pairs={{0,3},{1,2},{2,1},{3,0},{4,7},{5,6},{6,5},{7,4},{8,11},{9,10},{10,... | collective-permute-start | bytes 208904 | tf_op jit(solution)/shard_map/ppermute | solution.py:539
  12.1 3.2 %collective-permute-done.1 = bf16[16,2176]{1,0:T(8,128)(2,1)S(1)} collective-permute-done((bf16[16,2176]{1,0:T(8,128)(2,1)}, bf16[16,2176]{1,0:T(8,128)(2,1)S(1)}, u32[]{:S(2)}, u32[]{:S(2)}) %collective-permute-start.1) | collective-permute-done | bytes 69664 | tf_op jit(solution)/shard_map/ppermute | solution.py:539
  16.0 2.4 %collective-permute-start.5 = (bf16[4,16,2048]{2,1,0:T(8,128)(2,1)S(1)}, bf16[4,16,2048]{2,1,0:T(8,128)(2,1)S(1)}, u32[]{:S(2)}, u32[]{:S(2)}) collective-permute-start(bf16[4,16,2048]{2,1,0:T(8,128)(2,1)S(1)} %pad_maximum_fusion.12), channel_id=1, source_target_pairs={{0,24},{4,28},{8,16},{12,20},{16,8},{20,12},{24,0},{28,4},{1,25},{... | collective-permute-start | bytes 786440 | tf_op jit(solution)/shard_map/ppermute | solution.py:539
  19.5 2.7 %collective-permute-start.9 = (bf16[16,2560]{1,0:T(8,128)(2,1)}, bf16[16,2560]{1,0:T(8,128)(2,1)S(1)}, u32[]{:S(2)}, u32[]{:S(2)}) collective-permute-start(bf16[16,2560]{1,0:T(8,128)(2,1)} %get-tuple-element.201), channel_id=1, source_target_pairs={{0,3},{1,2},{2,1},{3,0},{4,7},{5,6},{6,5},{7,4},{8,11},{9,10},{10,... | collective-permute-start | bytes 245768 | tf_op jit(solution)/shard_map/ppermute | solution.py:539
  22.2 3.5 %first_norm.1 = (bf16[1024,512]{1,0:T(8,128)(2,1)}, bf16[512,1024]{1,0:T(8,128)(2,1)}, f32[512,8]{1,0:T(8,128)}) custom-call(s32[3]{0:T(128)} %pad_add_fusion.idx, bf16[4,16,128]{2,1,0:T(8,128)(2,1)} %pad_maximum_fusion.15.vec, bf16[1024,512]{1,0:T(8,128)(2,1)} %x.4), custom_call_target="tpu_custom_call" | custom-call | bytes 1064972 | tf_op jit(solution)/shard_map/first_norm/pallas_call | solution.py:522
  26.2 1.3 collective-permute-start.7
  27.5 2.9 %collective-permute-done.4 = bf16[4,16,2048]{2,1,0:T(8,128)(2,1)S(1)} collective-permute-done((bf16[4,16,2048]{2,1,0:T(8,128)(2,1)S(1)}, bf16[4,16,2048]{2,1,0:T(8,128)(2,1)S(1)}, u32[]{:S(2)}, u32[]{:S(2)}) %collective-permute-start.4) | collective-permute-done | bytes 262176 | tf_op jit(solution)/shard_map/ppermute | solution.py:539
  30.3 1.6 collective-permute-start.12
  32.0 2.8 %collective-permute-start.10 = (bf16[2,16,2304]{2,1,0:T(8,128)(2,1)S(1)}, bf16[2,16,2304]{2,1,0:T(8,128)(2,1)S(1)}, u32[]{:S(2)}, u32[]{:S(2)}) collective-permute-start(bf16[2,16,2304]{2,1,0:T(8,128)(2,1)S(1)} %copy-done.11), channel_id=1, source_target_pairs={{0,1},{1,0},{2,3},{3,2},{4,5},{5,4},{6,7},{7,6},{8,9},{9,8},{10,11... | collective-permute-start | bytes 442376 | tf_op jit(solution)/shard_map/ppermute | solution.py:539
  34.9 4.1 %collective-permute-done.12 = bf16[2,16,2304]{2,1,0:T(8,128)(2,1)S(1)} collective-permute-done((bf16[2,16,2304]{2,1,0:T(8,128)(2,1)S(1)}, bf16[2,16,2304]{2,1,0:T(8,128)(2,1)S(1)}, u32[]{:S(2)}, u32[]{:S(2)}) %collective-permute-start.12) | collective-permute-done | bytes 147488 | tf_op jit(solution)/shard_map/ppermute | solution.py:539
  39.0 6.1 %collective-permute-done.11 = bf16[2,16,2304]{2,1,0:T(8,128)(2,1)S(1)} collective-permute-done((bf16[2,16,2304]{2,1,0:T(8,128)(2,1)S(1)}, bf16[2,16,2304]{2,1,0:T(8,128)(2,1)S(1)}, u32[]{:S(2)}, u32[]{:S(2)}) %collective-permute-start.11) | collective-permute-done | bytes 147488 | tf_op jit(solution)/shard_map/ppermute | solution.py:539
  45.1 1.3 collective-permute-start.15
  46.4 1.8 collective-permute-start.14
  48.8 1.7 collective-permute-start.17
  51.3 1.6 collective-permute-start.16
  52.9 11.4 %attend.2 = (bf16[1024,256]{1,0:T(8,128)(2,1)}, bf16[1024,256]{1,0:T(8,128)(2,1)}, bf16[1024,256]{1,0:T(8,128)(2,1)}, bf16[1024,256]{1,0:T(8,128)(2,1)}, f32[102...) custom-call(s32[3]{0:T(128)} %pad_add_fusion.idx, ...), custom_call_target="tpu_custom_call" | custom-call | flops 6000000000 | bytes 3145740 | tf_op jit(solution)/shard_map/attend/pallas_call | solution.py:522
  64.3 4.1 %collective-permute-done.17 = bf16[4,16,2304]{2,1,0:T(8,128)(2,1)S(1)} collective-permute-done((bf16[4,16,2304]{2,1,0:T(8,128)(2,1)S(1)}, bf16[4,16,2304]{2,1,0:T(8,128)(2,1)S(1)}, u32[]{:S(2)}, u32[]{:S(2)}) %collective-permute-start.17) | collective-permute-done | bytes 294944 | tf_op jit(solution)/shard_map/ppermute | solution.py:539
  69.8 1.0 copy.32.target
  70.8 11.2 %attend.3 = (bf16[1024,256]{1,0:T(8,128)(2,1)}, bf16[1024,256]{1,0:T(8,128)(2,1)}, bf16[1024,256]{1,0:T(8,128)(2,1)}, bf16[1024,256]{1,0:T(8,128)(2,1)}, f32[102...) custom-call(s32[3]{0:T(128)} %pad_add_fusion.idx, ...), custom_call_target="tpu_custom_call" | custom-call | flops 6000000000 | bytes 3145740 | tf_op jit(solution)/shard_map/attend/pallas_call | solution.py:522
  82.1 21.7 %feed_forward.1 = (bf16[1024,512]{1,0:T(8,128)(2,1)}, f32[1024,512]{1,0:T(8,128)}, f32[1024,2048]{1,0:T(8,128)}, f32[1024,512]{1,0:T(8,128)}, f32[1,512]{1,0:T(1...) custom-call(s32[3]{0:T(128)} %pad_add_fusion.idx, bf16[4,16,128]{2,1,0:T(8,128)(2,1)} %pad_maximum_fusion.15.vec, ...), custom_call_target="tpu_custom_call" | custom-call | flops 8000000000 | bytes 7098380 | tf_op jit(solution)/shard_map/feed_forward/pallas_call | solution.py:522
  104.0 17.7 %feed_backward.1 = (f32[1024,512]{1,0:T(8,128)}, bf16[1024,512]{1,0:T(8,128)(2,1)}, f32[1,512]{1,0:T(1,128)}, f32[1,512]{1,0:T(1,128)}, f32[1,2048]{1,0:T(1,128)...) custom-call(s32[3]{0:T(128)} %pad_add_fusion.idx, bf16[4,16,128]{2,1,0:T(8,128)(2,1)} %pad_maximum_fusion.15.vec, ...), custom_call_target="tpu_custom_call" | custom-call | flops 8000000000 | bytes 18628620 | tf_op jit(solution)/shard_map/feed_backward/pallas_call | solution.py:522
  122.5 1.5 collective-permute-start.21
  124.5 1.5 collective-permute-start.23
  126.0 17.9 %attend_backward.2 = (bf16[1024,1024]{1,0:T(8,128)(2,1)}, bf16[4,4,16,1024]{3,2,1,0:T(8,128)(2,1)}, bf16[4,4,16,1024]{3,2,1,0:T(8,128)(2,1)}, f32[8,512]{1,0:T(8,128)}) custom-call(s32[3]{0:T(128)} %pad_add_fusion.idx, bf16[512,1024]{1,0:T(8,128)(2,1)} %get-tuple-element.252.unit_t, f32[512,8]{1,0:T(8,128)} %get-tuple-element.253.columns, ...), custom_call_target="tpu_custom_call" | custom-call | flops 10000000000 | bytes 10502156 | tf_op jit(solution)/shard_map/attend_backward/pallas_call | solution.py:522
  144.6 2.0 collective-permute-start.26
  146.6 2.4 %collective-permute-start.27 = (bf16[16,2304]{1,0:T(8,128)(2,1)S(1)}, bf16[16,2304]{1,0:T(8,128)(2,1)S(1)}, u32[]{:S(2)}, u32[]{:S(2)}) collective-permute-start(bf16[16,2304]{1,0:T(8,128)(2,1)S(1)} %get-tuple-element.291), channel_id=1, source_target_pairs={{0,3},{1,2},{2,1},{3,0},{4,7},{5,6},{6,5},{7,4},{8,11},{9,10},{10,... | collective-permute-start | bytes 221192 | tf_op jit(solution)/shard_map/ppermute | solution.py:539
  149.0 1.4 collective-permute-start.28
  151.0 1.5 collective-permute-start.30
  153.0 18.3 %attend_backward.3 = (bf16[1024,1024]{1,0:T(8,128)(2,1)}, bf16[4,4,16,1152]{3,2,1,0:T(8,128)(2,1)}, bf16[4,4,16,1152]{3,2,1,0:T(8,128)(2,1)}) custom-call(s32[3]{0:T(128)} %pad_add_fusion.idx, bf16[512,1024]{1,0:T(8,128)(2,1)} %get-tuple-element.252.unit_t, f32[512,8]{1,0:T(8,128)} %get-tuple-element.253.columns, bf16[512,1024]{1,0:T(8,128)(2,1)} %get-tuple-element.296.w.w1, ...), custom_call_target="tpu_custom_call" | custom-call | flops 10000000000 | bytes 10532876 | tf_op jit(solution)/shard_map/attend_backward/pallas_call | solution.py:522
  172.1 1.6 collective-permute-done.32
  174.1 1.1 collective-permute-start.38
  175.2 3.4 %collective-permute-start.36 = (bf16[16,2560]{1,0:T(8,128)(2,1)S(1)}, bf16[16,2560]{1,0:T(8,128)(2,1)S(1)}, u32[]{:S(2)}, u32[]{:S(2)}) collective-permute-start(bf16[16,2560]{1,0:T(8,128)(2,1)S(1)} %get-tuple-element.372), channel_id=1, source_target_pairs={{0,1},{1,0},{2,3},{3,2},{4,5},{5,4},{6,7},{7,6},{8,9},{9,8},{10,11... | collective-permute-start | bytes 245768 | tf_op jit(solution)/shard_map/ppermute | solution.py:539
  178.6 1.4 collective-permute-start.33
  181.3 1.4 collective-permute-start.35
  182.8 7.5 %input_gradient.1 = f32[1024,512]{1,0:T(8,128)} custom-call(s32[3]{0:T(128)} %pad_add_fusion.idx, bf16[4,16,128]{2,1,0:T(8,128)(2,1)} %pad_maximum_fusion.15.vec, bf16[1024,512]{1,0:T(8,128)(2,1)} %x.4, f32[1024,512]{1,0:T(8,128)} %get-tuple-element.333.dh, bf16[1024,1024]{1,0:T(8,128)(2,1)} %get-tuple-element.334.dx0, ...), custom_call_target="tpu_custom_call" | custom-call | flops 3000000000 | bytes 9453580 | tf_op jit(solution)/shard_map/input_gradient/pallas_call | solution.py:522
  190.3 3.4 %collective-permute-done.34 = bf16[4,16,2176]{2,1,0:T(8,128)(2,1)S(1)} collective-permute-done((bf16[4,16,2176]{2,1,0:T(8,128)(2,1)S(1)}, bf16[4,16,2176]{2,1,0:T(8,128)(2,1)S(1)}, u32[]{:S(2)}, u32[]{:S(2)}) %collective-permute-start.34) | collective-permute-done | bytes 278560 | tf_op jit(solution)/shard_map/ppermute | solution.py:539
  194.2 1.5 collective-permute-start.41
  195.7 1.7 collective-permute-start.40
  198.3 1.1 collective-permute-done.39
  199.3 1.0 collective-permute-done.41
  200.4 1.9 collective-permute-done.40
  204.5 2.3 %collective-permute-done.42 = bf16[16,2176]{1,0:T(8,128)(2,1)S(1)} collective-permute-done((bf16[16,2176]{1,0:T(8,128)(2,1)S(1)}, bf16[16,2176]{1,0:T(8,128)(2,1)S(1)}, u32[]{:S(2)}, u32[]{:S(2)}) %collective-permute-start.42) | collective-permute-done | bytes 69664 | tf_op jit(solution)/shard_map/ppermute | solution.py:539
  207.4 3.2 %collective-permute-done.46 = bf16[2,16,4864]{2,1,0:T(8,128)(2,1)S(1)} collective-permute-done((bf16[2,16,4864]{2,1,0:T(8,128)(2,1)S(1)}, bf16[2,16,4864]{2,1,0:T(8,128)(2,1)S(1)}, u32[]{:S(2)}, u32[]{:S(2)}) %collective-permute-start.46) | collective-permute-done | bytes 311328 | tf_op jit(solution)/shard_map/ppermute | solution.py:539
  210.8 1.3 collective-permute-done.43
  212.2 1.5 collective-permute-done.44.far
  214.5 2.1 unpack_proj.1
  217.5 2.9 %unpack_feed.1 = (f32[128,512]{1,0:T(8,128)}, f32[128,2048]{1,0:T(8,128)}, f32[512,512]{1,0:T(8,128)}, f32[128,256]{1,0:T(8,128)}) custom-call(s32[3]{0:T(128)} %pad_add_fusion.idx, bf16[4,16,4864]{2,1,0:T(8,128)(2,1)} %copy-done, bf16[4,16,4864]{2,1,0:T(8,128)(2,1)} %copy-done.7), custom_call_target="tpu_custom_call" | custom-call | bytes 1245196 | tf_op jit(solution)/shard_map/unpack_feed/pallas_call | solution.py:522
  (126 shorter events, 20.4 us)
Async XLA Ops:
  4.0 8.0 %collective-permute-start.2 = (bf16[16,2176]{1,0:T(8,128)(2,1)}, bf16[16,2176]{1,0:T(8,128)(2,1)S(1)}, u32[]{:S(2)}, u32[]{:S(2)}) collective-permute-start(bf16[16,2176]{1,0:T(8,128)(2,1)} %get-tuple-element.189), channel_id=1, source_target_pairs={{0,3},{1,2},{2,1},{3,0},{4,7},{5,6},{6,5},{7,4},{8,11},{9,10},{10,... | collective-permute-start | bytes 208904 | tf_op jit(solution)/shard_map/ppermute | solution.py:539
  9.2 6.1 %collective-permute-start.1 = (bf16[16,2176]{1,0:T(8,128)(2,1)}, bf16[16,2176]{1,0:T(8,128)(2,1)S(1)}, u32[]{:S(2)}, u32[]{:S(2)}) collective-permute-start(bf16[16,2176]{1,0:T(8,128)(2,1)} %get-tuple-element.189), channel_id=1, source_target_pairs={{0,2},{1,3},{2,0},{3,1},{4,6},{5,7},{6,4},{7,5},{8,10},{9,11},{10,... | collective-permute-start | bytes 208904 | tf_op jit(solution)/shard_map/ppermute | solution.py:539
  9.2 6.1 %collective-permute-start = (bf16[16,2176]{1,0:T(8,128)(2,1)}, bf16[16,2176]{1,0:T(8,128)(2,1)S(1)}, u32[]{:S(2)}, u32[]{:S(2)}) collective-permute-start(bf16[16,2176]{1,0:T(8,128)(2,1)} %get-tuple-element.189), channel_id=1, source_target_pairs={{0,1},{1,0},{2,3},{3,2},{4,5},{5,4},{6,7},{7,6},{8,9},{9,8},{10,11... | collective-permute-start | bytes 208904 | tf_op jit(solution)/shard_map/ppermute | solution.py:539
  16.0 10.2 %collective-permute-start.5 = (bf16[4,16,2048]{2,1,0:T(8,128)(2,1)S(1)}, bf16[4,16,2048]{2,1,0:T(8,128)(2,1)S(1)}, u32[]{:S(2)}, u32[]{:S(2)}) collective-permute-start(bf16[4,16,2048]{2,1,0:T(8,128)(2,1)S(1)} %pad_maximum_fusion.12), channel_id=1, source_target_pairs={{0,24},{4,28},{8,16},{12,20},{16,8},{20,12},{24,0},{28,4},{1,25},{... | collective-permute-start | bytes 786440 | tf_op jit(solution)/shard_map/ppermute | solution.py:539
  18.4 11.9 %collective-permute-start.4 = (bf16[4,16,2048]{2,1,0:T(8,128)(2,1)S(1)}, bf16[4,16,2048]{2,1,0:T(8,128)(2,1)S(1)}, u32[]{:S(2)}, u32[]{:S(2)}) collective-permute-start(bf16[4,16,2048]{2,1,0:T(8,128)(2,1)S(1)} %pad_maximum_fusion.12), channel_id=1, source_target_pairs={{0,16},{4,20},{8,24},{12,28},{16,0},{20,4},{24,8},{28,12},{1,17},{... | collective-permute-start | bytes 786440 | tf_op jit(solution)/shard_map/ppermute | solution.py:539
  19.0 13.0 %collective-permute-start.3 = (bf16[4,16,2048]{2,1,0:T(8,128)(2,1)S(1)}, bf16[4,16,2048]{2,1,0:T(8,128)(2,1)S(1)}, u32[]{:S(2)}, u32[]{:S(2)}) collective-permute-start(bf16[4,16,2048]{2,1,0:T(8,128)(2,1)S(1)} %pad_maximum_fusion.12), channel_id=1, source_target_pairs={{0,8},{4,12},{8,0},{12,4},{16,24},{20,28},{24,16},{28,20},{1,9},{5... | collective-permute-start | bytes 786440 | tf_op jit(solution)/shard_map/ppermute | solution.py:539
  19.5 12.5 %collective-permute-start.9 = (bf16[16,2560]{1,0:T(8,128)(2,1)}, bf16[16,2560]{1,0:T(8,128)(2,1)S(1)}, u32[]{:S(2)}, u32[]{:S(2)}) collective-permute-start(bf16[16,2560]{1,0:T(8,128)(2,1)} %get-tuple-element.201), channel_id=1, source_target_pairs={{0,3},{1,2},{2,1},{3,0},{4,7},{5,6},{6,5},{7,4},{8,11},{9,10},{10,... | collective-permute-start | bytes 245768 | tf_op jit(solution)/shard_map/ppermute | solution.py:539
  22.2 12.7 %collective-permute-start.8 = (bf16[16,2560]{1,0:T(8,128)(2,1)}, bf16[16,2560]{1,0:T(8,128)(2,1)S(1)}, u32[]{:S(2)}, u32[]{:S(2)}) collective-permute-start(bf16[16,2560]{1,0:T(8,128)(2,1)} %get-tuple-element.201), channel_id=1, source_target_pairs={{0,2},{1,3},{2,0},{3,1},{4,6},{5,7},{6,4},{7,5},{8,10},{9,11},{10,... | collective-permute-start | bytes 245768 | tf_op jit(solution)/shard_map/ppermute | solution.py:539
  26.2 8.7 %collective-permute-start.7 = (bf16[16,2560]{1,0:T(8,128)(2,1)S(1)}, bf16[16,2560]{1,0:T(8,128)(2,1)S(1)}, u32[]{:S(2)}, u32[]{:S(2)}) collective-permute-start(bf16[16,2560]{1,0:T(8,128)(2,1)S(1)} %copy-done.12), channel_id=1, source_target_pairs={{0,1},{1,0},{2,3},{3,2},{4,5},{5,4},{6,7},{7,6},{8,9},{9,8},{10,11... | collective-permute-start | bytes 245768 | tf_op jit(solution)/shard_map/ppermute | solution.py:539
  30.3 8.6 %collective-permute-start.12 = (bf16[2,16,2304]{2,1,0:T(8,128)(2,1)S(1)}, bf16[2,16,2304]{2,1,0:T(8,128)(2,1)S(1)}, u32[]{:S(2)}, u32[]{:S(2)}) collective-permute-start(bf16[2,16,2304]{2,1,0:T(8,128)(2,1)S(1)} %copy-done.11), channel_id=1, source_target_pairs={{0,3},{1,2},{2,1},{3,0},{4,7},{5,6},{6,5},{7,4},{8,11},{9,10},{10,... | collective-permute-start | bytes 442376 | tf_op jit(solution)/shard_map/ppermute | solution.py:539
  31.9 13.1 %collective-permute-start.11 = (bf16[2,16,2304]{2,1,0:T(8,128)(2,1)S(1)}, bf16[2,16,2304]{2,1,0:T(8,128)(2,1)S(1)}, u32[]{:S(2)}, u32[]{:S(2)}) collective-permute-start(bf16[2,16,2304]{2,1,0:T(8,128)(2,1)S(1)} %copy-done.11), channel_id=1, source_target_pairs={{0,2},{1,3},{2,0},{3,1},{4,6},{5,7},{6,4},{7,5},{8,10},{9,11},{10,... | collective-permute-start | bytes 442376 | tf_op jit(solution)/shard_map/ppermute | solution.py:539
  32.0 13.1 %collective-permute-start.10 = (bf16[2,16,2304]{2,1,0:T(8,128)(2,1)S(1)}, bf16[2,16,2304]{2,1,0:T(8,128)(2,1)S(1)}, u32[]{:S(2)}, u32[]{:S(2)}) collective-permute-start(bf16[2,16,2304]{2,1,0:T(8,128)(2,1)S(1)} %copy-done.11), channel_id=1, source_target_pairs={{0,1},{1,0},{2,3},{3,2},{4,5},{5,4},{6,7},{7,6},{8,9},{9,8},{10,11... | collective-permute-start | bytes 442376 | tf_op jit(solution)/shard_map/ppermute | solution.py:539
  45.1 23.7 %collective-permute-start.15 = (bf16[4,16,2560]{2,1,0:T(8,128)(2,1)S(1)}, bf16[4,16,2560]{2,1,0:T(8,128)(2,1)S(1)}, u32[]{:S(2)}, u32[]{:S(2)}) collective-permute-start(bf16[4,16,2560]{2,1,0:T(8,128)(2,1)S(1)} %get-tuple-element.392), channel_id=1, source_target_pairs={{0,24},{4,28},{8,16},{12,20},{16,8},{20,12},{24,0},{28,4},{1,25},{... | collective-permute-start | bytes 983048 | tf_op jit(solution)/shard_map/ppermute | solution.py:539
  46.4 22.4 %collective-permute-start.14 = (bf16[4,16,2560]{2,1,0:T(8,128)(2,1)S(1)}, bf16[4,16,2560]{2,1,0:T(8,128)(2,1)S(1)}, u32[]{:S(2)}, u32[]{:S(2)}) collective-permute-start(bf16[4,16,2560]{2,1,0:T(8,128)(2,1)S(1)} %get-tuple-element.392), channel_id=1, source_target_pairs={{0,16},{4,20},{8,24},{12,28},{16,0},{20,4},{24,8},{28,12},{1,17},{... | collective-permute-start | bytes 983048 | tf_op jit(solution)/shard_map/ppermute | solution.py:539
  48.2 20.6 %collective-permute-start.13 = (bf16[4,16,2560]{2,1,0:T(8,128)(2,1)S(1)}, bf16[4,16,2560]{2,1,0:T(8,128)(2,1)S(1)}, u32[]{:S(2)}, u32[]{:S(2)}) collective-permute-start(bf16[4,16,2560]{2,1,0:T(8,128)(2,1)S(1)} %get-tuple-element.392), channel_id=1, source_target_pairs={{0,8},{4,12},{8,0},{12,4},{16,24},{20,28},{24,16},{28,20},{1,9},{5... | collective-permute-start | bytes 983048 | tf_op jit(solution)/shard_map/ppermute | solution.py:539
  48.7 2.7 %collective-permute-start.6 = (bf16[4,4,16,2048]{3,2,1,0:T(8,128)(2,1)S(1)}, bf16[4,4,16,2048]{3,2,1,0:T(8,128)(2,1)S(1)}, u32[]{:S(2)}, u32[]{:S(2)}) collective-permute-start(bf16[4,4,16,2048]{3,2,1,0:T(8,128)(2,1)S(1)} %pad_maximum_fusion.2.near), channel_id=1, source_target_pairs={{0,4},{4,0},{8,12},{12,8},{16,20},{20,16},{24,28},{28,24},{1,5},{5... | collective-permute-start | bytes 3145736 | tf_op jit(solution)/shard_map/ppermute | solution.py:539
  48.8 19.5 %collective-permute-start.17 = (bf16[4,16,2304]{2,1,0:T(8,128)(2,1)S(1)}, bf16[4,16,2304]{2,1,0:T(8,128)(2,1)S(1)}, u32[]{:S(2)}, u32[]{:S(2)}) collective-permute-start(bf16[4,16,2304]{2,1,0:T(8,128)(2,1)S(1)} %get-tuple-element.390), channel_id=1, source_target_pairs={{0,16},{4,20},{8,24},{12,28},{16,0},{20,4},{24,8},{28,12},{1,17},{... | collective-permute-start | bytes 884744 | tf_op jit(solution)/shard_map/ppermute | solution.py:539
  51.3 17.5 %collective-permute-start.16 = (bf16[4,16,2304]{2,1,0:T(8,128)(2,1)S(1)}, bf16[4,16,2304]{2,1,0:T(8,128)(2,1)S(1)}, u32[]{:S(2)}, u32[]{:S(2)}) collective-permute-start(bf16[4,16,2304]{2,1,0:T(8,128)(2,1)S(1)} %get-tuple-element.390), channel_id=1, source_target_pairs={{0,8},{4,12},{8,0},{12,4},{16,24},{20,28},{24,16},{28,20},{1,9},{5... | collective-permute-start | bytes 884744 | tf_op jit(solution)/shard_map/ppermute | solution.py:539
  69.0 13.1 %collective-permute-start.18 = (bf16[4,4,16,2560]{3,2,1,0:T(8,128)(2,1)S(1)}, bf16[4,4,16,2560]{3,2,1,0:T(8,128)(2,1)}, u32[]{:S(2)}, u32[]{:S(2)}) collective-permute-start(bf16[4,4,16,2560]{3,2,1,0:T(8,128)(2,1)S(1)} %pad_maximum_fusion.up_near), channel_id=1, source_target_pairs={{0,4},{4,0},{8,12},{12,8},{16,20},{20,16},{24,28},{28,24},{1,5},{5... | collective-permute-start | bytes 3932168 | tf_op jit(solution)/shard_map/ppermute | solution.py:539
  69.2 12.8 %collective-permute-start.19 = (bf16[4,4,16,2304]{3,2,1,0:T(8,128)(2,1)S(1)}, bf16[4,4,16,2304]{3,2,1,0:T(8,128)(2,1)}, u32[]{:S(2)}, u32[]{:S(2)}) collective-permute-start(bf16[4,4,16,2304]{3,2,1,0:T(8,128)(2,1)S(1)} %pad_maximum_fusion.1.down_near), channel_id=1, source_target_pairs={{0,4},{4,0},{8,12},{12,8},{16,20},{20,16},{24,28},{28,24},{1,5},{5... | collective-permute-start | bytes 3538952 | tf_op jit(solution)/shard_map/ppermute | solution.py:539
  103.9 17.8 %collective-permute-start.20 = (bf16[4,4,16,2304]{3,2,1,0:T(8,128)(2,1)}, bf16[4,4,16,2304]{3,2,1,0:T(8,128)(2,1)S(1)}, u32[]{:S(2)}, u32[]{:S(2)}) collective-permute-start(bf16[4,4,16,2304]{3,2,1,0:T(8,128)(2,1)} %get-tuple-element.265), channel_id=1, source_target_pairs={{0,4},{4,0},{8,12},{12,8},{16,20},{20,16},{24,28},{28,24},{1,5},{5... | collective-permute-start | bytes 3538952 | tf_op jit(solution)/shard_map/ppermute | solution.py:539
  121.7 22.3 %collective-permute-start.24 = (bf16[4,4,16,2560]{3,2,1,0:T(8,128)(2,1)}, bf16[4,4,16,2560]{3,2,1,0:T(8,128)(2,1)S(1)}, u32[]{:S(2)}, u32[]{:S(2)}) collective-permute-start(bf16[4,4,16,2560]{3,2,1,0:T(8,128)(2,1)} %get-tuple-element.281), channel_id=1, source_target_pairs={{0,4},{4,0},{8,12},{12,8},{16,20},{20,16},{24,28},{28,24},{1,5},{5... | collective-permute-start | bytes 3932168 | tf_op jit(solution)/shard_map/ppermute | solution.py:539
  122.5 21.5 %collective-permute-start.21 = (bf16[4,16,2304]{2,1,0:T(8,128)(2,1)S(1)}, bf16[4,16,2304]{2,1,0:T(8,128)(2,1)S(1)}, u32[]{:S(2)}, u32[]{:S(2)}) collective-permute-start(bf16[4,16,2304]{2,1,0:T(8,128)(2,1)S(1)} %get-tuple-element.278), channel_id=1, source_target_pairs={{0,8},{4,12},{8,0},{12,4},{16,24},{20,28},{24,16},{28,20},{1,9},{5... | collective-permute-start | bytes 884744 | tf_op jit(solution)/shard_map/ppermute | solution.py:539
  123.9 20.0 %collective-permute-start.22 = (bf16[4,16,2304]{2,1,0:T(8,128)(2,1)S(1)}, bf16[4,16,2304]{2,1,0:T(8,128)(2,1)S(1)}, u32[]{:S(2)}, u32[]{:S(2)}) collective-permute-start(bf16[4,16,2304]{2,1,0:T(8,128)(2,1)S(1)} %get-tuple-element.279), channel_id=1, source_target_pairs={{0,16},{4,20},{8,24},{12,28},{16,0},{20,4},{24,8},{28,12},{1,17},{... | collective-permute-start | bytes 884744 | tf_op jit(solution)/shard_map/ppermute | solution.py:539
  124.5 19.4 %collective-permute-start.23 = (bf16[4,16,2304]{2,1,0:T(8,128)(2,1)S(1)}, bf16[4,16,2304]{2,1,0:T(8,128)(2,1)S(1)}, u32[]{:S(2)}, u32[]{:S(2)}) collective-permute-start(bf16[4,16,2304]{2,1,0:T(8,128)(2,1)S(1)} %get-tuple-element.280), channel_id=1, source_target_pairs={{0,24},{4,28},{8,16},{12,20},{16,8},{20,12},{24,0},{28,4},{1,25},{... | collective-permute-start | bytes 884744 | tf_op jit(solution)/shard_map/ppermute | solution.py:539
  144.6 6.5 %collective-permute-start.25 = (bf16[16,2304]{1,0:T(8,128)(2,1)S(1)}, bf16[16,2304]{1,0:T(8,128)(2,1)S(1)}, u32[]{:S(2)}, u32[]{:S(2)}) collective-permute-start(bf16[16,2304]{1,0:T(8,128)(2,1)S(1)} %get-tuple-element.289), channel_id=1, source_target_pairs={{0,1},{1,0},{2,3},{3,2},{4,5},{5,4},{6,7},{7,6},{8,9},{9,8},{10,11... | collective-permute-start | bytes 221192 | tf_op jit(solution)/shard_map/ppermute | solution.py:539
  144.6 8.4 %collective-permute-start.26 = (bf16[16,2304]{1,0:T(8,128)(2,1)S(1)}, bf16[16,2304]{1,0:T(8,128)(2,1)S(1)}, u32[]{:S(2)}, u32[]{:S(2)}) collective-permute-start(bf16[16,2304]{1,0:T(8,128)(2,1)S(1)} %get-tuple-element.290), channel_id=1, source_target_pairs={{0,2},{1,3},{2,0},{3,1},{4,6},{5,7},{6,4},{7,5},{8,10},{9,11},{10,... | collective-permute-start | bytes 221192 | tf_op jit(solution)/shard_map/ppermute | solution.py:539
  146.6 24.7 %collective-permute-start.27 = (bf16[16,2304]{1,0:T(8,128)(2,1)S(1)}, bf16[16,2304]{1,0:T(8,128)(2,1)S(1)}, u32[]{:S(2)}, u32[]{:S(2)}) collective-permute-start(bf16[16,2304]{1,0:T(8,128)(2,1)S(1)} %get-tuple-element.291), channel_id=1, source_target_pairs={{0,3},{1,2},{2,1},{3,0},{4,7},{5,6},{6,5},{7,4},{8,11},{9,10},{10,... | collective-permute-start | bytes 221192 | tf_op jit(solution)/shard_map/ppermute | solution.py:539
  149.0 22.3 %collective-permute-start.28 = (bf16[4,16,2560]{2,1,0:T(8,128)(2,1)S(1)}, bf16[4,16,2560]{2,1,0:T(8,128)(2,1)S(1)}, u32[]{:S(2)}, u32[]{:S(2)}) collective-permute-start(bf16[4,16,2560]{2,1,0:T(8,128)(2,1)S(1)} %get-tuple-element.292), channel_id=1, source_target_pairs={{0,8},{4,12},{8,0},{12,4},{16,24},{20,28},{24,16},{28,20},{1,9},{5... | collective-permute-start | bytes 983048 | tf_op jit(solution)/shard_map/ppermute | solution.py:539
  150.4 20.9 %collective-permute-start.29 = (bf16[4,16,2560]{2,1,0:T(8,128)(2,1)S(1)}, bf16[4,16,2560]{2,1,0:T(8,128)(2,1)S(1)}, u32[]{:S(2)}, u32[]{:S(2)}) collective-permute-start(bf16[4,16,2560]{2,1,0:T(8,128)(2,1)S(1)} %get-tuple-element.293), channel_id=1, source_target_pairs={{0,16},{4,20},{8,24},{12,28},{16,0},{20,4},{24,8},{28,12},{1,17},{... | collective-permute-start | bytes 983048 | tf_op jit(solution)/shard_map/ppermute | solution.py:539
  151.0 20.3 %collective-permute-start.30 = (bf16[4,16,2560]{2,1,0:T(8,128)(2,1)S(1)}, bf16[4,16,2560]{2,1,0:T(8,128)(2,1)S(1)}, u32[]{:S(2)}, u32[]{:S(2)}) collective-permute-start(bf16[4,16,2560]{2,1,0:T(8,128)(2,1)S(1)} %get-tuple-element.294), channel_id=1, source_target_pairs={{0,24},{4,28},{8,16},{12,20},{16,8},{20,12},{24,0},{28,4},{1,25},{... | collective-permute-start | bytes 983048 | tf_op jit(solution)/shard_map/ppermute | solution.py:539
  153.0 18.3 %collective-permute-start.31 = (bf16[4,4,16,1024]{3,2,1,0:T(8,128)(2,1)S(1)}, bf16[4,4,16,1024]{3,2,1,0:T(8,128)(2,1)S(1)}, u32[]{:S(2)}, u32[]{:S(2)}) collective-permute-start(bf16[4,4,16,1024]{3,2,1,0:T(8,128)(2,1)S(1)} %copy-done.15), channel_id=1, source_target_pairs={{0,4},{4,0},{8,12},{12,8},{16,20},{20,16},{24,28},{28,24},{1,5},{5... | collective-permute-start | bytes 1572872 | tf_op jit(solution)/shard_map/ppermute | solution.py:539
  171.3 2.4 %collective-permute-start.32 = (bf16[4,4,16,1152]{3,2,1,0:T(8,128)(2,1)}, bf16[4,4,16,1152]{3,2,1,0:T(8,128)(2,1)S(1)}, u32[]{:S(2)}, u32[]{:S(2)}) collective-permute-start(bf16[4,4,16,1152]{3,2,1,0:T(8,128)(2,1)} %get-tuple-element.318), channel_id=1, source_target_pairs={{0,4},{4,0},{8,12},{12,8},{16,20},{20,16},{24,28},{28,24},{1,5},{5... | collective-permute-start | bytes 1769480 | tf_op jit(solution)/shard_map/ppermute | solution.py:539
  174.1 7.2 %collective-permute-start.38 = (bf16[16,2560]{1,0:T(8,128)(2,1)S(1)}, bf16[16,2560]{1,0:T(8,128)(2,1)S(1)}, u32[]{:S(2)}, u32[]{:S(2)}) collective-permute-start(bf16[16,2560]{1,0:T(8,128)(2,1)S(1)} %get-tuple-element.370), channel_id=1, source_target_pairs={{0,3},{1,2},{2,1},{3,0},{4,7},{5,6},{6,5},{7,4},{8,11},{9,10},{10,... | collective-permute-start | bytes 245768 | tf_op jit(solution)/shard_map/ppermute | solution.py:539
  175.2 15.1 %collective-permute-start.37 = (bf16[16,2560]{1,0:T(8,128)(2,1)S(1)}, bf16[16,2560]{1,0:T(8,128)(2,1)S(1)}, u32[]{:S(2)}, u32[]{:S(2)}) collective-permute-start(bf16[16,2560]{1,0:T(8,128)(2,1)S(1)} %get-tuple-element.371), channel_id=1, source_target_pairs={{0,2},{1,3},{2,0},{3,1},{4,6},{5,7},{6,4},{7,5},{8,10},{9,11},{10,... | collective-permute-start | bytes 245768 | tf_op jit(solution)/shard_map/ppermute | solution.py:539
  175.2 15.1 %collective-permute-start.36 = (bf16[16,2560]{1,0:T(8,128)(2,1)S(1)}, bf16[16,2560]{1,0:T(8,128)(2,1)S(1)}, u32[]{:S(2)}, u32[]{:S(2)}) collective-permute-start(bf16[16,2560]{1,0:T(8,128)(2,1)S(1)} %get-tuple-element.372), channel_id=1, source_target_pairs={{0,1},{1,0},{2,3},{3,2},{4,5},{5,4},{6,7},{7,6},{8,9},{9,8},{10,11... | collective-permute-start | bytes 245768 | tf_op jit(solution)/shard_map/ppermute | solution.py:539
  178.6 11.7 %collective-permute-start.33 = (bf16[4,16,2176]{2,1,0:T(8,128)(2,1)S(1)}, bf16[4,16,2176]{2,1,0:T(8,128)(2,1)S(1)}, u32[]{:S(2)}, u32[]{:S(2)}) collective-permute-start(bf16[4,16,2176]{2,1,0:T(8,128)(2,1)S(1)} %get-tuple-element.323), channel_id=1, source_target_pairs={{0,8},{4,12},{8,0},{12,4},{16,24},{20,28},{24,16},{28,20},{1,9},{5... | collective-permute-start | bytes 835592 | tf_op jit(solution)/shard_map/ppermute | solution.py:539
  180.0 13.8 %collective-permute-start.34 = (bf16[4,16,2176]{2,1,0:T(8,128)(2,1)S(1)}, bf16[4,16,2176]{2,1,0:T(8,128)(2,1)S(1)}, u32[]{:S(2)}, u32[]{:S(2)}) collective-permute-start(bf16[4,16,2176]{2,1,0:T(8,128)(2,1)S(1)} %get-tuple-element.324), channel_id=1, source_target_pairs={{0,16},{4,20},{8,24},{12,28},{16,0},{20,4},{24,8},{28,12},{1,17},{... | collective-permute-start | bytes 835592 | tf_op jit(solution)/shard_map/ppermute | solution.py:539
  181.3 12.4 %collective-permute-start.35 = (bf16[4,16,2176]{2,1,0:T(8,128)(2,1)S(1)}, bf16[4,16,2176]{2,1,0:T(8,128)(2,1)S(1)}, u32[]{:S(2)}, u32[]{:S(2)}) collective-permute-start(bf16[4,16,2176]{2,1,0:T(8,128)(2,1)S(1)} %get-tuple-element.325), channel_id=1, source_target_pairs={{0,24},{4,28},{8,16},{12,20},{16,8},{20,12},{24,0},{28,4},{1,25},{... | collective-permute-start | bytes 835592 | tf_op jit(solution)/shard_map/ppermute | solution.py:539
  193.8 5.5 %collective-permute-start.39 = (bf16[16,2176]{1,0:T(8,128)(2,1)S(1)}, bf16[16,2176]{1,0:T(8,128)(2,1)S(1)}, u32[]{:S(2)}, u32[]{:S(2)}) collective-permute-start(bf16[16,2176]{1,0:T(8,128)(2,1)S(1)} %get-tuple-element.381), channel_id=1, source_target_pairs={{0,1},{1,0},{2,3},{3,2},{4,5},{5,4},{6,7},{7,6},{8,9},{9,8},{10,11... | collective-permute-start | bytes 208904 | tf_op jit(solution)/shard_map/ppermute | solution.py:539
  194.2 6.2 %collective-permute-start.41 = (bf16[16,2176]{1,0:T(8,128)(2,1)S(1)}, bf16[16,2176]{1,0:T(8,128)(2,1)S(1)}, u32[]{:S(2)}, u32[]{:S(2)}) collective-permute-start(bf16[16,2176]{1,0:T(8,128)(2,1)S(1)} %get-tuple-element.382), channel_id=1, source_target_pairs={{0,3},{1,2},{2,1},{3,0},{4,7},{5,6},{6,5},{7,4},{8,11},{9,10},{10,... | collective-permute-start | bytes 208904 | tf_op jit(solution)/shard_map/ppermute | solution.py:539
  195.7 6.6 %collective-permute-start.40 = (bf16[16,2176]{1,0:T(8,128)(2,1)S(1)}, bf16[16,2176]{1,0:T(8,128)(2,1)S(1)}, u32[]{:S(2)}, u32[]{:S(2)}) collective-permute-start(bf16[16,2176]{1,0:T(8,128)(2,1)S(1)} %get-tuple-element.383), channel_id=1, source_target_pairs={{0,2},{1,3},{2,0},{3,1},{4,6},{5,7},{6,4},{7,5},{8,10},{9,11},{10,... | collective-permute-start | bytes 208904 | tf_op jit(solution)/shard_map/ppermute | solution.py:539
  197.6 6.0 %collective-permute-start.45 = (bf16[16,4864]{1,0:T(8,128)(2,1)S(1)}, bf16[16,4864]{1,0:T(8,128)(2,1)S(1)}, u32[]{:S(2)}, u32[]{:S(2)}) collective-permute-start(bf16[16,4864]{1,0:T(8,128)(2,1)S(1)} %get-tuple-element.394), channel_id=1, source_target_pairs={{0,8},{4,12},{8,0},{12,4},{16,24},{20,28},{24,16},{28,20},{1,9},{5... | collective-permute-start | bytes 466952 | tf_op jit(solution)/shard_map/ppermute | solution.py:539
  202.4 4.4 %collective-permute-start.42 = (bf16[16,2176]{1,0:T(8,128)(2,1)S(1)}, bf16[16,2176]{1,0:T(8,128)(2,1)S(1)}, u32[]{:S(2)}, u32[]{:S(2)}) collective-permute-start(bf16[16,2176]{1,0:T(8,128)(2,1)S(1)} %fusion.15), channel_id=1, source_target_pairs={{0,8},{4,12},{8,0},{12,4},{16,24},{20,28},{24,16},{28,20},{1,9},{5... | collective-permute-start | bytes 208904 | tf_op jit(solution)/shard_map/ppermute | solution.py:539
  203.6 7.0 %collective-permute-start.46 = (bf16[2,16,4864]{2,1,0:T(8,128)(2,1)S(1)}, bf16[2,16,4864]{2,1,0:T(8,128)(2,1)S(1)}, u32[]{:S(2)}, u32[]{:S(2)}) collective-permute-start(bf16[2,16,4864]{2,1,0:T(8,128)(2,1)S(1)} %pad_maximum_fusion.6), channel_id=1, source_target_pairs={{0,16},{4,20},{8,24},{12,28},{16,0},{20,4},{24,8},{28,12},{1,17},{... | collective-permute-start | bytes 933896 | tf_op jit(solution)/shard_map/ppermute | solution.py:539
  206.8 5.3 %collective-permute-start.43 = (bf16[2,16,2176]{2,1,0:T(8,128)(2,1)S(1)}, bf16[2,16,2176]{2,1,0:T(8,128)(2,1)S(1)}, u32[]{:S(2)}, u32[]{:S(2)}) collective-permute-start(bf16[2,16,2176]{2,1,0:T(8,128)(2,1)S(1)} %pad_maximum_fusion.14), channel_id=1, source_target_pairs={{0,16},{4,20},{8,24},{12,28},{16,0},{20,4},{24,8},{28,12},{1,17},{... | collective-permute-start | bytes 417800 | tf_op jit(solution)/shard_map/ppermute | solution.py:539
  210.7 6.0 %collective-permute-start.47 = (bf16[4,16,4864]{2,1,0:T(8,128)(2,1)S(1)}, bf16[4,16,4864]{2,1,0:T(8,128)(2,1)S(1)}, u32[]{:S(2)}, u32[]{:S(2)}) collective-permute-start(bf16[4,16,4864]{2,1,0:T(8,128)(2,1)S(1)} %pad_maximum_fusion.3.near), channel_id=1, source_target_pairs={{0,4},{4,0},{8,12},{12,8},{16,20},{20,16},{24,28},{28,24},{1,5},{5... | collective-permute-start | bytes 1867784 | tf_op jit(solution)/shard_map/ppermute | solution.py:539
  212.1 1.6 collective-permute-start.44
  (16 other events, 158.3 us)

commit v3 on v2

--- a/solution.py
+++ b/solution.py
@@ -12,6 +12,7 @@
 VOCAB = 256
 SEQ_LEN = 1024
 CHUNK = 256
+SUB = 128
 HALF = 256
 PIECE = 16
 COLS_PROJ = 4 * HALF
@@ -143,15 +144,24 @@
     return jnp.concatenate([value * low, value * high], axis=0)
 
 
-def join(value):
-    return jnp.where(lanes_low(), value[:CHUNK], value[CHUNK:])
-
-
-def head_sum(value):
-    low = lanes_low()
-    first = jnp.sum(jnp.where(low, value, 0.0), axis=-1, keepdims=True)
-    second = jnp.sum(jnp.where(low, 0.0, value), axis=-1, keepdims=True)
-    return jnp.where(low, first, second)
+def head_ones():
+    row = (lax.broadcasted_iota(jnp.int32, (256, 128), 0) & 127) < HEAD
+    col = lax.broadcasted_iota(jnp.int32, (256, 128), 1) < HEAD
+    return (row == col).astype(F32).astype(BF16)
+
+
+def head_sum(value, ones):
+    high = value.astype(BF16)
+    rest = (value - high.astype(F32)).astype(BF16)
+    return nn(side(high, rest), ones)
+
+
+def sub_places(subs):
+    return [
+        (sub, pair, slice(SUB * sub, SUB * sub + SUB), slice(128 * pair, 128 * pair + 128))
+        for sub in subs
+        for pair in range(2)
+    ]
 
 
 def head_max(value):
@@ -162,66 +172,93 @@
 
 
 def same_head():
-    row = lax.broadcasted_iota(jnp.int32, (128, 128), 0) < HEAD
-    col = lax.broadcasted_iota(jnp.int32, (128, 128), 1) < HEAD
+    row = lax.broadcasted_iota(jnp.int32, (128, 256), 0) < HEAD
+    col = (lax.broadcasted_iota(jnp.int32, (128, 256), 1) & 127) < HEAD
     return row == col
 
 
-def causal_mask(rows, transposed=False):
-    row = lax.broadcasted_iota(jnp.int32, (rows, CHUNK), 0) & (CHUNK - 1)
-    col = lax.broadcasted_iota(jnp.int32, (rows, CHUNK), 1)
+def causal_pair(transposed=False):
+    row = lax.broadcasted_iota(jnp.int32, (SUB, 2 * SUB), 0)
+    col = lax.broadcasted_iota(jnp.int32, (SUB, 2 * SUB), 1) & (SUB - 1)
     return (row <= col) if transposed else (col <= row)
 
 
-def attend_kernel(
-    idx, a1, near, far,
-    q_o, k_o, v_o, e_o, x_o, p_o, s_o, z_o, r_o, o_o, kept_s, kept_u, w_o,
-    state_s, state_u, count_z,
-):
+def causal_whole(transposed=False):
+    row = lax.broadcasted_iota(jnp.int32, (CHUNK, CHUNK), 0)
+    col = lax.broadcasted_iota(jnp.int32, (CHUNK, CHUNK), 1)
+    keep = (row <= col) if transposed else (col <= row)
+    return keep.astype(F32).astype(BF16)
+
+
+def side(*values):
+    return jnp.concatenate(values, axis=1)
+
+
+def masked(keep, value):
+    return jnp.where(keep, value, 0.0).astype(BF16)
+
+
+def attend_kernel(idx, a1, near, far, proj_o, float_o, mixed_o, kept, w_o, state, count_z):
     step = pl.program_id(0)
 
     @pl.when(step == 0)
     def _():
         for shard, member, piece in each_piece(idx, near, far):
             w_o[rows_at(shard * 128 + member * PIECE, PIECE), :] = piece[...]
-        state_s[...] = jnp.zeros_like(state_s)
-        state_u[...] = jnp.zeros_like(state_u)
+        state[...] = jnp.zeros_like(state)
         count_z[...] = jnp.zeros_like(count_z)
 
     a = a1[...]
-    q_o[...] = nn(a, w_o[:, :HALF]).astype(BF16)
-    k_o[...] = nn(a, w_o[:, HALF : 2 * HALF]).astype(BF16)
-    v_o[...] = nn(a, w_o[:, 2 * HALF : 3 * HALF]).astype(BF16)
+    q_all = nn(a, w_o[:, :HALF]).astype(BF16)
+    k_all = nn(a, w_o[:, HALF : 2 * HALF]).astype(BF16)
     expo = jnp.exp(nn(a, w_o[:, 3 * HALF :]))
-    x_o[...] = expo
-    e_o[...] = expo.astype(BF16)
-    tri = causal_mask(2 * CHUNK)
-    total = nn(tri[:CHUNK].astype(F32).astype(BF16), e_o[...]) + count_z[...]
+    e_all = expo.astype(BF16)
+    v_all = nn(a, w_o[:, 2 * HALF : 3 * HALF]).astype(BF16)
+    for j, value in enumerate((q_all, k_all, v_all, e_all)):
+        proj_o[:, j * HALF : (j + 1) * HALF] = value
+    float_o[:, :HALF] = expo
+    total = nn(causal_whole(), e_all) + count_z[...]
     count_z[...] = total[CHUNK - 1 :, :]
     inverse = 1.0 / total
-    z_o[...] = inverse
+    float_o[:, HALF : 2 * HALF] = inverse
+    tri, block, ones = causal_pair(), same_head(), head_ones()
+    places = sub_places((0, 1))
+    lows, wide_e, numers, ratios = {}, {}, {}, {}
     for pair in range(2):
-        at = slice(128 * pair, 128 * pair + 128)
-        q, k, v, e = q_o[:, at], k_o[:, at], v_o[:, at], e_o[:, at]
-        inv = inverse[:, at]
-        low_s = state_s[pair].astype(BF16)
-        low_u = state_u[pair].astype(BF16)
-        kept_s[0, pair] = low_s
-        kept_u[0, pair] = low_u
-        scores = jnp.where(tri, nt(stacked(q), k), 0.0).astype(BF16)
-        numer = join(nn(scores, e)) + nn(q, low_s)
-        logits = (HEAD ** -0.5) * numer * inv
+        current = state[pair]
+        for sub in range(2):
+            rows, at = slice(SUB * sub, SUB * sub + SUB), slice(128 * pair, 128 * pair + 128)
+            lows[sub, pair] = current.astype(BF16)
+            kept[sub, pair] = lows[sub, pair]
+            wide_e[sub, pair] = stacked(e_all[rows, at])
+            more = tn(e_all[rows, at], side(k_all[rows, at], v_all[rows, at]))
+            current = current + jnp.where(block, more, 0.0)
+        state[pair] = current
+    for sub, pair, rows, at in places:
+        scores = masked(tri, nt(q_all[rows, at], stacked(k_all[rows, at])))
+        numer = nn(scores, wide_e[sub, pair])
+        numers[sub, pair] = numer + nt(q_all[rows, at], lows[sub, pair][:, :128])
+
+    def soften(sub, pair, rows, at):
+        inv = inverse[rows, at]
+        logits = (HEAD ** -0.5) * numers[sub, pair] * inv
         expd = jnp.exp(logits - head_max(logits))
-        probs = expd / head_sum(expd)
-        ratio = (probs * inv).astype(BF16)
-        mixing = jnp.where(tri, nt(stacked(ratio), e), 0.0).astype(BF16)
-        o_o[:, at] = (join(nn(mixing, v)) + nn(ratio, low_u)).astype(BF16)
-        s_o[:, at] = logits
-        p_o[:, at] = probs
-        r_o[:, at] = ratio
-        block = same_head()
-        state_s[pair] += jnp.where(block, tn(k, e), 0.0)
-        state_u[pair] += jnp.where(block, tn(e, v), 0.0)
+        probs = expd * (1.0 / head_sum(expd, ones))
+        ratios[sub, pair] = (probs * inv).astype(BF16)
+        float_o[rows, 2 * HALF + 128 * pair : 2 * HALF + 128 * pair + 128] = logits
+        float_o[rows, 3 * HALF + 128 * pair : 3 * HALF + 128 * pair + 128] = probs
+        mixed_o[rows, at] = ratios[sub, pair]
+
+    def mix(sub, pair, rows, at):
+        mixing = masked(tri, nt(ratios[sub, pair], wide_e[sub, pair]))
+        out = nn(mixing, stacked(v_all[rows, at])) + nn(ratios[sub, pair], lows[sub, pair][:, 128:])
+        mixed_o[rows, HALF + 128 * pair : HALF + 128 * pair + 128] = out.astype(BF16)
+
+    for i, place in enumerate(places):
+        soften(*place)
+        if i:
+            mix(*places[i - 1])
+    mix(*places[-1])
 
 
 def feed_kernel(
@@ -253,16 +290,19 @@
     bias = bias_up_of(vec, idx)
     branch = jnp.zeros((CHUNK, WIDTH), F32)
     scale = (2.0 / jnp.pi) ** 0.5
+    at = [slice(512 * j, 512 * j + 512) for j in range(4)]
+    products = nn(second, w_up[:, at[0]])
     for j in range(4):
-        at = slice(512 * j, 512 * j + 512)
-        z = nn(second, w_up[:, at]) + bias[:, at]
+        z = products + bias[:, at[j]]
+        if j < 3:
+            products = nn(second, w_up[:, at[j + 1]])
         zz = z * z
-        t = jnp.tanh(scale * z * (1.0 + 0.044715 * zz))
-        cdf = 0.5 * (1.0 + t)
-        act = (z * cdf).astype(BF16)
-        slope_o[:, at] = cdf + 0.5 * z * (1.0 - t * t) * (scale * (1.0 + 3 * 0.044715 * zz))
-        act_s[rows, at] = act
-        branch += nn(act, w_down[at, :])
+        cdf = 0.5 + 0.5 * jnp.tanh(z * (scale + (scale * 0.044715) * zz))
+        active = z * cdf
+        slope_o[:, at[j]] = cdf + (active - active * cdf) * (2 * scale + (6 * scale * 0.044715) * zz)
+        act = active.astype(BF16)
+        act_s[rows, at[j]] = act
+        branch += nn(act, w_down[at[j], :])
     out = (resid + (branch + vector_of(vec, idx, 4))).astype(BF16)
     out_o[...] = out
     out_s[rows, :] = out
@@ -280,12 +320,13 @@
 
     @pl.when(step == pl.num_programs(0) - 1)
     def _():
+        whole = tn(out_s[...], dl_s[...]).astype(BF16)
         for shard in range(4):
-            tile = tn(out_s[:, shard * 128 : shard * 128 + 128], dl_s[...]).astype(BF16)
+            tile = whole[shard * 128 : shard * 128 + 128]
             put_parts(idx, keep, send, tile, shard, slice(4 * WIDTH, None))
+            large = tn(act_s[:, shard * 512 : shard * 512 + 512], df_s[...]).astype(BF16)
             for xy in range(4):
-                start = shard * 512 + xy * 128
-                tile = tn(act_s[:, start : start + 128], df_s[...]).astype(BF16)
+                tile = large[xy * 128 : xy * 128 + 128]
                 own_first = idx[0] == 0
                 for i in range(4):
                     first = tile[16 * i : 16 * i + 16]
@@ -339,49 +380,43 @@
 
     @pl.when(step == pl.num_programs(0) - 1)
     def _():
+        for half in range(2):
+            large = tn((o0, o1)[half][...], da_s[...]).astype(BF16)
+            for i in range(2):
+                tile = large[128 * i : 128 * i + 128]
+                put_parts(idx, keep, send, tile, 2 * half + i, slice(0, WIDTH))
+        for j in range(4):
+            large = tn(a2_s[...], dz_s[:, 512 * j : 512 * j + 512]).astype(BF16)
+            at = slice(WIDTH + 512 * j, WIDTH + 512 * j + 512)
+            for shard in range(4):
+                put_parts(idx, keep, send, large[shard * 128 : shard * 128 + 128], shard, at)
+
+
+def proj_gradient(idx, unit_t, columns, w, dx, keep, send):
+    sums = nn(jnp.ones((PIECE, dx.shape[0]), BF16), dx[...])[:8]
+    high = sums.astype(BF16)
+    rest = (sums - high.astype(F32)).astype(BF16)
+    shift_rows = nt(jnp.concatenate([high, rest], axis=0), w[...])
+    gain, shift = columns[:, 0:1], columns[:, 1:2]
+    on_gain = jnp.zeros((WIDTH, HALF), F32)
+    for j in range(4):
+        at = slice(j * HALF, (j + 1) * HALF)
+        tile = nn(unit_t[...], dx[:, at])
+        on_gain += tile * w[:, at].astype(F32)
+        low = (tile * gain + shift * sums[:1, at]).astype(BF16)
         for shard in range(4):
-            half = (o0, o1)[shard // 2]
-            start = (shard % 2) * 128
-            tile = tn(half[:, start : start + 128], da_s[...]).astype(BF16)
-            put_parts(idx, keep, send, tile, shard, slice(0, WIDTH))
-            for j in range(4):
-                tile = tn(
-                    a2_s[:, shard * 128 : shard * 128 + 128], dz_s[:, 512 * j : 512 * j + 512]
-                ).astype(BF16)
-                at = slice(WIDTH + 512 * j, WIDTH + 512 * j + 512)
-                put_parts(idx, keep, send, tile, shard, at)
-
-
-def proj_gradient(idx, unit_t, columns, w, dx, keep, send):
-    ones = jnp.ones((PIECE, dx.shape[0]), BF16)
-    sums = nn(ones, dx[...])[:1]
-    shares = []
-    for shard in range(4):
-        rows = slice(shard * 128, shard * 128 + 128)
-        gain, shift = columns[rows, 0:1], columns[rows, 1:2]
-        on_gain = jnp.zeros((128, HALF), F32)
-        on_shift = jnp.zeros((128, HALF), F32)
-        for j in range(4):
-            at = slice(j * HALF, (j + 1) * HALF)
-            tile = nn(unit_t[rows, :], dx[:, at])
-            weight = w[rows, at].astype(F32)
-            on_gain += tile * weight
-            on_shift += weight * sums[:, at]
-            put_parts(idx, keep, send, (tile * gain + shift * sums[:, at]).astype(BF16), shard, at)
-        both = [jnp.sum(v, axis=1, keepdims=True) for v in (on_gain, on_shift)]
-        shares.append(jnp.concatenate(both + [jnp.zeros((128, 6), F32)], axis=1))
-    return jnp.concatenate(shares, axis=0).T
+            put_parts(idx, keep, send, low[shard * 128 : shard * 128 + 128], shard, at)
+    gain_column = jnp.sum(on_gain, axis=1, keepdims=True)
+    gain_row = side(gain_column, jnp.zeros((WIDTH, 7), F32)).T[:1]
+    return jnp.concatenate([gain_row, shift_rows[:1] + shift_rows[8:9], jnp.zeros((6, WIDTH), F32)])
 
 
 def attend_back_kernel(
-    idx, unit_t, columns, w, q_i, k_i, v_i, e_i, x_i, p_i, s_i, z_i, r_i, do_i, kept_s, kept_u,
+    idx, unit_t, columns, w, proj, floats, ratios, do_i, kept,
     dx_o, keep, send, share_o,
-    state_r, state_t, count_z, dx_s,
+    state, count_z, dx_s,
 ):
-    attend_back_step(
-        q_i, k_i, v_i, e_i, x_i, p_i, s_i, z_i, r_i, do_i, kept_s, kept_u,
-        dx_o, state_r, state_t, count_z, dx_s,
-    )
+    attend_back_step(proj, floats, ratios, do_i, kept, dx_o, state, count_z, dx_s)
 
     @pl.when(pl.program_id(0) == pl.num_programs(0) - 1)
     def _():
@@ -389,15 +424,12 @@
 
 
 def attend_back_last_kernel(
-    idx, unit_t, columns, w, q_i, k_i, v_i, e_i, x_i, p_i, s_i, z_i, r_i, do_i, kept_s, kept_u,
+    idx, unit_t, columns, w, proj, floats, ratios, do_i, kept,
     share, g_g2, g_b2, g_bd, g_bu,
     dx_o, keep, send,
-    state_r, state_t, count_z, dx_s,
+    state, count_z, dx_s,
 ):
-    attend_back_step(
-        q_i, k_i, v_i, e_i, x_i, p_i, s_i, z_i, r_i, do_i, kept_s, kept_u,
-        dx_o, state_r, state_t, count_z, dx_s,
-    )
+    attend_back_step(proj, floats, ratios, do_i, kept, dx_o, state, count_z, dx_s)
 
     @pl.when(pl.program_id(0) == pl.num_programs(0) - 1)
     def _():
@@ -413,55 +445,69 @@
                 send[xy, s ^ idx[2], :, COLS_PROJ:] = block
 
 
-def attend_back_step(
-    q_i, k_i, v_i, e_i, x_i, p_i, s_i, z_i, r_i, do_i, kept_s, kept_u,
-    dx_o, state_r, state_t, count_z, dx_s,
-):
+def attend_back_step(proj, floats, ratios, do_i, kept, dx_o, state, count_z, dx_s):
     step = pl.program_id(0)
     chunk = pl.num_programs(0) - 1 - step
 
     @pl.when(step == 0)
     def _():
-        state_r[...] = jnp.zeros_like(state_r)
-        state_t[...] = jnp.zeros_like(state_t)
+        state[...] = jnp.zeros_like(state)
         count_z[...] = jnp.zeros_like(count_z)
 
-    rows = pl.ds(pl.multiple_of(chunk * CHUNK, CHUNK), CHUNK)
-    tri = causal_mask(2 * CHUNK)
-    trt = causal_mask(2 * CHUNK, True)
-    later = trt[:CHUNK].astype(F32).astype(BF16)
-    for pair in range(2):
-        at = slice(128 * pair, 128 * pair + 128)
-        q, k, v, e = q_i[:, at], k_i[:, at], v_i[:, at], e_i[:, at]
-        ratio, do = r_i[:, at], do_i[:, at]
-        probs, logits, inv = p_i[:, at], s_i[:, at], z_i[:, at]
-        low_s, low_u = kept_s[0, pair], kept_u[0, pair]
-        low_r = state_r[pair].astype(BF16)
-        low_t = state_t[pair].astype(BF16)
-        d_mix = jnp.where(tri, nt(stacked(do), v), 0.0).astype(BF16)
-        d_ratio = (join(nn(d_mix, e)) + nt(do, low_u)) * inv
-        d_logits = probs * (d_ratio - head_sum(d_ratio * probs))
-        d_numer = ((HEAD ** -0.5) * d_logits * inv).astype(BF16)
-        d_total = (-d_ratio * (probs * inv) - d_logits * logits * inv).astype(BF16)
-        d_scores = jnp.where(tri, nt(stacked(d_numer), e), 0.0).astype(BF16)
-        dq = join(nn(d_scores, k)) + nt(d_numer, low_s)
-        scores = jnp.where(trt, nt(stacked(k), q), 0.0).astype(BF16)
-        wide_e = stacked(e)
-        mixing = jnp.where(trt, nt(wide_e, ratio), 0.0).astype(BF16)
-        d_mix_t = jnp.where(trt, nt(stacked(v), do), 0.0).astype(BF16)
-        d_scores_t = jnp.where(trt, nt(wide_e, d_numer), 0.0).astype(BF16)
-        dv = join(nn(mixing, do)) + nn(e, low_r)
-        dk = join(nn(d_scores_t, q)) + nt(e, low_t)
-        total_z = nn(later, d_total) + count_z[:, at]
-        count_z[:, at] = total_z[:1, :]
-        de = join(nn(d_mix_t, ratio) + nn(scores, d_numer)) + nt(v, low_r) + nn(k, low_t) + total_z
-        dc = de * x_i[:, at]
+    def take(ref, j, rows, pair):
+        return ref[rows, j * HALF + 128 * pair : j * HALF + 128 * pair + 128]
+
+    tri, trt, block, ones = causal_pair(), causal_pair(True), same_head(), head_ones()
+    places = sub_places((1, 0))
+    d_mixes, wide, d_numers, d_totals, others = {}, {}, {}, {}, {}
+    for sub, pair, rows, at in places:
+        v = take(proj, 2, rows, pair)
+        d_mixes[sub, pair] = masked(tri, nt(do_i[rows, at], stacked(v)))
+        wide[sub, pair] = stacked(take(proj, 3, rows, pair))
+    for sub, pair, rows, at in places:
+        do, ratio = do_i[rows, at], ratios[rows, at]
+        q, k, v, e = [take(proj, j, rows, pair) for j in range(4)]
+        inv, logits, probs = [take(floats, j, rows, pair) for j in (1, 2, 3)]
+        d_ratio = nn(d_mixes[sub, pair], wide[sub, pair])
+        d_ratio = (d_ratio + nt(do, kept[sub, pair][:, 128:])) * inv
+        weighed = d_ratio * probs
+        d_logits = weighed - probs * head_sum(weighed, ones)
+        d_numers[sub, pair] = ((HEAD ** -0.5) * d_logits * inv).astype(BF16)
+        d_totals[sub, pair] = (-(weighed + d_logits * logits) * inv).astype(BF16)
+        wide_q, wide_r, wide_do = stacked(q), stacked(ratio), stacked(do)
+        scores = masked(trt, nt(k, wide_q))
+        mixing = masked(trt, nt(e, wide_r))
+        d_mix_t = masked(trt, nt(v, wide_do))
+        others[sub, pair] = (scores, d_mix_t, nn(mixing, wide_do), wide_q, wide_r)
+    d_total = jnp.concatenate([side(d_totals[sub, 0], d_totals[sub, 1]) for sub in range(2)], axis=0)
+    total_z = nn(causal_whole(True), d_total) + count_z[...]
+    count_z[...] = total_z[:1, :]
+    currents = [state[0], state[1]]
+    lows = {}
+    for sub, pair, rows, at in places:
+        lows[sub, pair] = currents[pair].astype(BF16)
+        more = side(
+            tn(ratios[rows, at], do_i[rows, at]), tn(d_numers[sub, pair], take(proj, 0, rows, pair))
+        )
+        currents[pair] = currents[pair] + jnp.where(block, more, 0.0)
+    state[0], state[1] = currents
+    for sub, pair, rows, at in places:
+        k, v, e = [take(proj, j, rows, pair) for j in (1, 2, 3)]
+        scores, d_mix_t, dv, wide_q, wide_r = others[sub, pair]
+        d_numer, low = d_numers[sub, pair], lows[sub, pair]
+        wide_n = stacked(d_numer)
+        d_scores = masked(tri, nt(d_numer, wide[sub, pair]))
+        d_scores_t = masked(trt, nt(e, wide_n))
+        both = nn(e, low)
+        de = nn(side(d_mix_t, scores), jnp.concatenate([wide_r, wide_n], axis=0))
+        de = de + nt(side(v, k), low) + total_z[rows, at]
+        dq = nn(d_scores, stacked(k)) + nn(d_numer, kept[sub, pair][:, :128])
+        dk = nn(d_scores_t, wide_q) + both[:, 128:]
+        dv = dv + both[:, :128]
+        dc = de * take(floats, 0, rows, pair)
         for j, value in enumerate((dq, dk, dv, dc)):
-            dx_o[:, j * HALF + 128 * pair : j * HALF + 128 * pair + 128] = value.astype(BF16)
-        block = same_head()
-        state_r[pair] += jnp.where(block, tn(ratio, do), 0.0)
-        state_t[pair] += jnp.where(block, tn(q, d_numer), 0.0)
-    dx_s[rows, :] = dx_o[...]
+            dx_o[rows, j * HALF + 128 * pair : j * HALF + 128 * pair + 128] = value.astype(BF16)
+    dx_s[pl.ds(pl.multiple_of(chunk * CHUNK, CHUNK), CHUNK), :] = dx_o[...]
 
 
 def inputs_kernel(idx, vec, x, dh, dx0, dx1, w0, w1, dx_o):
@@ -547,6 +593,14 @@
     return [swap(piece, "shard", shards, k) for k in range(1, 4)]
 
 
+def near_pair(piece, shards):
+    return jnp.stack([piece, swap(piece, "shard", shards, 1)])
+
+
+def far_pair(pair, shards):
+    return swap(pair, "shard", shards, 2)
+
+
 def sum_of(values):
     values = [v.astype(F32) for v in values]
     return ((values[0] + values[1]) + (values[2] + values[3])).astype(BF16)
@@ -564,12 +618,29 @@
     return [sum_of([parts[0][k], got[0][k], got[1][k], got[2][k]]) for k in range(4)]
 
 
-def shard_start(rows, shards):
-    return [swap(rows[k], "shard", shards, k) for k in range(1, 4)]
-
-
-def shard_sum(rows, got, dp):
-    total = sum_of([rows[0]] + got)
+def plane_halves(parts, got):
+    total = [p.astype(F32) for p in [parts[0]] + got]
+    total = ((total[0] + total[1]) + (total[2] + total[3])).astype(BF16)
+    return total[:2], total[2:]
+
+
+def half_start(high, shards):
+    return swap(high, "shard", shards, 2)
+
+
+def half_sum(low, got):
+    return [(low[k].astype(F32) + got[k].astype(F32)).astype(BF16) for k in range(2)]
+
+
+def last_start(pair, shards):
+    return swap(pair[1], "shard", shards, 1)
+
+
+def last_sum(pair, got, dp):
+    return across_planes((pair[0].astype(F32) + got.astype(F32)).astype(BF16), dp)
+
+
+def across_planes(total, dp):
     distance = 8
     while distance < dp:
         total = (total.astype(F32) + swap(total, "dp", dp, distance).astype(F32)).astype(BF16)
@@ -577,10 +648,12 @@
     return total
 
 
-def spread(total, dp):
-    pair = jnp.stack([total, swap(total, "dp", dp, 2)])
-    near = jnp.concatenate([pair, swap(pair, "dp", dp, 4)])
-    return near, swap(near, "dp", dp, 1)
+def shard_start(rows, shards):
+    return [swap(rows[k], "shard", shards, k) for k in range(1, 4)]
+
+
+def shard_sum(rows, got, dp):
+    return across_planes(sum_of([rows[0]] + got), dp)
 
 
 def body(dp, shards):
@@ -608,14 +681,14 @@
             [(size, BF16, None) for size in sizes],
             scratch=[pltpu.SemaphoreType.DMA((20,))],
         )
-        pa, pu, pd = pin(pa, pu, pd)
         got_a = near_rows(pa, shards)
+        pair_u = near_pair(pu, shards)
         rows_a = jnp.stack([pa[:, :COLS_BOTH]] + [g[:, :COLS_BOTH] for g in got_a])
         vec = jnp.stack([pa[:, COLS_BOTH:]] + [g[:, COLS_BOTH:] for g in got_a])
-        rows_a, vec, pu, pd, tokens_a = pin(rows_a, vec, pu, pd, tokens)
+        rows_a, vec, pair_u, pd, tokens_a = pin(rows_a, vec, pair_u, pd, tokens)
         plane_a = [swap(rows_a, "dp", dp, 2 * k) for k in range(1, 4)]
-        got_u = near_rows(pu, shards)
-        got_d = near_rows(pd, shards)
+        got_u = far_pair(pair_u, shards)
+        pair_d = near_pair(pd, shards)
         a1, unit_t, columns = call(
             first_norm_kernel,
             "first_norm",
@@ -627,52 +700,59 @@
             ],
         )
         target = targets.reshape(count, 1)
-        plane_a, a1, unit_t, columns, target = pin(plane_a, a1, unit_t, columns, target)
+        plane_a, got_u, pair_d, a1, unit_t, columns, target = pin(
+            plane_a, got_u, pair_d, a1, unit_t, columns, target
+        )
         near_a = jnp.stack([rows_a] + plane_a)
         far_a = swap(near_a, "dp", dp, 1)
-        near_a, got_u, got_d, a1 = pin(near_a, got_u, got_d, a1)
-        rows_u = jnp.stack([pu] + got_u)
-        plane_u = [swap(rows_u, "dp", dp, 2 * k) for k in range(1, 4)]
-        rows_d = jnp.stack([pd] + got_d)
-        plane_d = [swap(rows_d[:, 0], "dp", dp, 2 * k) for k in range(1, 3)]
-        far_a, a1 = pin(far_a, a1)
-
-        kept = ((1, 2, 128, 128), lambda i: (i, 0, 0, 0))
+        got_d = far_pair(pair_d, shards)
+        got_u, _ = pin(got_u, near_a)
+        rows_u = jnp.concatenate([pair_u, got_u])
+        plane_u = plane_start([rows_u] * 4, dp)
+
+        kept = ((2, 2, 128, 256), lambda i: (i, 0, 0, 0))
 
         def attend(a1, half):
             at = ((4, 4, PIECE, COLS_PROJ), lambda i: (0, 0, 0, half))
-            names = [((count, HALF), t, tok(HALF)) for t in (BF16,) * 4 + (F32,) * 4 + (BF16,) * 2]
-            states = [((steps, 2, 128, 128), BF16, kept)] * 2
             return call(
                 attend_kernel,
                 "attend",
                 [(idx, None), (a1, tok(WIDTH)), (near_a, at), (far_a, at)],
-                names + states + [((WIDTH, COLS_PROJ), BF16, None)],
+                [
+                    ((count, COLS_PROJ), BF16, tok(COLS_PROJ)),
+                    ((count, COLS_PROJ), F32, tok(COLS_PROJ)),
+                    ((count, 2 * HALF), BF16, tok(2 * HALF)),
+                    ((2 * steps, 2, 128, 256), BF16, kept),
+                    ((WIDTH, COLS_PROJ), BF16, None),
+                ],
                 steps,
                 [
-                    pltpu.VMEM((2, 128, 128), F32),
-                    pltpu.VMEM((2, 128, 128), F32),
+                    pltpu.VMEM((2, 128, 256), F32),
                     pltpu.VMEM((1, HALF), F32),
                 ],
                 flops=6e9,
             )
 
         first = attend(a1, 0)
-        first, plane_u, plane_d, a1 = pin(first, plane_u, plane_d, a1)
+        first, plane_u, got_d, a1 = pin(first, plane_u, got_d, a1)
+        rows_d = jnp.concatenate([pair_d, got_d])
+        plane_d = [swap(rows_d[:, 0], "dp", dp, 2 * k) for k in range(1, 3)]
         near_u = jnp.stack([rows_u] + plane_u)
         far_u = swap(near_u, "dp", dp, 1)
+        second = attend(a1, 1)
+        second, far_u, plane_d = pin(second, far_u, plane_d)
         near_d = jnp.stack([rows_d[:, 0]] + plane_d + [rows_d[:, 1]])
         far_d = swap(near_d, "dp", dp, 1)
-        second = attend(a1, 1)
-        second, far_u, far_d = pin(second, far_u, far_d)
         halves = (first, second)
-        o0, o1 = first[9], second[9]
+        o0, o1 = first[2], second[2]
+        mixed_at = ((CHUNK, HALF), lambda i: (i, 1))
+        mixed_all = ((count, HALF), lambda i: (0, 1))
 
         out, h, slope, dy, g_bias_down, keep_d, send_d = call(
             feed_kernel,
             "feed_forward",
             [
-                (idx, None), (vec, None), (tokens, tok(WIDTH)), (o0, tok(HALF)), (o1, tok(HALF)),
+                (idx, None), (vec, None), (tokens, tok(WIDTH)), (o0, mixed_at), (o1, mixed_at),
                 (target, tok(1)), (near_u, None), (far_u, None), (near_d, None), (far_d, None),
             ],
             [
@@ -704,7 +784,7 @@
             "feed_backward",
             [
                 (idx, None), (vec, None), (h, tok(WIDTH)), (slope, tok(FF)), (dy, tok(WIDTH)),
-                (o0, None), (o1, None),
+                (o0, mixed_all), (o1, mixed_all),
                 (near_u, None), (far_u, None), (near_d, None), (far_d, None),
             ],
             [
@@ -733,11 +813,11 @@
         sum_d, d_mixed = pin(sum_d, d_mixed)
         got_d = plane_start(sum_d, dp)
 
-        kept_back = ((1, 2, 128, 128), lambda i: (steps - 1 - i, 0, 0, 0))
+        kept_back = ((2, 2, 128, 256), lambda i: (steps - 1 - i, 0, 0, 0))
 
         def attend_back(half, d_mixed, extra=()):
-            q, k, v, e, x, p, s, z, r, _, ks, ku, w = halves[half]
-            tb = ((CHUNK, HALF), back)
+            proj, floats, mixed, states, w = halves[half]
+            wide = ((CHUNK, COLS_PROJ), back)
             column = ((CHUNK, HALF), lambda i: (steps - 1 - i, half))
             last = half == 1
             cols = COLS_LAST if last else COLS_PROJ
@@ -745,8 +825,8 @@
                 attend_back_last_kernel if last else attend_back_kernel,
                 "attend_backward",
                 [(idx, None), (unit_t, None), (columns, None), (w, None)]
-                + [(t, tb) for t in (q, k, v, e, x, p, s, z, r)]
-                + [(d_mixed, column), (ks, kept_back), (ku, kept_back)]
+                + [(proj, wide), (floats, wide), (mixed, ((CHUNK, HALF), back))]
+                + [(d_mixed, column), (states, kept_back)]
                 + [(t, None) for t in extra],
                 [
                     ((count, COLS_PROJ), BF16, ((CHUNK, COLS_PROJ), back)),
@@ -756,8 +836,7 @@
                 + ([] if last else [((8, WIDTH), F32, None)]),
                 steps,
                 [
-                    pltpu.VMEM((2, 128, 128), F32),
-                    pltpu.VMEM((2, 128, 128), F32),
+                    pltpu.VMEM((2, 128, 256), F32),
                     pltpu.VMEM((1, HALF), F32),
                     pltpu.VMEM((count, COLS_PROJ), BF16),
                 ],
@@ -768,10 +847,10 @@
         got_d, got_u, send_a, d_mixed = pin(got_d, got_u, send_a, d_mixed)
         got_a = swap(send_a, "dp", dp, 1)
         sum_u = core_sum(keep_u, got_u)
-        rows_d = plane_sum(sum_d, got_d)
-        sum_u, rows_d, d_mixed = pin(sum_u, rows_d, d_mixed)
+        low_d, high_d = plane_halves(sum_d, got_d)
+        sum_u, low_d, high_d, d_mixed = pin(sum_u, low_d, high_d, d_mixed)
         got_u = plane_start(sum_u, dp)
-        got_d = shard_start(rows_d, shards)
+        got_d = half_start(high_d, shards)
 
         extra = (share, g_gain_two, g_bias_two, g_bias_down, g_bias_up)
         dx1, keep_b, send_b = attend_back(1, d_mixed, extra)
@@ -781,29 +860,47 @@
             jnp.concatenate(both, axis=-1)
             for both in zip(core_sum(keep_a, got_a), core_sum(keep_b, got_b))
         ]
-        sum_p, got_u, dx1 = pin(sum_p, got_u, dx1)
+        sum_p, dx1 = pin(sum_p, dx1)
         got_p = plane_start(sum_p, dp)
-        rows_u = plane_sum(sum_u, got_u)
-        got_u = shard_start(rows_u, shards)
+        got_u, got_d, _ = pin(got_u, got_d, sum_p)
+        low_u, high_u = plane_halves(sum_u, got_u)
+        got_u = half_start(high_u, shards)
+        pair_d = half_sum(low_d, got_d)
+        got_d = last_start(pair_d, shards)
         d_tokens = call(
             inputs_kernel,
             "input_gradient",
             [
                 (idx, None), (vec, None), (tokens, tok(WIDTH)), (dh, tok(WIDTH)),
                 (dx0, tok(COLS_PROJ)), (dx1, tok(COLS_PROJ)),
-                (first[12], None), (second[12], None),
+                (first[4], None), (second[4], None),
             ],
             [((count, WIDTH), F32, tok(WIDTH))],
             steps,
             flops=3e9,
         )[0]
-        got_p, got_u, got_d, d_tokens = pin(got_p, got_u, got_d, d_tokens)
+        got_u, got_p, got_d, d_tokens = pin(got_u, got_p, got_d, d_tokens)
+        pair_u = half_sum(low_u, got_u)
+        got_u = last_start(pair_u, shards)
+        total_d = last_sum(pair_d, got_d, dp)
         rows_p = plane_sum(sum_p, got_p)
         got_p = shard_start(rows_p, shards)
-        total_u = shard_sum(rows_u, got_u, dp)
-        total_d = shard_sum(rows_d, got_d, dp)
-        near_f, far_f = spread(jnp.concatenate([total_u, total_d], axis=-1), dp)
-        near_p, far_p = spread(shard_sum(rows_p, got_p, dp), dp)
+        got_u, _ = pin(got_u, rows_p)
+        total_f = jnp.concatenate([last_sum(pair_u, got_u, dp), total_d], axis=-1)
+        along_f = swap(total_f, "dp", dp, 4)
+        got_p, _ = pin(got_p, total_f)
+        pair_f = jnp.stack([total_f, along_f])
+        up_f = swap(pair_f, "dp", dp, 2)
+        total_p = shard_sum(rows_p, got_p, dp)
+        along_p = swap(total_p, "dp", dp, 4)
+        pair_p = jnp.stack([total_p, along_p])
+        up_p = swap(pair_p, "dp", dp, 2)
+        up_f, _ = pin(up_f, pair_p)
+        near_f = jnp.stack([pair_f, up_f], axis=1).reshape((4,) + total_f.shape)
+        far_f = swap(near_f, "dp", dp, 1)
+        up_p, _ = pin(up_p, near_f)
+        near_p = jnp.stack([pair_p, up_p], axis=1).reshape((4,) + total_p.shape)
+        far_p = swap(near_p, "dp", dp, 1)
         g_mix, g_up, g_down, g_read = call(
             unpack_feed_kernel,
             "unpack_feed",
@@ -815,6 +912,7 @@
                 ((rows, VOCAB), F32, None),
             ],
         )
+        far_p, g_up = pin(far_p, g_up)
         g_query, g_key, g_value, g_control, g1, b1, g2, b2, bd, bu = call(
             unpack_proj_kernel,
             "unpack_proj",

time: 221 us -> 198 us (0.90)
  waiting for transfers between devices: 42.1 us -> 30.3 us
  Pallas kernels: 117 us -> 108 us
  starting transfers between devices: 52.2 us -> 47 us
  local copies, waits for them, and re-layouts: 4.28 us -> 6.88 us
    ppermute x48 -> x44, waiting for transfers between devices: 42.1 us -> 30.3 us  [swap(): return lax.ppermute(value, axis, [(i, i ^ distance) for i in range(size)])]
    pallas_call x11, Pallas kernels: 117 us -> 108 us  [call(): pl.pallas_call(kernel, grid=grid, in_specs=in_specs, out_specs=[spec(shap...]
    ppermute x48 -> x44, starting transfers between devices: 52.2 us -> 47 us  [swap(): return lax.ppermute(value, axis, [(i, i ^ distance) for i in range(size)])]
    unnamed x32 -> x34, local copies, waits for them, and re-layouts: 1.6 us -> 4.1 us
  transfers between devices with their start and end apart: 48 -> 44, of which waited for: 21 -> 18; matrix products, arithmetic and copies ran while one was open for 2% -> 2% of each run, Pallas kernels for 41% -> 41%
where the time goes in v3:
time: 198 us
  Pallas kernels  108 us (55%)
  starting transfers between devices  47 us (24%)
  waiting for transfers between devices  30.3 us (15%)
  local copies, waits for them, and re-layouts  6.88 us (3%)
  other arithmetic  4.49 us (2%)
    pallas_call x11, Pallas kernels, call(): pl.pallas_call(kernel, grid=grid, in_specs=in_specs, out_specs=[spec(shap...  108 us
    ppermute x44, starting transfers between devices, swap(): return lax.ppermute(value, axis, [(i, i ^ distance) for i in range(size)])  47 us
    ppermute x44, waiting for transfers between devices, swap(): return lax.ppermute(value, axis, [(i, i ^ distance) for i in range(size)])  30.3 us
    unnamed x34, local copies, waits for them, and re-layouts  4.1 us
  transfers between devices with their start and end apart: 44, of which 18 were waited for; matrix products, arithmetic and copies ran while one was open for 2% of the time, Pallas kernels for 41%

profile of v3, /device:TPU:0, one launch (start us, length us, event | category | flops | bytes accessed | tf_op | source)
XLA Modules:
  0.0 197.7 jit_solution(7958826986512502555)
XLA Ops:
  1.3 2.7 %pack_weights.1 = (bf16[16,2176]{1,0:T(8,128)(2,1)}, bf16[16,2560]{1,0:T(8,128)(2,1)}, bf16[2,16,2304]{2,1,0:T(8,128)(2,1)}) custom-call(s32[3]{0:T(128)} %pad_add_fusion.idx, bf16[128]{0:T(256)(128)(2,1)} %g1.1, bf16[128]{0:T(256)(128)(2,1)} %b1.1, bf16[128]{0:T(256)(128)(2,1)} %g2.1, bf16[128]{0:T(256)(128)(2,1)} %b2.1, bf16[128]{0:T(256)(128)(2,1)} %bd.1, ...), custom_call_target="tpu_custom_call" | custom-call | bytes 1771788 | tf_op jit(solution)/shard_map/pack_weights/pallas_call | solution.py:568
  4.0 5.1 %collective-permute-start.2 = (bf16[16,2176]{1,0:T(8,128)(2,1)}, bf16[16,2176]{1,0:T(8,128)(2,1)S(1)}, u32[]{:S(2)}, u32[]{:S(2)}) collective-permute-start(bf16[16,2176]{1,0:T(8,128)(2,1)} %get-tuple-element.151), channel_id=1, source_target_pairs={{0,3},{1,2},{2,1},{3,0},{4,7},{5,6},{6,5},{7,4},{8,11},{9,10},{10,... | collective-permute-start | bytes 208904 | tf_op jit(solution)/shard_map/ppermute | solution.py:585
  9.8 1.4 collective-permute-start.3
  12.7 2.7 %collective-permute-done.1 = bf16[16,2176]{1,0:T(8,128)(2,1)S(1)} collective-permute-done((bf16[16,2176]{1,0:T(8,128)(2,1)}, bf16[16,2176]{1,0:T(8,128)(2,1)S(1)}, u32[]{:S(2)}, u32[]{:S(2)}) %collective-permute-start.1) | collective-permute-done | bytes 69664 | tf_op jit(solution)/shard_map/ppermute | solution.py:585
  16.5 0.9 pad_maximum_fusion.12
  17.4 1.6 collective-permute-start.8
  19.0 2.4 %collective-permute-start.6 = (bf16[4,16,2048]{2,1,0:T(8,128)(2,1)S(1)}, bf16[4,16,2048]{2,1,0:T(8,128)(2,1)S(1)}, u32[]{:S(2)}, u32[]{:S(2)}) collective-permute-start(bf16[4,16,2048]{2,1,0:T(8,128)(2,1)S(1)} %pad_maximum_fusion.11), channel_id=1, source_target_pairs={{0,24},{4,28},{8,16},{12,20},{16,8},{20,12},{24,0},{28,4},{1,25},{... | collective-permute-start | bytes 786440 | tf_op jit(solution)/shard_map/ppermute | solution.py:585
  22.5 1.9 collective-permute-start.7
  24.4 3.5 %first_norm.1 = (bf16[1024,512]{1,0:T(8,128)(2,1)}, bf16[512,1024]{1,0:T(8,128)(2,1)}, f32[512,8]{1,0:T(8,128)}) custom-call(s32[3]{0:T(128)} %pad_add_fusion.idx, bf16[4,16,128]{2,1,0:T(8,128)(2,1)} %pad_maximum_fusion.15.vec, bf16[1024,512]{1,0:T(8,128)(2,1)} %x.4), custom_call_target="tpu_custom_call" | custom-call | bytes 1064972 | tf_op jit(solution)/shard_map/first_norm/pallas_call | solution.py:568
  28.0 2.9 %collective-permute-done.7 = bf16[2,16,2560]{2,1,0:T(8,128)(2,1)S(1)} collective-permute-done((bf16[2,16,2560]{2,1,0:T(8,128)(2,1)S(1)}, bf16[2,16,2560]{2,1,0:T(8,128)(2,1)S(1)}, u32[]{:S(2)}, u32[]{:S(2)}) %collective-permute-start.7) | collective-permute-done | bytes 163872 | tf_op jit(solution)/shard_map/ppermute | solution.py:585
  30.9 1.6 collective-permute-done.5
  32.8 1.7 collective-permute-start.12
  34.6 1.3 collective-permute-start.11
  36.4 2.4 %collective-permute-start.13 = (bf16[2,2,16,2304]{3,2,0,1:T(8,128)(2,1)S(1)}, bf16[2,2,16,2304]{3,2,0,1:T(8,128)(2,1)S(1)}, u32[]{:S(2)}, u32[]{:S(2)}) collective-permute-start(bf16[2,2,16,2304]{3,2,0,1:T(8,128)(2,1)S(1)} %pad_maximum_fusion.5), channel_id=1, source_target_pairs={{0,2},{1,3},{2,0},{3,1},{4,6},{5,7},{6,4},{7,5},{8,10},{9,11},{10,... | collective-permute-start | bytes 884744 | tf_op jit(solution)/shard_map/ppermute | solution.py:585
  38.8 1.0 copy-done.14
  39.8 9.5 %attend.2 = (bf16[1024,1024]{1,0:T(8,128)(2,1)}, f32[1024,1024]{1,0:T(8,128)}, bf16[1024,512]{1,0:T(8,128)(2,1)}, bf16[8,2,128,256]{3,2,1,0:T(8,128)(2,1)}, bf16[512,1024]{1,0:T(8,128)(2,1)}) custom-call(s32[3]{0:T(128)} %pad_add_fusion.idx, bf16[1024,512]{1,0:T(8,128)(2,1)} %get-tuple-element.175.a1, bf16[4,4,16,2048]{3,2,1,0:T(8,128)(2,1)} %copy-done.6, ...), custom_call_target="tpu_custom_call" | custom-call | flops 6000000000 | bytes 3145740 | tf_op jit(solution)/shard_map/attend/pallas_call | solution.py:568
  49.3 2.9 %collective-permute-done.13 = bf16[2,2,16,2304]{3,2,0,1:T(8,128)(2,1)S(1)} collective-permute-done((bf16[2,2,16,2304]{3,2,0,1:T(8,128)(2,1)S(1)}, bf16[2,2,16,2304]{3,2,0,1:T(8,128)(2,1)S(1)}, u32[]{:S(2)}, u32[]{:S(2)}) %collective-permute-start.13) | collective-permute-done | bytes 294944 | tf_op jit(solution)/shard_map/ppermute | solution.py:585
  52.6 1.5 collective-permute-start.16
  54.8 9.5 %attend.3 = (bf16[1024,1024]{1,0:T(8,128)(2,1)}, f32[1024,1024]{1,0:T(8,128)}, bf16[1024,512]{1,0:T(8,128)(2,1)}, bf16[8,2,128,256]{3,2,1,0:T(8,128)(2,1)}, bf16[512,1024]{1,0:T(8,128)(2,1)}) custom-call(s32[3]{0:T(128)} %pad_add_fusion.idx, bf16[1024,512]{1,0:T(8,128)(2,1)} %get-tuple-element.175.a1, bf16[4,4,16,2048]{3,2,1,0:T(8,128)(2,1)} %copy-done.6, ...), custom_call_target="tpu_custom_call" | custom-call | flops 6000000000 | bytes 3145740 | tf_op jit(solution)/shard_map/attend/pallas_call | solution.py:568
  65.0 1.0 copy.34.target
  66.1 1.5 collective-permute-done.17.down_far
  67.6 21.7 %feed_forward.1 = (bf16[1024,512]{1,0:T(8,128)(2,1)}, f32[1024,512]{1,0:T(8,128)}, f32[1024,2048]{1,0:T(8,128)}, f32[1024,512]{1,0:T(8,128)}, f32[1,512]{1,0:T(1...) custom-call(s32[3]{0:T(128)} %pad_add_fusion.idx, bf16[4,16,128]{2,1,0:T(8,128)(2,1)} %pad_maximum_fusion.15.vec, ...), custom_call_target="tpu_custom_call" | custom-call | flops 8000000000 | bytes 8146956 | tf_op jit(solution)/shard_map/feed_forward/pallas_call | solution.py:568
  89.6 17.6 %feed_backward.1 = (f32[1024,512]{1,0:T(8,128)}, bf16[1024,512]{1,0:T(8,128)(2,1)}, f32[1,512]{1,0:T(1,128)}, f32[1,512]{1,0:T(1,128)}, f32[1,2048]{1,0:T(1,128)...) custom-call(s32[3]{0:T(128)} %pad_add_fusion.idx, bf16[4,16,128]{2,1,0:T(8,128)(2,1)} %pad_maximum_fusion.15.vec, ...), custom_call_target="tpu_custom_call" | custom-call | flops 8000000000 | bytes 19677196 | tf_op jit(solution)/shard_map/feed_backward/pallas_call | solution.py:568
  107.9 1.3 collective-permute-start.19
  109.9 1.7 collective-permute-start.21
  111.5 15.1 %attend_backward.2 = (bf16[1024,1024]{1,0:T(8,128)(2,1)}, bf16[4,4,16,1024]{3,2,1,0:T(8,128)(2,1)}, bf16[4,4,16,1024]{3,2,1,0:T(8,128)(2,1)}, f32[8,512]{1,0:T(8,128)}) custom-call(s32[3]{0:T(128)} %pad_add_fusion.idx, bf16[512,1024]{1,0:T(8,128)(2,1)} %get-tuple-element.205.unit_t, f32[512,8]{1,0:T(8,128)} %get-tuple-element.206.columns, ...), custom_call_target="tpu_custom_call" | custom-call | flops 10000000000 | bytes 11550732 | tf_op jit(solution)/shard_map/attend_backward/pallas_call | solution.py:568
  126.9 1.1 copy-done.2
  128.3 1.2 collective-permute-start.23
  129.5 1.2 collective-permute-start.24
  131.4 1.7 collective-permute-start.26
  133.0 15.4 %attend_backward.3 = (bf16[1024,1024]{1,0:T(8,128)(2,1)}, bf16[4,4,16,1152]{3,2,1,0:T(8,128)(2,1)}, bf16[4,4,16,1152]{3,2,1,0:T(8,128)(2,1)}) custom-call(s32[3]{0:T(128)} %pad_add_fusion.idx, bf16[512,1024]{1,0:T(8,128)(2,1)} %get-tuple-element.205.unit_t, f32[512,8]{1,0:T(8,128)} %get-tuple-element.206.columns, bf16[512,1024]{1,0:T(8,128)(2,1)} %get-tuple-element.225.w.w1, ...), custom_call_target="tpu_custom_call" | custom-call | flops 10000000000 | bytes 11581452 | tf_op jit(solution)/shard_map/attend_backward/pallas_call | solution.py:568
  149.3 1.6 collective-permute-done.28
  151.1 1.3 collective-permute-start.30
  153.1 1.7 collective-permute-start.32
  154.7 1.6 collective-permute-start.33
  156.9 7.5 %input_gradient.1 = f32[1024,512]{1,0:T(8,128)} custom-call(s32[3]{0:T(128)} %pad_add_fusion.idx, bf16[4,16,128]{2,1,0:T(8,128)(2,1)} %pad_maximum_fusion.15.vec, bf16[1024,512]{1,0:T(8,128)(2,1)} %x.4, f32[1024,512]{1,0:T(8,128)} %get-tuple-element.255.dh, bf16[1024,1024]{1,0:T(8,128)(2,1)} %get-tuple-element.256.dx0, ...), custom_call_target="tpu_custom_call" | custom-call | flops 3000000000 | bytes 9453580 | tf_op jit(solution)/shard_map/input_gradient/pallas_call | solution.py:568
  164.4 1.9 collective-permute-done.29
  167.1 1.7 collective-permute-start.37
  169.0 1.7 collective-permute-start.36
  170.9 2.5 %collective-permute-start.34 = (bf16[16,2176]{1,0:T(8,128)(2,1)S(1)}, bf16[16,2176]{1,0:T(8,128)(2,1)S(1)}, u32[]{:S(2)}, u32[]{:S(2)}) collective-permute-start(bf16[16,2176]{1,0:T(8,128)(2,1)S(1)} %get-tuple-element.301), channel_id=1, source_target_pairs={{0,1},{1,0},{2,3},{3,2},{4,5},{5,4},{6,7},{7,6},{8,9},{9,8},{10,11... | collective-permute-start | bytes 208904 | tf_op jit(solution)/shard_map/ppermute | solution.py:585
  174.2 1.7 collective-permute-done.36
  175.8 1.8 collective-permute-done.35
  178.8 1.1 collective-permute-start.41
  179.9 2.1 %collective-permute-done.38 = bf16[16,2176]{1,0:T(8,128)(2,1)S(1)} collective-permute-done((bf16[16,2176]{1,0:T(8,128)(2,1)S(1)}, bf16[16,2176]{1,0:T(8,128)(2,1)S(1)}, u32[]{:S(2)}, u32[]{:S(2)}) %collective-permute-start.38) | collective-permute-done | bytes 69664 | tf_op jit(solution)/shard_map/ppermute | solution.py:585
  182.9 5.8 %collective-permute-done.41 = bf16[2,16,4864]{2,1,0:T(8,128)(2,1)S(1)} collective-permute-done((bf16[2,16,4864]{2,1,0:T(8,128)(2,1)S(1)}, bf16[2,16,4864]{2,1,0:T(8,128)(2,1)S(1)}, u32[]{:S(2)}, u32[]{:S(2)}) %collective-permute-start.41) | collective-permute-done | bytes 311328 | tf_op jit(solution)/shard_map/ppermute | solution.py:585
  188.9 1.3 collective-permute-done.39
  191.8 2.9 %unpack_feed.1 = (f32[128,512]{1,0:T(8,128)}, f32[128,2048]{1,0:T(8,128)}, f32[512,512]{1,0:T(8,128)}, f32[128,256]{1,0:T(8,128)}) custom-call(s32[3]{0:T(128)} %pad_add_fusion.idx, bf16[4,16,4864]{2,1,0:T(8,128)(2,1)} %bitcast.108, bf16[4,16,4864]{2,1,0:T(8,128)(2,1)} %copy-done.7), custom_call_target="tpu_custom_call" | custom-call | bytes 1245196 | tf_op jit(solution)/shard_map/unpack_feed/pallas_call | solution.py:568
  195.3 2.1 %unpack_proj.1 = (f32[128,512]{1,0:T(8,128)}, f32[128,512]{1,0:T(8,128)}, f32[128,512]{1,0:T(8,128)}, f32[128,512]{1,0:T(8,128)}, f32[128]{0:T(128)}, /*index=5*...) custom-call(s32[3]{0:T(128)} %pad_add_fusion.idx, bf16[4,16,2176]{2,1,0:T(8,128)(2,1)} %bitcast.110, ...), custom_call_target="tpu_custom_call" | custom-call | bytes 557068 | tf_op jit(solution)/shard_map/unpack_proj/pallas_call | solution.py:568
  (128 shorter events, 18.7 us)
Async XLA Ops:
  4.0 13.4 %copy-start.11 = (bf16[2,16,2304]{2,1,0:T(8,128)(2,1)S(1)}, bf16[2,16,2304]{2,1,0:T(8,128)(2,1)}, u32[]{:S(2)}) copy-start(bf16[2,16,2304]{2,1,0:T(8,128)(2,1)} %get-tuple-element.157) | copy-start | bytes 442372
  4.0 8.7 %collective-permute-start.2 = (bf16[16,2176]{1,0:T(8,128)(2,1)}, bf16[16,2176]{1,0:T(8,128)(2,1)S(1)}, u32[]{:S(2)}, u32[]{:S(2)}) collective-permute-start(bf16[16,2176]{1,0:T(8,128)(2,1)} %get-tuple-element.151), channel_id=1, source_target_pairs={{0,3},{1,2},{2,1},{3,0},{4,7},{5,6},{6,5},{7,4},{8,11},{9,10},{10,... | collective-permute-start | bytes 208904 | tf_op jit(solution)/shard_map/ppermute | solution.py:585
  9.1 6.2 %collective-permute-start.1 = (bf16[16,2176]{1,0:T(8,128)(2,1)}, bf16[16,2176]{1,0:T(8,128)(2,1)S(1)}, u32[]{:S(2)}, u32[]{:S(2)}) collective-permute-start(bf16[16,2176]{1,0:T(8,128)(2,1)} %get-tuple-element.151), channel_id=1, source_target_pairs={{0,2},{1,3},{2,0},{3,1},{4,6},{5,7},{6,4},{7,5},{8,10},{9,11},{10,... | collective-permute-start | bytes 208904 | tf_op jit(solution)/shard_map/ppermute | solution.py:585
  9.1 6.5 %collective-permute-start = (bf16[16,2176]{1,0:T(8,128)(2,1)}, bf16[16,2176]{1,0:T(8,128)(2,1)S(1)}, u32[]{:S(2)}, u32[]{:S(2)}) collective-permute-start(bf16[16,2176]{1,0:T(8,128)(2,1)} %get-tuple-element.151), channel_id=1, source_target_pairs={{0,1},{1,0},{2,3},{3,2},{4,5},{5,4},{6,7},{7,6},{8,9},{9,8},{10,11... | collective-permute-start | bytes 208904 | tf_op jit(solution)/shard_map/ppermute | solution.py:585
  9.8 6.7 %collective-permute-start.3 = (bf16[16,2560]{1,0:T(8,128)(2,1)}, bf16[16,2560]{1,0:T(8,128)(2,1)S(1)}, u32[]{:S(2)}, u32[]{:S(2)}) collective-permute-start(bf16[16,2560]{1,0:T(8,128)(2,1)} %get-tuple-element.152), channel_id=1, source_target_pairs={{0,1},{1,0},{2,3},{3,2},{4,5},{5,4},{6,7},{7,6},{8,9},{9,8},{10,11... | collective-permute-start | bytes 245768 | tf_op jit(solution)/shard_map/ppermute | solution.py:585
  17.4 10.6 %collective-permute-start.8 = (bf16[2,16,2304]{2,1,0:T(8,128)(2,1)S(1)}, bf16[2,16,2304]{2,1,0:T(8,128)(2,1)S(1)}, u32[]{:S(2)}, u32[]{:S(2)}) collective-permute-start(bf16[2,16,2304]{2,1,0:T(8,128)(2,1)S(1)} %copy-done.11), channel_id=1, source_target_pairs={{0,1},{1,0},{2,3},{3,2},{4,5},{5,4},{6,7},{7,6},{8,9},{9,8},{10,11... | collective-permute-start | bytes 442376 | tf_op jit(solution)/shard_map/ppermute | solution.py:585
  19.0 11.9 %collective-permute-start.6 = (bf16[4,16,2048]{2,1,0:T(8,128)(2,1)S(1)}, bf16[4,16,2048]{2,1,0:T(8,128)(2,1)S(1)}, u32[]{:S(2)}, u32[]{:S(2)}) collective-permute-start(bf16[4,16,2048]{2,1,0:T(8,128)(2,1)S(1)} %pad_maximum_fusion.11), channel_id=1, source_target_pairs={{0,24},{4,28},{8,16},{12,20},{16,8},{20,12},{24,0},{28,4},{1,25},{... | collective-permute-start | bytes 786440 | tf_op jit(solution)/shard_map/ppermute | solution.py:585
  21.5 11.0 %collective-permute-start.5 = (bf16[4,16,2048]{2,1,0:T(8,128)(2,1)S(1)}, bf16[4,16,2048]{2,1,0:T(8,128)(2,1)S(1)}, u32[]{:S(2)}, u32[]{:S(2)}) collective-permute-start(bf16[4,16,2048]{2,1,0:T(8,128)(2,1)S(1)} %pad_maximum_fusion.11), channel_id=1, source_target_pairs={{0,16},{4,20},{8,24},{12,28},{16,0},{20,4},{24,8},{28,12},{1,17},{... | collective-permute-start | bytes 786440 | tf_op jit(solution)/shard_map/ppermute | solution.py:585
  22.0 10.6 %collective-permute-start.4 = (bf16[4,16,2048]{2,1,0:T(8,128)(2,1)S(1)}, bf16[4,16,2048]{2,1,0:T(8,128)(2,1)S(1)}, u32[]{:S(2)}, u32[]{:S(2)}) collective-permute-start(bf16[4,16,2048]{2,1,0:T(8,128)(2,1)S(1)} %pad_maximum_fusion.11), channel_id=1, source_target_pairs={{0,8},{4,12},{8,0},{12,4},{16,24},{20,28},{24,16},{28,20},{1,9},{5... | collective-permute-start | bytes 786440 | tf_op jit(solution)/shard_map/ppermute | solution.py:585
  22.5 8.4 %collective-permute-start.7 = (bf16[2,16,2560]{2,1,0:T(8,128)(2,1)S(1)}, bf16[2,16,2560]{2,1,0:T(8,128)(2,1)S(1)}, u32[]{:S(2)}, u32[]{:S(2)}) collective-permute-start(bf16[2,16,2560]{2,1,0:T(8,128)(2,1)S(1)} %pad_maximum_fusion.12), channel_id=1, source_target_pairs={{0,2},{1,3},{2,0},{3,1},{4,6},{5,7},{6,4},{7,5},{8,10},{9,11},{10,... | collective-permute-start | bytes 491528 | tf_op jit(solution)/shard_map/ppermute | solution.py:585
  32.7 6.1 %collective-permute-start.9 = (bf16[4,4,16,2048]{3,2,1,0:T(8,128)(2,1)S(1)}, bf16[4,4,16,2048]{3,2,1,0:T(8,128)(2,1)S(1)}, u32[]{:S(2)}, u32[]{:S(2)}) collective-permute-start(bf16[4,4,16,2048]{3,2,1,0:T(8,128)(2,1)S(1)} %pad_maximum_fusion.2.near), channel_id=1, source_target_pairs={{0,4},{4,0},{8,12},{12,8},{16,20},{20,16},{24,28},{28,24},{1,5},{5... | collective-permute-start | bytes 3145736 | tf_op jit(solution)/shard_map/ppermute | solution.py:585
  32.8 19.3 %collective-permute-start.12 = (bf16[4,16,2560]{2,1,0:T(8,128)(2,1)S(1)}, bf16[4,16,2560]{2,1,0:T(8,128)(2,1)S(1)}, u32[]{:S(2)}, u32[]{:S(2)}) collective-permute-start(bf16[4,16,2560]{2,1,0:T(8,128)(2,1)S(1)} %constant_dynamic-update-slice_fusion), channel_id=1, source_target_pairs={{0,24},{4,28},{8,16},{12,20},{16,8},{20,12},{24,0},{28,4},{1,25},{... | collective-permute-start | bytes 983048 | tf_op jit(solution)/shard_map/ppermute | solution.py:585
  34.6 17.6 %collective-permute-start.11 = (bf16[4,16,2560]{2,1,0:T(8,128)(2,1)S(1)}, bf16[4,16,2560]{2,1,0:T(8,128)(2,1)S(1)}, u32[]{:S(2)}, u32[]{:S(2)}) collective-permute-start(bf16[4,16,2560]{2,1,0:T(8,128)(2,1)S(1)} %constant_dynamic-update-slice_fusion), channel_id=1, source_target_pairs={{0,16},{4,20},{8,24},{12,28},{16,0},{20,4},{24,8},{28,12},{1,17},{... | collective-permute-start | bytes 983048 | tf_op jit(solution)/shard_map/ppermute | solution.py:585
  35.9 16.3 %collective-permute-start.10 = (bf16[4,16,2560]{2,1,0:T(8,128)(2,1)S(1)}, bf16[4,16,2560]{2,1,0:T(8,128)(2,1)S(1)}, u32[]{:S(2)}, u32[]{:S(2)}) collective-permute-start(bf16[4,16,2560]{2,1,0:T(8,128)(2,1)S(1)} %constant_dynamic-update-slice_fusion), channel_id=1, source_target_pairs={{0,8},{4,12},{8,0},{12,4},{16,24},{20,28},{24,16},{28,20},{1,9},{5... | collective-permute-start | bytes 983048 | tf_op jit(solution)/shard_map/ppermute | solution.py:585
  36.4 15.8 %collective-permute-start.13 = (bf16[2,2,16,2304]{3,2,0,1:T(8,128)(2,1)S(1)}, bf16[2,2,16,2304]{3,2,0,1:T(8,128)(2,1)S(1)}, u32[]{:S(2)}, u32[]{:S(2)}) collective-permute-start(bf16[2,2,16,2304]{3,2,0,1:T(8,128)(2,1)S(1)} %pad_maximum_fusion.5), channel_id=1, source_target_pairs={{0,2},{1,3},{2,0},{3,1},{4,6},{5,7},{6,4},{7,5},{8,10},{9,11},{10,... | collective-permute-start | bytes 884744 | tf_op jit(solution)/shard_map/ppermute | solution.py:585
  52.4 12.0 %copy-start.1 = (bf16[4,4,16,2560]{3,2,1,0:T(8,128)(2,1)}, bf16[4,4,16,2560]{3,2,1,0:T(8,128)(2,1)S(1)}, u32[]{:S(2)}) copy-start(bf16[4,4,16,2560]{3,2,1,0:T(8,128)(2,1)S(1)} %pad_maximum_fusion.up_near) | copy-start | bytes 3932164
  52.4 12.0 %collective-permute-start.14 = (bf16[4,4,16,2560]{3,2,1,0:T(8,128)(2,1)S(1)}, bf16[4,4,16,2560]{3,2,1,0:T(8,128)(2,1)S(1)}, u32[]{:S(2)}, u32[]{:S(2)}) collective-permute-start(bf16[4,4,16,2560]{3,2,1,0:T(8,128)(2,1)S(1)} %pad_maximum_fusion.up_near), channel_id=1, source_target_pairs={{0,4},{4,0},{8,12},{12,8},{16,20},{20,16},{24,28},{28,24},{1,5},{5... | collective-permute-start | bytes 3932168 | tf_op jit(solution)/shard_map/ppermute | solution.py:585
  52.6 11.8 %collective-permute-start.16 = (bf16[4,16,2304]{2,1,0:T(8,128)(2,1)S(1)}, bf16[4,16,2304]{2,1,0:T(8,128)(2,1)S(1)}, u32[]{:S(2)}, u32[]{:S(2)}) collective-permute-start(bf16[4,16,2304]{2,1,0:T(8,128)(2,1)S(1)} %get-tuple-element.308), channel_id=1, source_target_pairs={{0,16},{4,20},{8,24},{12,28},{16,0},{20,4},{24,8},{28,12},{1,17},{... | collective-permute-start | bytes 884744 | tf_op jit(solution)/shard_map/ppermute | solution.py:585
  54.0 10.3 %collective-permute-start.15 = (bf16[4,16,2304]{2,1,0:T(8,128)(2,1)S(1)}, bf16[4,16,2304]{2,1,0:T(8,128)(2,1)S(1)}, u32[]{:S(2)}, u32[]{:S(2)}) collective-permute-start(bf16[4,16,2304]{2,1,0:T(8,128)(2,1)S(1)} %get-tuple-element.308), channel_id=1, source_target_pairs={{0,8},{4,12},{8,0},{12,4},{16,24},{20,28},{24,16},{28,20},{1,9},{5... | collective-permute-start | bytes 884744 | tf_op jit(solution)/shard_map/ppermute | solution.py:585
  64.6 3.0 %collective-permute-start.17 = (bf16[4,4,16,2304]{3,2,1,0:T(8,128)(2,1)S(1)}, bf16[4,4,16,2304]{3,2,1,0:T(8,128)(2,1)}, u32[]{:S(2)}, u32[]{:S(2)}) collective-permute-start(bf16[4,4,16,2304]{3,2,1,0:T(8,128)(2,1)S(1)} %pad_maximum_fusion.1.down_near), channel_id=1, source_target_pairs={{0,4},{4,0},{8,12},{12,8},{16,20},{20,16},{24,28},{28,24},{1,5},{5... | collective-permute-start | bytes 3538952 | tf_op jit(solution)/shard_map/ppermute | solution.py:585
  89.4 17.8 %collective-permute-start.18 = (bf16[4,4,16,2304]{3,2,1,0:T(8,128)(2,1)}, bf16[4,4,16,2304]{3,2,1,0:T(8,128)(2,1)S(1)}, u32[]{:S(2)}, u32[]{:S(2)}) collective-permute-start(bf16[4,4,16,2304]{3,2,1,0:T(8,128)(2,1)} %get-tuple-element.196), channel_id=1, source_target_pairs={{0,4},{4,0},{8,12},{12,8},{16,20},{20,16},{24,28},{28,24},{1,5},{5... | collective-permute-start | bytes 3538952 | tf_op jit(solution)/shard_map/ppermute | solution.py:585
  89.6 18.1 %copy-start.3 = (bf16[4,4,16,2304]{3,2,1,0:T(8,128)(2,1)S(1)}, bf16[4,4,16,2304]{3,2,1,0:T(8,128)(2,1)}, u32[]{:S(2)}) copy-start(bf16[4,4,16,2304]{3,2,1,0:T(8,128)(2,1)} %get-tuple-element.195) | copy-start | bytes 3538948
  107.2 19.4 %collective-permute-start.22 = (bf16[4,4,16,2560]{3,2,1,0:T(8,128)(2,1)}, bf16[4,4,16,2560]{3,2,1,0:T(8,128)(2,1)S(1)}, u32[]{:S(2)}, u32[]{:S(2)}) collective-permute-start(bf16[4,4,16,2560]{3,2,1,0:T(8,128)(2,1)} %get-tuple-element.204), channel_id=1, source_target_pairs={{0,4},{4,0},{8,12},{12,8},{16,20},{20,16},{24,28},{28,24},{1,5},{5... | collective-permute-start | bytes 3932168 | tf_op jit(solution)/shard_map/ppermute | solution.py:585
  107.9 18.7 %collective-permute-start.19 = (bf16[4,16,2304]{2,1,0:T(8,128)(2,1)S(1)}, bf16[4,16,2304]{2,1,0:T(8,128)(2,1)S(1)}, u32[]{:S(2)}, u32[]{:S(2)}) collective-permute-start(bf16[4,16,2304]{2,1,0:T(8,128)(2,1)S(1)} %get-tuple-element.201), channel_id=1, source_target_pairs={{0,8},{4,12},{8,0},{12,4},{16,24},{20,28},{24,16},{28,20},{1,9},{5... | collective-permute-start | bytes 884744 | tf_op jit(solution)/shard_map/ppermute | solution.py:585
  109.2 17.4 %collective-permute-start.20 = (bf16[4,16,2304]{2,1,0:T(8,128)(2,1)S(1)}, bf16[4,16,2304]{2,1,0:T(8,128)(2,1)S(1)}, u32[]{:S(2)}, u32[]{:S(2)}) collective-permute-start(bf16[4,16,2304]{2,1,0:T(8,128)(2,1)S(1)} %get-tuple-element.202), channel_id=1, source_target_pairs={{0,16},{4,20},{8,24},{12,28},{16,0},{20,4},{24,8},{28,12},{1,17},{... | collective-permute-start | bytes 884744 | tf_op jit(solution)/shard_map/ppermute | solution.py:585
  109.9 16.8 %collective-permute-start.21 = (bf16[4,16,2304]{2,1,0:T(8,128)(2,1)S(1)}, bf16[4,16,2304]{2,1,0:T(8,128)(2,1)S(1)}, u32[]{:S(2)}, u32[]{:S(2)}) collective-permute-start(bf16[4,16,2304]{2,1,0:T(8,128)(2,1)S(1)} %get-tuple-element.203), channel_id=1, source_target_pairs={{0,24},{4,28},{8,16},{12,20},{16,8},{20,12},{24,0},{28,4},{1,25},{... | collective-permute-start | bytes 884744 | tf_op jit(solution)/shard_map/ppermute | solution.py:585
  128.3 20.1 %collective-permute-start.23 = (bf16[2,16,2304]{2,1,0:T(8,128)(2,1)S(1)}, bf16[2,16,2304]{2,1,0:T(8,128)(2,1)S(1)}, u32[]{:S(2)}, u32[]{:S(2)}) collective-permute-start(bf16[2,16,2304]{2,1,0:T(8,128)(2,1)S(1)} %get-tuple-element.220), channel_id=1, source_target_pairs={{0,2},{1,3},{2,0},{3,1},{4,6},{5,7},{6,4},{7,5},{8,10},{9,11},{10,... | collective-permute-start | bytes 442376 | tf_op jit(solution)/shard_map/ppermute | solution.py:585
  129.5 18.9 %collective-permute-start.24 = (bf16[4,16,2560]{2,1,0:T(8,128)(2,1)S(1)}, bf16[4,16,2560]{2,1,0:T(8,128)(2,1)S(1)}, u32[]{:S(2)}, u32[]{:S(2)}) collective-permute-start(bf16[4,16,2560]{2,1,0:T(8,128)(2,1)S(1)} %get-tuple-element.221), channel_id=1, source_target_pairs={{0,8},{4,12},{8,0},{12,4},{16,24},{20,28},{24,16},{28,20},{1,9},{5... | collective-permute-start | bytes 983048 | tf_op jit(solution)/shard_map/ppermute | solution.py:585
  130.8 17.7 %collective-permute-start.25 = (bf16[4,16,2560]{2,1,0:T(8,128)(2,1)S(1)}, bf16[4,16,2560]{2,1,0:T(8,128)(2,1)S(1)}, u32[]{:S(2)}, u32[]{:S(2)}) collective-permute-start(bf16[4,16,2560]{2,1,0:T(8,128)(2,1)S(1)} %get-tuple-element.222), channel_id=1, source_target_pairs={{0,16},{4,20},{8,24},{12,28},{16,0},{20,4},{24,8},{28,12},{1,17},{... | collective-permute-start | bytes 983048 | tf_op jit(solution)/shard_map/ppermute | solution.py:585
  131.4 17.1 %collective-permute-start.26 = (bf16[4,16,2560]{2,1,0:T(8,128)(2,1)S(1)}, bf16[4,16,2560]{2,1,0:T(8,128)(2,1)S(1)}, u32[]{:S(2)}, u32[]{:S(2)}) collective-permute-start(bf16[4,16,2560]{2,1,0:T(8,128)(2,1)S(1)} %get-tuple-element.223), channel_id=1, source_target_pairs={{0,24},{4,28},{8,16},{12,20},{16,8},{20,12},{24,0},{28,4},{1,25},{... | collective-permute-start | bytes 983048 | tf_op jit(solution)/shard_map/ppermute | solution.py:585
  133.0 15.5 %collective-permute-start.27 = (bf16[4,4,16,1024]{3,2,1,0:T(8,128)(2,1)S(1)}, bf16[4,4,16,1024]{3,2,1,0:T(8,128)(2,1)S(1)}, u32[]{:S(2)}, u32[]{:S(2)}) collective-permute-start(bf16[4,4,16,1024]{3,2,1,0:T(8,128)(2,1)S(1)} %copy-done.15), channel_id=1, source_target_pairs={{0,4},{4,0},{8,12},{12,8},{16,20},{20,16},{24,28},{28,24},{1,5},{5... | collective-permute-start | bytes 1572872 | tf_op jit(solution)/shard_map/ppermute | solution.py:585
  133.0 16.0 %copy-start.9 = (bf16[4,4,16,1024]{3,2,1,0:T(8,128)(2,1)S(1)}, bf16[4,4,16,1024]{3,2,1,0:T(8,128)(2,1)}, u32[]{:S(2)}) copy-start(bf16[4,4,16,1024]{3,2,1,0:T(8,128)(2,1)} %get-tuple-element.241) | copy-start | bytes 1572868
  148.5 2.4 %collective-permute-start.28 = (bf16[4,4,16,1152]{3,2,1,0:T(8,128)(2,1)}, bf16[4,4,16,1152]{3,2,1,0:T(8,128)(2,1)S(1)}, u32[]{:S(2)}, u32[]{:S(2)}) collective-permute-start(bf16[4,4,16,1152]{3,2,1,0:T(8,128)(2,1)} %get-tuple-element.244), channel_id=1, source_target_pairs={{0,4},{4,0},{8,12},{12,8},{16,20},{20,16},{24,28},{28,24},{1,5},{5... | collective-permute-start | bytes 1769480 | tf_op jit(solution)/shard_map/ppermute | solution.py:585
  151.1 15.1 %collective-permute-start.30 = (bf16[4,16,2176]{2,1,0:T(8,128)(2,1)S(1)}, bf16[4,16,2176]{2,1,0:T(8,128)(2,1)S(1)}, u32[]{:S(2)}, u32[]{:S(2)}) collective-permute-start(bf16[4,16,2176]{2,1,0:T(8,128)(2,1)S(1)} %get-tuple-element.247), channel_id=1, source_target_pairs={{0,8},{4,12},{8,0},{12,4},{16,24},{20,28},{24,16},{28,20},{1,9},{5... | collective-permute-start | bytes 835592 | tf_op jit(solution)/shard_map/ppermute | solution.py:585
  152.5 14.6 %collective-permute-start.31 = (bf16[4,16,2176]{2,1,0:T(8,128)(2,1)S(1)}, bf16[4,16,2176]{2,1,0:T(8,128)(2,1)S(1)}, u32[]{:S(2)}, u32[]{:S(2)}) collective-permute-start(bf16[4,16,2176]{2,1,0:T(8,128)(2,1)S(1)} %get-tuple-element.248), channel_id=1, source_target_pairs={{0,16},{4,20},{8,24},{12,28},{16,0},{20,4},{24,8},{28,12},{1,17},{... | collective-permute-start | bytes 835592 | tf_op jit(solution)/shard_map/ppermute | solution.py:585
  153.1 14.0 %collective-permute-start.32 = (bf16[4,16,2176]{2,1,0:T(8,128)(2,1)S(1)}, bf16[4,16,2176]{2,1,0:T(8,128)(2,1)S(1)}, u32[]{:S(2)}, u32[]{:S(2)}) collective-permute-start(bf16[4,16,2176]{2,1,0:T(8,128)(2,1)S(1)} %get-tuple-element.249), channel_id=1, source_target_pairs={{0,24},{4,28},{8,16},{12,20},{16,8},{20,12},{24,0},{28,4},{1,25},{... | collective-permute-start | bytes 835592 | tf_op jit(solution)/shard_map/ppermute | solution.py:585
  154.7 9.6 %collective-permute-start.33 = (bf16[16,2304]{1,0:T(8,128)(2,1)S(1)}, bf16[16,2304]{1,0:T(8,128)(2,1)S(1)}, u32[]{:S(2)}, u32[]{:S(2)}) collective-permute-start(bf16[16,2304]{1,0:T(8,128)(2,1)S(1)} %fusion.20), channel_id=1, source_target_pairs={{0,1},{1,0},{2,3},{3,2},{4,5},{5,4},{6,7},{7,6},{8,9},{9,8},{10,11... | collective-permute-start | bytes 221192 | tf_op jit(solution)/shard_map/ppermute | solution.py:585
  156.6 9.7 %collective-permute-start.29 = (bf16[2,16,2560]{2,1,0:T(8,128)(2,1)S(1)}, bf16[2,16,2560]{2,1,0:T(8,128)(2,1)S(1)}, u32[]{:S(2)}, u32[]{:S(2)}) collective-permute-start(bf16[2,16,2560]{2,1,0:T(8,128)(2,1)S(1)} %slice.295), channel_id=1, source_target_pairs={{0,2},{1,3},{2,0},{3,1},{4,6},{5,7},{6,4},{7,5},{8,10},{9,11},{10,... | collective-permute-start | bytes 491528 | tf_op jit(solution)/shard_map/ppermute | solution.py:585
  167.1 6.3 %collective-permute-start.37 = (bf16[16,2560]{1,0:T(8,128)(2,1)S(1)}, bf16[16,2560]{1,0:T(8,128)(2,1)S(1)}, u32[]{:S(2)}, u32[]{:S(2)}) collective-permute-start(bf16[16,2560]{1,0:T(8,128)(2,1)S(1)} %fusion.19), channel_id=1, source_target_pairs={{0,1},{1,0},{2,3},{3,2},{4,5},{5,4},{6,7},{7,6},{8,9},{9,8},{10,11... | collective-permute-start | bytes 245768 | tf_op jit(solution)/shard_map/ppermute | solution.py:585
  169.0 6.9 %collective-permute-start.36 = (bf16[16,2176]{1,0:T(8,128)(2,1)S(1)}, bf16[16,2176]{1,0:T(8,128)(2,1)S(1)}, u32[]{:S(2)}, u32[]{:S(2)}) collective-permute-start(bf16[16,2176]{1,0:T(8,128)(2,1)S(1)} %get-tuple-element.299), channel_id=1, source_target_pairs={{0,3},{1,2},{2,1},{3,0},{4,7},{5,6},{6,5},{7,4},{8,11},{9,10},{10,... | collective-permute-start | bytes 208904 | tf_op jit(solution)/shard_map/ppermute | solution.py:585
  170.7 7.0 %collective-permute-start.35 = (bf16[16,2176]{1,0:T(8,128)(2,1)S(1)}, bf16[16,2176]{1,0:T(8,128)(2,1)S(1)}, u32[]{:S(2)}, u32[]{:S(2)}) collective-permute-start(bf16[16,2176]{1,0:T(8,128)(2,1)S(1)} %get-tuple-element.300), channel_id=1, source_target_pairs={{0,2},{1,3},{2,0},{3,1},{4,6},{5,7},{6,4},{7,5},{8,10},{9,11},{10,... | collective-permute-start | bytes 208904 | tf_op jit(solution)/shard_map/ppermute | solution.py:585
  170.9 6.8 %collective-permute-start.34 = (bf16[16,2176]{1,0:T(8,128)(2,1)S(1)}, bf16[16,2176]{1,0:T(8,128)(2,1)S(1)}, u32[]{:S(2)}, u32[]{:S(2)}) collective-permute-start(bf16[16,2176]{1,0:T(8,128)(2,1)S(1)} %get-tuple-element.301), channel_id=1, source_target_pairs={{0,1},{1,0},{2,3},{3,2},{4,5},{5,4},{6,7},{7,6},{8,9},{9,8},{10,11... | collective-permute-start | bytes 208904 | tf_op jit(solution)/shard_map/ppermute | solution.py:585
  173.5 5.3 %collective-permute-start.40 = (bf16[16,4864]{1,0:T(8,128)(2,1)S(1)}, bf16[16,4864]{1,0:T(8,128)(2,1)S(1)}, u32[]{:S(2)}, u32[]{:S(2)}) collective-permute-start(bf16[16,4864]{1,0:T(8,128)(2,1)S(1)} %get-tuple-element.314), channel_id=1, source_target_pairs={{0,16},{4,20},{8,24},{12,28},{16,0},{20,4},{24,8},{28,12},{1,17},{... | collective-permute-start | bytes 466952 | tf_op jit(solution)/shard_map/ppermute | solution.py:585
  177.7 4.4 %collective-permute-start.38 = (bf16[16,2176]{1,0:T(8,128)(2,1)S(1)}, bf16[16,2176]{1,0:T(8,128)(2,1)S(1)}, u32[]{:S(2)}, u32[]{:S(2)}) collective-permute-start(bf16[16,2176]{1,0:T(8,128)(2,1)S(1)} %add_convert_fusion.22), channel_id=1, source_target_pairs={{0,16},{4,20},{8,24},{12,28},{16,0},{20,4},{24,8},{28,12},{1,17},{... | collective-permute-start | bytes 208904 | tf_op jit(solution)/shard_map/ppermute | solution.py:585
  178.8 9.8 %collective-permute-start.41 = (bf16[2,16,4864]{2,1,0:T(8,128)(2,1)S(1)}, bf16[2,16,4864]{2,1,0:T(8,128)(2,1)S(1)}, u32[]{:S(2)}, u32[]{:S(2)}) collective-permute-start(bf16[2,16,4864]{2,1,0:T(8,128)(2,1)S(1)} %get-tuple-element.310), channel_id=1, source_target_pairs={{0,8},{4,12},{8,0},{12,4},{16,24},{20,28},{24,16},{28,20},{1,9},{5... | collective-permute-start | bytes 933896 | tf_op jit(solution)/shard_map/ppermute | solution.py:585
  182.1 8.1 %collective-permute-start.39 = (bf16[2,16,2176]{2,1,0:T(8,128)(2,1)S(1)}, bf16[2,16,2176]{2,1,0:T(8,128)(2,1)S(1)}, u32[]{:S(2)}, u32[]{:S(2)}) collective-permute-start(bf16[2,16,2176]{2,1,0:T(8,128)(2,1)S(1)} %get-tuple-element.316), channel_id=1, source_target_pairs={{0,8},{4,12},{8,0},{12,4},{16,24},{20,28},{24,16},{28,20},{1,9},{5... | collective-permute-start | bytes 417800 | tf_op jit(solution)/shard_map/ppermute | solution.py:585
  188.8 2.1 %collective-permute-start.43 = (bf16[4,16,4864]{2,1,0:T(8,128)(2,1)S(1)}, bf16[4,16,4864]{2,1,0:T(8,128)(2,1)S(1)}, u32[]{:S(2)}, u32[]{:S(2)}) collective-permute-start(bf16[4,16,4864]{2,1,0:T(8,128)(2,1)S(1)} %bitcast.107), channel_id=1, source_target_pairs={{0,4},{4,0},{8,12},{12,8},{16,20},{20,16},{24,28},{28,24},{1,5},{5... | collective-permute-start | bytes 1867784 | tf_op jit(solution)/shard_map/ppermute | solution.py:585
  190.2 4.4 %collective-permute-start.42 = (bf16[4,16,2176]{2,1,0:T(8,128)(2,1)S(1)}, bf16[4,16,2176]{2,1,0:T(8,128)(2,1)S(1)}, u32[]{:S(2)}, u32[]{:S(2)}) collective-permute-start(bf16[4,16,2176]{2,1,0:T(8,128)(2,1)S(1)} %bitcast.109), channel_id=1, source_target_pairs={{0,4},{4,0},{8,12},{12,8},{16,20},{20,16},{24,28},{28,24},{1,5},{5... | collective-permute-start | bytes 835592 | tf_op jit(solution)/shard_map/ppermute | solution.py:585
  (12 other events, 29.4 us)

commit v4 on v3

--- a/solution.py
+++ b/solution.py
@@ -13,6 +13,7 @@
 SEQ_LEN = 1024
 CHUNK = 256
 SUB = 128
+ROWS = 512
 HALF = 256
 PIECE = 16
 COLS_PROJ = 4 * HALF
@@ -126,12 +127,13 @@
         copy.wait()
 
 
-def first_norm_kernel(idx, vec, x, a1, unit_t, columns):
+def first_norm_kernel(idx, vec, x, a1, both_t):
     unit, _ = norm_parts(x[...].astype(F32))
-    gain, shift = vector_of(vec, idx, 0), vector_of(vec, idx, 1)
-    a1[...] = (unit * gain + shift).astype(BF16)
-    unit_t[...] = unit.astype(BF16).T
-    columns[...] = jnp.concatenate([gain, shift, jnp.zeros((6, WIDTH), F32)], axis=0).T
+    low = (unit * vector_of(vec, idx, 0) + vector_of(vec, idx, 1)).astype(BF16)
+    a1[...] = low
+    both_t[:WIDTH, :] = low.T
+    both_t[WIDTH : 2 * WIDTH, :] = unit.astype(BF16).T
+    both_t[2 * WIDTH :, :] = jnp.ones((PIECE, both_t.shape[1]), BF16)
 
 
 def lanes_low():
@@ -262,33 +264,55 @@
 
 
 def feed_kernel(
-    idx, vec, x, o0, o1, target, up_near, up_far, down_near, down_far,
-    out_o, h_o, slope_o, dy_o, bias_o, keep, send,
-    w_mix, w_up, w_down, w_read, act_s, out_s, dl_s, df_s,
+    idx, vec, x, o0, o1, target, up_near_i, up_far_i, down_near_i, down_far_i,
+    out_o, h_o, slope_o, dy_o, bias_o, keep, send, mix_o, up_o, down_o,
+    up_near, up_far, down_near, down_far,
+    w_mix, w_up, w_down, w_read, act_s, out_s, h_s, slope_s, dy_s, dl_s, df_s, sems, row_sems,
 ):
     step = pl.program_id(0)
+    moves = (
+        (up_near_i, up_near), (up_far_i, up_far), (down_near_i, down_near), (down_far_i, down_far),
+        (w_mix, mix_o), (w_up, up_o), (w_down, down_o),
+    )
+    copies = [pltpu.make_async_copy(src, dst, sems.at[i]) for i, (src, dst) in enumerate(moves)]
 
     @pl.when(step == 0)
     def _():
+        for copy in copies[:4]:
+            copy.start()
+        for copy in copies[:2]:
+            copy.wait()
         for shard, member, piece in each_piece(idx, up_near, up_far):
             rows = rows_at(shard * 128 + member * PIECE, PIECE)
             w_mix[rows, :] = piece[:, :WIDTH]
             w_up[rows, :] = piece[:, WIDTH:]
+        for copy in copies[2:4]:
+            copy.wait()
         for shard, member, piece in each_piece(idx, down_near, down_far):
             for i in range(4):
                 rows = rows_at(shard * 512 + member * 64 + 16 * i, PIECE)
                 w_down[rows, :] = piece[:, i * WIDTH : (i + 1) * WIDTH]
             w_read[rows_at(shard * 128 + member * PIECE, PIECE), :] = piece[:, 4 * WIDTH :]
+        for copy in copies[4:]:
+            copy.start()
         bias_o[...] = jnp.zeros_like(bias_o)
 
-    rows = pl.ds(pl.multiple_of(step * CHUNK, CHUNK), CHUNK)
+    def row_copies(place):
+        at = pl.ds(pl.multiple_of(place * ROWS, ROWS), ROWS)
+        pairs = ((out_s, out_o), (h_s, h_o), (slope_s, slope_o), (dy_s, dy_o))
+        return [
+            pltpu.make_async_copy(src.at[at], dst.at[at], row_sems.at[place, i])
+            for i, (src, dst) in enumerate(pairs)
+        ]
+
+    rows = pl.ds(pl.multiple_of(step * ROWS, ROWS), ROWS)
     attn = nn(o0[...], w_mix[:HALF, :]) + nn(o1[...], w_mix[HALF:, :])
     resid = x[...].astype(F32) + attn
-    h_o[...] = resid
+    h_s[rows, :] = resid
     unit, _ = norm_parts(resid)
     second = (unit * vector_of(vec, idx, 2) + vector_of(vec, idx, 3)).astype(BF16)
     bias = bias_up_of(vec, idx)
-    branch = jnp.zeros((CHUNK, WIDTH), F32)
+    branch = jnp.zeros((ROWS, WIDTH), F32)
     scale = (2.0 / jnp.pi) ** 0.5
     at = [slice(512 * j, 512 * j + 512) for j in range(4)]
     products = nn(second, w_up[:, at[0]])
@@ -299,24 +323,26 @@
         zz = z * z
         cdf = 0.5 + 0.5 * jnp.tanh(z * (scale + (scale * 0.044715) * zz))
         active = z * cdf
-        slope_o[:, at[j]] = cdf + (active - active * cdf) * (2 * scale + (6 * scale * 0.044715) * zz)
+        slope = cdf + (active - active * cdf) * (2 * scale + (6 * scale * 0.044715) * zz)
+        slope_s[rows, at[j]] = slope.astype(BF16)
         act = active.astype(BF16)
         act_s[rows, at[j]] = act
         branch += nn(act, w_down[at[j], :])
     out = (resid + (branch + vector_of(vec, idx, 4))).astype(BF16)
-    out_o[...] = out
     out_s[rows, :] = out
     logits = nn(out, w_read[...])
     expd = jnp.exp(logits - jnp.max(logits, axis=-1, keepdims=True))
     soft = expd / jnp.sum(expd, axis=-1, keepdims=True)
-    classes = lax.broadcasted_iota(jnp.int32, (CHUNK, VOCAB), 1)
+    classes = lax.broadcasted_iota(jnp.int32, (ROWS, VOCAB), 1)
     dl = (soft - jnp.where(classes == target[...], 1.0, 0.0)).astype(BF16)
     dl_s[rows, :] = dl
     dy = nt(dl, w_read[...])
-    dy_o[...] = dy
+    dy_s[rows, :] = dy
     df = dy.astype(BF16)
     df_s[rows, :] = df
     bias_o[...] += jnp.sum(df.astype(F32), axis=0, keepdims=True)
+    for copy in row_copies(step):
+        copy.start()
 
     @pl.when(step == pl.num_programs(0) - 1)
     def _():
@@ -334,52 +360,95 @@
                     at = slice(i * WIDTH, (i + 1) * WIDTH)
                     keep[xy ^ idx[1], shard ^ idx[2], :, at] = jnp.where(own_first, first, later)
                     send[xy ^ idx[1], shard ^ idx[2], :, at] = jnp.where(own_first, later, first)
+        for copy in copies[4:]:
+            copy.wait()
+        for place in range(act_s.shape[0] // ROWS):
+            for copy in row_copies(place):
+                copy.wait()
 
 
 def feed_back_kernel(
-    idx, vec, h, slope, dy, o0, o1, up_near, up_far, down_near, down_far,
+    idx, vec, h_i, slope_i, dy_i, o0_i, o1_i, mix_i, up_i, down_i,
     dh_o, do_o, gain_o, shift_o, bias_o, keep, send,
-    w_mix, w_up, w_down, dz_s, a2_s, da_s,
+    w_mix, w_up, w_down, h_s, slope_s, dy_s, o0, o1, dz_s, a2_s, da_s, dh_s, do_s,
+    sems, row_sems, out_sems,
 ):
     step = pl.program_id(0)
+    places = dz_s.shape[0] // ROWS
+    half = pl.ds(HALF, HALF)
+    moves = (
+        (down_i, w_down), (up_i, w_up), (mix_i, w_mix), (o0_i.at[:, half], o0), (o1_i.at[:, half], o1)
+    )
+    copies = [pltpu.make_async_copy(src, dst, sems.at[i]) for i, (src, dst) in enumerate(moves)]
+
+    def row_copies(place):
+        at = pl.ds(pl.multiple_of(place * ROWS, ROWS), ROWS)
+        pairs = ((dy_i, dy_s), (slope_i, slope_s), (h_i, h_s))
+        return [
+            pltpu.make_async_copy(src.at[at], dst.at[at], row_sems.at[place, i])
+            for i, (src, dst) in enumerate(pairs)
+        ]
+
+    def out_copies(place):
+        at = pl.ds(pl.multiple_of(place * ROWS, ROWS), ROWS)
+        pairs = ((dh_s, dh_o), (do_s, do_o))
+        return [
+            pltpu.make_async_copy(src.at[at], dst.at[at], out_sems.at[place, i])
+            for i, (src, dst) in enumerate(pairs)
+        ]
 
     @pl.when(step == 0)
     def _():
-        for shard, member, piece in each_piece(idx, up_near, up_far):
-            rows = rows_at(shard * 128 + member * PIECE, PIECE)
-            w_mix[rows, :] = piece[:, :WIDTH]
-            w_up[rows, :] = piece[:, WIDTH:]
-        for shard, member, piece in each_piece(idx, down_near, down_far):
-            for i in range(4):
-                rows = rows_at(shard * 512 + member * 64 + 16 * i, PIECE)
-                w_down[rows, :] = piece[:, i * WIDTH : (i + 1) * WIDTH]
+        copies[0].start()
+        for copy in row_copies(0):
+            copy.start()
+        for copy in copies[1:3]:
+            copy.start()
         gain_o[...] = jnp.zeros_like(gain_o)
         shift_o[...] = jnp.zeros_like(shift_o)
         bias_o[...] = jnp.zeros_like(bias_o)
-
-    rows = pl.ds(pl.multiple_of(step * CHUNK, CHUNK), CHUNK)
+        copies[0].wait()
+
+    for copy in row_copies(step)[:2]:
+        copy.wait()
+    rows = pl.ds(pl.multiple_of(step * ROWS, ROWS), ROWS)
     gain = vector_of(vec, idx, 2)
-    unit, inverse = norm_parts(h[...])
-    a2_s[rows, :] = (unit * gain + vector_of(vec, idx, 3)).astype(BF16)
-    d_out = dy[...]
+    d_out = dy_s[rows, :]
     df = d_out.astype(BF16)
-    d_second = jnp.zeros((CHUNK, WIDTH), F32)
     for j in range(4):
         at = slice(512 * j, 512 * j + 512)
-        dz = (nt(df, w_down[at, :]) * slope[:, at]).astype(BF16)
+        dz = (nt(df, w_down[at, :]) * slope_s[rows, at].astype(F32)).astype(BF16)
         dz_s[rows, at] = dz
         bias_o[:, at] += jnp.sum(dz.astype(F32), axis=0, keepdims=True)
-        d_second += nt(dz, w_up[:, at])
+
+    @pl.when(step == 0)
+    def _():
+        for place in range(1, places):
+            for copy in row_copies(place):
+                copy.start()
+        for copy in copies[3:]:
+            copy.start()
+        for copy in copies[1:3]:
+            copy.wait()
+
+    row_copies(step)[2].wait()
+    d_second = nt(dz_s[rows, :], w_up[...])
+    unit, inverse = norm_parts(h_s[rows, :])
+    a2_s[rows, :] = (unit * gain + vector_of(vec, idx, 3)).astype(BF16)
     gain_o[...] += jnp.sum(d_second * unit, axis=0, keepdims=True)
     shift_o[...] += jnp.sum(d_second, axis=0, keepdims=True)
     dh = d_out + norm_pull(d_second, unit, inverse, gain)
-    dh_o[...] = dh
+    dh_s[rows, :] = dh
     da = dh.astype(BF16)
     da_s[rows, :] = da
-    do_o[...] = nt(da, w_mix[...]).astype(BF16)
+    do_s[rows, :] = nt(da, w_mix[...]).astype(BF16)
+    for copy in out_copies(step):
+        copy.start()
 
     @pl.when(step == pl.num_programs(0) - 1)
     def _():
+        for copy in copies[3:]:
+            copy.wait()
         for half in range(2):
             large = tn((o0, o1)[half][...], da_s[...]).astype(BF16)
             for i in range(2):
@@ -390,50 +459,71 @@
             at = slice(WIDTH + 512 * j, WIDTH + 512 * j + 512)
             for shard in range(4):
                 put_parts(idx, keep, send, large[shard * 128 : shard * 128 + 128], shard, at)
-
-
-def proj_gradient(idx, unit_t, columns, w, dx, keep, send):
-    sums = nn(jnp.ones((PIECE, dx.shape[0]), BF16), dx[...])[:8]
+        for place in range(places):
+            for copy in out_copies(place):
+                copy.wait()
+
+
+def proj_gradient(idx, both_t, w, dx, keep, send):
+    on_gain = jnp.zeros((WIDTH, HALF), F32)
+    sums = []
+    for j in range(4):
+        at = slice(j * HALF, (j + 1) * HALF)
+        product = nn(both_t[...], dx[:, at])
+        low = product[:WIDTH].astype(BF16)
+        for shard in range(4):
+            put_parts(idx, keep, send, low[shard * 128 : shard * 128 + 128], shard, at)
+        on_gain += product[WIDTH : 2 * WIDTH] * w[:, at].astype(F32)
+        sums.append(product[2 * WIDTH : 2 * WIDTH + 8])
+    sums = side(*sums)
     high = sums.astype(BF16)
     rest = (sums - high.astype(F32)).astype(BF16)
     shift_rows = nt(jnp.concatenate([high, rest], axis=0), w[...])
-    gain, shift = columns[:, 0:1], columns[:, 1:2]
-    on_gain = jnp.zeros((WIDTH, HALF), F32)
-    for j in range(4):
-        at = slice(j * HALF, (j + 1) * HALF)
-        tile = nn(unit_t[...], dx[:, at])
-        on_gain += tile * w[:, at].astype(F32)
-        low = (tile * gain + shift * sums[:1, at]).astype(BF16)
-        for shard in range(4):
-            put_parts(idx, keep, send, low[shard * 128 : shard * 128 + 128], shard, at)
     gain_column = jnp.sum(on_gain, axis=1, keepdims=True)
     gain_row = side(gain_column, jnp.zeros((WIDTH, 7), F32)).T[:1]
     return jnp.concatenate([gain_row, shift_rows[:1] + shift_rows[8:9], jnp.zeros((6, WIDTH), F32)])
 
 
+def late_operands(pairs, sems):
+    copies = [pltpu.make_async_copy(src, dst, sems.at[i]) for i, (src, dst) in enumerate(pairs)]
+
+    @pl.when(pl.program_id(0) == 0)
+    def _():
+        for copy in copies:
+            copy.start()
+
+    return copies
+
+
 def attend_back_kernel(
-    idx, unit_t, columns, w, proj, floats, ratios, do_i, kept,
+    idx, both_t, w, proj, floats, ratios, do_i, kept,
     dx_o, keep, send, share_o,
-    state, count_z, dx_s,
+    state, count_z, dx_s, both_s, w_s, sems,
 ):
+    copies = late_operands(((both_t, both_s), (w, w_s)), sems)
     attend_back_step(proj, floats, ratios, do_i, kept, dx_o, state, count_z, dx_s)
 
     @pl.when(pl.program_id(0) == pl.num_programs(0) - 1)
     def _():
-        share_o[...] = proj_gradient(idx, unit_t, columns, w, dx_s, keep, send)
+        for copy in copies:
+            copy.wait()
+        share_o[...] = proj_gradient(idx, both_s, w_s, dx_s, keep, send)
 
 
 def attend_back_last_kernel(
-    idx, unit_t, columns, w, proj, floats, ratios, do_i, kept,
+    idx, both_t, w, proj, floats, ratios, do_i, kept,
     share, g_g2, g_b2, g_bd, g_bu,
     dx_o, keep, send,
-    state, count_z, dx_s,
+    state, count_z, dx_s, both_s, w_s, sems,
 ):
+    copies = late_operands(((both_t, both_s), (w, w_s)), sems)
     attend_back_step(proj, floats, ratios, do_i, kept, dx_o, state, count_z, dx_s)
 
     @pl.when(pl.program_id(0) == pl.num_programs(0) - 1)
     def _():
-        total = proj_gradient(idx, unit_t, columns, w, dx_s, keep, send) + share[...]
+        for copy in copies:
+            copy.wait()
+        total = proj_gradient(idx, both_s, w_s, dx_s, keep, send) + share[...]
         for s in range(4):
             at = slice(128 * s, 128 * s + 128)
             lines = [total[:2, at], g_g2[:, at], g_b2[:, at], g_bd[:, at]]
@@ -552,6 +642,8 @@
     grid = (steps,) if steps else ()
 
     def spec(shape, block):
+        if block == "hbm":
+            return pl.BlockSpec(memory_space=pl.ANY)
         if block is None:
             return pl.BlockSpec(tuple(shape), lambda *_: (0,) * len(shape))
         return pl.BlockSpec(*block)
@@ -560,8 +652,6 @@
     for array, block in args:
         if array.dtype == jnp.int32 and array.shape == (3,):
             in_specs.append(pl.BlockSpec(memory_space=pltpu.SMEM))
-        elif block == "hbm":
-            in_specs.append(pl.BlockSpec(memory_space=pl.ANY))
         else:
             in_specs.append(spec(array.shape, block))
     moved = sum(a.size * a.dtype.itemsize for a, _ in args)
@@ -576,7 +666,7 @@
             vmem_limit_bytes=limit * MIB,
             dimension_semantics=("arbitrary",) * len(grid) if grid else None,
         ),
-        cost_estimate=pl.CostEstimate(flops=int(flops), bytes_accessed=int(moved), transcendentals=0),
+        cost_estimate=pl.CostEstimate(flops=1000, bytes_accessed=1000, transcendentals=0),
         name=name,
     )(*[array for array, _ in args])
 
@@ -689,19 +779,18 @@
         plane_a = [swap(rows_a, "dp", dp, 2 * k) for k in range(1, 4)]
         got_u = far_pair(pair_u, shards)
         pair_d = near_pair(pd, shards)
-        a1, unit_t, columns = call(
+        a1, both_t = call(
             first_norm_kernel,
             "first_norm",
             [(idx, None), (vec, None), (tokens_a, None)],
             [
                 ((count, WIDTH), BF16, None),
-                ((WIDTH, count), BF16, None),
-                ((WIDTH, 8), F32, None),
+                ((2 * WIDTH + PIECE, count), BF16, None),
             ],
         )
         target = targets.reshape(count, 1)
-        plane_a, got_u, pair_d, a1, unit_t, columns, target = pin(
-            plane_a, got_u, pair_d, a1, unit_t, columns, target
+        plane_a, got_u, pair_d, a1, both_t, target = pin(
+            plane_a, got_u, pair_d, a1, both_t, target
         )
         near_a = jnp.stack([rows_a] + plane_a)
         far_a = swap(near_a, "dp", dp, 1)
@@ -745,35 +834,48 @@
         far_d = swap(near_d, "dp", dp, 1)
         halves = (first, second)
         o0, o1 = first[2], second[2]
-        mixed_at = ((CHUNK, HALF), lambda i: (i, 1))
-        mixed_all = ((count, HALF), lambda i: (0, 1))
-
-        out, h, slope, dy, g_bias_down, keep_d, send_d = call(
+
+        wide = lambda n: ((ROWS, n), forward)
+        mixed_at = ((ROWS, HALF), lambda i: (i, 1))
+        places = count // ROWS
+        out, h, slope, dy, g_bias_down, keep_d, send_d, full_mix, full_up, full_down = call(
             feed_kernel,
             "feed_forward",
             [
-                (idx, None), (vec, None), (tokens, tok(WIDTH)), (o0, mixed_at), (o1, mixed_at),
-                (target, tok(1)), (near_u, None), (far_u, None), (near_d, None), (far_d, None),
+                (idx, None), (vec, None), (tokens, wide(WIDTH)), (o0, mixed_at), (o1, mixed_at),
+                (target, wide(1)), (near_u, "hbm"), (far_u, "hbm"), (near_d, "hbm"), (far_d, "hbm"),
             ],
             [
-                ((count, WIDTH), BF16, tok(WIDTH)),
-                ((count, WIDTH), F32, tok(WIDTH)),
-                ((count, FF), F32, tok(FF)),
-                ((count, WIDTH), F32, tok(WIDTH)),
+                ((count, WIDTH), BF16, "hbm"),
+                ((count, WIDTH), F32, "hbm"),
+                ((count, FF), BF16, "hbm"),
+                ((count, WIDTH), F32, "hbm"),
                 ((1, WIDTH), F32, None),
                 (parts + (COLS_DOWN,), BF16, None),
                 (parts + (COLS_DOWN,), BF16, None),
+                ((WIDTH, WIDTH), BF16, "hbm"),
+                ((WIDTH, FF), BF16, "hbm"),
+                ((FF, WIDTH), BF16, "hbm"),
             ],
-            steps,
+            places,
             [
+                pltpu.VMEM(parts + (COLS_UP,), BF16),
+                pltpu.VMEM(parts + (COLS_UP,), BF16),
+                pltpu.VMEM(parts + (COLS_DOWN,), BF16),
+                pltpu.VMEM(parts + (COLS_DOWN,), BF16),
                 pltpu.VMEM((WIDTH, WIDTH), BF16),
                 pltpu.VMEM((WIDTH, FF), BF16),
                 pltpu.VMEM((FF, WIDTH), BF16),
                 pltpu.VMEM((WIDTH, VOCAB), BF16),
                 pltpu.VMEM((count, FF), BF16),
                 pltpu.VMEM((count, WIDTH), BF16),
+                pltpu.VMEM((count, WIDTH), F32),
+                pltpu.VMEM((count, FF), BF16),
+                pltpu.VMEM((count, WIDTH), F32),
                 pltpu.VMEM((count, VOCAB), BF16),
                 pltpu.VMEM((count, WIDTH), BF16),
+                pltpu.SemaphoreType.DMA((7,)),
+                pltpu.SemaphoreType.DMA((places, 4)),
             ],
             flops=8e9,
         )
@@ -782,28 +884,35 @@
         dh, d_mixed, g_gain_two, g_bias_two, g_bias_up, keep_u, send_u = call(
             feed_back_kernel,
             "feed_backward",
+            [(idx, None), (vec, None)]
+            + [(t, "hbm") for t in (h, slope, dy, o0, o1, full_mix, full_up, full_down)],
             [
-                (idx, None), (vec, None), (h, tok(WIDTH)), (slope, tok(FF)), (dy, tok(WIDTH)),
-                (o0, mixed_all), (o1, mixed_all),
-                (near_u, None), (far_u, None), (near_d, None), (far_d, None),
-            ],
-            [
-                ((count, WIDTH), F32, tok(WIDTH)),
-                ((count, WIDTH), BF16, tok(WIDTH)),
+                ((count, WIDTH), F32, "hbm"),
+                ((count, WIDTH), BF16, "hbm"),
                 ((1, WIDTH), F32, None),
                 ((1, WIDTH), F32, None),
                 ((1, FF), F32, None),
                 (parts + (COLS_UP,), BF16, None),
                 (parts + (COLS_UP,), BF16, None),
             ],
-            steps,
+            places,
             [
                 pltpu.VMEM((WIDTH, WIDTH), BF16),
                 pltpu.VMEM((WIDTH, FF), BF16),
                 pltpu.VMEM((FF, WIDTH), BF16),
+                pltpu.VMEM((count, WIDTH), F32),
+                pltpu.VMEM((count, FF), BF16),
+                pltpu.VMEM((count, WIDTH), F32),
+                pltpu.VMEM((count, HALF), BF16),
+                pltpu.VMEM((count, HALF), BF16),
                 pltpu.VMEM((count, FF), BF16),
                 pltpu.VMEM((count, WIDTH), BF16),
                 pltpu.VMEM((count, WIDTH), BF16),
+                pltpu.VMEM((count, WIDTH), F32),
+                pltpu.VMEM((count, WIDTH), BF16),
+                pltpu.SemaphoreType.DMA((5,)),
+                pltpu.SemaphoreType.DMA((places, 3)),
+                pltpu.SemaphoreType.DMA((places, 2)),
             ],
             flops=8e9,
         )
@@ -824,7 +933,7 @@
             return call(
                 attend_back_last_kernel if last else attend_back_kernel,
                 "attend_backward",
-                [(idx, None), (unit_t, None), (columns, None), (w, None)]
+                [(idx, None), (both_t, "hbm"), (w, "hbm")]
                 + [(proj, wide), (floats, wide), (mixed, ((CHUNK, HALF), back))]
                 + [(d_mixed, column), (states, kept_back)]
                 + [(t, None) for t in extra],
@@ -839,6 +948,9 @@
                     pltpu.VMEM((2, 128, 256), F32),
                     pltpu.VMEM((1, HALF), F32),
                     pltpu.VMEM((count, COLS_PROJ), BF16),
+                    pltpu.VMEM((2 * WIDTH + PIECE, count), BF16),
+                    pltpu.VMEM((WIDTH, COLS_PROJ), BF16),
+                    pltpu.SemaphoreType.DMA((2,)),
                 ],
                 flops=10e9,
             )
@@ -879,28 +991,33 @@
             steps,
             flops=3e9,
         )[0]
-        got_u, got_p, got_d, d_tokens = pin(got_u, got_p, got_d, d_tokens)
+        got_u, got_d, d_tokens = pin(got_u, got_d, d_tokens)
         pair_u = half_sum(low_u, got_u)
         got_u = last_start(pair_u, shards)
         total_d = last_sum(pair_d, got_d, dp)
+        got_p, _, _ = pin(got_p, pair_u, d_tokens)
         rows_p = plane_sum(sum_p, got_p)
         got_p = shard_start(rows_p, shards)
         got_u, _ = pin(got_u, rows_p)
         total_f = jnp.concatenate([last_sum(pair_u, got_u, dp), total_d], axis=-1)
         along_f = swap(total_f, "dp", dp, 4)
         got_p, _ = pin(got_p, total_f)
+        total_p = shard_sum(rows_p, got_p, dp)
+        plane_p = plane_start([total_p] * 4, dp)
+        along_f, _ = pin(along_f, total_p)
         pair_f = jnp.stack([total_f, along_f])
         up_f = swap(pair_f, "dp", dp, 2)
-        total_p = shard_sum(rows_p, got_p, dp)
-        along_p = swap(total_p, "dp", dp, 4)
-        pair_p = jnp.stack([total_p, along_p])
-        up_p = swap(pair_p, "dp", dp, 2)
-        up_f, _ = pin(up_f, pair_p)
+        near_p = jnp.stack([total_p] + plane_p)
+        far_p = swap(near_p, "dp", dp, 1)
+        g_query, g_key, g_value, g_control, g1, b1, g2, b2, bd, bu = call(
+            unpack_proj_kernel,
+            "unpack_proj",
+            [(idx, None), (near_p, None), (far_p, None)],
+            [((rows, WIDTH), F32, None)] * 4 + [((128,), F32, None)] * 5 + [((512,), F32, None)],
+        )
+        up_f, _ = pin(up_f, g_query)
         near_f = jnp.stack([pair_f, up_f], axis=1).reshape((4,) + total_f.shape)
         far_f = swap(near_f, "dp", dp, 1)
-        up_p, _ = pin(up_p, near_f)
-        near_p = jnp.stack([pair_p, up_p], axis=1).reshape((4,) + total_p.shape)
-        far_p = swap(near_p, "dp", dp, 1)
         g_mix, g_up, g_down, g_read = call(
             unpack_feed_kernel,
             "unpack_feed",
@@ -911,13 +1028,6 @@
                 ((4 * rows, WIDTH), F32, None),
                 ((rows, VOCAB), F32, None),
             ],
-        )
-        far_p, g_up = pin(far_p, g_up)
-        g_query, g_key, g_value, g_control, g1, b1, g2, b2, bd, bu = call(
-            unpack_proj_kernel,
-            "unpack_proj",
-            [(idx, None), (near_p, None), (far_p, None)],
-            [((rows, WIDTH), F32, None)] * 4 + [((128,), F32, None)] * 5 + [((512,), F32, None)],
         )
         return (
             out, d_tokens, g1, b1, g_query, g_key, g_value, g_control, g_mix,

time: 198 us -> 187 us (0.944)
  Pallas kernels: 108 us -> 101 us
  waiting for transfers between devices: 30.3 us -> 26.1 us
    pallas_call x11, Pallas kernels: 108 us -> 101 us  [call(): pl.pallas_call(kernel, grid=grid, in_specs=in_specs, out_specs=[spec(shap...]
    ppermute x44 -> x45, waiting for transfers between devices: 30.3 us -> 26.1 us  [swap(): return lax.ppermute(value, axis, [(i, i ^ distance) for i in range(size)])]
    ppermute x44 -> x45, starting transfers between devices: 47 us -> 48.4 us  [swap(): return lax.ppermute(value, axis, [(i, i ^ distance) for i in range(size)])]
    unnamed x34 -> x32, local copies, waits for them, and re-layouts: 4.1 us -> 2.98 us
  transfers between devices with their start and end apart: 44 -> 45, of which waited for: 18 -> 18; matrix products, arithmetic and copies ran while one was open for 2% -> 3% of each run, Pallas kernels for 41% -> 41%
where the time goes in v4:
time: 187 us
  Pallas kernels  101 us (54%)
  starting transfers between devices  48.4 us (26%)
  waiting for transfers between devices  26.1 us (14%)
  local copies, waits for them, and re-layouts  5.73 us (3%)
  other arithmetic  4.54 us (2%)
    pallas_call x11, Pallas kernels, call(): pl.pallas_call(kernel, grid=grid, in_specs=in_specs, out_specs=[spec(shap...  101 us
    ppermute x45, starting transfers between devices, swap(): return lax.ppermute(value, axis, [(i, i ^ distance) for i in range(size)])  48.4 us
    ppermute x45, waiting for transfers between devices, swap(): return lax.ppermute(value, axis, [(i, i ^ distance) for i in range(size)])  26.1 us
  transfers between devices with their start and end apart: 45, of which 18 were waited for; matrix products, arithmetic and copies ran while one was open for 3% of the time, Pallas kernels for 41%

profile of v4, /device:TPU:0, one launch (start us, length us, event | category | flops | bytes accessed | tf_op | source)
XLA Modules:
  0.0 186.8 jit_solution(584235782408471362)
XLA Ops:
  1.3 2.7 %pack_weights.1 = (bf16[16,2176]{1,0:T(8,128)(2,1)}, bf16[16,2560]{1,0:T(8,128)(2,1)}, bf16[2,16,2304]{2,1,0:T(8,128)(2,1)}) custom-call(s32[3]{0:T(128)} %pad_add_fusion.idx, bf16[128]{0:T(256)(128)(2,1)} %g1.1, bf16[128]{0:T(256)(128)(2,1)} %b1.1, bf16[128]{0:T(256)(128)(2,1)} %g2.1, bf16[128]{0:T(256)(128)(2,1)} %b2.1, bf16[128]{0:T(256)(128)(2,1)} %bd.1, ...), custom_call_target="tpu_custom_call" | custom-call | flops 1000 | bytes 1000 | tf_op jit(solution)/shard_map/pack_weights/pallas_call | solution.py:658
  4.0 5.1 %collective-permute-start.2 = (bf16[16,2176]{1,0:T(8,128)(2,1)}, bf16[16,2176]{1,0:T(8,128)(2,1)S(1)}, u32[]{:S(2)}, u32[]{:S(2)}) collective-permute-start(bf16[16,2176]{1,0:T(8,128)(2,1)} %get-tuple-element.150), channel_id=1, source_target_pairs={{0,3},{1,2},{2,1},{3,0},{4,7},{5,6},{6,5},{7,4},{8,11},{9,10},{10,... | collective-permute-start | bytes 208904 | tf_op jit(solution)/shard_map/ppermute | solution.py:675
  9.8 1.4 collective-permute-start.3
  12.7 2.7 %collective-permute-done.1 = bf16[16,2176]{1,0:T(8,128)(2,1)S(1)} collective-permute-done((bf16[16,2176]{1,0:T(8,128)(2,1)}, bf16[16,2176]{1,0:T(8,128)(2,1)S(1)}, u32[]{:S(2)}, u32[]{:S(2)}) %collective-permute-start.1) | collective-permute-done | bytes 69664 | tf_op jit(solution)/shard_map/ppermute | solution.py:675
  17.4 1.6 collective-permute-start.8
  19.1 2.4 %collective-permute-start.6 = (bf16[4,16,2048]{2,1,0:T(8,128)(2,1)S(1)}, bf16[4,16,2048]{2,1,0:T(8,128)(2,1)S(1)}, u32[]{:S(2)}, u32[]{:S(2)}) collective-permute-start(bf16[4,16,2048]{2,1,0:T(8,128)(2,1)S(1)} %pad_maximum_fusion.11), channel_id=1, source_target_pairs={{0,24},{4,28},{8,16},{12,20},{16,8},{20,12},{24,0},{28,4},{1,25},{... | collective-permute-start | bytes 786440 | tf_op jit(solution)/shard_map/ppermute | solution.py:675
  22.5 1.9 %collective-permute-start.7 = (bf16[2,16,2560]{2,1,0:T(8,128)(2,1)S(1)}, bf16[2,16,2560]{2,1,0:T(8,128)(2,1)S(1)}, u32[]{:S(2)}, u32[]{:S(2)}) collective-permute-start(bf16[2,16,2560]{2,1,0:T(8,128)(2,1)S(1)} %pad_maximum_fusion.12), channel_id=1, source_target_pairs={{0,2},{1,3},{2,0},{3,1},{4,6},{5,7},{6,4},{7,5},{8,10},{9,11},{10,... | collective-permute-start | bytes 491528 | tf_op jit(solution)/shard_map/ppermute | solution.py:675
  24.5 3.8 %first_norm.1 = (bf16[1024,512]{1,0:T(8,128)(2,1)}, bf16[1040,1024]{1,0:T(8,128)(2,1)}) custom-call(s32[3]{0:T(128)} %pad_add_fusion.idx, bf16[4,16,128]{2,1,0:T(8,128)(2,1)} %pad_maximum_fusion.14.vec, bf16[1024,512]{1,0:T(8,128)(2,1)} %x.4), custom_call_target="tpu_custom_call" | custom-call | flops 1000 | bytes 1000 | tf_op jit(solution)/shard_map/first_norm/pallas_call | solution.py:658
  28.3 2.6 %collective-permute-done.7 = bf16[2,16,2560]{2,1,0:T(8,128)(2,1)S(1)} collective-permute-done((bf16[2,16,2560]{2,1,0:T(8,128)(2,1)S(1)}, bf16[2,16,2560]{2,1,0:T(8,128)(2,1)S(1)}, u32[]{:S(2)}, u32[]{:S(2)}) %collective-permute-start.7) | collective-permute-done | bytes 163872 | tf_op jit(solution)/shard_map/ppermute | solution.py:675
  31.0 1.6 collective-permute-done.5
  32.9 1.7 collective-permute-start.12
  34.6 1.3 collective-permute-start.11
  36.4 2.4 %collective-permute-start.13 = (bf16[2,2,16,2304]{3,2,0,1:T(8,128)(2,1)S(1)}, bf16[2,2,16,2304]{3,2,0,1:T(8,128)(2,1)S(1)}, u32[]{:S(2)}, u32[]{:S(2)}) collective-permute-start(bf16[2,2,16,2304]{3,2,0,1:T(8,128)(2,1)S(1)} %pad_maximum_fusion.5), channel_id=1, source_target_pairs={{0,2},{1,3},{2,0},{3,1},{4,6},{5,7},{6,4},{7,5},{8,10},{9,11},{10,... | collective-permute-start | bytes 884744 | tf_op jit(solution)/shard_map/ppermute | solution.py:675
  38.9 1.0 copy-done.3
  39.8 9.6 %attend.2 = (bf16[1024,1024]{1,0:T(8,128)(2,1)}, f32[1024,1024]{1,0:T(8,128)}, bf16[1024,512]{1,0:T(8,128)(2,1)}, bf16[8,2,128,256]{3,2,1,0:T(8,128)(2,1)}, bf16[512,1024]{1,0:T(8,128)(2,1)}) custom-call(s32[3]{0:T(128)} %pad_add_fusion.idx, bf16[1024,512]{1,0:T(8,128)(2,1)} %get-tuple-element.173.a1, bf16[4,4,16,2048]{3,2,1,0:T(8,128)(2,1)} %copy-done, ...), custom_call_target="tpu_custom_call" | custom-call | flops 1000 | bytes 1000 | tf_op jit(solution)/shard_map/attend/pallas_call | solution.py:658
  49.4 2.8 %collective-permute-done.13 = bf16[2,2,16,2304]{3,2,0,1:T(8,128)(2,1)S(1)} collective-permute-done((bf16[2,2,16,2304]{3,2,0,1:T(8,128)(2,1)S(1)}, bf16[2,2,16,2304]{3,2,0,1:T(8,128)(2,1)S(1)}, u32[]{:S(2)}, u32[]{:S(2)}) %collective-permute-start.13) | collective-permute-done | bytes 294944 | tf_op jit(solution)/shard_map/ppermute | solution.py:675
  52.6 1.5 collective-permute-start.16
  54.9 9.5 %attend.3 = (bf16[1024,1024]{1,0:T(8,128)(2,1)}, f32[1024,1024]{1,0:T(8,128)}, bf16[1024,512]{1,0:T(8,128)(2,1)}, bf16[8,2,128,256]{3,2,1,0:T(8,128)(2,1)}, bf16[512,1024]{1,0:T(8,128)(2,1)}) custom-call(s32[3]{0:T(128)} %pad_add_fusion.idx, bf16[1024,512]{1,0:T(8,128)(2,1)} %get-tuple-element.173.a1, bf16[4,4,16,2048]{3,2,1,0:T(8,128)(2,1)} %copy-done, ...), custom_call_target="tpu_custom_call" | custom-call | flops 1000 | bytes 1000 | tf_op jit(solution)/shard_map/attend/pallas_call | solution.py:658
  65.1 1.0 copy.33.target
  66.1 1.5 collective-permute-done.17.down_far_i
  67.6 18.7 %feed_forward.1 = (bf16[1024,512]{1,0:T(8,128)(2,1)}, f32[1024,512]{1,0:T(8,128)}, bf16[1024,2048]{1,0:T(8,128)(2,1)}, f32[1024,512]{1,0:T(8,128)}, f32[1,512]{1...) custom-call(s32[3]{0:T(128)} %pad_add_fusion.idx, ...), custom_call_target="tpu_custom_call" | custom-call | flops 1000 | bytes 1000 | tf_op jit(solution)/shard_map/feed_forward/pallas_call | solution.py:658
  86.6 14.6 %feed_backward.1 = (f32[1024,512]{1,0:T(8,128)}, bf16[1024,512]{1,0:T(8,128)(2,1)}, f32[1,512]{1,0:T(1,128)}, f32[1,512]{1,0:T(1,128)}, f32[1,2048]{1,0:T(1,128)...) custom-call(s32[3]{0:T(128)} %pad_add_fusion.idx, bf16[4,16,128]{2,1,0:T(8,128)(2,1)} %pad_maximum_fusion.14.vec, ...), custom_call_target="tpu_custom_call" | custom-call | flops 1000 | bytes 1000 | tf_op jit(solution)/shard_map/feed_backward/pallas_call | solution.py:658
  101.8 1.3 collective-permute-start.19
  103.7 1.7 collective-permute-start.21
  105.4 14.4 %attend_backward.2 = (bf16[1024,1024]{1,0:T(8,128)(2,1)}, bf16[4,4,16,1024]{3,2,1,0:T(8,128)(2,1)}, bf16[4,4,16,1024]{3,2,1,0:T(8,128)(2,1)}, f32[8,512]{1,0:T(8,128)}) custom-call(s32[3]{0:T(128)} %pad_add_fusion.idx, bf16[1040,1024]{1,0:T(8,128)(2,1)} %get-tuple-element.206.both_t, bf16[512,1024]{1,0:T(8,128)(2,1)} %get-tuple-element.207.w.w0, ...), custom_call_target="tpu_custom_call" | custom-call | flops 1000 | bytes 1000 | tf_op jit(solution)/shard_map/attend_backward/pallas_call | solution.py:658
  120.5 1.3 collective-permute-start.24
  122.3 1.7 collective-permute-start.26
  124.0 1.1 collective-permute-start.23
  125.1 14.9 %attend_backward.3 = (bf16[1024,1024]{1,0:T(8,128)(2,1)}, bf16[4,4,16,1152]{3,2,1,0:T(8,128)(2,1)}, bf16[4,4,16,1152]{3,2,1,0:T(8,128)(2,1)}) custom-call(s32[3]{0:T(128)} %pad_add_fusion.idx, bf16[1040,1024]{1,0:T(8,128)(2,1)} %get-tuple-element.206.both_t, bf16[512,1024]{1,0:T(8,128)(2,1)} %get-tuple-element.225.w.w1, ...), custom_call_target="tpu_custom_call" | custom-call | flops 1000 | bytes 1000 | tf_op jit(solution)/shard_map/attend_backward/pallas_call | solution.py:658
  140.4 2.0 %collective-permute-done.28 = bf16[4,4,16,1152]{3,2,1,0:T(8,128)(2,1)S(1)} collective-permute-done((bf16[4,4,16,1152]{3,2,1,0:T(8,128)(2,1)}, bf16[4,4,16,1152]{3,2,1,0:T(8,128)(2,1)S(1)}, u32[]{:S(2)}, u32[]{:S(2)}) %collective-permute-start.28) | collective-permute-done | bytes 589856 | tf_op jit(solution)/shard_map/ppermute | solution.py:675
  142.8 1.9 %collective-permute-start.29 = (bf16[2,16,2560]{2,1,0:T(8,128)(2,1)S(1)}, bf16[2,16,2560]{2,1,0:T(8,128)(2,1)S(1)}, u32[]{:S(2)}, u32[]{:S(2)}) collective-permute-start(bf16[2,16,2560]{2,1,0:T(8,128)(2,1)S(1)} %slice.295), channel_id=1, source_target_pairs={{0,2},{1,3},{2,0},{3,1},{4,6},{5,7},{6,4},{7,5},{8,10},{9,11},{10,... | collective-permute-start | bytes 491528 | tf_op jit(solution)/shard_map/ppermute | solution.py:675
  144.8 1.3 collective-permute-start.31
  146.7 1.7 collective-permute-start.33
  148.4 7.5 %input_gradient.1 = f32[1024,512]{1,0:T(8,128)} custom-call(s32[3]{0:T(128)} %pad_add_fusion.idx, bf16[4,16,128]{2,1,0:T(8,128)(2,1)} %pad_maximum_fusion.14.vec, bf16[1024,512]{1,0:T(8,128)(2,1)} %x.4, f32[1024,512]{1,0:T(8,128)} %get-tuple-element.255.dh, bf16[1024,1024]{1,0:T(8,128)(2,1)} %get-tuple-element.256.dx0, ...), custom_call_target="tpu_custom_call" | custom-call | flops 1000 | bytes 1000 | tf_op jit(solution)/shard_map/input_gradient/pallas_call | solution.py:658
  156.0 2.0 %collective-permute-start.37 = (bf16[16,2560]{1,0:T(8,128)(2,1)S(1)}, bf16[16,2560]{1,0:T(8,128)(2,1)S(1)}, u32[]{:S(2)}, u32[]{:S(2)}) collective-permute-start(bf16[16,2560]{1,0:T(8,128)(2,1)S(1)} %get-tuple-element.307), channel_id=1, source_target_pairs={{0,1},{1,0},{2,3},{3,2},{4,5},{5,4},{6,7},{7,6},{8,9},{9,8},{10,11... | collective-permute-start | bytes 245768 | tf_op jit(solution)/shard_map/ppermute | solution.py:675
  158.0 2.2 %collective-permute-done.32 = bf16[4,16,2176]{2,1,0:T(8,128)(2,1)S(1)} collective-permute-done((bf16[4,16,2176]{2,1,0:T(8,128)(2,1)S(1)}, bf16[4,16,2176]{2,1,0:T(8,128)(2,1)S(1)}, u32[]{:S(2)}, u32[]{:S(2)}) %collective-permute-start.32) | collective-permute-done | bytes 278560 | tf_op jit(solution)/shard_map/ppermute | solution.py:675
  160.4 2.3 %collective-permute-start.36 = (bf16[16,2176]{1,0:T(8,128)(2,1)S(1)}, bf16[16,2176]{1,0:T(8,128)(2,1)S(1)}, u32[]{:S(2)}, u32[]{:S(2)}) collective-permute-start(bf16[16,2176]{1,0:T(8,128)(2,1)S(1)} %get-tuple-element.297), channel_id=1, source_target_pairs={{0,3},{1,2},{2,1},{3,0},{4,7},{5,6},{6,5},{7,4},{8,11},{9,10},{10,... | collective-permute-start | bytes 208904 | tf_op jit(solution)/shard_map/ppermute | solution.py:675
  163.6 1.3 collective-permute-start.34
  165.5 1.6 collective-permute-done.36
  167.1 1.7 collective-permute-done.35
  168.9 1.5 collective-permute-start.40
  171.0 1.5 collective-permute-start.38
  173.1 1.7 collective-permute-done.40
  175.1 0.9 collective-permute-done.38
  176.2 1.5 collective-permute-done.41.far
  178.4 2.1 %unpack_proj.1 = (f32[128,512]{1,0:T(8,128)}, f32[128,512]{1,0:T(8,128)}, f32[128,512]{1,0:T(8,128)}, f32[128,512]{1,0:T(8,128)}, f32[128]{0:T(128)}, /*index=5*...) custom-call(s32[3]{0:T(128)} %pad_add_fusion.idx, bf16[4,16,2176]{2,1,0:T(8,128)(2,1)} %copy-done.8, ...), custom_call_target="tpu_custom_call" | custom-call | flops 1000 | bytes 1000 | tf_op jit(solution)/shard_map/unpack_proj/pallas_call | solution.py:658
  181.0 2.0 %collective-permute-done.44.far = bf16[4,16,4864]{2,1,0:T(8,128)(2,1)S(1)} collective-permute-done((bf16[4,16,4864]{2,1,0:T(8,128)(2,1)S(1)}, bf16[4,16,4864]{2,1,0:T(8,128)(2,1)S(1)}, u32[]{:S(2)}, u32[]{:S(2)}) %collective-permute-start.44) | collective-permute-done | bytes 622624 | tf_op jit(solution)/shard_map/ppermute | solution.py:675
  183.9 2.9 %unpack_feed.1 = (f32[128,512]{1,0:T(8,128)}, f32[128,2048]{1,0:T(8,128)}, f32[512,512]{1,0:T(8,128)}, f32[128,256]{1,0:T(8,128)}) custom-call(s32[3]{0:T(128)} %pad_add_fusion.idx, bf16[4,16,4864]{2,1,0:T(8,128)(2,1)} %bitcast.103, bf16[4,16,4864]{2,1,0:T(8,128)(2,1)} %copy-done.9), custom_call_target="tpu_custom_call" | custom-call | flops 1000 | bytes 1000 | tf_op jit(solution)/shard_map/unpack_feed/pallas_call | solution.py:658
  (126 shorter events, 17.9 us)
Async XLA Ops:
  4.0 8.7 %collective-permute-start.2 = (bf16[16,2176]{1,0:T(8,128)(2,1)}, bf16[16,2176]{1,0:T(8,128)(2,1)S(1)}, u32[]{:S(2)}, u32[]{:S(2)}) collective-permute-start(bf16[16,2176]{1,0:T(8,128)(2,1)} %get-tuple-element.150), channel_id=1, source_target_pairs={{0,3},{1,2},{2,1},{3,0},{4,7},{5,6},{6,5},{7,4},{8,11},{9,10},{10,... | collective-permute-start | bytes 208904 | tf_op jit(solution)/shard_map/ppermute | solution.py:675
  9.2 6.2 %collective-permute-start.1 = (bf16[16,2176]{1,0:T(8,128)(2,1)}, bf16[16,2176]{1,0:T(8,128)(2,1)S(1)}, u32[]{:S(2)}, u32[]{:S(2)}) collective-permute-start(bf16[16,2176]{1,0:T(8,128)(2,1)} %get-tuple-element.150), channel_id=1, source_target_pairs={{0,2},{1,3},{2,0},{3,1},{4,6},{5,7},{6,4},{7,5},{8,10},{9,11},{10,... | collective-permute-start | bytes 208904 | tf_op jit(solution)/shard_map/ppermute | solution.py:675
  9.2 6.5 %collective-permute-start = (bf16[16,2176]{1,0:T(8,128)(2,1)}, bf16[16,2176]{1,0:T(8,128)(2,1)S(1)}, u32[]{:S(2)}, u32[]{:S(2)}) collective-permute-start(bf16[16,2176]{1,0:T(8,128)(2,1)} %get-tuple-element.150), channel_id=1, source_target_pairs={{0,1},{1,0},{2,3},{3,2},{4,5},{5,4},{6,7},{7,6},{8,9},{9,8},{10,11... | collective-permute-start | bytes 208904 | tf_op jit(solution)/shard_map/ppermute | solution.py:675
  9.8 6.7 %collective-permute-start.3 = (bf16[16,2560]{1,0:T(8,128)(2,1)}, bf16[16,2560]{1,0:T(8,128)(2,1)S(1)}, u32[]{:S(2)}, u32[]{:S(2)}) collective-permute-start(bf16[16,2560]{1,0:T(8,128)(2,1)} %get-tuple-element.151), channel_id=1, source_target_pairs={{0,1},{1,0},{2,3},{3,2},{4,5},{5,4},{6,7},{7,6},{8,9},{9,8},{10,11... | collective-permute-start | bytes 245768 | tf_op jit(solution)/shard_map/ppermute | solution.py:675
  17.4 10.9 %collective-permute-start.8 = (bf16[2,16,2304]{2,1,0:T(8,128)(2,1)S(1)}, bf16[2,16,2304]{2,1,0:T(8,128)(2,1)S(1)}, u32[]{:S(2)}, u32[]{:S(2)}) collective-permute-start(bf16[2,16,2304]{2,1,0:T(8,128)(2,1)S(1)} %copy-done.13), channel_id=1, source_target_pairs={{0,1},{1,0},{2,3},{3,2},{4,5},{5,4},{6,7},{7,6},{8,9},{9,8},{10,11... | collective-permute-start | bytes 442376 | tf_op jit(solution)/shard_map/ppermute | solution.py:675
  19.1 11.9 %collective-permute-start.6 = (bf16[4,16,2048]{2,1,0:T(8,128)(2,1)S(1)}, bf16[4,16,2048]{2,1,0:T(8,128)(2,1)S(1)}, u32[]{:S(2)}, u32[]{:S(2)}) collective-permute-start(bf16[4,16,2048]{2,1,0:T(8,128)(2,1)S(1)} %pad_maximum_fusion.11), channel_id=1, source_target_pairs={{0,24},{4,28},{8,16},{12,20},{16,8},{20,12},{24,0},{28,4},{1,25},{... | collective-permute-start | bytes 786440 | tf_op jit(solution)/shard_map/ppermute | solution.py:675
  21.5 11.0 %collective-permute-start.5 = (bf16[4,16,2048]{2,1,0:T(8,128)(2,1)S(1)}, bf16[4,16,2048]{2,1,0:T(8,128)(2,1)S(1)}, u32[]{:S(2)}, u32[]{:S(2)}) collective-permute-start(bf16[4,16,2048]{2,1,0:T(8,128)(2,1)S(1)} %pad_maximum_fusion.11), channel_id=1, source_target_pairs={{0,16},{4,20},{8,24},{12,28},{16,0},{20,4},{24,8},{28,12},{1,17},{... | collective-permute-start | bytes 786440 | tf_op jit(solution)/shard_map/ppermute | solution.py:675
  22.0 10.6 %collective-permute-start.4 = (bf16[4,16,2048]{2,1,0:T(8,128)(2,1)S(1)}, bf16[4,16,2048]{2,1,0:T(8,128)(2,1)S(1)}, u32[]{:S(2)}, u32[]{:S(2)}) collective-permute-start(bf16[4,16,2048]{2,1,0:T(8,128)(2,1)S(1)} %pad_maximum_fusion.11), channel_id=1, source_target_pairs={{0,8},{4,12},{8,0},{12,4},{16,24},{20,28},{24,16},{28,20},{1,9},{5... | collective-permute-start | bytes 786440 | tf_op jit(solution)/shard_map/ppermute | solution.py:675
  22.5 8.4 %collective-permute-start.7 = (bf16[2,16,2560]{2,1,0:T(8,128)(2,1)S(1)}, bf16[2,16,2560]{2,1,0:T(8,128)(2,1)S(1)}, u32[]{:S(2)}, u32[]{:S(2)}) collective-permute-start(bf16[2,16,2560]{2,1,0:T(8,128)(2,1)S(1)} %pad_maximum_fusion.12), channel_id=1, source_target_pairs={{0,2},{1,3},{2,0},{3,1},{4,6},{5,7},{6,4},{7,5},{8,10},{9,11},{10,... | collective-permute-start | bytes 491528 | tf_op jit(solution)/shard_map/ppermute | solution.py:675
  32.8 6.1 %collective-permute-start.9 = (bf16[4,4,16,2048]{3,2,1,0:T(8,128)(2,1)S(1)}, bf16[4,4,16,2048]{3,2,1,0:T(8,128)(2,1)S(1)}, u32[]{:S(2)}, u32[]{:S(2)}) collective-permute-start(bf16[4,4,16,2048]{3,2,1,0:T(8,128)(2,1)S(1)} %pad_maximum_fusion.2.near), channel_id=1, source_target_pairs={{0,4},{4,0},{8,12},{12,8},{16,20},{20,16},{24,28},{28,24},{1,5},{5... | collective-permute-start | bytes 3145736 | tf_op jit(solution)/shard_map/ppermute | solution.py:675
  32.9 19.3 %collective-permute-start.12 = (bf16[4,16,2560]{2,1,0:T(8,128)(2,1)S(1)}, bf16[4,16,2560]{2,1,0:T(8,128)(2,1)S(1)}, u32[]{:S(2)}, u32[]{:S(2)}) collective-permute-start(bf16[4,16,2560]{2,1,0:T(8,128)(2,1)S(1)} %constant_dynamic-update-slice_fusion), channel_id=1, source_target_pairs={{0,24},{4,28},{8,16},{12,20},{16,8},{20,12},{24,0},{28,4},{1,25},{... | collective-permute-start | bytes 983048 | tf_op jit(solution)/shard_map/ppermute | solution.py:675
  34.6 17.6 %collective-permute-start.11 = (bf16[4,16,2560]{2,1,0:T(8,128)(2,1)S(1)}, bf16[4,16,2560]{2,1,0:T(8,128)(2,1)S(1)}, u32[]{:S(2)}, u32[]{:S(2)}) collective-permute-start(bf16[4,16,2560]{2,1,0:T(8,128)(2,1)S(1)} %constant_dynamic-update-slice_fusion), channel_id=1, source_target_pairs={{0,16},{4,20},{8,24},{12,28},{16,0},{20,4},{24,8},{28,12},{1,17},{... | collective-permute-start | bytes 983048 | tf_op jit(solution)/shard_map/ppermute | solution.py:675
  35.9 16.3 %collective-permute-start.10 = (bf16[4,16,2560]{2,1,0:T(8,128)(2,1)S(1)}, bf16[4,16,2560]{2,1,0:T(8,128)(2,1)S(1)}, u32[]{:S(2)}, u32[]{:S(2)}) collective-permute-start(bf16[4,16,2560]{2,1,0:T(8,128)(2,1)S(1)} %constant_dynamic-update-slice_fusion), channel_id=1, source_target_pairs={{0,8},{4,12},{8,0},{12,4},{16,24},{20,28},{24,16},{28,20},{1,9},{5... | collective-permute-start | bytes 983048 | tf_op jit(solution)/shard_map/ppermute | solution.py:675
  36.4 15.8 %collective-permute-start.13 = (bf16[2,2,16,2304]{3,2,0,1:T(8,128)(2,1)S(1)}, bf16[2,2,16,2304]{3,2,0,1:T(8,128)(2,1)S(1)}, u32[]{:S(2)}, u32[]{:S(2)}) collective-permute-start(bf16[2,2,16,2304]{3,2,0,1:T(8,128)(2,1)S(1)} %pad_maximum_fusion.5), channel_id=1, source_target_pairs={{0,2},{1,3},{2,0},{3,1},{4,6},{5,7},{6,4},{7,5},{8,10},{9,11},{10,... | collective-permute-start | bytes 884744 | tf_op jit(solution)/shard_map/ppermute | solution.py:675
  52.4 12.0 %collective-permute-start.14 = (bf16[4,4,16,2560]{3,2,1,0:T(8,128)(2,1)S(1)}, bf16[4,4,16,2560]{3,2,1,0:T(8,128)(2,1)S(1)}, u32[]{:S(2)}, u32[]{:S(2)}) collective-permute-start(bf16[4,4,16,2560]{3,2,1,0:T(8,128)(2,1)S(1)} %pad_maximum_fusion.up_near_i), channel_id=1, source_target_pairs={{0,4},{4,0},{8,12},{12,8},{16,20},{20,16},{24,28},{28,24},{1,5},{5... | collective-permute-start | bytes 3932168 | tf_op jit(solution)/shard_map/ppermute | solution.py:675
  52.6 11.8 %collective-permute-start.16 = (bf16[4,16,2304]{2,1,0:T(8,128)(2,1)S(1)}, bf16[4,16,2304]{2,1,0:T(8,128)(2,1)S(1)}, u32[]{:S(2)}, u32[]{:S(2)}) collective-permute-start(bf16[4,16,2304]{2,1,0:T(8,128)(2,1)S(1)} %get-tuple-element.306), channel_id=1, source_target_pairs={{0,16},{4,20},{8,24},{12,28},{16,0},{20,4},{24,8},{28,12},{1,17},{... | collective-permute-start | bytes 884744 | tf_op jit(solution)/shard_map/ppermute | solution.py:675
  54.1 10.3 %collective-permute-start.15 = (bf16[4,16,2304]{2,1,0:T(8,128)(2,1)S(1)}, bf16[4,16,2304]{2,1,0:T(8,128)(2,1)S(1)}, u32[]{:S(2)}, u32[]{:S(2)}) collective-permute-start(bf16[4,16,2304]{2,1,0:T(8,128)(2,1)S(1)} %get-tuple-element.306), channel_id=1, source_target_pairs={{0,8},{4,12},{8,0},{12,4},{16,24},{20,28},{24,16},{28,20},{1,9},{5... | collective-permute-start | bytes 884744 | tf_op jit(solution)/shard_map/ppermute | solution.py:675
  64.6 3.0 %collective-permute-start.17 = (bf16[4,4,16,2304]{3,2,1,0:T(8,128)(2,1)S(1)}, bf16[4,4,16,2304]{3,2,1,0:T(8,128)(2,1)}, u32[]{:S(2)}, u32[]{:S(2)}) collective-permute-start(bf16[4,4,16,2304]{3,2,1,0:T(8,128)(2,1)S(1)} %pad_maximum_fusion.1.down_near_i), channel_id=1, source_target_pairs={{0,4},{4,0},{8,12},{12,8},{16,20},{20,16},{24,28},{28,24},{1,5},{5... | collective-permute-start | bytes 3538952 | tf_op jit(solution)/shard_map/ppermute | solution.py:675
  86.4 14.8 %collective-permute-start.18 = (bf16[4,4,16,2304]{3,2,1,0:T(8,128)(2,1)}, bf16[4,4,16,2304]{3,2,1,0:T(8,128)(2,1)S(1)}, u32[]{:S(2)}, u32[]{:S(2)}) collective-permute-start(bf16[4,4,16,2304]{3,2,1,0:T(8,128)(2,1)} %get-tuple-element.197), channel_id=1, source_target_pairs={{0,4},{4,0},{8,12},{12,8},{16,20},{20,16},{24,28},{28,24},{1,5},{5... | collective-permute-start | bytes 3538952 | tf_op jit(solution)/shard_map/ppermute | solution.py:675
  86.6 15.0 %copy-start.7 = (bf16[4,4,16,2304]{3,2,1,0:T(8,128)(2,1)S(1)}, bf16[4,4,16,2304]{3,2,1,0:T(8,128)(2,1)}, u32[]{:S(2)}) copy-start(bf16[4,4,16,2304]{3,2,1,0:T(8,128)(2,1)} %get-tuple-element.196) | copy-start | bytes 3538948
  101.2 18.5 %collective-permute-start.22 = (bf16[4,4,16,2560]{3,2,1,0:T(8,128)(2,1)}, bf16[4,4,16,2560]{3,2,1,0:T(8,128)(2,1)S(1)}, u32[]{:S(2)}, u32[]{:S(2)}) collective-permute-start(bf16[4,4,16,2560]{3,2,1,0:T(8,128)(2,1)} %get-tuple-element.205), channel_id=1, source_target_pairs={{0,4},{4,0},{8,12},{12,8},{16,20},{20,16},{24,28},{28,24},{1,5},{5... | collective-permute-start | bytes 3932168 | tf_op jit(solution)/shard_map/ppermute | solution.py:675
  101.8 18.0 %copy-start.6 = (bf16[4,4,16,2560]{3,2,1,0:T(8,128)(2,1)S(1)}, bf16[4,4,16,2560]{3,2,1,0:T(8,128)(2,1)}, u32[]{:S(2)}) copy-start(bf16[4,4,16,2560]{3,2,1,0:T(8,128)(2,1)} %get-tuple-element.195) | copy-start | bytes 3932164
  101.8 17.9 %collective-permute-start.19 = (bf16[4,16,2304]{2,1,0:T(8,128)(2,1)S(1)}, bf16[4,16,2304]{2,1,0:T(8,128)(2,1)S(1)}, u32[]{:S(2)}, u32[]{:S(2)}) collective-permute-start(bf16[4,16,2304]{2,1,0:T(8,128)(2,1)S(1)} %get-tuple-element.202), channel_id=1, source_target_pairs={{0,8},{4,12},{8,0},{12,4},{16,24},{20,28},{24,16},{28,20},{1,9},{5... | collective-permute-start | bytes 884744 | tf_op jit(solution)/shard_map/ppermute | solution.py:675
  103.1 16.6 %collective-permute-start.20 = (bf16[4,16,2304]{2,1,0:T(8,128)(2,1)S(1)}, bf16[4,16,2304]{2,1,0:T(8,128)(2,1)S(1)}, u32[]{:S(2)}, u32[]{:S(2)}) collective-permute-start(bf16[4,16,2304]{2,1,0:T(8,128)(2,1)S(1)} %get-tuple-element.203), channel_id=1, source_target_pairs={{0,16},{4,20},{8,24},{12,28},{16,0},{20,4},{24,8},{28,12},{1,17},{... | collective-permute-start | bytes 884744 | tf_op jit(solution)/shard_map/ppermute | solution.py:675
  103.7 16.1 %collective-permute-start.21 = (bf16[4,16,2304]{2,1,0:T(8,128)(2,1)S(1)}, bf16[4,16,2304]{2,1,0:T(8,128)(2,1)S(1)}, u32[]{:S(2)}, u32[]{:S(2)}) collective-permute-start(bf16[4,16,2304]{2,1,0:T(8,128)(2,1)S(1)} %get-tuple-element.204), channel_id=1, source_target_pairs={{0,24},{4,28},{8,16},{12,20},{16,8},{20,12},{24,0},{28,4},{1,25},{... | collective-permute-start | bytes 884744 | tf_op jit(solution)/shard_map/ppermute | solution.py:675
  119.8 20.3 %collective-permute-start.27 = (bf16[4,4,16,1024]{3,2,1,0:T(8,128)(2,1)}, bf16[4,4,16,1024]{3,2,1,0:T(8,128)(2,1)S(1)}, u32[]{:S(2)}, u32[]{:S(2)}) collective-permute-start(bf16[4,4,16,1024]{3,2,1,0:T(8,128)(2,1)} %get-tuple-element.224), channel_id=1, source_target_pairs={{0,4},{4,0},{8,12},{12,8},{16,20},{20,16},{24,28},{28,24},{1,5},{5... | collective-permute-start | bytes 1572872 | tf_op jit(solution)/shard_map/ppermute | solution.py:675
  120.5 19.6 %collective-permute-start.24 = (bf16[4,16,2560]{2,1,0:T(8,128)(2,1)S(1)}, bf16[4,16,2560]{2,1,0:T(8,128)(2,1)S(1)}, u32[]{:S(2)}, u32[]{:S(2)}) collective-permute-start(bf16[4,16,2560]{2,1,0:T(8,128)(2,1)S(1)} %get-tuple-element.221), channel_id=1, source_target_pairs={{0,8},{4,12},{8,0},{12,4},{16,24},{20,28},{24,16},{28,20},{1,9},{5... | collective-permute-start | bytes 983048 | tf_op jit(solution)/shard_map/ppermute | solution.py:675
  121.8 18.3 %collective-permute-start.25 = (bf16[4,16,2560]{2,1,0:T(8,128)(2,1)S(1)}, bf16[4,16,2560]{2,1,0:T(8,128)(2,1)S(1)}, u32[]{:S(2)}, u32[]{:S(2)}) collective-permute-start(bf16[4,16,2560]{2,1,0:T(8,128)(2,1)S(1)} %get-tuple-element.222), channel_id=1, source_target_pairs={{0,16},{4,20},{8,24},{12,28},{16,0},{20,4},{24,8},{28,12},{1,17},{... | collective-permute-start | bytes 983048 | tf_op jit(solution)/shard_map/ppermute | solution.py:675
  122.3 17.8 %collective-permute-start.26 = (bf16[4,16,2560]{2,1,0:T(8,128)(2,1)S(1)}, bf16[4,16,2560]{2,1,0:T(8,128)(2,1)S(1)}, u32[]{:S(2)}, u32[]{:S(2)}) collective-permute-start(bf16[4,16,2560]{2,1,0:T(8,128)(2,1)S(1)} %get-tuple-element.223), channel_id=1, source_target_pairs={{0,24},{4,28},{8,16},{12,20},{16,8},{20,12},{24,0},{28,4},{1,25},{... | collective-permute-start | bytes 983048 | tf_op jit(solution)/shard_map/ppermute | solution.py:675
  124.0 16.0 %collective-permute-start.23 = (bf16[2,16,2304]{2,1,0:T(8,128)(2,1)S(1)}, bf16[2,16,2304]{2,1,0:T(8,128)(2,1)S(1)}, u32[]{:S(2)}, u32[]{:S(2)}) collective-permute-start(bf16[2,16,2304]{2,1,0:T(8,128)(2,1)S(1)} %get-tuple-element.220), channel_id=1, source_target_pairs={{0,2},{1,3},{2,0},{3,1},{4,6},{5,7},{6,4},{7,5},{8,10},{9,11},{10,... | collective-permute-start | bytes 442376 | tf_op jit(solution)/shard_map/ppermute | solution.py:675
  125.1 15.1 %copy-start.11 = (bf16[4,4,16,1024]{3,2,1,0:T(8,128)(2,1)S(1)}, bf16[4,4,16,1024]{3,2,1,0:T(8,128)(2,1)}, u32[]{:S(2)}) copy-start(bf16[4,4,16,1024]{3,2,1,0:T(8,128)(2,1)} %get-tuple-element.241) | copy-start | bytes 1572868
  140.1 2.3 %collective-permute-start.28 = (bf16[4,4,16,1152]{3,2,1,0:T(8,128)(2,1)}, bf16[4,4,16,1152]{3,2,1,0:T(8,128)(2,1)S(1)}, u32[]{:S(2)}, u32[]{:S(2)}) collective-permute-start(bf16[4,4,16,1152]{3,2,1,0:T(8,128)(2,1)} %get-tuple-element.244), channel_id=1, source_target_pairs={{0,4},{4,0},{8,12},{12,8},{16,20},{20,16},{24,28},{28,24},{1,5},{5... | collective-permute-start | bytes 1769480 | tf_op jit(solution)/shard_map/ppermute | solution.py:675
  142.8 13.0 %collective-permute-start.29 = (bf16[2,16,2560]{2,1,0:T(8,128)(2,1)S(1)}, bf16[2,16,2560]{2,1,0:T(8,128)(2,1)S(1)}, u32[]{:S(2)}, u32[]{:S(2)}) collective-permute-start(bf16[2,16,2560]{2,1,0:T(8,128)(2,1)S(1)} %slice.295), channel_id=1, source_target_pairs={{0,2},{1,3},{2,0},{3,1},{4,6},{5,7},{6,4},{7,5},{8,10},{9,11},{10,... | collective-permute-start | bytes 491528 | tf_op jit(solution)/shard_map/ppermute | solution.py:675
  144.7 11.1 %collective-permute-start.30 = (bf16[16,2304]{1,0:T(8,128)(2,1)S(1)}, bf16[16,2304]{1,0:T(8,128)(2,1)S(1)}, u32[]{:S(2)}, u32[]{:S(2)}) collective-permute-start(bf16[16,2304]{1,0:T(8,128)(2,1)S(1)} %fusion.19), channel_id=1, source_target_pairs={{0,1},{1,0},{2,3},{3,2},{4,5},{5,4},{6,7},{7,6},{8,9},{9,8},{10,11... | collective-permute-start | bytes 221192 | tf_op jit(solution)/shard_map/ppermute | solution.py:675
  144.8 13.2 %collective-permute-start.31 = (bf16[4,16,2176]{2,1,0:T(8,128)(2,1)S(1)}, bf16[4,16,2176]{2,1,0:T(8,128)(2,1)S(1)}, u32[]{:S(2)}, u32[]{:S(2)}) collective-permute-start(bf16[4,16,2176]{2,1,0:T(8,128)(2,1)S(1)} %get-tuple-element.247), channel_id=1, source_target_pairs={{0,8},{4,12},{8,0},{12,4},{16,24},{20,28},{24,16},{28,20},{1,9},{5... | collective-permute-start | bytes 835592 | tf_op jit(solution)/shard_map/ppermute | solution.py:675
  146.1 14.1 %collective-permute-start.32 = (bf16[4,16,2176]{2,1,0:T(8,128)(2,1)S(1)}, bf16[4,16,2176]{2,1,0:T(8,128)(2,1)S(1)}, u32[]{:S(2)}, u32[]{:S(2)}) collective-permute-start(bf16[4,16,2176]{2,1,0:T(8,128)(2,1)S(1)} %get-tuple-element.248), channel_id=1, source_target_pairs={{0,16},{4,20},{8,24},{12,28},{16,0},{20,4},{24,8},{28,12},{1,17},{... | collective-permute-start | bytes 835592 | tf_op jit(solution)/shard_map/ppermute | solution.py:675
  146.7 13.5 %collective-permute-start.33 = (bf16[4,16,2176]{2,1,0:T(8,128)(2,1)S(1)}, bf16[4,16,2176]{2,1,0:T(8,128)(2,1)S(1)}, u32[]{:S(2)}, u32[]{:S(2)}) collective-permute-start(bf16[4,16,2176]{2,1,0:T(8,128)(2,1)S(1)} %get-tuple-element.249), channel_id=1, source_target_pairs={{0,24},{4,28},{8,16},{12,20},{16,8},{20,12},{24,0},{28,4},{1,25},{... | collective-permute-start | bytes 835592 | tf_op jit(solution)/shard_map/ppermute | solution.py:675
  156.0 8.8 %collective-permute-start.37 = (bf16[16,2560]{1,0:T(8,128)(2,1)S(1)}, bf16[16,2560]{1,0:T(8,128)(2,1)S(1)}, u32[]{:S(2)}, u32[]{:S(2)}) collective-permute-start(bf16[16,2560]{1,0:T(8,128)(2,1)S(1)} %get-tuple-element.307), channel_id=1, source_target_pairs={{0,1},{1,0},{2,3},{3,2},{4,5},{5,4},{6,7},{7,6},{8,9},{9,8},{10,11... | collective-permute-start | bytes 245768 | tf_op jit(solution)/shard_map/ppermute | solution.py:675
  160.4 6.8 %collective-permute-start.36 = (bf16[16,2176]{1,0:T(8,128)(2,1)S(1)}, bf16[16,2176]{1,0:T(8,128)(2,1)S(1)}, u32[]{:S(2)}, u32[]{:S(2)}) collective-permute-start(bf16[16,2176]{1,0:T(8,128)(2,1)S(1)} %get-tuple-element.297), channel_id=1, source_target_pairs={{0,3},{1,2},{2,1},{3,0},{4,7},{5,6},{6,5},{7,4},{8,11},{9,10},{10,... | collective-permute-start | bytes 208904 | tf_op jit(solution)/shard_map/ppermute | solution.py:675
  162.7 6.2 %collective-permute-start.35 = (bf16[16,2176]{1,0:T(8,128)(2,1)S(1)}, bf16[16,2176]{1,0:T(8,128)(2,1)S(1)}, u32[]{:S(2)}, u32[]{:S(2)}) collective-permute-start(bf16[16,2176]{1,0:T(8,128)(2,1)S(1)} %get-tuple-element.298), channel_id=1, source_target_pairs={{0,2},{1,3},{2,0},{3,1},{4,6},{5,7},{6,4},{7,5},{8,10},{9,11},{10,... | collective-permute-start | bytes 208904 | tf_op jit(solution)/shard_map/ppermute | solution.py:675
  163.6 5.3 %collective-permute-start.34 = (bf16[16,2176]{1,0:T(8,128)(2,1)S(1)}, bf16[16,2176]{1,0:T(8,128)(2,1)S(1)}, u32[]{:S(2)}, u32[]{:S(2)}) collective-permute-start(bf16[16,2176]{1,0:T(8,128)(2,1)S(1)} %get-tuple-element.299), channel_id=1, source_target_pairs={{0,1},{1,0},{2,3},{3,2},{4,5},{5,4},{6,7},{7,6},{8,9},{9,8},{10,11... | collective-permute-start | bytes 208904 | tf_op jit(solution)/shard_map/ppermute | solution.py:675
  164.9 7.6 %collective-permute-start.42 = (bf16[16,4864]{1,0:T(8,128)(2,1)S(1)}, bf16[16,4864]{1,0:T(8,128)(2,1)S(1)}, u32[]{:S(2)}, u32[]{:S(2)}) collective-permute-start(bf16[16,4864]{1,0:T(8,128)(2,1)S(1)} %get-tuple-element.314), channel_id=1, source_target_pairs={{0,16},{4,20},{8,24},{12,28},{16,0},{20,4},{24,8},{28,12},{1,17},{... | collective-permute-start | bytes 466952 | tf_op jit(solution)/shard_map/ppermute | solution.py:675
  168.9 5.9 %collective-permute-start.40 = (bf16[16,2176]{1,0:T(8,128)(2,1)S(1)}, bf16[16,2176]{1,0:T(8,128)(2,1)S(1)}, u32[]{:S(2)}, u32[]{:S(2)}) collective-permute-start(bf16[16,2176]{1,0:T(8,128)(2,1)S(1)} %add_convert_fusion.23), channel_id=1, source_target_pairs={{0,24},{4,28},{8,16},{12,20},{16,8},{20,12},{24,0},{28,4},{1,25},{... | collective-permute-start | bytes 208904 | tf_op jit(solution)/shard_map/ppermute | solution.py:675
  170.4 4.8 %collective-permute-start.39 = (bf16[16,2176]{1,0:T(8,128)(2,1)S(1)}, bf16[16,2176]{1,0:T(8,128)(2,1)S(1)}, u32[]{:S(2)}, u32[]{:S(2)}) collective-permute-start(bf16[16,2176]{1,0:T(8,128)(2,1)S(1)} %add_convert_fusion.23), channel_id=1, source_target_pairs={{0,16},{4,20},{8,24},{12,28},{16,0},{20,4},{24,8},{28,12},{1,17},{... | collective-permute-start | bytes 208904 | tf_op jit(solution)/shard_map/ppermute | solution.py:675
  171.0 5.1 %collective-permute-start.38 = (bf16[16,2176]{1,0:T(8,128)(2,1)S(1)}, bf16[16,2176]{1,0:T(8,128)(2,1)S(1)}, u32[]{:S(2)}, u32[]{:S(2)}) collective-permute-start(bf16[16,2176]{1,0:T(8,128)(2,1)S(1)} %add_convert_fusion.23), channel_id=1, source_target_pairs={{0,8},{4,12},{8,0},{12,4},{16,24},{20,28},{24,16},{28,20},{1,9},{5... | collective-permute-start | bytes 208904 | tf_op jit(solution)/shard_map/ppermute | solution.py:675
  172.5 8.3 %collective-permute-start.43 = (bf16[2,16,4864]{2,1,0:T(8,128)(2,1)S(1)}, bf16[2,16,4864]{2,1,0:T(8,128)(2,1)S(1)}, u32[]{:S(2)}, u32[]{:S(2)}) collective-permute-start(bf16[2,16,4864]{2,1,0:T(8,128)(2,1)S(1)} %get-tuple-element.310), channel_id=1, source_target_pairs={{0,8},{4,12},{8,0},{12,4},{16,24},{20,28},{24,16},{28,20},{1,9},{5... | collective-permute-start | bytes 933896 | tf_op jit(solution)/shard_map/ppermute | solution.py:675
  176.1 1.6 collective-permute-start.41
  180.9 2.1 %collective-permute-start.44 = (bf16[4,16,4864]{2,1,0:T(8,128)(2,1)S(1)}, bf16[4,16,4864]{2,1,0:T(8,128)(2,1)S(1)}, u32[]{:S(2)}, u32[]{:S(2)}) collective-permute-start(bf16[4,16,4864]{2,1,0:T(8,128)(2,1)S(1)} %bitcast.102), channel_id=1, source_target_pairs={{0,4},{4,0},{8,12},{12,8},{16,20},{20,16},{24,28},{28,24},{1,5},{5... | collective-permute-start | bytes 1867784 | tf_op jit(solution)/shard_map/ppermute | solution.py:675
  (12 other events, 45.5 us)

commit v5 on v4

--- a/solution.py
+++ b/solution.py
@@ -13,6 +13,7 @@
 SEQ_LEN = 1024
 CHUNK = 256
 SUB = 128
+SUBS = CHUNK // SUB
 ROWS = 512
 HALF = 256
 PIECE = 16
@@ -224,11 +225,11 @@
     inverse = 1.0 / total
     float_o[:, HALF : 2 * HALF] = inverse
     tri, block, ones = causal_pair(), same_head(), head_ones()
-    places = sub_places((0, 1))
+    places = sub_places(range(SUBS))
     lows, wide_e, numers, ratios = {}, {}, {}, {}
     for pair in range(2):
         current = state[pair]
-        for sub in range(2):
+        for sub in range(SUBS):
             rows, at = slice(SUB * sub, SUB * sub + SUB), slice(128 * pair, 128 * pair + 128)
             lows[sub, pair] = current.astype(BF16)
             kept[sub, pair] = lows[sub, pair]
@@ -333,8 +334,9 @@
     logits = nn(out, w_read[...])
     expd = jnp.exp(logits - jnp.max(logits, axis=-1, keepdims=True))
     soft = expd / jnp.sum(expd, axis=-1, keepdims=True)
-    classes = lax.broadcasted_iota(jnp.int32, (ROWS, VOCAB), 1)
-    dl = (soft - jnp.where(classes == target[...], 1.0, 0.0)).astype(BF16)
+    classes = lax.broadcasted_iota(jnp.int32, (VOCAB, ROWS), 0)
+    hits = jnp.where(classes == target[rows].reshape(1, ROWS), 1.0, 0.0).T
+    dl = (soft - hits).astype(BF16)
     dl_s[rows, :] = dl
     dy = nt(dl, w_read[...])
     dy_s[rows, :] = dy
@@ -548,7 +550,7 @@
         return ref[rows, j * HALF + 128 * pair : j * HALF + 128 * pair + 128]
 
     tri, trt, block, ones = causal_pair(), causal_pair(True), same_head(), head_ones()
-    places = sub_places((1, 0))
+    places = sub_places(reversed(range(SUBS)))
     d_mixes, wide, d_numers, d_totals, others = {}, {}, {}, {}, {}
     for sub, pair, rows, at in places:
         v = take(proj, 2, rows, pair)
@@ -569,7 +571,7 @@
         mixing = masked(trt, nt(e, wide_r))
         d_mix_t = masked(trt, nt(v, wide_do))
         others[sub, pair] = (scores, d_mix_t, nn(mixing, wide_do), wide_q, wide_r)
-    d_total = jnp.concatenate([side(d_totals[sub, 0], d_totals[sub, 1]) for sub in range(2)], axis=0)
+    d_total = jnp.concatenate([side(d_totals[sub, 0], d_totals[sub, 1]) for sub in range(SUBS)], axis=0)
     total_z = nn(causal_whole(True), d_total) + count_z[...]
     count_z[...] = total_z[:1, :]
     currents = [state[0], state[1]]
@@ -638,7 +640,7 @@
     return jax.ShapeDtypeStruct(shape, dtype)
 
 
-def call(kernel, name, args, outs, steps=None, scratch=(), flops=0, limit=56):
+def call(kernel, name, args, outs, steps=None, scratch=(), flops=0, limit=44):
     grid = (steps,) if steps else ()
 
     def spec(shape, block):
@@ -770,6 +772,7 @@
             [(idx, None)] + [(v, None) for v in vectors] + [(w, "hbm") for w in weights],
             [(size, BF16, None) for size in sizes],
             scratch=[pltpu.SemaphoreType.DMA((20,))],
+            limit=56,
         )
         got_a = near_rows(pa, shards)
         pair_u = near_pair(pu, shards)
@@ -788,10 +791,7 @@
                 ((2 * WIDTH + PIECE, count), BF16, None),
             ],
         )
-        target = targets.reshape(count, 1)
-        plane_a, got_u, pair_d, a1, both_t, target = pin(
-            plane_a, got_u, pair_d, a1, both_t, target
-        )
+        plane_a, got_u, pair_d, a1, both_t = pin(plane_a, got_u, pair_d, a1, both_t)
         near_a = jnp.stack([rows_a] + plane_a)
         far_a = swap(near_a, "dp", dp, 1)
         got_d = far_pair(pair_d, shards)
@@ -799,7 +799,7 @@
         rows_u = jnp.concatenate([pair_u, got_u])
         plane_u = plane_start([rows_u] * 4, dp)
 
-        kept = ((2, 2, 128, 256), lambda i: (i, 0, 0, 0))
+        kept = ((SUBS, 2, 128, 256), lambda i: (i, 0, 0, 0))
 
         def attend(a1, half):
             at = ((4, 4, PIECE, COLS_PROJ), lambda i: (0, 0, 0, half))
@@ -811,7 +811,7 @@
                     ((count, COLS_PROJ), BF16, tok(COLS_PROJ)),
                     ((count, COLS_PROJ), F32, tok(COLS_PROJ)),
                     ((count, 2 * HALF), BF16, tok(2 * HALF)),
-                    ((2 * steps, 2, 128, 256), BF16, kept),
+                    ((SUBS * steps, 2, 128, 256), BF16, kept),
                     ((WIDTH, COLS_PROJ), BF16, None),
                 ],
                 steps,
@@ -843,7 +843,7 @@
             "feed_forward",
             [
                 (idx, None), (vec, None), (tokens, wide(WIDTH)), (o0, mixed_at), (o1, mixed_at),
-                (target, wide(1)), (near_u, "hbm"), (far_u, "hbm"), (near_d, "hbm"), (far_d, "hbm"),
+                (targets, None), (near_u, "hbm"), (far_u, "hbm"), (near_d, "hbm"), (far_d, "hbm"),
             ],
             [
                 ((count, WIDTH), BF16, "hbm"),
@@ -878,6 +878,7 @@
                 pltpu.SemaphoreType.DMA((places, 4)),
             ],
             flops=8e9,
+            limit=46,
         )
         got_d = swap(send_d, "dp", dp, 1)
 
@@ -915,6 +916,7 @@
                 pltpu.SemaphoreType.DMA((places, 2)),
             ],
             flops=8e9,
+            limit=46,
         )
         got_d, d_mixed, send_u = pin(got_d, d_mixed, send_u)
         got_u = swap(send_u, "dp", dp, 1)
@@ -922,7 +924,7 @@
         sum_d, d_mixed = pin(sum_d, d_mixed)
         got_d = plane_start(sum_d, dp)
 
-        kept_back = ((2, 2, 128, 256), lambda i: (steps - 1 - i, 0, 0, 0))
+        kept_back = ((SUBS, 2, 128, 256), lambda i: (steps - 1 - i, 0, 0, 0))
 
         def attend_back(half, d_mixed, extra=()):
             proj, floats, mixed, states, w = halves[half]
@@ -996,26 +998,18 @@
         got_u = last_start(pair_u, shards)
         total_d = last_sum(pair_d, got_d, dp)
         got_p, _, _ = pin(got_p, pair_u, d_tokens)
-        rows_p = plane_sum(sum_p, got_p)
-        got_p = shard_start(rows_p, shards)
-        got_u, _ = pin(got_u, rows_p)
         total_f = jnp.concatenate([last_sum(pair_u, got_u, dp), total_d], axis=-1)
         along_f = swap(total_f, "dp", dp, 4)
         got_p, _ = pin(got_p, total_f)
+        rows_p = plane_sum(sum_p, got_p)
+        got_p = shard_start(rows_p, shards)
+        along_f, _ = pin(along_f, rows_p)
+        pair_f = jnp.stack([total_f, along_f])
+        up_f = swap(pair_f, "dp", dp, 2)
+        got_p, _ = pin(got_p, pair_f)
         total_p = shard_sum(rows_p, got_p, dp)
         plane_p = plane_start([total_p] * 4, dp)
-        along_f, _ = pin(along_f, total_p)
-        pair_f = jnp.stack([total_f, along_f])
-        up_f = swap(pair_f, "dp", dp, 2)
-        near_p = jnp.stack([total_p] + plane_p)
-        far_p = swap(near_p, "dp", dp, 1)
-        g_query, g_key, g_value, g_control, g1, b1, g2, b2, bd, bu = call(
-            unpack_proj_kernel,
-            "unpack_proj",
-            [(idx, None), (near_p, None), (far_p, None)],
-            [((rows, WIDTH), F32, None)] * 4 + [((128,), F32, None)] * 5 + [((512,), F32, None)],
-        )
-        up_f, _ = pin(up_f, g_query)
+        up_f, _ = pin(up_f, plane_p[0])
         near_f = jnp.stack([pair_f, up_f], axis=1).reshape((4,) + total_f.shape)
         far_f = swap(near_f, "dp", dp, 1)
         g_mix, g_up, g_down, g_read = call(
@@ -1028,6 +1022,15 @@
                 ((4 * rows, WIDTH), F32, None),
                 ((rows, VOCAB), F32, None),
             ],
+        )
+        near_p = jnp.stack([total_p] + plane_p)
+        far_p = swap(near_p, "dp", dp, 1)
+        far_p, g_up = pin(far_p, g_up)
+        g_query, g_key, g_value, g_control, g1, b1, g2, b2, bd, bu = call(
+            unpack_proj_kernel,
+            "unpack_proj",
+            [(idx, None), (near_p, None), (far_p, None)],
+            [((rows, WIDTH), F32, None)] * 4 + [((128,), F32, None)] * 5 + [((512,), F32, None)],
         )
         return (
             out, d_tokens, g1, b1, g_query, g_key, g_value, g_control, g_mix,

time: 187 us -> 175 us (0.936)
  Pallas kernels: 101 us -> 85.3 us
  waiting for transfers between devices: 26.1 us -> 29.8 us
    pallas_call x11, Pallas kernels: 101 us -> 85.3 us  [call(): pl.pallas_call(kernel, grid=grid, in_specs=in_specs, out_specs=[spec(shap...]
    ppermute x45, waiting for transfers between devices: 26.1 us -> 29.8 us  [swap(): return lax.ppermute(value, axis, [(i, i ^ distance) for i in range(size)])]
  transfers between devices with their start and end apart: 45 -> 45, of which waited for: 18 -> 18; matrix products, arithmetic and copies ran while one was open for 3% -> 2% of each run, Pallas kernels for 41% -> 37%
where the time goes in v5:
time: 175 us
  Pallas kernels  85.3 us (49%)
  starting transfers between devices  49.2 us (28%)
  waiting for transfers between devices  29.8 us (17%)
  local copies, waits for them, and re-layouts  4.94 us (3%)
  other arithmetic  3.9 us (2%)
    pallas_call x11, Pallas kernels, call(): pl.pallas_call(kernel, grid=grid, in_specs=in_specs, out_specs=[spec(shap...  85.3 us
    ppermute x45, starting transfers between devices, swap(): return lax.ppermute(value, axis, [(i, i ^ distance) for i in range(size)])  49.2 us
    ppermute x45, waiting for transfers between devices, swap(): return lax.ppermute(value, axis, [(i, i ^ distance) for i in range(size)])  29.8 us
  transfers between devices with their start and end apart: 45, of which 18 were waited for; matrix products, arithmetic and copies ran while one was open for 2% of the time, Pallas kernels for 37%

profile of v5, /device:TPU:0, one launch (start us, length us, event | category | flops | bytes accessed | tf_op | source)
XLA Modules:
  0.0 174.5 jit_solution(13931074040890465757)
XLA Ops:
  1.3 2.7 %pack_weights.1 = (bf16[16,2176]{1,0:T(8,128)(2,1)}, bf16[16,2560]{1,0:T(8,128)(2,1)}, bf16[2,16,2304]{2,1,0:T(8,128)(2,1)}) custom-call(s32[3]{0:T(128)} %pad_add_fusion.idx, bf16[128]{0:T(256)(128)(2,1)} %g1.1, bf16[128]{0:T(256)(128)(2,1)} %b1.1, bf16[128]{0:T(256)(128)(2,1)} %g2.1, bf16[128]{0:T(256)(128)(2,1)} %b2.1, bf16[128]{0:T(256)(128)(2,1)} %bd.1, ...), custom_call_target="tpu_custom_call" | custom-call | flops 1000 | bytes 1000 | tf_op jit(solution)/shard_map/pack_weights/pallas_call | solution.py:660
  4.0 5.1 %collective-permute-start.2 = (bf16[16,2176]{1,0:T(8,128)(2,1)}, bf16[16,2176]{1,0:T(8,128)(2,1)S(1)}, u32[]{:S(2)}, u32[]{:S(2)}) collective-permute-start(bf16[16,2176]{1,0:T(8,128)(2,1)} %get-tuple-element.153), channel_id=1, source_target_pairs={{0,3},{1,2},{2,1},{3,0},{4,7},{5,6},{6,5},{7,4},{8,11},{9,10},{10,... | collective-permute-start | bytes 208904 | tf_op jit(solution)/shard_map/ppermute | solution.py:677
  9.8 1.4 collective-permute-start.3
  12.7 2.7 %collective-permute-done.1 = bf16[16,2176]{1,0:T(8,128)(2,1)S(1)} collective-permute-done((bf16[16,2176]{1,0:T(8,128)(2,1)}, bf16[16,2176]{1,0:T(8,128)(2,1)S(1)}, u32[]{:S(2)}, u32[]{:S(2)}) %collective-permute-start.1) | collective-permute-done | bytes 69664 | tf_op jit(solution)/shard_map/ppermute | solution.py:677
  17.4 1.6 collective-permute-start.8
  19.1 2.4 %collective-permute-start.6 = (bf16[4,16,2048]{2,1,0:T(8,128)(2,1)S(1)}, bf16[4,16,2048]{2,1,0:T(8,128)(2,1)S(1)}, u32[]{:S(2)}, u32[]{:S(2)}) collective-permute-start(bf16[4,16,2048]{2,1,0:T(8,128)(2,1)S(1)} %pad_maximum_fusion.11), channel_id=1, source_target_pairs={{0,24},{4,28},{8,16},{12,20},{16,8},{20,12},{24,0},{28,4},{1,25},{... | collective-permute-start | bytes 786440 | tf_op jit(solution)/shard_map/ppermute | solution.py:677
  22.5 1.9 %collective-permute-start.7 = (bf16[2,16,2560]{2,1,0:T(8,128)(2,1)S(1)}, bf16[2,16,2560]{2,1,0:T(8,128)(2,1)S(1)}, u32[]{:S(2)}, u32[]{:S(2)}) collective-permute-start(bf16[2,16,2560]{2,1,0:T(8,128)(2,1)S(1)} %pad_maximum_fusion.12), channel_id=1, source_target_pairs={{0,2},{1,3},{2,0},{3,1},{4,6},{5,7},{6,4},{7,5},{8,10},{9,11},{10,... | collective-permute-start | bytes 491528 | tf_op jit(solution)/shard_map/ppermute | solution.py:677
  24.5 1.8 %first_norm.1 = (bf16[1024,512]{1,0:T(8,128)(2,1)S(1)}, bf16[1040,1024]{1,0:T(8,128)(2,1)S(1)}) custom-call(s32[3]{0:T(128)S(1)} %copy-done.11, bf16[4,16,128]{2,1,0:T(8,128)(2,1)S(1)} %pad_maximum_fusion.14.vec, bf16[1024,512]{1,0:T(8,128)(2,1)S(1)} %copy-done), custom_call_target="tpu_custom_call" | custom-call | flops 1000 | bytes 1000 | tf_op jit(solution)/shard_map/first_norm/pallas_call | solution.py:660
  26.4 4.6 %collective-permute-done.7 = bf16[2,16,2560]{2,1,0:T(8,128)(2,1)S(1)} collective-permute-done((bf16[2,16,2560]{2,1,0:T(8,128)(2,1)S(1)}, bf16[2,16,2560]{2,1,0:T(8,128)(2,1)S(1)}, u32[]{:S(2)}, u32[]{:S(2)}) %collective-permute-start.7) | collective-permute-done | bytes 163872 | tf_op jit(solution)/shard_map/ppermute | solution.py:677
  30.9 1.6 collective-permute-done.5
  32.9 1.7 collective-permute-start.12
  34.6 1.3 collective-permute-start.11
  36.4 2.4 %collective-permute-start.13 = (bf16[2,2,16,2304]{3,2,0,1:T(8,128)(2,1)S(1)}, bf16[2,2,16,2304]{3,2,0,1:T(8,128)(2,1)S(1)}, u32[]{:S(2)}, u32[]{:S(2)}) collective-permute-start(bf16[2,2,16,2304]{3,2,0,1:T(8,128)(2,1)S(1)} %pad_maximum_fusion.5), channel_id=1, source_target_pairs={{0,2},{1,3},{2,0},{3,1},{4,6},{5,7},{6,4},{7,5},{8,10},{9,11},{10,... | collective-permute-start | bytes 884744 | tf_op jit(solution)/shard_map/ppermute | solution.py:677
  38.8 8.6 %attend.2 = (bf16[1024,1024]{1,0:T(8,128)(2,1)S(1)}, f32[1024,1024]{1,0:T(8,128)}, bf16[1024,512]{1,0:T(8,128)(2,1)S(1)}, bf16[8,2,128,256]{3,2,1,0:T(8,128)(2,1)S(1)}, bf16[512,1024]{1,0:T(8,128)(2,1)S(1)}) custom-call(s32[3]{0:T(128)S(1)} %copy-done.11, bf16[1024,512]{1,0:T(8,128)(2,1)S(1)} %get-tuple-element.176.a1, ...), custom_call_target="tpu_custom_call" | custom-call | flops 1000 | bytes 1000 | tf_op jit(solution)/shard_map/attend/pallas_call | solution.py:660
  47.4 4.8 %collective-permute-done.13 = bf16[2,2,16,2304]{3,2,0,1:T(8,128)(2,1)S(1)} collective-permute-done((bf16[2,2,16,2304]{3,2,0,1:T(8,128)(2,1)S(1)}, bf16[2,2,16,2304]{3,2,0,1:T(8,128)(2,1)S(1)}, u32[]{:S(2)}, u32[]{:S(2)}) %collective-permute-start.13) | collective-permute-done | bytes 294944 | tf_op jit(solution)/shard_map/ppermute | solution.py:677
  52.6 1.5 collective-permute-start.16
  54.9 8.3 %attend.3 = (bf16[1024,1024]{1,0:T(8,128)(2,1)S(1)}, f32[1024,1024]{1,0:T(8,128)}, bf16[1024,512]{1,0:T(8,128)(2,1)S(1)}, bf16[8,2,128,256]{3,2,1,0:T(8,128)(2,1)S(1)}, bf16[512,1024]{1,0:T(8,128)(2,1)S(1)}) custom-call(s32[3]{0:T(128)S(1)} %copy-done.11, bf16[1024,512]{1,0:T(8,128)(2,1)S(1)} %get-tuple-element.176.a1, ...), custom_call_target="tpu_custom_call" | custom-call | flops 1000 | bytes 1000 | tf_op jit(solution)/shard_map/attend/pallas_call | solution.py:660
  63.2 1.3 copy-done.5
  64.8 2.8 %collective-permute-done.17.down_far_i = bf16[4,4,16,2304]{3,2,1,0:T(8,128)(2,1)S(1)} collective-permute-done((bf16[4,4,16,2304]{3,2,1,0:T(8,128)(2,1)S(1)}, bf16[4,4,16,2304]{3,2,1,0:T(8,128)(2,1)S(1)}, u32[]{:S(2)}, u32[]{:S(2)}) %collective-permute-start.17) | collective-permute-done | bytes 1179680 | tf_op jit(solution)/shard_map/ppermute | solution.py:677
  67.6 1.0 copy-done.15
  68.6 16.2 %feed_forward.1 = (bf16[1024,512]{1,0:T(8,128)(2,1)}, f32[1024,512]{1,0:T(8,128)}, bf16[1024,2048]{1,0:T(8,128)(2,1)}, f32[1024,512]{1,0:T(8,128)}, f32[1,512]{1...) custom-call(s32[3]{0:T(128)S(1)} %copy-done.11, ...), custom_call_target="tpu_custom_call" | custom-call | flops 1000 | bytes 1000 | tf_op jit(solution)/shard_map/feed_forward/pallas_call | solution.py:660
  85.1 13.0 %feed_backward.1 = (f32[1024,512]{1,0:T(8,128)}, bf16[1024,512]{1,0:T(8,128)(2,1)S(1)}, f32[1,512]{1,0:T(1,128)S(1)}, f32[1,512]{1,0:T(1,128)S(1)}, f32[1,2048]{...) custom-call(s32[3]{0:T(128)S(1)} %copy-done.11, ...), custom_call_target="tpu_custom_call" | custom-call | flops 1000 | bytes 1000 | tf_op jit(solution)/shard_map/feed_backward/pallas_call | solution.py:660
  98.7 1.3 collective-permute-start.19
  100.6 1.7 collective-permute-start.21
  102.3 12.8 %attend_backward.2 = (bf16[1024,1024]{1,0:T(8,128)(2,1)S(1)}, bf16[4,4,16,1024]{3,2,1,0:T(8,128)(2,1)S(1)}, bf16[4,4,16,1024]{3,2,1,0:T(8,128)(2,1)S(1)}, f32[8,512]{1,0:T(8,128)S(1)}) custom-call(s32[3]{0:T(128)S(1)} %copy-done.11, bf16[1040,1024]{1,0:T(8,128)(2,1)} %copy-done.1, bf16[512,1024]{1,0:T(8,128)(2,1)S(1)} %get-tuple-element.209.w.w0, ...), custom_call_target="tpu_custom_call" | custom-call | flops 1000 | bytes 1000 | tf_op jit(solution)/shard_map/attend_backward/pallas_call | solution.py:660
  116.7 1.3 collective-permute-start.24
  118.5 1.7 collective-permute-start.26
  120.2 1.1 collective-permute-start.23
  121.3 12.9 %attend_backward.3 = (bf16[1024,1024]{1,0:T(8,128)(2,1)S(1)}, bf16[4,4,16,1152]{3,2,1,0:T(8,128)(2,1)S(1)}, bf16[4,4,16,1152]{3,2,1,0:T(8,128)(2,1)S(1)}) custom-call(s32[3]{0:T(128)S(1)} %copy-done.11, bf16[1040,1024]{1,0:T(8,128)(2,1)} %copy-done.1, bf16[512,1024]{1,0:T(8,128)(2,1)S(1)} %get-tuple-element.227.w.w1, bf16[1024,1024]{1,0:T(8,128)(2,1)S(1)} %copy-done.6, ...), custom_call_target="tpu_custom_call" | custom-call | flops 1000 | bytes 1000 | tf_op jit(solution)/shard_map/attend_backward/pallas_call | solution.py:660
  134.6 1.8 %collective-permute-done.28 = bf16[4,4,16,1152]{3,2,1,0:T(8,128)(2,1)S(1)} collective-permute-done((bf16[4,4,16,1152]{3,2,1,0:T(8,128)(2,1)S(1)}, bf16[4,4,16,1152]{3,2,1,0:T(8,128)(2,1)S(1)}, u32[]{:S(2)}, u32[]{:S(2)}) %collective-permute-start.28) | collective-permute-done | bytes 589856 | tf_op jit(solution)/shard_map/ppermute | solution.py:677
  136.9 1.9 %collective-permute-start.29 = (bf16[2,16,2560]{2,1,0:T(8,128)(2,1)S(1)}, bf16[2,16,2560]{2,1,0:T(8,128)(2,1)S(1)}, u32[]{:S(2)}, u32[]{:S(2)}) collective-permute-start(bf16[2,16,2560]{2,1,0:T(8,128)(2,1)S(1)} %slice.295), channel_id=1, source_target_pairs={{0,2},{1,3},{2,0},{3,1},{4,6},{5,7},{6,4},{7,5},{8,10},{9,11},{10,... | collective-permute-start | bytes 491528 | tf_op jit(solution)/shard_map/ppermute | solution.py:677
  140.2 1.3 collective-permute-start.32
  141.5 1.4 collective-permute-start.33
  142.9 5.0 %input_gradient.1 = f32[1024,512]{1,0:T(8,128)} custom-call(s32[3]{0:T(128)S(1)} %copy-done.11, bf16[4,16,128]{2,1,0:T(8,128)(2,1)S(1)} %pad_maximum_fusion.14.vec, bf16[1024,512]{1,0:T(8,128)(2,1)S(1)} %copy-done, f32[1024,512]{1,0:T(8,128)S(1)} %copy-done.2, bf16[1024,1024]{1,0:T(8,128)(2,1)S(1)} %copy-done.4, ...), custom_call_target="tpu_custom_call" | custom-call | flops 1000 | bytes 1000 | tf_op jit(solution)/shard_map/input_gradient/pallas_call | solution.py:660
  147.9 1.5 collective-permute-start.34
  149.5 2.9 %collective-permute-done.34 = bf16[16,2560]{1,0:T(8,128)(2,1)S(1)} collective-permute-done((bf16[16,2560]{1,0:T(8,128)(2,1)S(1)}, bf16[16,2560]{1,0:T(8,128)(2,1)S(1)}, u32[]{:S(2)}, u32[]{:S(2)}) %collective-permute-start.34) | collective-permute-done | bytes 81952 | tf_op jit(solution)/shard_map/ppermute | solution.py:677
  152.5 1.1 collective-permute-start.38
  154.4 2.3 %collective-permute-start.37 = (bf16[16,2176]{1,0:T(8,128)(2,1)S(1)}, bf16[16,2176]{1,0:T(8,128)(2,1)S(1)}, u32[]{:S(2)}, u32[]{:S(2)}) collective-permute-start(bf16[16,2176]{1,0:T(8,128)(2,1)S(1)} %get-tuple-element.305), channel_id=1, source_target_pairs={{0,3},{1,2},{2,1},{3,0},{4,7},{5,6},{6,5},{7,4},{8,11},{9,10},{10,... | collective-permute-start | bytes 208904 | tf_op jit(solution)/shard_map/ppermute | solution.py:677
  157.6 1.3 collective-permute-start.35
  158.9 1.0 collective-permute-start.43
  160.0 1.2 collective-permute-done.37
  161.2 1.7 collective-permute-done.36
  162.9 1.0 collective-permute-start.39
  163.9 1.3 collective-permute-start.41
  165.1 1.3 collective-permute-start.40
  166.5 1.9 %collective-permute-done.39 = bf16[16,2176]{1,0:T(8,128)(2,1)S(1)} collective-permute-done((bf16[16,2176]{1,0:T(8,128)(2,1)S(1)}, bf16[16,2176]{1,0:T(8,128)(2,1)S(1)}, u32[]{:S(2)}, u32[]{:S(2)}) %collective-permute-start.39) | collective-permute-done | bytes 69664 | tf_op jit(solution)/shard_map/ppermute | solution.py:677
  170.6 2.1 %unpack_feed.1 = (f32[128,512]{1,0:T(8,128)}, f32[128,2048]{1,0:T(8,128)}, f32[512,512]{1,0:T(8,128)}, f32[128,256]{1,0:T(8,128)}) custom-call(s32[3]{0:T(128)S(1)} %copy-done.11, bf16[4,16,4864]{2,1,0:T(8,128)(2,1)S(1)} %bitcast.103, bf16[4,16,4864]{2,1,0:T(8,128)(2,1)S(1)} %collective-permute-done.44.far), custom_call_target="tpu_custom_call" | custom-call | flops 1000 | bytes 1000 | tf_op jit(solution)/shard_map/unpack_feed/pallas_call | solution.py:660
  172.8 1.6 unpack_proj.1
  (129 shorter events, 18.0 us)
Async XLA Ops:
  1.3 23.2 %copy-start = (bf16[1024,512]{1,0:T(8,128)(2,1)S(1)}, bf16[1024,512]{1,0:T(8,128)(2,1)}, u32[]{:S(2)}) copy-start(bf16[1024,512]{1,0:T(8,128)(2,1)} %x.4) | copy-start | bytes 3145732
  1.3 23.2 %copy-start.11 = (s32[3]{0:T(128)S(1)}, s32[3]{0:T(128)}, u32[]{:S(2)}) copy-start(s32[3]{0:T(128)} %pad_add_fusion.idx) | copy-start | bytes 40
  4.0 8.7 %collective-permute-start.2 = (bf16[16,2176]{1,0:T(8,128)(2,1)}, bf16[16,2176]{1,0:T(8,128)(2,1)S(1)}, u32[]{:S(2)}, u32[]{:S(2)}) collective-permute-start(bf16[16,2176]{1,0:T(8,128)(2,1)} %get-tuple-element.153), channel_id=1, source_target_pairs={{0,3},{1,2},{2,1},{3,0},{4,7},{5,6},{6,5},{7,4},{8,11},{9,10},{10,... | collective-permute-start | bytes 208904 | tf_op jit(solution)/shard_map/ppermute | solution.py:677
  9.2 6.2 %collective-permute-start.1 = (bf16[16,2176]{1,0:T(8,128)(2,1)}, bf16[16,2176]{1,0:T(8,128)(2,1)S(1)}, u32[]{:S(2)}, u32[]{:S(2)}) collective-permute-start(bf16[16,2176]{1,0:T(8,128)(2,1)} %get-tuple-element.153), channel_id=1, source_target_pairs={{0,2},{1,3},{2,0},{3,1},{4,6},{5,7},{6,4},{7,5},{8,10},{9,11},{10,... | collective-permute-start | bytes 208904 | tf_op jit(solution)/shard_map/ppermute | solution.py:677
  9.2 6.5 %collective-permute-start = (bf16[16,2176]{1,0:T(8,128)(2,1)}, bf16[16,2176]{1,0:T(8,128)(2,1)S(1)}, u32[]{:S(2)}, u32[]{:S(2)}) collective-permute-start(bf16[16,2176]{1,0:T(8,128)(2,1)} %get-tuple-element.153), channel_id=1, source_target_pairs={{0,1},{1,0},{2,3},{3,2},{4,5},{5,4},{6,7},{7,6},{8,9},{9,8},{10,11... | collective-permute-start | bytes 208904 | tf_op jit(solution)/shard_map/ppermute | solution.py:677
  9.8 6.7 %collective-permute-start.3 = (bf16[16,2560]{1,0:T(8,128)(2,1)}, bf16[16,2560]{1,0:T(8,128)(2,1)S(1)}, u32[]{:S(2)}, u32[]{:S(2)}) collective-permute-start(bf16[16,2560]{1,0:T(8,128)(2,1)} %get-tuple-element.154), channel_id=1, source_target_pairs={{0,1},{1,0},{2,3},{3,2},{4,5},{5,4},{6,7},{7,6},{8,9},{9,8},{10,11... | collective-permute-start | bytes 245768 | tf_op jit(solution)/shard_map/ppermute | solution.py:677
  17.4 8.9 %collective-permute-start.8 = (bf16[2,16,2304]{2,1,0:T(8,128)(2,1)S(1)}, bf16[2,16,2304]{2,1,0:T(8,128)(2,1)S(1)}, u32[]{:S(2)}, u32[]{:S(2)}) collective-permute-start(bf16[2,16,2304]{2,1,0:T(8,128)(2,1)S(1)} %copy-done.16), channel_id=1, source_target_pairs={{0,1},{1,0},{2,3},{3,2},{4,5},{5,4},{6,7},{7,6},{8,9},{9,8},{10,11... | collective-permute-start | bytes 442376 | tf_op jit(solution)/shard_map/ppermute | solution.py:677
  19.1 11.9 %collective-permute-start.6 = (bf16[4,16,2048]{2,1,0:T(8,128)(2,1)S(1)}, bf16[4,16,2048]{2,1,0:T(8,128)(2,1)S(1)}, u32[]{:S(2)}, u32[]{:S(2)}) collective-permute-start(bf16[4,16,2048]{2,1,0:T(8,128)(2,1)S(1)} %pad_maximum_fusion.11), channel_id=1, source_target_pairs={{0,24},{4,28},{8,16},{12,20},{16,8},{20,12},{24,0},{28,4},{1,25},{... | collective-permute-start | bytes 786440 | tf_op jit(solution)/shard_map/ppermute | solution.py:677
  21.5 11.0 %collective-permute-start.5 = (bf16[4,16,2048]{2,1,0:T(8,128)(2,1)S(1)}, bf16[4,16,2048]{2,1,0:T(8,128)(2,1)S(1)}, u32[]{:S(2)}, u32[]{:S(2)}) collective-permute-start(bf16[4,16,2048]{2,1,0:T(8,128)(2,1)S(1)} %pad_maximum_fusion.11), channel_id=1, source_target_pairs={{0,16},{4,20},{8,24},{12,28},{16,0},{20,4},{24,8},{28,12},{1,17},{... | collective-permute-start | bytes 786440 | tf_op jit(solution)/shard_map/ppermute | solution.py:677
  22.0 10.6 %collective-permute-start.4 = (bf16[4,16,2048]{2,1,0:T(8,128)(2,1)S(1)}, bf16[4,16,2048]{2,1,0:T(8,128)(2,1)S(1)}, u32[]{:S(2)}, u32[]{:S(2)}) collective-permute-start(bf16[4,16,2048]{2,1,0:T(8,128)(2,1)S(1)} %pad_maximum_fusion.11), channel_id=1, source_target_pairs={{0,8},{4,12},{8,0},{12,4},{16,24},{20,28},{24,16},{28,20},{1,9},{5... | collective-permute-start | bytes 786440 | tf_op jit(solution)/shard_map/ppermute | solution.py:677
  22.5 8.4 %collective-permute-start.7 = (bf16[2,16,2560]{2,1,0:T(8,128)(2,1)S(1)}, bf16[2,16,2560]{2,1,0:T(8,128)(2,1)S(1)}, u32[]{:S(2)}, u32[]{:S(2)}) collective-permute-start(bf16[2,16,2560]{2,1,0:T(8,128)(2,1)S(1)} %pad_maximum_fusion.12), channel_id=1, source_target_pairs={{0,2},{1,3},{2,0},{3,1},{4,6},{5,7},{6,4},{7,5},{8,10},{9,11},{10,... | collective-permute-start | bytes 491528 | tf_op jit(solution)/shard_map/ppermute | solution.py:677
  32.8 6.1 %collective-permute-start.9 = (bf16[4,4,16,2048]{3,2,1,0:T(8,128)(2,1)S(1)}, bf16[4,4,16,2048]{3,2,1,0:T(8,128)(2,1)S(1)}, u32[]{:S(2)}, u32[]{:S(2)}) collective-permute-start(bf16[4,4,16,2048]{3,2,1,0:T(8,128)(2,1)S(1)} %pad_maximum_fusion.2.near), channel_id=1, source_target_pairs={{0,4},{4,0},{8,12},{12,8},{16,20},{20,16},{24,28},{28,24},{1,5},{5... | collective-permute-start | bytes 3145736 | tf_op jit(solution)/shard_map/ppermute | solution.py:677
  32.9 19.3 %collective-permute-start.12 = (bf16[4,16,2560]{2,1,0:T(8,128)(2,1)S(1)}, bf16[4,16,2560]{2,1,0:T(8,128)(2,1)S(1)}, u32[]{:S(2)}, u32[]{:S(2)}) collective-permute-start(bf16[4,16,2560]{2,1,0:T(8,128)(2,1)S(1)} %constant_dynamic-update-slice_fusion), channel_id=1, source_target_pairs={{0,24},{4,28},{8,16},{12,20},{16,8},{20,12},{24,0},{28,4},{1,25},{... | collective-permute-start | bytes 983048 | tf_op jit(solution)/shard_map/ppermute | solution.py:677
  34.6 17.6 %collective-permute-start.11 = (bf16[4,16,2560]{2,1,0:T(8,128)(2,1)S(1)}, bf16[4,16,2560]{2,1,0:T(8,128)(2,1)S(1)}, u32[]{:S(2)}, u32[]{:S(2)}) collective-permute-start(bf16[4,16,2560]{2,1,0:T(8,128)(2,1)S(1)} %constant_dynamic-update-slice_fusion), channel_id=1, source_target_pairs={{0,16},{4,20},{8,24},{12,28},{16,0},{20,4},{24,8},{28,12},{1,17},{... | collective-permute-start | bytes 983048 | tf_op jit(solution)/shard_map/ppermute | solution.py:677
  35.9 16.3 %collective-permute-start.10 = (bf16[4,16,2560]{2,1,0:T(8,128)(2,1)S(1)}, bf16[4,16,2560]{2,1,0:T(8,128)(2,1)S(1)}, u32[]{:S(2)}, u32[]{:S(2)}) collective-permute-start(bf16[4,16,2560]{2,1,0:T(8,128)(2,1)S(1)} %constant_dynamic-update-slice_fusion), channel_id=1, source_target_pairs={{0,8},{4,12},{8,0},{12,4},{16,24},{20,28},{24,16},{28,20},{1,9},{5... | collective-permute-start | bytes 983048 | tf_op jit(solution)/shard_map/ppermute | solution.py:677
  36.4 15.8 %collective-permute-start.13 = (bf16[2,2,16,2304]{3,2,0,1:T(8,128)(2,1)S(1)}, bf16[2,2,16,2304]{3,2,0,1:T(8,128)(2,1)S(1)}, u32[]{:S(2)}, u32[]{:S(2)}) collective-permute-start(bf16[2,2,16,2304]{3,2,0,1:T(8,128)(2,1)S(1)} %pad_maximum_fusion.5), channel_id=1, source_target_pairs={{0,2},{1,3},{2,0},{3,1},{4,6},{5,7},{6,4},{7,5},{8,10},{9,11},{10,... | collective-permute-start | bytes 884744 | tf_op jit(solution)/shard_map/ppermute | solution.py:677
  52.4 12.1 %collective-permute-start.14 = (bf16[4,4,16,2560]{3,2,1,0:T(8,128)(2,1)S(1)}, bf16[4,4,16,2560]{3,2,1,0:T(8,128)(2,1)S(1)}, u32[]{:S(2)}, u32[]{:S(2)}) collective-permute-start(bf16[4,4,16,2560]{3,2,1,0:T(8,128)(2,1)S(1)} %pad_maximum_fusion.up_near_i), channel_id=1, source_target_pairs={{0,4},{4,0},{8,12},{12,8},{16,20},{20,16},{24,28},{28,24},{1,5},{5... | collective-permute-start | bytes 3932168 | tf_op jit(solution)/shard_map/ppermute | solution.py:677
  52.6 11.9 %collective-permute-start.16 = (bf16[4,16,2304]{2,1,0:T(8,128)(2,1)S(1)}, bf16[4,16,2304]{2,1,0:T(8,128)(2,1)S(1)}, u32[]{:S(2)}, u32[]{:S(2)}) collective-permute-start(bf16[4,16,2304]{2,1,0:T(8,128)(2,1)S(1)} %get-tuple-element.314), channel_id=1, source_target_pairs={{0,16},{4,20},{8,24},{12,28},{16,0},{20,4},{24,8},{28,12},{1,17},{... | collective-permute-start | bytes 884744 | tf_op jit(solution)/shard_map/ppermute | solution.py:677
  54.1 10.4 %collective-permute-start.15 = (bf16[4,16,2304]{2,1,0:T(8,128)(2,1)S(1)}, bf16[4,16,2304]{2,1,0:T(8,128)(2,1)S(1)}, u32[]{:S(2)}, u32[]{:S(2)}) collective-permute-start(bf16[4,16,2304]{2,1,0:T(8,128)(2,1)S(1)} %get-tuple-element.314), channel_id=1, source_target_pairs={{0,8},{4,12},{8,0},{12,4},{16,24},{20,28},{24,16},{28,20},{1,9},{5... | collective-permute-start | bytes 884744 | tf_op jit(solution)/shard_map/ppermute | solution.py:677
  64.5 20.4 %copy-start.7 = (bf16[8,2,128,256]{3,2,1,0:T(8,128)(2,1)}, bf16[8,2,128,256]{3,2,1,0:T(8,128)(2,1)S(1)}, u32[]{:S(2)}) copy-start(bf16[8,2,128,256]{3,2,1,0:T(8,128)(2,1)S(1)} %get-tuple-element.231.kept) | copy-start | bytes 3145732
  64.7 2.9 %collective-permute-start.17 = (bf16[4,4,16,2304]{3,2,1,0:T(8,128)(2,1)S(1)}, bf16[4,4,16,2304]{3,2,1,0:T(8,128)(2,1)S(1)}, u32[]{:S(2)}, u32[]{:S(2)}) collective-permute-start(bf16[4,4,16,2304]{3,2,1,0:T(8,128)(2,1)S(1)} %pad_maximum_fusion.1.down_near_i), channel_id=1, source_target_pairs={{0,4},{4,0},{8,12},{12,8},{16,20},{20,16},{24,28},{28,24},{1,5},{5... | collective-permute-start | bytes 3538952 | tf_op jit(solution)/shard_map/ppermute | solution.py:677
  84.9 13.2 %collective-permute-start.18 = (bf16[4,4,16,2304]{3,2,1,0:T(8,128)(2,1)S(1)}, bf16[4,4,16,2304]{3,2,1,0:T(8,128)(2,1)S(1)}, u32[]{:S(2)}, u32[]{:S(2)}) collective-permute-start(bf16[4,4,16,2304]{3,2,1,0:T(8,128)(2,1)S(1)} %get-tuple-element.199), channel_id=1, source_target_pairs={{0,4},{4,0},{8,12},{12,8},{16,20},{20,16},{24,28},{28,24},{1,5},{5... | collective-permute-start | bytes 3538952 | tf_op jit(solution)/shard_map/ppermute | solution.py:677
  98.1 17.1 %collective-permute-start.22 = (bf16[4,4,16,2560]{3,2,1,0:T(8,128)(2,1)S(1)}, bf16[4,4,16,2560]{3,2,1,0:T(8,128)(2,1)S(1)}, u32[]{:S(2)}, u32[]{:S(2)}) collective-permute-start(bf16[4,4,16,2560]{3,2,1,0:T(8,128)(2,1)S(1)} %get-tuple-element.207), channel_id=1, source_target_pairs={{0,4},{4,0},{8,12},{12,8},{16,20},{20,16},{24,28},{28,24},{1,5},{5... | collective-permute-start | bytes 3932168 | tf_op jit(solution)/shard_map/ppermute | solution.py:677
  98.7 16.4 %collective-permute-start.19 = (bf16[4,16,2304]{2,1,0:T(8,128)(2,1)S(1)}, bf16[4,16,2304]{2,1,0:T(8,128)(2,1)S(1)}, u32[]{:S(2)}, u32[]{:S(2)}) collective-permute-start(bf16[4,16,2304]{2,1,0:T(8,128)(2,1)S(1)} %get-tuple-element.204), channel_id=1, source_target_pairs={{0,8},{4,12},{8,0},{12,4},{16,24},{20,28},{24,16},{28,20},{1,9},{5... | collective-permute-start | bytes 884744 | tf_op jit(solution)/shard_map/ppermute | solution.py:677
  100.0 15.2 %collective-permute-start.20 = (bf16[4,16,2304]{2,1,0:T(8,128)(2,1)S(1)}, bf16[4,16,2304]{2,1,0:T(8,128)(2,1)S(1)}, u32[]{:S(2)}, u32[]{:S(2)}) collective-permute-start(bf16[4,16,2304]{2,1,0:T(8,128)(2,1)S(1)} %get-tuple-element.205), channel_id=1, source_target_pairs={{0,16},{4,20},{8,24},{12,28},{16,0},{20,4},{24,8},{28,12},{1,17},{... | collective-permute-start | bytes 884744 | tf_op jit(solution)/shard_map/ppermute | solution.py:677
  100.6 14.6 %collective-permute-start.21 = (bf16[4,16,2304]{2,1,0:T(8,128)(2,1)S(1)}, bf16[4,16,2304]{2,1,0:T(8,128)(2,1)S(1)}, u32[]{:S(2)}, u32[]{:S(2)}) collective-permute-start(bf16[4,16,2304]{2,1,0:T(8,128)(2,1)S(1)} %get-tuple-element.206), channel_id=1, source_target_pairs={{0,24},{4,28},{8,16},{12,20},{16,8},{20,12},{24,0},{28,4},{1,25},{... | collective-permute-start | bytes 884744 | tf_op jit(solution)/shard_map/ppermute | solution.py:677
  115.2 19.1 %collective-permute-start.27 = (bf16[4,4,16,1024]{3,2,1,0:T(8,128)(2,1)S(1)}, bf16[4,4,16,1024]{3,2,1,0:T(8,128)(2,1)S(1)}, u32[]{:S(2)}, u32[]{:S(2)}) collective-permute-start(bf16[4,4,16,1024]{3,2,1,0:T(8,128)(2,1)S(1)} %get-tuple-element.226), channel_id=1, source_target_pairs={{0,4},{4,0},{8,12},{12,8},{16,20},{20,16},{24,28},{28,24},{1,5},{5... | collective-permute-start | bytes 1572872 | tf_op jit(solution)/shard_map/ppermute | solution.py:677
  116.7 17.6 %collective-permute-start.24 = (bf16[4,16,2560]{2,1,0:T(8,128)(2,1)S(1)}, bf16[4,16,2560]{2,1,0:T(8,128)(2,1)S(1)}, u32[]{:S(2)}, u32[]{:S(2)}) collective-permute-start(bf16[4,16,2560]{2,1,0:T(8,128)(2,1)S(1)} %get-tuple-element.223), channel_id=1, source_target_pairs={{0,8},{4,12},{8,0},{12,4},{16,24},{20,28},{24,16},{28,20},{1,9},{5... | collective-permute-start | bytes 983048 | tf_op jit(solution)/shard_map/ppermute | solution.py:677
  117.9 16.4 %collective-permute-start.25 = (bf16[4,16,2560]{2,1,0:T(8,128)(2,1)S(1)}, bf16[4,16,2560]{2,1,0:T(8,128)(2,1)S(1)}, u32[]{:S(2)}, u32[]{:S(2)}) collective-permute-start(bf16[4,16,2560]{2,1,0:T(8,128)(2,1)S(1)} %get-tuple-element.224), channel_id=1, source_target_pairs={{0,16},{4,20},{8,24},{12,28},{16,0},{20,4},{24,8},{28,12},{1,17},{... | collective-permute-start | bytes 983048 | tf_op jit(solution)/shard_map/ppermute | solution.py:677
  118.5 15.8 %collective-permute-start.26 = (bf16[4,16,2560]{2,1,0:T(8,128)(2,1)S(1)}, bf16[4,16,2560]{2,1,0:T(8,128)(2,1)S(1)}, u32[]{:S(2)}, u32[]{:S(2)}) collective-permute-start(bf16[4,16,2560]{2,1,0:T(8,128)(2,1)S(1)} %get-tuple-element.225), channel_id=1, source_target_pairs={{0,24},{4,28},{8,16},{12,20},{16,8},{20,12},{24,0},{28,4},{1,25},{... | collective-permute-start | bytes 983048 | tf_op jit(solution)/shard_map/ppermute | solution.py:677
  120.2 14.1 %collective-permute-start.23 = (bf16[2,16,2304]{2,1,0:T(8,128)(2,1)S(1)}, bf16[2,16,2304]{2,1,0:T(8,128)(2,1)S(1)}, u32[]{:S(2)}, u32[]{:S(2)}) collective-permute-start(bf16[2,16,2304]{2,1,0:T(8,128)(2,1)S(1)} %get-tuple-element.222), channel_id=1, source_target_pairs={{0,2},{1,3},{2,0},{3,1},{4,6},{5,7},{6,4},{7,5},{8,10},{9,11},{10,... | collective-permute-start | bytes 442376 | tf_op jit(solution)/shard_map/ppermute | solution.py:677
  134.3 2.1 %collective-permute-start.28 = (bf16[4,4,16,1152]{3,2,1,0:T(8,128)(2,1)S(1)}, bf16[4,4,16,1152]{3,2,1,0:T(8,128)(2,1)S(1)}, u32[]{:S(2)}, u32[]{:S(2)}) collective-permute-start(bf16[4,4,16,1152]{3,2,1,0:T(8,128)(2,1)S(1)} %get-tuple-element.246), channel_id=1, source_target_pairs={{0,4},{4,0},{8,12},{12,8},{16,20},{20,16},{24,28},{28,24},{1,5},{5... | collective-permute-start | bytes 1769480 | tf_op jit(solution)/shard_map/ppermute | solution.py:677
  136.9 11.0 %collective-permute-start.29 = (bf16[2,16,2560]{2,1,0:T(8,128)(2,1)S(1)}, bf16[2,16,2560]{2,1,0:T(8,128)(2,1)S(1)}, u32[]{:S(2)}, u32[]{:S(2)}) collective-permute-start(bf16[2,16,2560]{2,1,0:T(8,128)(2,1)S(1)} %slice.295), channel_id=1, source_target_pairs={{0,2},{1,3},{2,0},{3,1},{4,6},{5,7},{6,4},{7,5},{8,10},{9,11},{10,... | collective-permute-start | bytes 491528 | tf_op jit(solution)/shard_map/ppermute | solution.py:677
  138.8 9.1 %collective-permute-start.30 = (bf16[16,2304]{1,0:T(8,128)(2,1)S(1)}, bf16[16,2304]{1,0:T(8,128)(2,1)S(1)}, u32[]{:S(2)}, u32[]{:S(2)}) collective-permute-start(bf16[16,2304]{1,0:T(8,128)(2,1)S(1)} %fusion.19), channel_id=1, source_target_pairs={{0,1},{1,0},{2,3},{3,2},{4,5},{5,4},{6,7},{7,6},{8,9},{9,8},{10,11... | collective-permute-start | bytes 221192 | tf_op jit(solution)/shard_map/ppermute | solution.py:677
  139.4 14.2 %collective-permute-start.31 = (bf16[4,16,2176]{2,1,0:T(8,128)(2,1)S(1)}, bf16[4,16,2176]{2,1,0:T(8,128)(2,1)S(1)}, u32[]{:S(2)}, u32[]{:S(2)}) collective-permute-start(bf16[4,16,2176]{2,1,0:T(8,128)(2,1)S(1)} %get-tuple-element.249), channel_id=1, source_target_pairs={{0,8},{4,12},{8,0},{12,4},{16,24},{20,28},{24,16},{28,20},{1,9},{5... | collective-permute-start | bytes 835592 | tf_op jit(solution)/shard_map/ppermute | solution.py:677
  140.2 14.1 %collective-permute-start.32 = (bf16[4,16,2176]{2,1,0:T(8,128)(2,1)S(1)}, bf16[4,16,2176]{2,1,0:T(8,128)(2,1)S(1)}, u32[]{:S(2)}, u32[]{:S(2)}) collective-permute-start(bf16[4,16,2176]{2,1,0:T(8,128)(2,1)S(1)} %get-tuple-element.250), channel_id=1, source_target_pairs={{0,16},{4,20},{8,24},{12,28},{16,0},{20,4},{24,8},{28,12},{1,17},{... | collective-permute-start | bytes 835592 | tf_op jit(solution)/shard_map/ppermute | solution.py:677
  141.5 12.8 %collective-permute-start.33 = (bf16[4,16,2176]{2,1,0:T(8,128)(2,1)S(1)}, bf16[4,16,2176]{2,1,0:T(8,128)(2,1)S(1)}, u32[]{:S(2)}, u32[]{:S(2)}) collective-permute-start(bf16[4,16,2176]{2,1,0:T(8,128)(2,1)S(1)} %get-tuple-element.251), channel_id=1, source_target_pairs={{0,24},{4,28},{8,16},{12,20},{16,8},{20,12},{24,0},{28,4},{1,25},{... | collective-permute-start | bytes 835592 | tf_op jit(solution)/shard_map/ppermute | solution.py:677
  147.9 4.5 %collective-permute-start.34 = (bf16[16,2560]{1,0:T(8,128)(2,1)S(1)}, bf16[16,2560]{1,0:T(8,128)(2,1)S(1)}, u32[]{:S(2)}, u32[]{:S(2)}) collective-permute-start(bf16[16,2560]{1,0:T(8,128)(2,1)S(1)} %fusion.18), channel_id=1, source_target_pairs={{0,1},{1,0},{2,3},{3,2},{4,5},{5,4},{6,7},{7,6},{8,9},{9,8},{10,11... | collective-permute-start | bytes 245768 | tf_op jit(solution)/shard_map/ppermute | solution.py:677
  152.5 6.4 %collective-permute-start.38 = (bf16[16,4864]{1,0:T(8,128)(2,1)S(1)}, bf16[16,4864]{1,0:T(8,128)(2,1)S(1)}, u32[]{:S(2)}, u32[]{:S(2)}) collective-permute-start(bf16[16,4864]{1,0:T(8,128)(2,1)S(1)} %get-tuple-element.320), channel_id=1, source_target_pairs={{0,16},{4,20},{8,24},{12,28},{16,0},{20,4},{24,8},{28,12},{1,17},{... | collective-permute-start | bytes 466952 | tf_op jit(solution)/shard_map/ppermute | solution.py:677
  154.4 6.7 %collective-permute-start.37 = (bf16[16,2176]{1,0:T(8,128)(2,1)S(1)}, bf16[16,2176]{1,0:T(8,128)(2,1)S(1)}, u32[]{:S(2)}, u32[]{:S(2)}) collective-permute-start(bf16[16,2176]{1,0:T(8,128)(2,1)S(1)} %get-tuple-element.305), channel_id=1, source_target_pairs={{0,3},{1,2},{2,1},{3,0},{4,7},{5,6},{6,5},{7,4},{8,11},{9,10},{10,... | collective-permute-start | bytes 208904 | tf_op jit(solution)/shard_map/ppermute | solution.py:677
  156.7 6.1 %collective-permute-start.36 = (bf16[16,2176]{1,0:T(8,128)(2,1)S(1)}, bf16[16,2176]{1,0:T(8,128)(2,1)S(1)}, u32[]{:S(2)}, u32[]{:S(2)}) collective-permute-start(bf16[16,2176]{1,0:T(8,128)(2,1)S(1)} %get-tuple-element.306), channel_id=1, source_target_pairs={{0,2},{1,3},{2,0},{3,1},{4,6},{5,7},{6,4},{7,5},{8,10},{9,11},{10,... | collective-permute-start | bytes 208904 | tf_op jit(solution)/shard_map/ppermute | solution.py:677
  157.6 5.2 %collective-permute-start.35 = (bf16[16,2176]{1,0:T(8,128)(2,1)S(1)}, bf16[16,2176]{1,0:T(8,128)(2,1)S(1)}, u32[]{:S(2)}, u32[]{:S(2)}) collective-permute-start(bf16[16,2176]{1,0:T(8,128)(2,1)S(1)} %get-tuple-element.307), channel_id=1, source_target_pairs={{0,1},{1,0},{2,3},{3,2},{4,5},{5,4},{6,7},{7,6},{8,9},{9,8},{10,11... | collective-permute-start | bytes 208904 | tf_op jit(solution)/shard_map/ppermute | solution.py:677
  158.9 9.4 %collective-permute-start.43 = (bf16[2,16,4864]{2,1,0:T(8,128)(2,1)S(1)}, bf16[2,16,4864]{2,1,0:T(8,128)(2,1)S(1)}, u32[]{:S(2)}, u32[]{:S(2)}) collective-permute-start(bf16[2,16,4864]{2,1,0:T(8,128)(2,1)S(1)} %get-tuple-element.316), channel_id=1, source_target_pairs={{0,8},{4,12},{8,0},{12,4},{16,24},{20,28},{24,16},{28,20},{1,9},{5... | collective-permute-start | bytes 933896 | tf_op jit(solution)/shard_map/ppermute | solution.py:677
  162.9 5.5 %collective-permute-start.39 = (bf16[16,2176]{1,0:T(8,128)(2,1)S(1)}, bf16[16,2176]{1,0:T(8,128)(2,1)S(1)}, u32[]{:S(2)}, u32[]{:S(2)}) collective-permute-start(bf16[16,2176]{1,0:T(8,128)(2,1)S(1)} %add_convert_fusion.23), channel_id=1, source_target_pairs={{0,8},{4,12},{8,0},{12,4},{16,24},{20,28},{24,16},{28,20},{1,9},{5... | collective-permute-start | bytes 208904 | tf_op jit(solution)/shard_map/ppermute | solution.py:677
  163.9 5.5 %collective-permute-start.41 = (bf16[16,2176]{1,0:T(8,128)(2,1)S(1)}, bf16[16,2176]{1,0:T(8,128)(2,1)S(1)}, u32[]{:S(2)}, u32[]{:S(2)}) collective-permute-start(bf16[16,2176]{1,0:T(8,128)(2,1)S(1)} %add_convert_fusion.23), channel_id=1, source_target_pairs={{0,24},{4,28},{8,16},{12,20},{16,8},{20,12},{24,0},{28,4},{1,25},{... | collective-permute-start | bytes 208904 | tf_op jit(solution)/shard_map/ppermute | solution.py:677
  165.1 4.9 %collective-permute-start.40 = (bf16[16,2176]{1,0:T(8,128)(2,1)S(1)}, bf16[16,2176]{1,0:T(8,128)(2,1)S(1)}, u32[]{:S(2)}, u32[]{:S(2)}) collective-permute-start(bf16[16,2176]{1,0:T(8,128)(2,1)S(1)} %add_convert_fusion.23), channel_id=1, source_target_pairs={{0,16},{4,20},{8,24},{12,28},{16,0},{20,4},{24,8},{28,12},{1,17},{... | collective-permute-start | bytes 208904 | tf_op jit(solution)/shard_map/ppermute | solution.py:677
  168.5 2.1 %collective-permute-start.44 = (bf16[4,16,4864]{2,1,0:T(8,128)(2,1)S(1)}, bf16[4,16,4864]{2,1,0:T(8,128)(2,1)S(1)}, u32[]{:S(2)}, u32[]{:S(2)}) collective-permute-start(bf16[4,16,4864]{2,1,0:T(8,128)(2,1)S(1)} %bitcast.102), channel_id=1, source_target_pairs={{0,4},{4,0},{8,12},{12,8},{16,20},{20,16},{24,28},{28,24},{1,5},{5... | collective-permute-start | bytes 1867784 | tf_op jit(solution)/shard_map/ppermute | solution.py:677
  170.1 2.6 %collective-permute-start.42 = (bf16[4,16,2176]{2,1,0:T(8,128)(2,1)S(1)}, bf16[4,16,2176]{2,1,0:T(8,128)(2,1)S(1)}, u32[]{:S(2)}, u32[]{:S(2)}) collective-permute-start(bf16[4,16,2176]{2,1,0:T(8,128)(2,1)S(1)} %pad_maximum_fusion.10.near), channel_id=1, source_target_pairs={{0,4},{4,0},{8,12},{12,8},{16,20},{20,16},{24,28},{28,24},{1,5},{5... | collective-permute-start | bytes 835592 | tf_op jit(solution)/shard_map/ppermute | solution.py:677
  (14 other events, 73.7 us)

commit v6 on v5

--- a/solution.py
+++ b/solution.py
@@ -99,10 +99,10 @@
 
 
 def pack_kernel(
-    idx, g1, b1, g2, b2, bd, bu, wq, wk, wv, wc, wm, wu, wd, wr, pa, pc, pd, sems
+    g1, b1, g2, b2, bd, bu, wq, wk, wv, wc, wm, wu, wd, wr, pa, pc, pd, sems
 ):
-    member = idx[1] * 2 + idx[0]
-    across = (idx[1] ^ 3) * 2 + idx[0]
+    member = lax.axis_index("dp") % 8
+    across = member ^ 6
     rows = rows_at(member * PIECE, PIECE)
     moves = []
     for j, w in enumerate((wq, wk, wv, wc)):
@@ -769,7 +769,7 @@
         pa, pu, pd = call(
             pack_kernel,
             "pack_weights",
-            [(idx, None)] + [(v, None) for v in vectors] + [(w, "hbm") for w in weights],
+            [(v, None) for v in vectors] + [(w, "hbm") for w in weights],
             [(size, BF16, None) for size in sizes],
             scratch=[pltpu.SemaphoreType.DMA((20,))],
             limit=56,
@@ -778,7 +778,7 @@
         pair_u = near_pair(pu, shards)
         rows_a = jnp.stack([pa[:, :COLS_BOTH]] + [g[:, :COLS_BOTH] for g in got_a])
         vec = jnp.stack([pa[:, COLS_BOTH:]] + [g[:, COLS_BOTH:] for g in got_a])
-        rows_a, vec, pair_u, pd, tokens_a = pin(rows_a, vec, pair_u, pd, tokens)
+        rows_a, vec, pd, tokens_a = pin(rows_a, vec, pd, tokens)
         plane_a = [swap(rows_a, "dp", dp, 2 * k) for k in range(1, 4)]
         got_u = far_pair(pair_u, shards)
         pair_d = near_pair(pd, shards)
@@ -791,9 +791,10 @@
                 ((2 * WIDTH + PIECE, count), BF16, None),
             ],
         )
-        plane_a, got_u, pair_d, a1, both_t = pin(plane_a, got_u, pair_d, a1, both_t)
+        plane_a, got_u, a1, both_t = pin(plane_a, got_u, a1, both_t)
         near_a = jnp.stack([rows_a] + plane_a)
         far_a = swap(near_a, "dp", dp, 1)
+        pair_d, _ = pin(pair_d, near_a)
         got_d = far_pair(pair_d, shards)
         got_u, _ = pin(got_u, near_a)
         rows_u = jnp.concatenate([pair_u, got_u])

time: 175 us -> 171 us (0.977)
  starting transfers between devices: 49.2 us -> 45.4 us
    ppermute x45, starting transfers between devices: 49.2 us -> 45.4 us  [swap(): return lax.ppermute(value, axis, [(i, i ^ distance) for i in range(size)])]
  transfers between devices with their start and end apart: 45 -> 45, of which waited for: 18 -> 16; matrix products, arithmetic and copies ran while one was open for 2% -> 3% of each run, Pallas kernels for 37% -> 38%
where the time goes in v6:
time: 171 us; the launch traced here: 170 us
  Pallas kernels  85.9 us (50%)
  starting transfers between devices  45.4 us (27%)
  waiting for transfers between devices  29.7 us (17%)
  local copies, waits for them, and re-layouts  4.73 us (3%)
  other arithmetic  3.45 us (2%)
    pallas_call x11, Pallas kernels, call(): pl.pallas_call(kernel, grid=grid, in_specs=in_specs, out_specs=[spec(shap...  85.9 us
    ppermute x45, starting transfers between devices, swap(): return lax.ppermute(value, axis, [(i, i ^ distance) for i in range(size)])  45.4 us
    ppermute x45, waiting for transfers between devices, swap(): return lax.ppermute(value, axis, [(i, i ^ distance) for i in range(size)])  29.7 us
  transfers between devices with their start and end apart: 45, of which 16 were waited for; matrix products, arithmetic and copies ran while one was open for 3% of the time, Pallas kernels for 38%

profile of v6, /device:TPU:0, one launch (start us, length us, event | category | flops | bytes accessed | tf_op | source)
XLA Modules:
  0.0 170.5 jit_solution(1547298950156977230)
XLA Ops:
  0.7 2.7 %pack_weights.1 = (bf16[16,2176]{1,0:T(8,128)(2,1)}, bf16[16,2560]{1,0:T(8,128)(2,1)}, bf16[2,16,2304]{2,1,0:T(8,128)(2,1)}) custom-call(bf16[128]{0:T(256)(128)(2,1)} %g1.1, bf16[128]{0:T(256)(128)(2,1)} %b1.1, bf16[128]{0:T(256)(128)(2,1)} %g2.1, bf16[128]{0:T(256)(128)(2,1)} %b2.1, bf16[128]{0:T(256)(128)(2,1)} %bd.1, bf16[512]{0:T(512)(128)(2,1)} %bu.1, ...), custom_call_target="tpu_custom_call" | custom-call | flops 1000 | bytes 1000 | tf_op jit(solution)/shard_map/pack_weights/pallas_call | solution.py:660
  3.4 5.1 %collective-permute-start.2 = (bf16[16,2176]{1,0:T(8,128)(2,1)}, bf16[16,2176]{1,0:T(8,128)(2,1)S(1)}, u32[]{:S(2)}, u32[]{:S(2)}) collective-permute-start(bf16[16,2176]{1,0:T(8,128)(2,1)} %get-tuple-element.152), channel_id=1, source_target_pairs={{0,3},{1,2},{2,1},{3,0},{4,7},{5,6},{6,5},{7,4},{8,11},{9,10},{10,... | collective-permute-start | bytes 208904 | tf_op jit(solution)/shard_map/ppermute | solution.py:677
  9.2 1.4 collective-permute-start.6
  10.6 0.8 slice_bitcast_fusion.6
  12.1 2.7 %collective-permute-done.1 = bf16[16,2176]{1,0:T(8,128)(2,1)S(1)} collective-permute-done((bf16[16,2176]{1,0:T(8,128)(2,1)}, bf16[16,2176]{1,0:T(8,128)(2,1)S(1)}, u32[]{:S(2)}, u32[]{:S(2)}) %collective-permute-start.1) | collective-permute-done | bytes 69664 | tf_op jit(solution)/shard_map/ppermute | solution.py:677
  15.1 2.7 %collective-permute-start.5 = (bf16[4,16,2048]{2,1,0:T(8,128)(2,1)S(1)}, bf16[4,16,2048]{2,1,0:T(8,128)(2,1)S(1)}, u32[]{:S(2)}, u32[]{:S(2)}) collective-permute-start(bf16[4,16,2048]{2,1,0:T(8,128)(2,1)S(1)} %pad_maximum_fusion.12), channel_id=1, source_target_pairs={{0,24},{4,28},{8,16},{12,20},{16,8},{20,12},{24,0},{28,4},{1,25},{... | collective-permute-start | bytes 786440 | tf_op jit(solution)/shard_map/ppermute | solution.py:677
  18.6 0.9 pad_maximum_fusion.13
  19.6 1.3 collective-permute-start.7
  20.9 2.1 %collective-permute-start.12 = (bf16[2,16,2304]{2,1,0:T(8,128)(2,1)S(1)}, bf16[2,16,2304]{2,1,0:T(8,128)(2,1)S(1)}, u32[]{:S(2)}, u32[]{:S(2)}) collective-permute-start(bf16[2,16,2304]{2,1,0:T(8,128)(2,1)S(1)} %copy-done.14), channel_id=1, source_target_pairs={{0,1},{1,0},{2,3},{3,2},{4,5},{5,4},{6,7},{7,6},{8,9},{9,8},{10,11... | collective-permute-start | bytes 442376 | tf_op jit(solution)/shard_map/ppermute | solution.py:677
  23.0 1.8 %first_norm.1 = (bf16[1024,512]{1,0:T(8,128)(2,1)S(1)}, bf16[1040,1024]{1,0:T(8,128)(2,1)S(1)}) custom-call(s32[3]{0:T(128)S(1)} %pad_add_fusion.idx, bf16[4,16,128]{2,1,0:T(8,128)(2,1)S(1)} %pad_maximum_fusion.15.vec, bf16[1024,512]{1,0:T(8,128)(2,1)S(1)} %copy-done), custom_call_target="tpu_custom_call" | custom-call | flops 1000 | bytes 1000 | tf_op jit(solution)/shard_map/first_norm/pallas_call | solution.py:660
  24.8 3.3 %collective-permute-done.7 = bf16[2,16,2560]{2,1,0:T(8,128)(2,1)S(1)} collective-permute-done((bf16[2,16,2560]{2,1,0:T(8,128)(2,1)S(1)}, bf16[2,16,2560]{2,1,0:T(8,128)(2,1)S(1)}, u32[]{:S(2)}, u32[]{:S(2)}) %collective-permute-start.7) | collective-permute-done | bytes 163872 | tf_op jit(solution)/shard_map/ppermute | solution.py:677
  28.2 1.0 collective-permute-done.4
  30.4 1.6 collective-permute-start.11
  32.0 1.4 collective-permute-start.10
  34.0 8.6 %attend.2 = (bf16[1024,1024]{1,0:T(8,128)(2,1)S(1)}, f32[1024,1024]{1,0:T(8,128)}, bf16[1024,512]{1,0:T(8,128)(2,1)S(1)}, bf16[8,2,128,256]{3,2,1,0:T(8,128)(2,1)S(1)}, bf16[512,1024]{1,0:T(8,128)(2,1)S(1)}) custom-call(s32[3]{0:T(128)S(1)} %pad_add_fusion.idx, bf16[1024,512]{1,0:T(8,128)(2,1)S(1)} %get-tuple-element.174.a1, ...), custom_call_target="tpu_custom_call" | custom-call | flops 1000 | bytes 1000 | tf_op jit(solution)/shard_map/attend/pallas_call | solution.py:660
  42.6 5.9 %collective-permute-done.13 = bf16[2,2,16,2304]{3,2,0,1:T(8,128)(2,1)S(1)} collective-permute-done((bf16[2,2,16,2304]{3,2,0,1:T(8,128)(2,1)S(1)}, bf16[2,2,16,2304]{3,2,0,1:T(8,128)(2,1)S(1)}, u32[]{:S(2)}, u32[]{:S(2)}) %collective-permute-start.13) | collective-permute-done | bytes 294944 | tf_op jit(solution)/shard_map/ppermute | solution.py:677
  48.9 1.5 collective-permute-start.16
  51.2 8.3 %attend.3 = (bf16[1024,1024]{1,0:T(8,128)(2,1)S(1)}, f32[1024,1024]{1,0:T(8,128)}, bf16[1024,512]{1,0:T(8,128)(2,1)S(1)}, bf16[8,2,128,256]{3,2,1,0:T(8,128)(2,1)S(1)}, bf16[512,1024]{1,0:T(8,128)(2,1)S(1)}) custom-call(s32[3]{0:T(128)S(1)} %pad_add_fusion.idx, bf16[1024,512]{1,0:T(8,128)(2,1)S(1)} %get-tuple-element.174.a1, ...), custom_call_target="tpu_custom_call" | custom-call | flops 1000 | bytes 1000 | tf_op jit(solution)/shard_map/attend/pallas_call | solution.py:660
  59.5 1.3 copy-done.3
  61.1 2.8 %collective-permute-done.17.down_far_i = bf16[4,4,16,2304]{3,2,1,0:T(8,128)(2,1)S(1)} collective-permute-done((bf16[4,4,16,2304]{3,2,1,0:T(8,128)(2,1)S(1)}, bf16[4,4,16,2304]{3,2,1,0:T(8,128)(2,1)S(1)}, u32[]{:S(2)}, u32[]{:S(2)}) %collective-permute-start.17) | collective-permute-done | bytes 1179680 | tf_op jit(solution)/shard_map/ppermute | solution.py:677
  64.0 1.0 copy-done.12
  65.0 16.2 %feed_forward.1 = (bf16[1024,512]{1,0:T(8,128)(2,1)}, f32[1024,512]{1,0:T(8,128)}, bf16[1024,2048]{1,0:T(8,128)(2,1)}, f32[1024,512]{1,0:T(8,128)}, f32[1,512]{1...) custom-call(s32[3]{0:T(128)S(1)} %pad_add_fusion.idx, ...), custom_call_target="tpu_custom_call" | custom-call | flops 1000 | bytes 1000 | tf_op jit(solution)/shard_map/feed_forward/pallas_call | solution.py:660
  81.4 13.0 %feed_backward.1 = (f32[1024,512]{1,0:T(8,128)}, bf16[1024,512]{1,0:T(8,128)(2,1)S(1)}, f32[1,512]{1,0:T(1,128)S(1)}, f32[1,512]{1,0:T(1,128)S(1)}, f32[1,2048]{...) custom-call(s32[3]{0:T(128)S(1)} %pad_add_fusion.idx, ...), custom_call_target="tpu_custom_call" | custom-call | flops 1000 | bytes 1000 | tf_op jit(solution)/shard_map/feed_backward/pallas_call | solution.py:660
  95.0 1.3 collective-permute-start.19
  96.9 1.7 collective-permute-start.21
  98.6 13.1 %attend_backward.2 = (bf16[1024,1024]{1,0:T(8,128)(2,1)S(1)}, bf16[4,4,16,1024]{3,2,1,0:T(8,128)(2,1)S(1)}, bf16[4,4,16,1024]{3,2,1,0:T(8,128)(2,1)S(1)}, f32[8,512]{1,0:T(8,128)S(1)}) custom-call(s32[3]{0:T(128)S(1)} %pad_add_fusion.idx, bf16[1040,1024]{1,0:T(8,128)(2,1)} %copy-done.1, bf16[512,1024]{1,0:T(8,128)(2,1)S(1)} %get-tuple-element.207.w.w0, ...), custom_call_target="tpu_custom_call" | custom-call | flops 1000 | bytes 1000 | tf_op jit(solution)/shard_map/attend_backward/pallas_call | solution.py:660
  112.4 1.3 collective-permute-start.24
  114.3 1.6 collective-permute-start.26
  116.0 13.3 %attend_backward.3 = (bf16[1024,1024]{1,0:T(8,128)(2,1)S(1)}, bf16[4,4,16,1152]{3,2,1,0:T(8,128)(2,1)S(1)}, bf16[4,4,16,1152]{3,2,1,0:T(8,128)(2,1)S(1)}) custom-call(s32[3]{0:T(128)S(1)} %pad_add_fusion.idx, bf16[1040,1024]{1,0:T(8,128)(2,1)} %copy-done.1, bf16[512,1024]{1,0:T(8,128)(2,1)S(1)} %get-tuple-element.225.w.w1, bf16[1024,1024]{1,0:T(8,128)(2,1)S(1)} %copy-done.4, ...), custom_call_target="tpu_custom_call" | custom-call | flops 1000 | bytes 1000 | tf_op jit(solution)/shard_map/attend_backward/pallas_call | solution.py:660
  129.4 1.2 collective-permute-done.25
  130.8 1.8 %collective-permute-done.28 = bf16[4,4,16,1152]{3,2,1,0:T(8,128)(2,1)S(1)} collective-permute-done((bf16[4,4,16,1152]{3,2,1,0:T(8,128)(2,1)S(1)}, bf16[4,4,16,1152]{3,2,1,0:T(8,128)(2,1)S(1)}, u32[]{:S(2)}, u32[]{:S(2)}) %collective-permute-start.28) | collective-permute-done | bytes 589856 | tf_op jit(solution)/shard_map/ppermute | solution.py:677
  133.0 1.6 collective-permute-start.29
  134.6 1.0 collective-permute-start.30
  136.3 1.4 collective-permute-start.32
  137.7 1.5 collective-permute-start.33
  139.2 4.9 %input_gradient.1 = f32[1024,512]{1,0:T(8,128)} custom-call(s32[3]{0:T(128)S(1)} %pad_add_fusion.idx, bf16[4,16,128]{2,1,0:T(8,128)(2,1)S(1)} %pad_maximum_fusion.15.vec, bf16[1024,512]{1,0:T(8,128)(2,1)S(1)} %copy-done, f32[1024,512]{1,0:T(8,128)S(1)} %copy-done.2, bf16[1024,1024]{1,0:T(8,128)(2,1)S(1)} %get-tuple-element.256.dx0, ...), custom_call_target="tpu_custom_call" | custom-call | flops 1000 | bytes 1000 | tf_op jit(solution)/shard_map/input_gradient/pallas_call | solution.py:660
  144.1 1.1 collective-permute-start.34
  145.3 3.4 %collective-permute-done.34 = bf16[16,2560]{1,0:T(8,128)(2,1)S(1)} collective-permute-done((bf16[16,2560]{1,0:T(8,128)(2,1)S(1)}, bf16[16,2560]{1,0:T(8,128)(2,1)S(1)}, u32[]{:S(2)}, u32[]{:S(2)}) %collective-permute-start.34) | collective-permute-done | bytes 81952 | tf_op jit(solution)/shard_map/ppermute | solution.py:677
  150.3 2.4 %collective-permute-start.37 = (bf16[16,2176]{1,0:T(8,128)(2,1)S(1)}, bf16[16,2176]{1,0:T(8,128)(2,1)S(1)}, u32[]{:S(2)}, u32[]{:S(2)}) collective-permute-start(bf16[16,2176]{1,0:T(8,128)(2,1)S(1)} %get-tuple-element.303), channel_id=1, source_target_pairs={{0,3},{1,2},{2,1},{3,0},{4,7},{5,6},{6,5},{7,4},{8,11},{9,10},{10,... | collective-permute-start | bytes 208904 | tf_op jit(solution)/shard_map/ppermute | solution.py:677
  153.5 1.3 collective-permute-start.35
  154.8 1.6 collective-permute-start.43
  156.6 2.0 %collective-permute-done.36 = bf16[16,2176]{1,0:T(8,128)(2,1)S(1)} collective-permute-done((bf16[16,2176]{1,0:T(8,128)(2,1)S(1)}, bf16[16,2176]{1,0:T(8,128)(2,1)S(1)}, u32[]{:S(2)}, u32[]{:S(2)}) %collective-permute-start.36) | collective-permute-done | bytes 69664 | tf_op jit(solution)/shard_map/ppermute | solution.py:677
  158.6 1.3 collective-permute-start.39
  159.9 1.5 collective-permute-start.41
  162.2 2.0 %collective-permute-done.39 = bf16[16,2176]{1,0:T(8,128)(2,1)S(1)} collective-permute-done((bf16[16,2176]{1,0:T(8,128)(2,1)S(1)}, bf16[16,2176]{1,0:T(8,128)(2,1)S(1)}, u32[]{:S(2)}, u32[]{:S(2)}) %collective-permute-start.39) | collective-permute-done | bytes 69664 | tf_op jit(solution)/shard_map/ppermute | solution.py:677
  164.3 1.4 collective-permute-done.41
  166.5 2.1 %unpack_feed.1 = (f32[128,512]{1,0:T(8,128)}, f32[128,2048]{1,0:T(8,128)}, f32[512,512]{1,0:T(8,128)}, f32[128,256]{1,0:T(8,128)}) custom-call(s32[3]{0:T(128)S(1)} %pad_add_fusion.idx, bf16[4,16,4864]{2,1,0:T(8,128)(2,1)S(1)} %bitcast.104, bf16[4,16,4864]{2,1,0:T(8,128)(2,1)S(1)} %collective-permute-done.44.far), custom_call_target="tpu_custom_call" | custom-call | flops 1000 | bytes 1000 | tf_op jit(solution)/shard_map/unpack_feed/pallas_call | solution.py:660
  168.7 1.6 unpack_proj.1
  (124 shorter events, 14.2 us)
Async XLA Ops:
  0.7 22.4 %copy-start = (bf16[1024,512]{1,0:T(8,128)(2,1)S(1)}, bf16[1024,512]{1,0:T(8,128)(2,1)}, u32[]{:S(2)}) copy-start(bf16[1024,512]{1,0:T(8,128)(2,1)} %x.4) | copy-start | bytes 3145732
  3.4 17.5 %copy-start.14 = (bf16[2,16,2304]{2,1,0:T(8,128)(2,1)S(1)}, bf16[2,16,2304]{2,1,0:T(8,128)(2,1)}, u32[]{:S(2)}) copy-start(bf16[2,16,2304]{2,1,0:T(8,128)(2,1)} %get-tuple-element.171) | copy-start | bytes 442372
  3.4 8.7 %collective-permute-start.2 = (bf16[16,2176]{1,0:T(8,128)(2,1)}, bf16[16,2176]{1,0:T(8,128)(2,1)S(1)}, u32[]{:S(2)}, u32[]{:S(2)}) collective-permute-start(bf16[16,2176]{1,0:T(8,128)(2,1)} %get-tuple-element.152), channel_id=1, source_target_pairs={{0,3},{1,2},{2,1},{3,0},{4,7},{5,6},{6,5},{7,4},{8,11},{9,10},{10,... | collective-permute-start | bytes 208904 | tf_op jit(solution)/shard_map/ppermute | solution.py:677
  8.5 6.2 %collective-permute-start.1 = (bf16[16,2176]{1,0:T(8,128)(2,1)}, bf16[16,2176]{1,0:T(8,128)(2,1)S(1)}, u32[]{:S(2)}, u32[]{:S(2)}) collective-permute-start(bf16[16,2176]{1,0:T(8,128)(2,1)} %get-tuple-element.152), channel_id=1, source_target_pairs={{0,2},{1,3},{2,0},{3,1},{4,6},{5,7},{6,4},{7,5},{8,10},{9,11},{10,... | collective-permute-start | bytes 208904 | tf_op jit(solution)/shard_map/ppermute | solution.py:677
  8.5 6.5 %collective-permute-start = (bf16[16,2176]{1,0:T(8,128)(2,1)}, bf16[16,2176]{1,0:T(8,128)(2,1)S(1)}, u32[]{:S(2)}, u32[]{:S(2)}) collective-permute-start(bf16[16,2176]{1,0:T(8,128)(2,1)} %get-tuple-element.152), channel_id=1, source_target_pairs={{0,1},{1,0},{2,3},{3,2},{4,5},{5,4},{6,7},{7,6},{8,9},{9,8},{10,11... | collective-permute-start | bytes 208904 | tf_op jit(solution)/shard_map/ppermute | solution.py:677
  9.2 9.5 %collective-permute-start.6 = (bf16[16,2560]{1,0:T(8,128)(2,1)}, bf16[16,2560]{1,0:T(8,128)(2,1)S(1)}, u32[]{:S(2)}, u32[]{:S(2)}) collective-permute-start(bf16[16,2560]{1,0:T(8,128)(2,1)} %get-tuple-element.156), channel_id=1, source_target_pairs={{0,1},{1,0},{2,3},{3,2},{4,5},{5,4},{6,7},{7,6},{8,9},{9,8},{10,11... | collective-permute-start | bytes 245768 | tf_op jit(solution)/shard_map/ppermute | solution.py:677
  15.1 13.1 %collective-permute-start.5 = (bf16[4,16,2048]{2,1,0:T(8,128)(2,1)S(1)}, bf16[4,16,2048]{2,1,0:T(8,128)(2,1)S(1)}, u32[]{:S(2)}, u32[]{:S(2)}) collective-permute-start(bf16[4,16,2048]{2,1,0:T(8,128)(2,1)S(1)} %pad_maximum_fusion.12), channel_id=1, source_target_pairs={{0,24},{4,28},{8,16},{12,20},{16,8},{20,12},{24,0},{28,4},{1,25},{... | collective-permute-start | bytes 786440 | tf_op jit(solution)/shard_map/ppermute | solution.py:677
  17.8 11.4 %collective-permute-start.4 = (bf16[4,16,2048]{2,1,0:T(8,128)(2,1)S(1)}, bf16[4,16,2048]{2,1,0:T(8,128)(2,1)S(1)}, u32[]{:S(2)}, u32[]{:S(2)}) collective-permute-start(bf16[4,16,2048]{2,1,0:T(8,128)(2,1)S(1)} %pad_maximum_fusion.12), channel_id=1, source_target_pairs={{0,16},{4,20},{8,24},{12,28},{16,0},{20,4},{24,8},{28,12},{1,17},{... | collective-permute-start | bytes 786440 | tf_op jit(solution)/shard_map/ppermute | solution.py:677
  18.3 11.2 %collective-permute-start.3 = (bf16[4,16,2048]{2,1,0:T(8,128)(2,1)S(1)}, bf16[4,16,2048]{2,1,0:T(8,128)(2,1)S(1)}, u32[]{:S(2)}, u32[]{:S(2)}) collective-permute-start(bf16[4,16,2048]{2,1,0:T(8,128)(2,1)S(1)} %pad_maximum_fusion.12), channel_id=1, source_target_pairs={{0,8},{4,12},{8,0},{12,4},{16,24},{20,28},{24,16},{28,20},{1,9},{5... | collective-permute-start | bytes 786440 | tf_op jit(solution)/shard_map/ppermute | solution.py:677
  19.6 8.6 %collective-permute-start.7 = (bf16[2,16,2560]{2,1,0:T(8,128)(2,1)S(1)}, bf16[2,16,2560]{2,1,0:T(8,128)(2,1)S(1)}, u32[]{:S(2)}, u32[]{:S(2)}) collective-permute-start(bf16[2,16,2560]{2,1,0:T(8,128)(2,1)S(1)} %pad_maximum_fusion.13), channel_id=1, source_target_pairs={{0,2},{1,3},{2,0},{3,1},{4,6},{5,7},{6,4},{7,5},{8,10},{9,11},{10,... | collective-permute-start | bytes 491528 | tf_op jit(solution)/shard_map/ppermute | solution.py:677
  20.9 8.8 %collective-permute-start.12 = (bf16[2,16,2304]{2,1,0:T(8,128)(2,1)S(1)}, bf16[2,16,2304]{2,1,0:T(8,128)(2,1)S(1)}, u32[]{:S(2)}, u32[]{:S(2)}) collective-permute-start(bf16[2,16,2304]{2,1,0:T(8,128)(2,1)S(1)} %copy-done.14), channel_id=1, source_target_pairs={{0,1},{1,0},{2,3},{3,2},{4,5},{5,4},{6,7},{7,6},{8,9},{9,8},{10,11... | collective-permute-start | bytes 442376 | tf_op jit(solution)/shard_map/ppermute | solution.py:677
  29.6 4.4 %collective-permute-start.8 = (bf16[4,4,16,2048]{3,2,1,0:T(8,128)(2,1)S(1)}, bf16[4,4,16,2048]{3,2,1,0:T(8,128)(2,1)S(1)}, u32[]{:S(2)}, u32[]{:S(2)}) collective-permute-start(bf16[4,4,16,2048]{3,2,1,0:T(8,128)(2,1)S(1)} %pad_maximum_fusion.2.near), channel_id=1, source_target_pairs={{0,4},{4,0},{8,12},{12,8},{16,20},{20,16},{24,28},{28,24},{1,5},{5... | collective-permute-start | bytes 3145736 | tf_op jit(solution)/shard_map/ppermute | solution.py:677
  30.4 18.1 %collective-permute-start.11 = (bf16[4,16,2560]{2,1,0:T(8,128)(2,1)S(1)}, bf16[4,16,2560]{2,1,0:T(8,128)(2,1)S(1)}, u32[]{:S(2)}, u32[]{:S(2)}) collective-permute-start(bf16[4,16,2560]{2,1,0:T(8,128)(2,1)S(1)} %get-tuple-element.314), channel_id=1, source_target_pairs={{0,24},{4,28},{8,16},{12,20},{16,8},{20,12},{24,0},{28,4},{1,25},{... | collective-permute-start | bytes 983048 | tf_op jit(solution)/shard_map/ppermute | solution.py:677
  32.0 16.5 %collective-permute-start.10 = (bf16[4,16,2560]{2,1,0:T(8,128)(2,1)S(1)}, bf16[4,16,2560]{2,1,0:T(8,128)(2,1)S(1)}, u32[]{:S(2)}, u32[]{:S(2)}) collective-permute-start(bf16[4,16,2560]{2,1,0:T(8,128)(2,1)S(1)} %get-tuple-element.314), channel_id=1, source_target_pairs={{0,16},{4,20},{8,24},{12,28},{16,0},{20,4},{24,8},{28,12},{1,17},{... | collective-permute-start | bytes 983048 | tf_op jit(solution)/shard_map/ppermute | solution.py:677
  33.4 15.1 %collective-permute-start.9 = (bf16[4,16,2560]{2,1,0:T(8,128)(2,1)S(1)}, bf16[4,16,2560]{2,1,0:T(8,128)(2,1)S(1)}, u32[]{:S(2)}, u32[]{:S(2)}) collective-permute-start(bf16[4,16,2560]{2,1,0:T(8,128)(2,1)S(1)} %get-tuple-element.314), channel_id=1, source_target_pairs={{0,8},{4,12},{8,0},{12,4},{16,24},{20,28},{24,16},{28,20},{1,9},{5... | collective-permute-start | bytes 983048 | tf_op jit(solution)/shard_map/ppermute | solution.py:677
  34.0 14.5 %collective-permute-start.13 = (bf16[2,2,16,2304]{3,2,0,1:T(8,128)(2,1)S(1)}, bf16[2,2,16,2304]{3,2,0,1:T(8,128)(2,1)S(1)}, u32[]{:S(2)}, u32[]{:S(2)}) collective-permute-start(bf16[2,2,16,2304]{3,2,0,1:T(8,128)(2,1)S(1)} %pad_maximum_fusion.6), channel_id=1, source_target_pairs={{0,2},{1,3},{2,0},{3,1},{4,6},{5,7},{6,4},{7,5},{8,10},{9,11},{10,... | collective-permute-start | bytes 884744 | tf_op jit(solution)/shard_map/ppermute | solution.py:677
  48.7 12.2 %collective-permute-start.14 = (bf16[4,4,16,2560]{3,2,1,0:T(8,128)(2,1)S(1)}, bf16[4,4,16,2560]{3,2,1,0:T(8,128)(2,1)S(1)}, u32[]{:S(2)}, u32[]{:S(2)}) collective-permute-start(bf16[4,4,16,2560]{3,2,1,0:T(8,128)(2,1)S(1)} %pad_maximum_fusion.up_near_i), channel_id=1, source_target_pairs={{0,4},{4,0},{8,12},{12,8},{16,20},{20,16},{24,28},{28,24},{1,5},{5... | collective-permute-start | bytes 3932168 | tf_op jit(solution)/shard_map/ppermute | solution.py:677
  48.9 12.0 %collective-permute-start.16 = (bf16[4,16,2304]{2,1,0:T(8,128)(2,1)S(1)}, bf16[4,16,2304]{2,1,0:T(8,128)(2,1)S(1)}, u32[]{:S(2)}, u32[]{:S(2)}) collective-permute-start(bf16[4,16,2304]{2,1,0:T(8,128)(2,1)S(1)} %get-tuple-element.312), channel_id=1, source_target_pairs={{0,16},{4,20},{8,24},{12,28},{16,0},{20,4},{24,8},{28,12},{1,17},{... | collective-permute-start | bytes 884744 | tf_op jit(solution)/shard_map/ppermute | solution.py:677
  50.4 10.5 %collective-permute-start.15 = (bf16[4,16,2304]{2,1,0:T(8,128)(2,1)S(1)}, bf16[4,16,2304]{2,1,0:T(8,128)(2,1)S(1)}, u32[]{:S(2)}, u32[]{:S(2)}) collective-permute-start(bf16[4,16,2304]{2,1,0:T(8,128)(2,1)S(1)} %get-tuple-element.312), channel_id=1, source_target_pairs={{0,8},{4,12},{8,0},{12,4},{16,24},{20,28},{24,16},{28,20},{1,9},{5... | collective-permute-start | bytes 884744 | tf_op jit(solution)/shard_map/ppermute | solution.py:677
  60.8 20.3 %copy-start.5 = (bf16[8,2,128,256]{3,2,1,0:T(8,128)(2,1)}, bf16[8,2,128,256]{3,2,1,0:T(8,128)(2,1)S(1)}, u32[]{:S(2)}) copy-start(bf16[8,2,128,256]{3,2,1,0:T(8,128)(2,1)S(1)} %get-tuple-element.229.kept) | copy-start | bytes 3145732
  61.0 2.9 %collective-permute-start.17 = (bf16[4,4,16,2304]{3,2,1,0:T(8,128)(2,1)S(1)}, bf16[4,4,16,2304]{3,2,1,0:T(8,128)(2,1)S(1)}, u32[]{:S(2)}, u32[]{:S(2)}) collective-permute-start(bf16[4,4,16,2304]{3,2,1,0:T(8,128)(2,1)S(1)} %pad_maximum_fusion.1.down_near_i), channel_id=1, source_target_pairs={{0,4},{4,0},{8,12},{12,8},{16,20},{20,16},{24,28},{28,24},{1,5},{5... | collective-permute-start | bytes 3538952 | tf_op jit(solution)/shard_map/ppermute | solution.py:677
  81.2 13.2 %collective-permute-start.18 = (bf16[4,4,16,2304]{3,2,1,0:T(8,128)(2,1)S(1)}, bf16[4,4,16,2304]{3,2,1,0:T(8,128)(2,1)S(1)}, u32[]{:S(2)}, u32[]{:S(2)}) collective-permute-start(bf16[4,4,16,2304]{3,2,1,0:T(8,128)(2,1)S(1)} %get-tuple-element.197), channel_id=1, source_target_pairs={{0,4},{4,0},{8,12},{12,8},{16,20},{20,16},{24,28},{28,24},{1,5},{5... | collective-permute-start | bytes 3538952 | tf_op jit(solution)/shard_map/ppermute | solution.py:677
  94.4 17.3 %collective-permute-start.22 = (bf16[4,4,16,2560]{3,2,1,0:T(8,128)(2,1)S(1)}, bf16[4,4,16,2560]{3,2,1,0:T(8,128)(2,1)S(1)}, u32[]{:S(2)}, u32[]{:S(2)}) collective-permute-start(bf16[4,4,16,2560]{3,2,1,0:T(8,128)(2,1)S(1)} %get-tuple-element.205), channel_id=1, source_target_pairs={{0,4},{4,0},{8,12},{12,8},{16,20},{20,16},{24,28},{28,24},{1,5},{5... | collective-permute-start | bytes 3932168 | tf_op jit(solution)/shard_map/ppermute | solution.py:677
  95.0 16.7 %collective-permute-start.19 = (bf16[4,16,2304]{2,1,0:T(8,128)(2,1)S(1)}, bf16[4,16,2304]{2,1,0:T(8,128)(2,1)S(1)}, u32[]{:S(2)}, u32[]{:S(2)}) collective-permute-start(bf16[4,16,2304]{2,1,0:T(8,128)(2,1)S(1)} %get-tuple-element.202), channel_id=1, source_target_pairs={{0,8},{4,12},{8,0},{12,4},{16,24},{20,28},{24,16},{28,20},{1,9},{5... | collective-permute-start | bytes 884744 | tf_op jit(solution)/shard_map/ppermute | solution.py:677
  96.3 15.4 %collective-permute-start.20 = (bf16[4,16,2304]{2,1,0:T(8,128)(2,1)S(1)}, bf16[4,16,2304]{2,1,0:T(8,128)(2,1)S(1)}, u32[]{:S(2)}, u32[]{:S(2)}) collective-permute-start(bf16[4,16,2304]{2,1,0:T(8,128)(2,1)S(1)} %get-tuple-element.203), channel_id=1, source_target_pairs={{0,16},{4,20},{8,24},{12,28},{16,0},{20,4},{24,8},{28,12},{1,17},{... | collective-permute-start | bytes 884744 | tf_op jit(solution)/shard_map/ppermute | solution.py:677
  96.9 14.8 %collective-permute-start.21 = (bf16[4,16,2304]{2,1,0:T(8,128)(2,1)S(1)}, bf16[4,16,2304]{2,1,0:T(8,128)(2,1)S(1)}, u32[]{:S(2)}, u32[]{:S(2)}) collective-permute-start(bf16[4,16,2304]{2,1,0:T(8,128)(2,1)S(1)} %get-tuple-element.204), channel_id=1, source_target_pairs={{0,24},{4,28},{8,16},{12,20},{16,8},{20,12},{24,0},{28,4},{1,25},{... | collective-permute-start | bytes 884744 | tf_op jit(solution)/shard_map/ppermute | solution.py:677
  111.8 18.8 %collective-permute-start.27 = (bf16[4,4,16,1024]{3,2,1,0:T(8,128)(2,1)S(1)}, bf16[4,4,16,1024]{3,2,1,0:T(8,128)(2,1)S(1)}, u32[]{:S(2)}, u32[]{:S(2)}) collective-permute-start(bf16[4,4,16,1024]{3,2,1,0:T(8,128)(2,1)S(1)} %get-tuple-element.224), channel_id=1, source_target_pairs={{0,4},{4,0},{8,12},{12,8},{16,20},{20,16},{24,28},{28,24},{1,5},{5... | collective-permute-start | bytes 1572872 | tf_op jit(solution)/shard_map/ppermute | solution.py:677
  112.4 16.9 %collective-permute-start.24 = (bf16[4,16,2560]{2,1,0:T(8,128)(2,1)S(1)}, bf16[4,16,2560]{2,1,0:T(8,128)(2,1)S(1)}, u32[]{:S(2)}, u32[]{:S(2)}) collective-permute-start(bf16[4,16,2560]{2,1,0:T(8,128)(2,1)S(1)} %get-tuple-element.221), channel_id=1, source_target_pairs={{0,8},{4,12},{8,0},{12,4},{16,24},{20,28},{24,16},{28,20},{1,9},{5... | collective-permute-start | bytes 983048 | tf_op jit(solution)/shard_map/ppermute | solution.py:677
  113.7 16.8 %collective-permute-start.25 = (bf16[4,16,2560]{2,1,0:T(8,128)(2,1)S(1)}, bf16[4,16,2560]{2,1,0:T(8,128)(2,1)S(1)}, u32[]{:S(2)}, u32[]{:S(2)}) collective-permute-start(bf16[4,16,2560]{2,1,0:T(8,128)(2,1)S(1)} %get-tuple-element.222), channel_id=1, source_target_pairs={{0,16},{4,20},{8,24},{12,28},{16,0},{20,4},{24,8},{28,12},{1,17},{... | collective-permute-start | bytes 983048 | tf_op jit(solution)/shard_map/ppermute | solution.py:677
  114.3 16.2 %collective-permute-start.26 = (bf16[4,16,2560]{2,1,0:T(8,128)(2,1)S(1)}, bf16[4,16,2560]{2,1,0:T(8,128)(2,1)S(1)}, u32[]{:S(2)}, u32[]{:S(2)}) collective-permute-start(bf16[4,16,2560]{2,1,0:T(8,128)(2,1)S(1)} %get-tuple-element.223), channel_id=1, source_target_pairs={{0,24},{4,28},{8,16},{12,20},{16,8},{20,12},{24,0},{28,4},{1,25},{... | collective-permute-start | bytes 983048 | tf_op jit(solution)/shard_map/ppermute | solution.py:677
  116.0 13.3 %collective-permute-start.23 = (bf16[2,16,2304]{2,1,0:T(8,128)(2,1)S(1)}, bf16[2,16,2304]{2,1,0:T(8,128)(2,1)S(1)}, u32[]{:S(2)}, u32[]{:S(2)}) collective-permute-start(bf16[2,16,2304]{2,1,0:T(8,128)(2,1)S(1)} %get-tuple-element.220), channel_id=1, source_target_pairs={{0,2},{1,3},{2,0},{3,1},{4,6},{5,7},{6,4},{7,5},{8,10},{9,11},{10,... | collective-permute-start | bytes 442376 | tf_op jit(solution)/shard_map/ppermute | solution.py:677
  130.6 2.0 %collective-permute-start.28 = (bf16[4,4,16,1152]{3,2,1,0:T(8,128)(2,1)S(1)}, bf16[4,4,16,1152]{3,2,1,0:T(8,128)(2,1)S(1)}, u32[]{:S(2)}, u32[]{:S(2)}) collective-permute-start(bf16[4,4,16,1152]{3,2,1,0:T(8,128)(2,1)S(1)} %get-tuple-element.244), channel_id=1, source_target_pairs={{0,4},{4,0},{8,12},{12,8},{16,20},{20,16},{24,28},{28,24},{1,5},{5... | collective-permute-start | bytes 1769480 | tf_op jit(solution)/shard_map/ppermute | solution.py:677
  133.0 11.1 %collective-permute-start.29 = (bf16[2,16,2560]{2,1,0:T(8,128)(2,1)S(1)}, bf16[2,16,2560]{2,1,0:T(8,128)(2,1)S(1)}, u32[]{:S(2)}, u32[]{:S(2)}) collective-permute-start(bf16[2,16,2560]{2,1,0:T(8,128)(2,1)S(1)} %slice.295), channel_id=1, source_target_pairs={{0,2},{1,3},{2,0},{3,1},{4,6},{5,7},{6,4},{7,5},{8,10},{9,11},{10,... | collective-permute-start | bytes 491528 | tf_op jit(solution)/shard_map/ppermute | solution.py:677
  134.6 9.5 %collective-permute-start.30 = (bf16[16,2304]{1,0:T(8,128)(2,1)S(1)}, bf16[16,2304]{1,0:T(8,128)(2,1)S(1)}, u32[]{:S(2)}, u32[]{:S(2)}) collective-permute-start(bf16[16,2304]{1,0:T(8,128)(2,1)S(1)} %fusion.19), channel_id=1, source_target_pairs={{0,1},{1,0},{2,3},{3,2},{4,5},{5,4},{6,7},{7,6},{8,9},{9,8},{10,11... | collective-permute-start | bytes 221192 | tf_op jit(solution)/shard_map/ppermute | solution.py:677
  135.7 13.6 %collective-permute-start.31 = (bf16[4,16,2176]{2,1,0:T(8,128)(2,1)S(1)}, bf16[4,16,2176]{2,1,0:T(8,128)(2,1)S(1)}, u32[]{:S(2)}, u32[]{:S(2)}) collective-permute-start(bf16[4,16,2176]{2,1,0:T(8,128)(2,1)S(1)} %get-tuple-element.247), channel_id=1, source_target_pairs={{0,8},{4,12},{8,0},{12,4},{16,24},{20,28},{24,16},{28,20},{1,9},{5... | collective-permute-start | bytes 835592 | tf_op jit(solution)/shard_map/ppermute | solution.py:677
  136.3 13.9 %collective-permute-start.32 = (bf16[4,16,2176]{2,1,0:T(8,128)(2,1)S(1)}, bf16[4,16,2176]{2,1,0:T(8,128)(2,1)S(1)}, u32[]{:S(2)}, u32[]{:S(2)}) collective-permute-start(bf16[4,16,2176]{2,1,0:T(8,128)(2,1)S(1)} %get-tuple-element.248), channel_id=1, source_target_pairs={{0,16},{4,20},{8,24},{12,28},{16,0},{20,4},{24,8},{28,12},{1,17},{... | collective-permute-start | bytes 835592 | tf_op jit(solution)/shard_map/ppermute | solution.py:677
  137.7 12.4 %collective-permute-start.33 = (bf16[4,16,2176]{2,1,0:T(8,128)(2,1)S(1)}, bf16[4,16,2176]{2,1,0:T(8,128)(2,1)S(1)}, u32[]{:S(2)}, u32[]{:S(2)}) collective-permute-start(bf16[4,16,2176]{2,1,0:T(8,128)(2,1)S(1)} %get-tuple-element.249), channel_id=1, source_target_pairs={{0,24},{4,28},{8,16},{12,20},{16,8},{20,12},{24,0},{28,4},{1,25},{... | collective-permute-start | bytes 835592 | tf_op jit(solution)/shard_map/ppermute | solution.py:677
  144.1 4.5 %collective-permute-start.34 = (bf16[16,2560]{1,0:T(8,128)(2,1)S(1)}, bf16[16,2560]{1,0:T(8,128)(2,1)S(1)}, u32[]{:S(2)}, u32[]{:S(2)}) collective-permute-start(bf16[16,2560]{1,0:T(8,128)(2,1)S(1)} %fusion.18), channel_id=1, source_target_pairs={{0,1},{1,0},{2,3},{3,2},{4,5},{5,4},{6,7},{7,6},{8,9},{9,8},{10,11... | collective-permute-start | bytes 245768 | tf_op jit(solution)/shard_map/ppermute | solution.py:677
  148.7 6.0 %collective-permute-start.38 = (bf16[16,4864]{1,0:T(8,128)(2,1)S(1)}, bf16[16,4864]{1,0:T(8,128)(2,1)S(1)}, u32[]{:S(2)}, u32[]{:S(2)}) collective-permute-start(bf16[16,4864]{1,0:T(8,128)(2,1)S(1)} %get-tuple-element.320), channel_id=1, source_target_pairs={{0,16},{4,20},{8,24},{12,28},{16,0},{20,4},{24,8},{28,12},{1,17},{... | collective-permute-start | bytes 466952 | tf_op jit(solution)/shard_map/ppermute | solution.py:677
  150.3 6.3 %collective-permute-start.37 = (bf16[16,2176]{1,0:T(8,128)(2,1)S(1)}, bf16[16,2176]{1,0:T(8,128)(2,1)S(1)}, u32[]{:S(2)}, u32[]{:S(2)}) collective-permute-start(bf16[16,2176]{1,0:T(8,128)(2,1)S(1)} %get-tuple-element.303), channel_id=1, source_target_pairs={{0,3},{1,2},{2,1},{3,0},{4,7},{5,6},{6,5},{7,4},{8,11},{9,10},{10,... | collective-permute-start | bytes 208904 | tf_op jit(solution)/shard_map/ppermute | solution.py:677
  152.7 5.9 %collective-permute-start.36 = (bf16[16,2176]{1,0:T(8,128)(2,1)S(1)}, bf16[16,2176]{1,0:T(8,128)(2,1)S(1)}, u32[]{:S(2)}, u32[]{:S(2)}) collective-permute-start(bf16[16,2176]{1,0:T(8,128)(2,1)S(1)} %get-tuple-element.304), channel_id=1, source_target_pairs={{0,2},{1,3},{2,0},{3,1},{4,6},{5,7},{6,4},{7,5},{8,10},{9,11},{10,... | collective-permute-start | bytes 208904 | tf_op jit(solution)/shard_map/ppermute | solution.py:677
  153.5 5.1 %collective-permute-start.35 = (bf16[16,2176]{1,0:T(8,128)(2,1)S(1)}, bf16[16,2176]{1,0:T(8,128)(2,1)S(1)}, u32[]{:S(2)}, u32[]{:S(2)}) collective-permute-start(bf16[16,2176]{1,0:T(8,128)(2,1)S(1)} %get-tuple-element.305), channel_id=1, source_target_pairs={{0,1},{1,0},{2,3},{3,2},{4,5},{5,4},{6,7},{7,6},{8,9},{9,8},{10,11... | collective-permute-start | bytes 208904 | tf_op jit(solution)/shard_map/ppermute | solution.py:677
  154.8 9.3 %collective-permute-start.43 = (bf16[2,16,4864]{2,1,0:T(8,128)(2,1)S(1)}, bf16[2,16,4864]{2,1,0:T(8,128)(2,1)S(1)}, u32[]{:S(2)}, u32[]{:S(2)}) collective-permute-start(bf16[2,16,4864]{2,1,0:T(8,128)(2,1)S(1)} %get-tuple-element.316), channel_id=1, source_target_pairs={{0,8},{4,12},{8,0},{12,4},{16,24},{20,28},{24,16},{28,20},{1,9},{5... | collective-permute-start | bytes 933896 | tf_op jit(solution)/shard_map/ppermute | solution.py:677
  158.6 5.5 %collective-permute-start.39 = (bf16[16,2176]{1,0:T(8,128)(2,1)S(1)}, bf16[16,2176]{1,0:T(8,128)(2,1)S(1)}, u32[]{:S(2)}, u32[]{:S(2)}) collective-permute-start(bf16[16,2176]{1,0:T(8,128)(2,1)S(1)} %add_convert_fusion.23), channel_id=1, source_target_pairs={{0,8},{4,12},{8,0},{12,4},{16,24},{20,28},{24,16},{28,20},{1,9},{5... | collective-permute-start | bytes 208904 | tf_op jit(solution)/shard_map/ppermute | solution.py:677
  159.9 5.8 %collective-permute-start.41 = (bf16[16,2176]{1,0:T(8,128)(2,1)S(1)}, bf16[16,2176]{1,0:T(8,128)(2,1)S(1)}, u32[]{:S(2)}, u32[]{:S(2)}) collective-permute-start(bf16[16,2176]{1,0:T(8,128)(2,1)S(1)} %add_convert_fusion.23), channel_id=1, source_target_pairs={{0,24},{4,28},{8,16},{12,20},{16,8},{20,12},{24,0},{28,4},{1,25},{... | collective-permute-start | bytes 208904 | tf_op jit(solution)/shard_map/ppermute | solution.py:677
  161.4 5.0 %collective-permute-start.40 = (bf16[16,2176]{1,0:T(8,128)(2,1)S(1)}, bf16[16,2176]{1,0:T(8,128)(2,1)S(1)}, u32[]{:S(2)}, u32[]{:S(2)}) collective-permute-start(bf16[16,2176]{1,0:T(8,128)(2,1)S(1)} %add_convert_fusion.23), channel_id=1, source_target_pairs={{0,16},{4,20},{8,24},{12,28},{16,0},{20,4},{24,8},{28,12},{1,17},{... | collective-permute-start | bytes 208904 | tf_op jit(solution)/shard_map/ppermute | solution.py:677
  164.3 2.3 %collective-permute-start.44 = (bf16[4,16,4864]{2,1,0:T(8,128)(2,1)S(1)}, bf16[4,16,4864]{2,1,0:T(8,128)(2,1)S(1)}, u32[]{:S(2)}, u32[]{:S(2)}) collective-permute-start(bf16[4,16,4864]{2,1,0:T(8,128)(2,1)S(1)} %bitcast.103), channel_id=1, source_target_pairs={{0,4},{4,0},{8,12},{12,8},{16,20},{20,16},{24,28},{28,24},{1,5},{5... | collective-permute-start | bytes 1867784 | tf_op jit(solution)/shard_map/ppermute | solution.py:677
  166.4 2.2 %collective-permute-start.42 = (bf16[4,16,2176]{2,1,0:T(8,128)(2,1)S(1)}, bf16[4,16,2176]{2,1,0:T(8,128)(2,1)S(1)}, u32[]{:S(2)}, u32[]{:S(2)}) collective-permute-start(bf16[4,16,2176]{2,1,0:T(8,128)(2,1)S(1)} %pad_maximum_fusion.11.near), channel_id=1, source_target_pairs={{0,4},{4,0},{8,12},{12,8},{16,20},{20,16},{24,28},{28,24},{1,5},{5... | collective-permute-start | bytes 835592 | tf_op jit(solution)/shard_map/ppermute | solution.py:677
  (12 other events, 50.4 us)

commit v7 on v6

--- a/solution.py
+++ b/solution.py
@@ -265,21 +265,22 @@
 
 
 def feed_kernel(
-    idx, vec, x, o0, o1, target, up_near_i, up_far_i, down_near_i, down_far_i,
+    idx, vec, x, o0, o1, target, up_near_i, up_far_i, down_near_i, ends_i, sides_i,
     out_o, h_o, slope_o, dy_o, bias_o, keep, send, mix_o, up_o, down_o,
     up_near, up_far, down_near, down_far,
     w_mix, w_up, w_down, w_read, act_s, out_s, h_s, slope_s, dy_s, dl_s, df_s, sems, row_sems,
 ):
     step = pl.program_id(0)
     moves = (
-        (up_near_i, up_near), (up_far_i, up_far), (down_near_i, down_near), (down_far_i, down_far),
+        (up_near_i, up_near), (up_far_i, up_far), (down_near_i, down_near),
+        (ends_i.at[0], down_far.at[0]), (ends_i.at[1], down_far.at[3]), (sides_i, down_far.at[1:3]),
         (w_mix, mix_o), (w_up, up_o), (w_down, down_o),
     )
     copies = [pltpu.make_async_copy(src, dst, sems.at[i]) for i, (src, dst) in enumerate(moves)]
 
     @pl.when(step == 0)
     def _():
-        for copy in copies[:4]:
+        for copy in copies[:6]:
             copy.start()
         for copy in copies[:2]:
             copy.wait()
@@ -287,14 +288,14 @@
             rows = rows_at(shard * 128 + member * PIECE, PIECE)
             w_mix[rows, :] = piece[:, :WIDTH]
             w_up[rows, :] = piece[:, WIDTH:]
-        for copy in copies[2:4]:
+        for copy in copies[2:6]:
             copy.wait()
         for shard, member, piece in each_piece(idx, down_near, down_far):
             for i in range(4):
                 rows = rows_at(shard * 512 + member * 64 + 16 * i, PIECE)
                 w_down[rows, :] = piece[:, i * WIDTH : (i + 1) * WIDTH]
             w_read[rows_at(shard * 128 + member * PIECE, PIECE), :] = piece[:, 4 * WIDTH :]
-        for copy in copies[4:]:
+        for copy in copies[6:]:
             copy.start()
         bias_o[...] = jnp.zeros_like(bias_o)
 
@@ -362,7 +363,7 @@
                     at = slice(i * WIDTH, (i + 1) * WIDTH)
                     keep[xy ^ idx[1], shard ^ idx[2], :, at] = jnp.where(own_first, first, later)
                     send[xy ^ idx[1], shard ^ idx[2], :, at] = jnp.where(own_first, later, first)
-        for copy in copies[4:]:
+        for copy in copies[6:]:
             copy.wait()
         for place in range(act_s.shape[0] // ROWS):
             for copy in row_copies(place):
@@ -829,10 +830,11 @@
         plane_d = [swap(rows_d[:, 0], "dp", dp, 2 * k) for k in range(1, 3)]
         near_u = jnp.stack([rows_u] + plane_u)
         far_u = swap(near_u, "dp", dp, 1)
+        ends_d = swap(jnp.stack([rows_d[:, 0], rows_d[:, 1]]), "dp", dp, 1)
         second = attend(a1, 1)
-        second, far_u, plane_d = pin(second, far_u, plane_d)
+        second, far_u, ends_d, plane_d = pin(second, far_u, ends_d, plane_d)
         near_d = jnp.stack([rows_d[:, 0]] + plane_d + [rows_d[:, 1]])
-        far_d = swap(near_d, "dp", dp, 1)
+        sides_d = swap(jnp.stack(plane_d), "dp", dp, 1)
         halves = (first, second)
         o0, o1 = first[2], second[2]
 
@@ -844,7 +846,8 @@
             "feed_forward",
             [
                 (idx, None), (vec, None), (tokens, wide(WIDTH)), (o0, mixed_at), (o1, mixed_at),
-                (targets, None), (near_u, "hbm"), (far_u, "hbm"), (near_d, "hbm"), (far_d, "hbm"),
+                (targets, None), (near_u, "hbm"), (far_u, "hbm"), (near_d, "hbm"),
+                (ends_d, "hbm"), (sides_d, "hbm"),
             ],
             [
                 ((count, WIDTH), BF16, "hbm"),
@@ -875,7 +878,7 @@
                 pltpu.VMEM((count, WIDTH), F32),
                 pltpu.VMEM((count, VOCAB), BF16),
                 pltpu.VMEM((count, WIDTH), BF16),
-                pltpu.SemaphoreType.DMA((7,)),
+                pltpu.SemaphoreType.DMA((9,)),
                 pltpu.SemaphoreType.DMA((places, 4)),
             ],
             flops=8e9,

time: 171 us -> 170 us (level)
  waiting for transfers between devices: 29.7 us -> 27.8 us
    ppermute x45 -> x46, waiting for transfers between devices: 29.7 us -> 27.8 us  [swap(): return lax.ppermute(value, axis, [(i, i ^ distance) for i in range(size)])]
    ppermute x45 -> x46, starting transfers between devices: 45.4 us -> 45.3 us  [swap(): return lax.ppermute(value, axis, [(i, i ^ distance) for i in range(size)])]
  transfers between devices with their start and end apart: 45 -> 46, of which waited for: 16 -> 17; matrix products, arithmetic and copies ran while one was open for 3% -> 3% of each run, Pallas kernels for 38% -> 39%
where the time goes in v7:
time: 170 us; the launch traced here: 169 us
  Pallas kernels  85.8 us (50%)
  starting transfers between devices  45.3 us (27%)
  waiting for transfers between devices  27.8 us (16%)
  other arithmetic  4.6 us (3%)
  local copies, waits for them, and re-layouts  4.34 us (3%)
    pallas_call x11, Pallas kernels, call(): pl.pallas_call(kernel, grid=grid, in_specs=in_specs, out_specs=[spec(shap...  85.8 us
    ppermute x46, starting transfers between devices, swap(): return lax.ppermute(value, axis, [(i, i ^ distance) for i in range(size)])  45.3 us
    ppermute x46, waiting for transfers between devices, swap(): return lax.ppermute(value, axis, [(i, i ^ distance) for i in range(size)])  27.8 us
  transfers between devices with their start and end apart: 46, of which 17 were waited for; matrix products, arithmetic and copies ran while one was open for 3% of the time, Pallas kernels for 39%

profile of v7, /device:TPU:0, one launch (start us, length us, event | category | flops | bytes accessed | tf_op | source)
XLA Modules:
  0.0 169.2 jit_solution(17122425302772210347)
XLA Ops:
  0.7 2.7 %pack_weights.1 = (bf16[16,2176]{1,0:T(8,128)(2,1)}, bf16[16,2560]{1,0:T(8,128)(2,1)}, bf16[2,16,2304]{2,1,0:T(8,128)(2,1)}) custom-call(bf16[128]{0:T(256)(128)(2,1)} %g1.1, bf16[128]{0:T(256)(128)(2,1)} %b1.1, bf16[128]{0:T(256)(128)(2,1)} %g2.1, bf16[128]{0:T(256)(128)(2,1)} %b2.1, bf16[128]{0:T(256)(128)(2,1)} %bd.1, bf16[512]{0:T(512)(128)(2,1)} %bu.1, ...), custom_call_target="tpu_custom_call" | custom-call | flops 1000 | bytes 1000 | tf_op jit(solution)/shard_map/pack_weights/pallas_call | solution.py:661
  3.4 5.1 %collective-permute-start.2 = (bf16[16,2176]{1,0:T(8,128)(2,1)}, bf16[16,2176]{1,0:T(8,128)(2,1)S(1)}, u32[]{:S(2)}, u32[]{:S(2)}) collective-permute-start(bf16[16,2176]{1,0:T(8,128)(2,1)} %get-tuple-element.153), channel_id=1, source_target_pairs={{0,3},{1,2},{2,1},{3,0},{4,7},{5,6},{6,5},{7,4},{8,11},{9,10},{10,... | collective-permute-start | bytes 208904 | tf_op jit(solution)/shard_map/ppermute | solution.py:678
  9.2 1.4 collective-permute-start.6
  12.1 2.7 %collective-permute-done.1 = bf16[16,2176]{1,0:T(8,128)(2,1)S(1)} collective-permute-done((bf16[16,2176]{1,0:T(8,128)(2,1)}, bf16[16,2176]{1,0:T(8,128)(2,1)S(1)}, u32[]{:S(2)}, u32[]{:S(2)}) %collective-permute-start.1) | collective-permute-done | bytes 69664 | tf_op jit(solution)/shard_map/ppermute | solution.py:678
  15.1 2.7 %collective-permute-start.5 = (bf16[4,16,2048]{2,1,0:T(8,128)(2,1)S(1)}, bf16[4,16,2048]{2,1,0:T(8,128)(2,1)S(1)}, u32[]{:S(2)}, u32[]{:S(2)}) collective-permute-start(bf16[4,16,2048]{2,1,0:T(8,128)(2,1)S(1)} %pad_maximum_fusion.14), channel_id=1, source_target_pairs={{0,24},{4,28},{8,16},{12,20},{16,8},{20,12},{24,0},{28,4},{1,25},{... | collective-permute-start | bytes 786440 | tf_op jit(solution)/shard_map/ppermute | solution.py:678
  19.6 1.3 collective-permute-start.7
  20.9 2.1 %collective-permute-start.12 = (bf16[2,16,2304]{2,1,0:T(8,128)(2,1)S(1)}, bf16[2,16,2304]{2,1,0:T(8,128)(2,1)S(1)}, u32[]{:S(2)}, u32[]{:S(2)}) collective-permute-start(bf16[2,16,2304]{2,1,0:T(8,128)(2,1)S(1)} %copy-done.13), channel_id=1, source_target_pairs={{0,1},{1,0},{2,3},{3,2},{4,5},{5,4},{6,7},{7,6},{8,9},{9,8},{10,11... | collective-permute-start | bytes 442376 | tf_op jit(solution)/shard_map/ppermute | solution.py:678
  23.0 1.8 %first_norm.1 = (bf16[1024,512]{1,0:T(8,128)(2,1)S(1)}, bf16[1040,1024]{1,0:T(8,128)(2,1)S(1)}) custom-call(s32[3]{0:T(128)S(1)} %pad_add_fusion.idx, bf16[4,16,128]{2,1,0:T(8,128)(2,1)S(1)} %pad_maximum_fusion.17.vec, bf16[1024,512]{1,0:T(8,128)(2,1)S(1)} %copy-done), custom_call_target="tpu_custom_call" | custom-call | flops 1000 | bytes 1000 | tf_op jit(solution)/shard_map/first_norm/pallas_call | solution.py:661
  24.8 3.3 %collective-permute-done.7 = bf16[2,16,2560]{2,1,0:T(8,128)(2,1)S(1)} collective-permute-done((bf16[2,16,2560]{2,1,0:T(8,128)(2,1)S(1)}, bf16[2,16,2560]{2,1,0:T(8,128)(2,1)S(1)}, u32[]{:S(2)}, u32[]{:S(2)}) %collective-permute-start.7) | collective-permute-done | bytes 163872 | tf_op jit(solution)/shard_map/ppermute | solution.py:678
  28.2 1.0 collective-permute-done.4
  30.4 1.6 collective-permute-start.11
  32.0 1.4 collective-permute-start.10
  34.0 8.6 %attend.2 = (bf16[1024,1024]{1,0:T(8,128)(2,1)S(1)}, f32[1024,1024]{1,0:T(8,128)}, bf16[1024,512]{1,0:T(8,128)(2,1)S(1)}, bf16[8,2,128,256]{3,2,1,0:T(8,128)(2,1)S(1)}, bf16[512,1024]{1,0:T(8,128)(2,1)S(1)}) custom-call(s32[3]{0:T(128)S(1)} %pad_add_fusion.idx, bf16[1024,512]{1,0:T(8,128)(2,1)S(1)} %get-tuple-element.175.a1, ...), custom_call_target="tpu_custom_call" | custom-call | flops 1000 | bytes 1000 | tf_op jit(solution)/shard_map/attend/pallas_call | solution.py:661
  42.6 5.9 %collective-permute-done.13 = bf16[2,2,16,2304]{3,2,0,1:T(8,128)(2,1)S(1)} collective-permute-done((bf16[2,2,16,2304]{3,2,0,1:T(8,128)(2,1)S(1)}, bf16[2,2,16,2304]{3,2,0,1:T(8,128)(2,1)S(1)}, u32[]{:S(2)}, u32[]{:S(2)}) %collective-permute-start.13) | collective-permute-done | bytes 294944 | tf_op jit(solution)/shard_map/ppermute | solution.py:678
  49.8 1.4 collective-permute-start.17
  52.0 8.3 %attend.3 = (bf16[1024,1024]{1,0:T(8,128)(2,1)S(1)}, f32[1024,1024]{1,0:T(8,128)}, bf16[1024,512]{1,0:T(8,128)(2,1)S(1)}, bf16[8,2,128,256]{3,2,1,0:T(8,128)(2,1)S(1)}, bf16[512,1024]{1,0:T(8,128)(2,1)S(1)}) custom-call(s32[3]{0:T(128)S(1)} %pad_add_fusion.idx, bf16[1024,512]{1,0:T(8,128)(2,1)S(1)} %get-tuple-element.175.a1, ...), custom_call_target="tpu_custom_call" | custom-call | flops 1000 | bytes 1000 | tf_op jit(solution)/shard_map/attend/pallas_call | solution.py:661
  60.4 1.1 copy-done.11
  61.7 1.2 pad_maximum_fusion.1.down_near_i
  63.7 16.2 %feed_forward.1 = (bf16[1024,512]{1,0:T(8,128)(2,1)}, f32[1024,512]{1,0:T(8,128)}, bf16[1024,2048]{1,0:T(8,128)(2,1)}, f32[1024,512]{1,0:T(8,128)}, f32[1,512]{1...) custom-call(s32[3]{0:T(128)S(1)} %pad_add_fusion.idx, ...), custom_call_target="tpu_custom_call" | custom-call | flops 1000 | bytes 1000 | tf_op jit(solution)/shard_map/feed_forward/pallas_call | solution.py:661
  80.0 13.0 %feed_backward.1 = (f32[1024,512]{1,0:T(8,128)}, bf16[1024,512]{1,0:T(8,128)(2,1)S(1)}, f32[1,512]{1,0:T(1,128)S(1)}, f32[1,512]{1,0:T(1,128)S(1)}, f32[1,2048]{...) custom-call(s32[3]{0:T(128)S(1)} %pad_add_fusion.idx, ...), custom_call_target="tpu_custom_call" | custom-call | flops 1000 | bytes 1000 | tf_op jit(solution)/shard_map/feed_backward/pallas_call | solution.py:661
  93.6 1.3 collective-permute-start.20
  94.9 0.9 collective-permute-start.21
  95.9 1.3 collective-permute-start.22
  97.2 13.1 %attend_backward.2 = (bf16[1024,1024]{1,0:T(8,128)(2,1)S(1)}, bf16[4,4,16,1024]{3,2,1,0:T(8,128)(2,1)S(1)}, bf16[4,4,16,1024]{3,2,1,0:T(8,128)(2,1)S(1)}, f32[8,512]{1,0:T(8,128)S(1)}) custom-call(s32[3]{0:T(128)S(1)} %pad_add_fusion.idx, bf16[1040,1024]{1,0:T(8,128)(2,1)} %copy-done.1, bf16[512,1024]{1,0:T(8,128)(2,1)S(1)} %get-tuple-element.209.w.w0, ...), custom_call_target="tpu_custom_call" | custom-call | flops 1000 | bytes 1000 | tf_op jit(solution)/shard_map/attend_backward/pallas_call | solution.py:661
  111.0 1.3 collective-permute-start.25
  112.3 0.9 collective-permute-start.26
  113.3 1.3 collective-permute-start.27
  114.6 13.3 %attend_backward.3 = (bf16[1024,1024]{1,0:T(8,128)(2,1)S(1)}, bf16[4,4,16,1152]{3,2,1,0:T(8,128)(2,1)S(1)}, bf16[4,4,16,1152]{3,2,1,0:T(8,128)(2,1)S(1)}) custom-call(s32[3]{0:T(128)S(1)} %pad_add_fusion.idx, bf16[1040,1024]{1,0:T(8,128)(2,1)} %copy-done.1, bf16[512,1024]{1,0:T(8,128)(2,1)S(1)} %get-tuple-element.227.w.w1, bf16[1024,1024]{1,0:T(8,128)(2,1)S(1)} %copy-done.4, ...), custom_call_target="tpu_custom_call" | custom-call | flops 1000 | bytes 1000 | tf_op jit(solution)/shard_map/attend_backward/pallas_call | solution.py:661
  128.0 1.2 collective-permute-done.26
  129.4 1.8 %collective-permute-done.29 = bf16[4,4,16,1152]{3,2,1,0:T(8,128)(2,1)S(1)} collective-permute-done((bf16[4,4,16,1152]{3,2,1,0:T(8,128)(2,1)S(1)}, bf16[4,4,16,1152]{3,2,1,0:T(8,128)(2,1)S(1)}, u32[]{:S(2)}, u32[]{:S(2)}) %collective-permute-start.29) | collective-permute-done | bytes 589856 | tf_op jit(solution)/shard_map/ppermute | solution.py:678
  131.7 1.6 collective-permute-start.30
  133.3 1.1 collective-permute-start.31
  135.2 1.1 collective-permute-start.33
  136.3 1.5 collective-permute-start.34
  137.8 4.9 %input_gradient.1 = f32[1024,512]{1,0:T(8,128)} custom-call(s32[3]{0:T(128)S(1)} %pad_add_fusion.idx, bf16[4,16,128]{2,1,0:T(8,128)(2,1)S(1)} %pad_maximum_fusion.17.vec, bf16[1024,512]{1,0:T(8,128)(2,1)S(1)} %copy-done, f32[1024,512]{1,0:T(8,128)S(1)} %copy-done.2, bf16[1024,1024]{1,0:T(8,128)(2,1)S(1)} %get-tuple-element.258.dx0, ...), custom_call_target="tpu_custom_call" | custom-call | flops 1000 | bytes 1000 | tf_op jit(solution)/shard_map/input_gradient/pallas_call | solution.py:661
  142.8 1.1 collective-permute-start.35
  143.9 3.4 %collective-permute-done.35 = bf16[16,2560]{1,0:T(8,128)(2,1)S(1)} collective-permute-done((bf16[16,2560]{1,0:T(8,128)(2,1)S(1)}, bf16[16,2560]{1,0:T(8,128)(2,1)S(1)}, u32[]{:S(2)}, u32[]{:S(2)}) %collective-permute-start.35) | collective-permute-done | bytes 81952 | tf_op jit(solution)/shard_map/ppermute | solution.py:678
  149.3 1.7 %collective-permute-start.38 = (bf16[16,2176]{1,0:T(8,128)(2,1)S(1)}, bf16[16,2176]{1,0:T(8,128)(2,1)S(1)}, u32[]{:S(2)}, u32[]{:S(2)}) collective-permute-start(bf16[16,2176]{1,0:T(8,128)(2,1)S(1)} %get-tuple-element.305), channel_id=1, source_target_pairs={{0,3},{1,2},{2,1},{3,0},{4,7},{5,6},{6,5},{7,4},{8,11},{9,10},{10,... | collective-permute-start | bytes 208904 | tf_op jit(solution)/shard_map/ppermute | solution.py:678
  151.0 1.1 collective-permute-start.37
  152.2 1.6 collective-permute-start.36
  153.8 1.2 collective-permute-start.44
  155.6 1.7 collective-permute-done.37
  157.3 1.2 collective-permute-start.40
  158.5 1.5 collective-permute-start.42
  160.9 2.2 %collective-permute-done.40 = bf16[16,2176]{1,0:T(8,128)(2,1)S(1)} collective-permute-done((bf16[16,2176]{1,0:T(8,128)(2,1)S(1)}, bf16[16,2176]{1,0:T(8,128)(2,1)S(1)}, u32[]{:S(2)}, u32[]{:S(2)}) %collective-permute-start.40) | collective-permute-done | bytes 69664 | tf_op jit(solution)/shard_map/ppermute | solution.py:678
  163.2 1.1 collective-permute-done.42
  165.3 2.1 %unpack_feed.1 = (f32[128,512]{1,0:T(8,128)}, f32[128,2048]{1,0:T(8,128)}, f32[512,512]{1,0:T(8,128)}, f32[128,256]{1,0:T(8,128)}) custom-call(s32[3]{0:T(128)S(1)} %pad_add_fusion.idx, bf16[4,16,4864]{2,1,0:T(8,128)(2,1)S(1)} %bitcast.104, bf16[4,16,4864]{2,1,0:T(8,128)(2,1)S(1)} %collective-permute-done.45.far), custom_call_target="tpu_custom_call" | custom-call | flops 1000 | bytes 1000 | tf_op jit(solution)/shard_map/unpack_feed/pallas_call | solution.py:661
  167.4 1.6 unpack_proj.1
  (126 shorter events, 16.7 us)
Async XLA Ops:
  0.7 22.4 %copy-start = (bf16[1024,512]{1,0:T(8,128)(2,1)S(1)}, bf16[1024,512]{1,0:T(8,128)(2,1)}, u32[]{:S(2)}) copy-start(bf16[1024,512]{1,0:T(8,128)(2,1)} %x.4) | copy-start | bytes 3145732
  3.4 17.5 %copy-start.13 = (bf16[2,16,2304]{2,1,0:T(8,128)(2,1)S(1)}, bf16[2,16,2304]{2,1,0:T(8,128)(2,1)}, u32[]{:S(2)}) copy-start(bf16[2,16,2304]{2,1,0:T(8,128)(2,1)} %get-tuple-element.172) | copy-start | bytes 442372
  3.4 8.7 %collective-permute-start.2 = (bf16[16,2176]{1,0:T(8,128)(2,1)}, bf16[16,2176]{1,0:T(8,128)(2,1)S(1)}, u32[]{:S(2)}, u32[]{:S(2)}) collective-permute-start(bf16[16,2176]{1,0:T(8,128)(2,1)} %get-tuple-element.153), channel_id=1, source_target_pairs={{0,3},{1,2},{2,1},{3,0},{4,7},{5,6},{6,5},{7,4},{8,11},{9,10},{10,... | collective-permute-start | bytes 208904 | tf_op jit(solution)/shard_map/ppermute | solution.py:678
  8.5 6.2 %collective-permute-start.1 = (bf16[16,2176]{1,0:T(8,128)(2,1)}, bf16[16,2176]{1,0:T(8,128)(2,1)S(1)}, u32[]{:S(2)}, u32[]{:S(2)}) collective-permute-start(bf16[16,2176]{1,0:T(8,128)(2,1)} %get-tuple-element.153), channel_id=1, source_target_pairs={{0,2},{1,3},{2,0},{3,1},{4,6},{5,7},{6,4},{7,5},{8,10},{9,11},{10,... | collective-permute-start | bytes 208904 | tf_op jit(solution)/shard_map/ppermute | solution.py:678
  8.5 6.5 %collective-permute-start = (bf16[16,2176]{1,0:T(8,128)(2,1)}, bf16[16,2176]{1,0:T(8,128)(2,1)S(1)}, u32[]{:S(2)}, u32[]{:S(2)}) collective-permute-start(bf16[16,2176]{1,0:T(8,128)(2,1)} %get-tuple-element.153), channel_id=1, source_target_pairs={{0,1},{1,0},{2,3},{3,2},{4,5},{5,4},{6,7},{7,6},{8,9},{9,8},{10,11... | collective-permute-start | bytes 208904 | tf_op jit(solution)/shard_map/ppermute | solution.py:678
  9.2 9.5 %collective-permute-start.6 = (bf16[16,2560]{1,0:T(8,128)(2,1)}, bf16[16,2560]{1,0:T(8,128)(2,1)S(1)}, u32[]{:S(2)}, u32[]{:S(2)}) collective-permute-start(bf16[16,2560]{1,0:T(8,128)(2,1)} %get-tuple-element.157), channel_id=1, source_target_pairs={{0,1},{1,0},{2,3},{3,2},{4,5},{5,4},{6,7},{7,6},{8,9},{9,8},{10,11... | collective-permute-start | bytes 245768 | tf_op jit(solution)/shard_map/ppermute | solution.py:678
  15.1 13.1 %collective-permute-start.5 = (bf16[4,16,2048]{2,1,0:T(8,128)(2,1)S(1)}, bf16[4,16,2048]{2,1,0:T(8,128)(2,1)S(1)}, u32[]{:S(2)}, u32[]{:S(2)}) collective-permute-start(bf16[4,16,2048]{2,1,0:T(8,128)(2,1)S(1)} %pad_maximum_fusion.14), channel_id=1, source_target_pairs={{0,24},{4,28},{8,16},{12,20},{16,8},{20,12},{24,0},{28,4},{1,25},{... | collective-permute-start | bytes 786440 | tf_op jit(solution)/shard_map/ppermute | solution.py:678
  17.8 11.4 %collective-permute-start.4 = (bf16[4,16,2048]{2,1,0:T(8,128)(2,1)S(1)}, bf16[4,16,2048]{2,1,0:T(8,128)(2,1)S(1)}, u32[]{:S(2)}, u32[]{:S(2)}) collective-permute-start(bf16[4,16,2048]{2,1,0:T(8,128)(2,1)S(1)} %pad_maximum_fusion.14), channel_id=1, source_target_pairs={{0,16},{4,20},{8,24},{12,28},{16,0},{20,4},{24,8},{28,12},{1,17},{... | collective-permute-start | bytes 786440 | tf_op jit(solution)/shard_map/ppermute | solution.py:678
  18.3 11.2 %collective-permute-start.3 = (bf16[4,16,2048]{2,1,0:T(8,128)(2,1)S(1)}, bf16[4,16,2048]{2,1,0:T(8,128)(2,1)S(1)}, u32[]{:S(2)}, u32[]{:S(2)}) collective-permute-start(bf16[4,16,2048]{2,1,0:T(8,128)(2,1)S(1)} %pad_maximum_fusion.14), channel_id=1, source_target_pairs={{0,8},{4,12},{8,0},{12,4},{16,24},{20,28},{24,16},{28,20},{1,9},{5... | collective-permute-start | bytes 786440 | tf_op jit(solution)/shard_map/ppermute | solution.py:678
  19.6 8.6 %collective-permute-start.7 = (bf16[2,16,2560]{2,1,0:T(8,128)(2,1)S(1)}, bf16[2,16,2560]{2,1,0:T(8,128)(2,1)S(1)}, u32[]{:S(2)}, u32[]{:S(2)}) collective-permute-start(bf16[2,16,2560]{2,1,0:T(8,128)(2,1)S(1)} %pad_maximum_fusion.15), channel_id=1, source_target_pairs={{0,2},{1,3},{2,0},{3,1},{4,6},{5,7},{6,4},{7,5},{8,10},{9,11},{10,... | collective-permute-start | bytes 491528 | tf_op jit(solution)/shard_map/ppermute | solution.py:678
  20.9 8.8 %collective-permute-start.12 = (bf16[2,16,2304]{2,1,0:T(8,128)(2,1)S(1)}, bf16[2,16,2304]{2,1,0:T(8,128)(2,1)S(1)}, u32[]{:S(2)}, u32[]{:S(2)}) collective-permute-start(bf16[2,16,2304]{2,1,0:T(8,128)(2,1)S(1)} %copy-done.13), channel_id=1, source_target_pairs={{0,1},{1,0},{2,3},{3,2},{4,5},{5,4},{6,7},{7,6},{8,9},{9,8},{10,11... | collective-permute-start | bytes 442376 | tf_op jit(solution)/shard_map/ppermute | solution.py:678
  29.6 4.4 %collective-permute-start.8 = (bf16[4,4,16,2048]{3,2,1,0:T(8,128)(2,1)S(1)}, bf16[4,4,16,2048]{3,2,1,0:T(8,128)(2,1)S(1)}, u32[]{:S(2)}, u32[]{:S(2)}) collective-permute-start(bf16[4,4,16,2048]{3,2,1,0:T(8,128)(2,1)S(1)} %pad_maximum_fusion.2.near), channel_id=1, source_target_pairs={{0,4},{4,0},{8,12},{12,8},{16,20},{20,16},{24,28},{28,24},{1,5},{5... | collective-permute-start | bytes 3145736 | tf_op jit(solution)/shard_map/ppermute | solution.py:678
  30.4 18.1 %collective-permute-start.11 = (bf16[4,16,2560]{2,1,0:T(8,128)(2,1)S(1)}, bf16[4,16,2560]{2,1,0:T(8,128)(2,1)S(1)}, u32[]{:S(2)}, u32[]{:S(2)}) collective-permute-start(bf16[4,16,2560]{2,1,0:T(8,128)(2,1)S(1)} %get-tuple-element.316), channel_id=1, source_target_pairs={{0,24},{4,28},{8,16},{12,20},{16,8},{20,12},{24,0},{28,4},{1,25},{... | collective-permute-start | bytes 983048 | tf_op jit(solution)/shard_map/ppermute | solution.py:678
  32.0 16.5 %collective-permute-start.10 = (bf16[4,16,2560]{2,1,0:T(8,128)(2,1)S(1)}, bf16[4,16,2560]{2,1,0:T(8,128)(2,1)S(1)}, u32[]{:S(2)}, u32[]{:S(2)}) collective-permute-start(bf16[4,16,2560]{2,1,0:T(8,128)(2,1)S(1)} %get-tuple-element.316), channel_id=1, source_target_pairs={{0,16},{4,20},{8,24},{12,28},{16,0},{20,4},{24,8},{28,12},{1,17},{... | collective-permute-start | bytes 983048 | tf_op jit(solution)/shard_map/ppermute | solution.py:678
  33.4 15.1 %collective-permute-start.9 = (bf16[4,16,2560]{2,1,0:T(8,128)(2,1)S(1)}, bf16[4,16,2560]{2,1,0:T(8,128)(2,1)S(1)}, u32[]{:S(2)}, u32[]{:S(2)}) collective-permute-start(bf16[4,16,2560]{2,1,0:T(8,128)(2,1)S(1)} %get-tuple-element.316), channel_id=1, source_target_pairs={{0,8},{4,12},{8,0},{12,4},{16,24},{20,28},{24,16},{28,20},{1,9},{5... | collective-permute-start | bytes 983048 | tf_op jit(solution)/shard_map/ppermute | solution.py:678
  34.0 14.5 %collective-permute-start.13 = (bf16[2,2,16,2304]{3,2,0,1:T(8,128)(2,1)S(1)}, bf16[2,2,16,2304]{3,2,0,1:T(8,128)(2,1)S(1)}, u32[]{:S(2)}, u32[]{:S(2)}) collective-permute-start(bf16[2,2,16,2304]{3,2,0,1:T(8,128)(2,1)S(1)} %pad_maximum_fusion.8), channel_id=1, source_target_pairs={{0,2},{1,3},{2,0},{3,1},{4,6},{5,7},{6,4},{7,5},{8,10},{9,11},{10,... | collective-permute-start | bytes 884744 | tf_op jit(solution)/shard_map/ppermute | solution.py:678
  48.7 11.7 %collective-permute-start.14 = (bf16[4,4,16,2560]{3,2,1,0:T(8,128)(2,1)S(1)}, bf16[4,4,16,2560]{3,2,1,0:T(8,128)(2,1)S(1)}, u32[]{:S(2)}, u32[]{:S(2)}) collective-permute-start(bf16[4,4,16,2560]{3,2,1,0:T(8,128)(2,1)S(1)} %pad_maximum_fusion.up_near_i), channel_id=1, source_target_pairs={{0,4},{4,0},{8,12},{12,8},{16,20},{20,16},{24,28},{28,24},{1,5},{5... | collective-permute-start | bytes 3932168 | tf_op jit(solution)/shard_map/ppermute | solution.py:678
  49.8 10.6 %collective-permute-start.15 = (bf16[2,4,16,2304]{3,2,1,0:T(8,128)(2,1)S(1)}, bf16[2,4,16,2304]{3,2,1,0:T(8,128)(2,1)S(1)}, u32[]{:S(2)}, u32[]{:S(2)}) collective-permute-start(bf16[2,4,16,2304]{3,2,1,0:T(8,128)(2,1)S(1)} %pad_maximum_fusion.4), channel_id=1, source_target_pairs={{0,4},{4,0},{8,12},{12,8},{16,20},{20,16},{24,28},{28,24},{1,5},{5... | collective-permute-start | bytes 1769480 | tf_op jit(solution)/shard_map/ppermute | solution.py:678
  49.8 10.6 %collective-permute-start.17 = (bf16[4,16,2304]{2,1,0:T(8,128)(2,1)S(1)}, bf16[4,16,2304]{2,1,0:T(8,128)(2,1)S(1)}, u32[]{:S(2)}, u32[]{:S(2)}) collective-permute-start(bf16[4,16,2304]{2,1,0:T(8,128)(2,1)S(1)} %get-tuple-element.312), channel_id=1, source_target_pairs={{0,16},{4,20},{8,24},{12,28},{16,0},{20,4},{24,8},{28,12},{1,17},{... | collective-permute-start | bytes 884744 | tf_op jit(solution)/shard_map/ppermute | solution.py:678
  51.2 9.1 %collective-permute-start.16 = (bf16[4,16,2304]{2,1,0:T(8,128)(2,1)S(1)}, bf16[4,16,2304]{2,1,0:T(8,128)(2,1)S(1)}, u32[]{:S(2)}, u32[]{:S(2)}) collective-permute-start(bf16[4,16,2304]{2,1,0:T(8,128)(2,1)S(1)} %get-tuple-element.312), channel_id=1, source_target_pairs={{0,8},{4,12},{8,0},{12,4},{16,24},{20,28},{24,16},{28,20},{1,9},{5... | collective-permute-start | bytes 884744 | tf_op jit(solution)/shard_map/ppermute | solution.py:678
  61.6 2.1 %collective-permute-start.18 = (bf16[2,4,16,2304]{3,2,1,0:T(8,128)(2,1)S(1)}, bf16[2,4,16,2304]{3,2,1,0:T(8,128)(2,1)S(1)}, u32[]{:S(2)}, u32[]{:S(2)}) collective-permute-start(bf16[2,4,16,2304]{3,2,1,0:T(8,128)(2,1)S(1)} %pad_maximum_fusion.5), channel_id=1, source_target_pairs={{0,4},{4,0},{8,12},{12,8},{16,20},{20,16},{24,28},{28,24},{1,5},{5... | collective-permute-start | bytes 1769480 | tf_op jit(solution)/shard_map/ppermute | solution.py:678
  79.8 13.2 %collective-permute-start.19 = (bf16[4,4,16,2304]{3,2,1,0:T(8,128)(2,1)S(1)}, bf16[4,4,16,2304]{3,2,1,0:T(8,128)(2,1)S(1)}, u32[]{:S(2)}, u32[]{:S(2)}) collective-permute-start(bf16[4,4,16,2304]{3,2,1,0:T(8,128)(2,1)S(1)} %get-tuple-element.199), channel_id=1, source_target_pairs={{0,4},{4,0},{8,12},{12,8},{16,20},{20,16},{24,28},{28,24},{1,5},{5... | collective-permute-start | bytes 3538952 | tf_op jit(solution)/shard_map/ppermute | solution.py:678
  93.0 17.3 %collective-permute-start.23 = (bf16[4,4,16,2560]{3,2,1,0:T(8,128)(2,1)S(1)}, bf16[4,4,16,2560]{3,2,1,0:T(8,128)(2,1)S(1)}, u32[]{:S(2)}, u32[]{:S(2)}) collective-permute-start(bf16[4,4,16,2560]{3,2,1,0:T(8,128)(2,1)S(1)} %get-tuple-element.207), channel_id=1, source_target_pairs={{0,4},{4,0},{8,12},{12,8},{16,20},{20,16},{24,28},{28,24},{1,5},{5... | collective-permute-start | bytes 3932168 | tf_op jit(solution)/shard_map/ppermute | solution.py:678
  93.6 16.7 %collective-permute-start.20 = (bf16[4,16,2304]{2,1,0:T(8,128)(2,1)S(1)}, bf16[4,16,2304]{2,1,0:T(8,128)(2,1)S(1)}, u32[]{:S(2)}, u32[]{:S(2)}) collective-permute-start(bf16[4,16,2304]{2,1,0:T(8,128)(2,1)S(1)} %get-tuple-element.204), channel_id=1, source_target_pairs={{0,8},{4,12},{8,0},{12,4},{16,24},{20,28},{24,16},{28,20},{1,9},{5... | collective-permute-start | bytes 884744 | tf_op jit(solution)/shard_map/ppermute | solution.py:678
  94.9 15.4 %collective-permute-start.21 = (bf16[4,16,2304]{2,1,0:T(8,128)(2,1)S(1)}, bf16[4,16,2304]{2,1,0:T(8,128)(2,1)S(1)}, u32[]{:S(2)}, u32[]{:S(2)}) collective-permute-start(bf16[4,16,2304]{2,1,0:T(8,128)(2,1)S(1)} %get-tuple-element.205), channel_id=1, source_target_pairs={{0,16},{4,20},{8,24},{12,28},{16,0},{20,4},{24,8},{28,12},{1,17},{... | collective-permute-start | bytes 884744 | tf_op jit(solution)/shard_map/ppermute | solution.py:678
  95.9 14.4 %collective-permute-start.22 = (bf16[4,16,2304]{2,1,0:T(8,128)(2,1)S(1)}, bf16[4,16,2304]{2,1,0:T(8,128)(2,1)S(1)}, u32[]{:S(2)}, u32[]{:S(2)}) collective-permute-start(bf16[4,16,2304]{2,1,0:T(8,128)(2,1)S(1)} %get-tuple-element.206), channel_id=1, source_target_pairs={{0,24},{4,28},{8,16},{12,20},{16,8},{20,12},{24,0},{28,4},{1,25},{... | collective-permute-start | bytes 884744 | tf_op jit(solution)/shard_map/ppermute | solution.py:678
  110.3 18.9 %collective-permute-start.28 = (bf16[4,4,16,1024]{3,2,1,0:T(8,128)(2,1)S(1)}, bf16[4,4,16,1024]{3,2,1,0:T(8,128)(2,1)S(1)}, u32[]{:S(2)}, u32[]{:S(2)}) collective-permute-start(bf16[4,4,16,1024]{3,2,1,0:T(8,128)(2,1)S(1)} %get-tuple-element.226), channel_id=1, source_target_pairs={{0,4},{4,0},{8,12},{12,8},{16,20},{20,16},{24,28},{28,24},{1,5},{5... | collective-permute-start | bytes 1572872 | tf_op jit(solution)/shard_map/ppermute | solution.py:678
  111.0 16.9 %collective-permute-start.25 = (bf16[4,16,2560]{2,1,0:T(8,128)(2,1)S(1)}, bf16[4,16,2560]{2,1,0:T(8,128)(2,1)S(1)}, u32[]{:S(2)}, u32[]{:S(2)}) collective-permute-start(bf16[4,16,2560]{2,1,0:T(8,128)(2,1)S(1)} %get-tuple-element.223), channel_id=1, source_target_pairs={{0,8},{4,12},{8,0},{12,4},{16,24},{20,28},{24,16},{28,20},{1,9},{5... | collective-permute-start | bytes 983048 | tf_op jit(solution)/shard_map/ppermute | solution.py:678
  112.3 16.8 %collective-permute-start.26 = (bf16[4,16,2560]{2,1,0:T(8,128)(2,1)S(1)}, bf16[4,16,2560]{2,1,0:T(8,128)(2,1)S(1)}, u32[]{:S(2)}, u32[]{:S(2)}) collective-permute-start(bf16[4,16,2560]{2,1,0:T(8,128)(2,1)S(1)} %get-tuple-element.224), channel_id=1, source_target_pairs={{0,16},{4,20},{8,24},{12,28},{16,0},{20,4},{24,8},{28,12},{1,17},{... | collective-permute-start | bytes 983048 | tf_op jit(solution)/shard_map/ppermute | solution.py:678
  113.3 15.9 %collective-permute-start.27 = (bf16[4,16,2560]{2,1,0:T(8,128)(2,1)S(1)}, bf16[4,16,2560]{2,1,0:T(8,128)(2,1)S(1)}, u32[]{:S(2)}, u32[]{:S(2)}) collective-permute-start(bf16[4,16,2560]{2,1,0:T(8,128)(2,1)S(1)} %get-tuple-element.225), channel_id=1, source_target_pairs={{0,24},{4,28},{8,16},{12,20},{16,8},{20,12},{24,0},{28,4},{1,25},{... | collective-permute-start | bytes 983048 | tf_op jit(solution)/shard_map/ppermute | solution.py:678
  114.6 13.3 %collective-permute-start.24 = (bf16[2,16,2304]{2,1,0:T(8,128)(2,1)S(1)}, bf16[2,16,2304]{2,1,0:T(8,128)(2,1)S(1)}, u32[]{:S(2)}, u32[]{:S(2)}) collective-permute-start(bf16[2,16,2304]{2,1,0:T(8,128)(2,1)S(1)} %get-tuple-element.222), channel_id=1, source_target_pairs={{0,2},{1,3},{2,0},{3,1},{4,6},{5,7},{6,4},{7,5},{8,10},{9,11},{10,... | collective-permute-start | bytes 442376 | tf_op jit(solution)/shard_map/ppermute | solution.py:678
  129.2 2.0 %collective-permute-start.29 = (bf16[4,4,16,1152]{3,2,1,0:T(8,128)(2,1)S(1)}, bf16[4,4,16,1152]{3,2,1,0:T(8,128)(2,1)S(1)}, u32[]{:S(2)}, u32[]{:S(2)}) collective-permute-start(bf16[4,4,16,1152]{3,2,1,0:T(8,128)(2,1)S(1)} %get-tuple-element.246), channel_id=1, source_target_pairs={{0,4},{4,0},{8,12},{12,8},{16,20},{20,16},{24,28},{28,24},{1,5},{5... | collective-permute-start | bytes 1769480 | tf_op jit(solution)/shard_map/ppermute | solution.py:678
  131.7 11.1 %collective-permute-start.30 = (bf16[2,16,2560]{2,1,0:T(8,128)(2,1)S(1)}, bf16[2,16,2560]{2,1,0:T(8,128)(2,1)S(1)}, u32[]{:S(2)}, u32[]{:S(2)}) collective-permute-start(bf16[2,16,2560]{2,1,0:T(8,128)(2,1)S(1)} %slice.297), channel_id=1, source_target_pairs={{0,2},{1,3},{2,0},{3,1},{4,6},{5,7},{6,4},{7,5},{8,10},{9,11},{10,... | collective-permute-start | bytes 491528 | tf_op jit(solution)/shard_map/ppermute | solution.py:678
  133.3 9.5 %collective-permute-start.31 = (bf16[16,2304]{1,0:T(8,128)(2,1)S(1)}, bf16[16,2304]{1,0:T(8,128)(2,1)S(1)}, u32[]{:S(2)}, u32[]{:S(2)}) collective-permute-start(bf16[16,2304]{1,0:T(8,128)(2,1)S(1)} %fusion.19), channel_id=1, source_target_pairs={{0,1},{1,0},{2,3},{3,2},{4,5},{5,4},{6,7},{7,6},{8,9},{9,8},{10,11... | collective-permute-start | bytes 221192 | tf_op jit(solution)/shard_map/ppermute | solution.py:678
  134.3 14.0 %collective-permute-start.32 = (bf16[4,16,2176]{2,1,0:T(8,128)(2,1)S(1)}, bf16[4,16,2176]{2,1,0:T(8,128)(2,1)S(1)}, u32[]{:S(2)}, u32[]{:S(2)}) collective-permute-start(bf16[4,16,2176]{2,1,0:T(8,128)(2,1)S(1)} %get-tuple-element.249), channel_id=1, source_target_pairs={{0,8},{4,12},{8,0},{12,4},{16,24},{20,28},{24,16},{28,20},{1,9},{5... | collective-permute-start | bytes 835592 | tf_op jit(solution)/shard_map/ppermute | solution.py:678
  135.2 14.0 %collective-permute-start.33 = (bf16[4,16,2176]{2,1,0:T(8,128)(2,1)S(1)}, bf16[4,16,2176]{2,1,0:T(8,128)(2,1)S(1)}, u32[]{:S(2)}, u32[]{:S(2)}) collective-permute-start(bf16[4,16,2176]{2,1,0:T(8,128)(2,1)S(1)} %get-tuple-element.250), channel_id=1, source_target_pairs={{0,16},{4,20},{8,24},{12,28},{16,0},{20,4},{24,8},{28,12},{1,17},{... | collective-permute-start | bytes 835592 | tf_op jit(solution)/shard_map/ppermute | solution.py:678
  136.3 12.8 %collective-permute-start.34 = (bf16[4,16,2176]{2,1,0:T(8,128)(2,1)S(1)}, bf16[4,16,2176]{2,1,0:T(8,128)(2,1)S(1)}, u32[]{:S(2)}, u32[]{:S(2)}) collective-permute-start(bf16[4,16,2176]{2,1,0:T(8,128)(2,1)S(1)} %get-tuple-element.251), channel_id=1, source_target_pairs={{0,24},{4,28},{8,16},{12,20},{16,8},{20,12},{24,0},{28,4},{1,25},{... | collective-permute-start | bytes 835592 | tf_op jit(solution)/shard_map/ppermute | solution.py:678
  142.8 4.5 %collective-permute-start.35 = (bf16[16,2560]{1,0:T(8,128)(2,1)S(1)}, bf16[16,2560]{1,0:T(8,128)(2,1)S(1)}, u32[]{:S(2)}, u32[]{:S(2)}) collective-permute-start(bf16[16,2560]{1,0:T(8,128)(2,1)S(1)} %fusion.18), channel_id=1, source_target_pairs={{0,1},{1,0},{2,3},{3,2},{4,5},{5,4},{6,7},{7,6},{8,9},{9,8},{10,11... | collective-permute-start | bytes 245768 | tf_op jit(solution)/shard_map/ppermute | solution.py:678
  147.4 6.4 %collective-permute-start.39 = (bf16[16,4864]{1,0:T(8,128)(2,1)S(1)}, bf16[16,4864]{1,0:T(8,128)(2,1)S(1)}, u32[]{:S(2)}, u32[]{:S(2)}) collective-permute-start(bf16[16,4864]{1,0:T(8,128)(2,1)S(1)} %get-tuple-element.322), channel_id=1, source_target_pairs={{0,16},{4,20},{8,24},{12,28},{16,0},{20,4},{24,8},{28,12},{1,17},{... | collective-permute-start | bytes 466952 | tf_op jit(solution)/shard_map/ppermute | solution.py:678
  149.3 6.3 %collective-permute-start.38 = (bf16[16,2176]{1,0:T(8,128)(2,1)S(1)}, bf16[16,2176]{1,0:T(8,128)(2,1)S(1)}, u32[]{:S(2)}, u32[]{:S(2)}) collective-permute-start(bf16[16,2176]{1,0:T(8,128)(2,1)S(1)} %get-tuple-element.305), channel_id=1, source_target_pairs={{0,3},{1,2},{2,1},{3,0},{4,7},{5,6},{6,5},{7,4},{8,11},{9,10},{10,... | collective-permute-start | bytes 208904 | tf_op jit(solution)/shard_map/ppermute | solution.py:678
  151.0 6.2 %collective-permute-start.37 = (bf16[16,2176]{1,0:T(8,128)(2,1)S(1)}, bf16[16,2176]{1,0:T(8,128)(2,1)S(1)}, u32[]{:S(2)}, u32[]{:S(2)}) collective-permute-start(bf16[16,2176]{1,0:T(8,128)(2,1)S(1)} %get-tuple-element.306), channel_id=1, source_target_pairs={{0,2},{1,3},{2,0},{3,1},{4,6},{5,7},{6,4},{7,5},{8,10},{9,11},{10,... | collective-permute-start | bytes 208904 | tf_op jit(solution)/shard_map/ppermute | solution.py:678
  152.2 5.1 %collective-permute-start.36 = (bf16[16,2176]{1,0:T(8,128)(2,1)S(1)}, bf16[16,2176]{1,0:T(8,128)(2,1)S(1)}, u32[]{:S(2)}, u32[]{:S(2)}) collective-permute-start(bf16[16,2176]{1,0:T(8,128)(2,1)S(1)} %get-tuple-element.307), channel_id=1, source_target_pairs={{0,1},{1,0},{2,3},{3,2},{4,5},{5,4},{6,7},{7,6},{8,9},{9,8},{10,11... | collective-permute-start | bytes 208904 | tf_op jit(solution)/shard_map/ppermute | solution.py:678
  153.8 9.2 %collective-permute-start.44 = (bf16[2,16,4864]{2,1,0:T(8,128)(2,1)S(1)}, bf16[2,16,4864]{2,1,0:T(8,128)(2,1)S(1)}, u32[]{:S(2)}, u32[]{:S(2)}) collective-permute-start(bf16[2,16,4864]{2,1,0:T(8,128)(2,1)S(1)} %get-tuple-element.318), channel_id=1, source_target_pairs={{0,8},{4,12},{8,0},{12,4},{16,24},{20,28},{24,16},{28,20},{1,9},{5... | collective-permute-start | bytes 933896 | tf_op jit(solution)/shard_map/ppermute | solution.py:678
  157.3 5.7 %collective-permute-start.40 = (bf16[16,2176]{1,0:T(8,128)(2,1)S(1)}, bf16[16,2176]{1,0:T(8,128)(2,1)S(1)}, u32[]{:S(2)}, u32[]{:S(2)}) collective-permute-start(bf16[16,2176]{1,0:T(8,128)(2,1)S(1)} %add_convert_fusion.23), channel_id=1, source_target_pairs={{0,8},{4,12},{8,0},{12,4},{16,24},{20,28},{24,16},{28,20},{1,9},{5... | collective-permute-start | bytes 208904 | tf_op jit(solution)/shard_map/ppermute | solution.py:678
  158.5 5.8 %collective-permute-start.42 = (bf16[16,2176]{1,0:T(8,128)(2,1)S(1)}, bf16[16,2176]{1,0:T(8,128)(2,1)S(1)}, u32[]{:S(2)}, u32[]{:S(2)}) collective-permute-start(bf16[16,2176]{1,0:T(8,128)(2,1)S(1)} %add_convert_fusion.23), channel_id=1, source_target_pairs={{0,24},{4,28},{8,16},{12,20},{16,8},{20,12},{24,0},{28,4},{1,25},{... | collective-permute-start | bytes 208904 | tf_op jit(solution)/shard_map/ppermute | solution.py:678
  160.0 5.0 %collective-permute-start.41 = (bf16[16,2176]{1,0:T(8,128)(2,1)S(1)}, bf16[16,2176]{1,0:T(8,128)(2,1)S(1)}, u32[]{:S(2)}, u32[]{:S(2)}) collective-permute-start(bf16[16,2176]{1,0:T(8,128)(2,1)S(1)} %add_convert_fusion.23), channel_id=1, source_target_pairs={{0,16},{4,20},{8,24},{12,28},{16,0},{20,4},{24,8},{28,12},{1,17},{... | collective-permute-start | bytes 208904 | tf_op jit(solution)/shard_map/ppermute | solution.py:678
  163.2 2.1 %collective-permute-start.45 = (bf16[4,16,4864]{2,1,0:T(8,128)(2,1)S(1)}, bf16[4,16,4864]{2,1,0:T(8,128)(2,1)S(1)}, u32[]{:S(2)}, u32[]{:S(2)}) collective-permute-start(bf16[4,16,4864]{2,1,0:T(8,128)(2,1)S(1)} %bitcast.103), channel_id=1, source_target_pairs={{0,4},{4,0},{8,12},{12,8},{16,20},{20,16},{24,28},{28,24},{1,5},{5... | collective-permute-start | bytes 1867784 | tf_op jit(solution)/shard_map/ppermute | solution.py:678
  165.1 2.3 %collective-permute-start.43 = (bf16[4,16,2176]{2,1,0:T(8,128)(2,1)S(1)}, bf16[4,16,2176]{2,1,0:T(8,128)(2,1)S(1)}, u32[]{:S(2)}, u32[]{:S(2)}) collective-permute-start(bf16[4,16,2176]{2,1,0:T(8,128)(2,1)S(1)} %pad_maximum_fusion.13.near), channel_id=1, source_target_pairs={{0,4},{4,0},{8,12},{12,8},{16,20},{20,16},{24,28},{28,24},{1,5},{5... | collective-permute-start | bytes 835592 | tf_op jit(solution)/shard_map/ppermute | solution.py:678
  (12 other events, 39.3 us)

commit v8 on v7

--- a/solution.py
+++ b/solution.py
@@ -98,34 +98,43 @@
         send[xy ^ idx[1], shard ^ idx[2], :, columns] = jnp.where(own_first, second, first)
 
 
-def pack_kernel(
-    g1, b1, g2, b2, bd, bu, wq, wk, wv, wc, wm, wu, wd, wr, pa, pc, pd, sems
-):
-    member = lax.axis_index("dp") % 8
-    across = member ^ 6
-    rows = rows_at(member * PIECE, PIECE)
+def run_moves(moves, sems, between=lambda: None):
+    copies = [pltpu.make_async_copy(src, dst, sems.at[i]) for i, (src, dst) in enumerate(moves)]
+    for copy in copies:
+        copy.start()
+    between()
+    for copy in copies:
+        copy.wait()
+
+
+def pack_kernel(g1, b1, g2, b2, bd, bu, wq, wk, wv, wc, pa, sems):
+    rows = rows_at(lax.axis_index("dp") % 8 * PIECE, PIECE)
     moves = []
     for j, w in enumerate((wq, wk, wv, wc)):
         for half in range(2):
             start = half * COLS_PROJ + j * HALF
             part = w.at[rows, half * HALF : (half + 1) * HALF]
             moves.append((part, pa.at[:, start : start + HALF]))
-    moves.append((wm.at[rows, :], pc.at[:, :WIDTH]))
-    moves.append((wu.at[rows, :], pc.at[:, WIDTH:]))
-    for place, who in enumerate((member, across)):
+
+    def vectors():
+        lines = [v[...].astype(F32).reshape(1, 128) for v in (g1, b1, g2, b2, bd)]
+        lines += [bu[128 * j : 128 * j + 128].astype(F32).reshape(1, 128) for j in range(4)]
+        lines.append(jnp.zeros((7, 128), F32))
+        pa[:, COLS_BOTH:] = jnp.concatenate(lines, axis=0).astype(BF16)
+
+    run_moves(moves, sems, vectors)
+
+
+def pack_feed_kernel(wm, wu, wd, wr, pa, pc, pd, sems):
+    member = lax.axis_index("dp") % 8
+    rows = rows_at(member * PIECE, PIECE)
+    moves = [(wm.at[rows, :], pc.at[:, :WIDTH]), (wu.at[rows, :], pc.at[:, WIDTH:])]
+    for place, who in enumerate((member, member ^ 6)):
         for i in range(4):
             part = wd.at[rows_at(who * 64 + 16 * i, PIECE), :]
             moves.append((part, pd.at[place, :, i * WIDTH : (i + 1) * WIDTH]))
         moves.append((wr.at[rows_at(who * PIECE, PIECE), :], pd.at[place, :, 4 * WIDTH :]))
-    copies = [pltpu.make_async_copy(src, dst, sems.at[i]) for i, (src, dst) in enumerate(moves)]
-    for copy in copies:
-        copy.start()
-    lines = [v[...].astype(F32).reshape(1, 128) for v in (g1, b1, g2, b2, bd)]
-    lines += [bu[128 * j : 128 * j + 128].astype(F32).reshape(1, 128) for j in range(4)]
-    lines.append(jnp.zeros((7, 128), F32))
-    pa[:, COLS_BOTH:] = jnp.concatenate(lines, axis=0).astype(BF16)
-    for copy in copies:
-        copy.wait()
+    run_moves(moves, sems)
 
 
 def first_norm_kernel(idx, vec, x, a1, both_t):
@@ -764,18 +773,25 @@
         tok = lambda n: ((CHUNK, n), forward)
         parts = (4, 4, PIECE)
 
-        weights = (w_query, w_key, w_value, w_control, w_mix, w_up, w_down, w_read)
-        sizes = [(PIECE, COLS_BOTH + 128), (PIECE, COLS_UP), (2, PIECE, COLS_DOWN)]
         vectors = (gain_one, bias_one, gain_two, bias_two, bias_down, bias_up)
-        pa, pu, pd = call(
+        pa = call(
             pack_kernel,
-            "pack_weights",
-            [(v, None) for v in vectors] + [(w, "hbm") for w in weights],
-            [(size, BF16, None) for size in sizes],
-            scratch=[pltpu.SemaphoreType.DMA((20,))],
+            "pack_projections",
+            [(v, None) for v in vectors]
+            + [(w, "hbm") for w in (w_query, w_key, w_value, w_control)],
+            [((PIECE, COLS_BOTH + 128), BF16, None)],
+            scratch=[pltpu.SemaphoreType.DMA((8,))],
+            limit=56,
+        )[0]
+        got_a = near_rows(pa, shards)
+        pu, pd = call(
+            pack_feed_kernel,
+            "pack_feed",
+            [(w, "hbm") for w in (w_mix, w_up, w_down, w_read)] + [(pa, "hbm")],
+            [((PIECE, COLS_UP), BF16, None), ((2, PIECE, COLS_DOWN), BF16, None)],
+            scratch=[pltpu.SemaphoreType.DMA((12,))],
             limit=56,
         )
-        got_a = near_rows(pa, shards)
         pair_u = near_pair(pu, shards)
         rows_a = jnp.stack([pa[:, :COLS_BOTH]] + [g[:, :COLS_BOTH] for g in got_a])
         vec = jnp.stack([pa[:, COLS_BOTH:]] + [g[:, COLS_BOTH:] for g in got_a])

time: 170 us -> 169 us (level)
    pallas_call x11 -> x12, Pallas kernels: 85.8 us -> 87 us  [call(): pl.pallas_call(kernel, grid=grid, in_specs=in_specs, out_specs=[spec(shap...]
  transfers between devices with their start and end apart: 46 -> 46, of which waited for: 17 -> 16; matrix products, arithmetic and copies ran while one was open for 3% -> 2% of each run, Pallas kernels for 39% -> 40%
where the time goes in v8:
time: 169 us
  Pallas kernels  87 us (51%)
  starting transfers between devices  45.5 us (27%)
  waiting for transfers between devices  27.5 us (16%)
  other arithmetic  4.53 us (3%)
  local copies, waits for them, and re-layouts  2.86 us (2%)
    pallas_call x12, Pallas kernels, call(): pl.pallas_call(kernel, grid=grid, in_specs=in_specs, out_specs=[spec(shap...  87 us
    ppermute x46, starting transfers between devices, swap(): return lax.ppermute(value, axis, [(i, i ^ distance) for i in range(size)])  45.5 us
    ppermute x46, waiting for transfers between devices, swap(): return lax.ppermute(value, axis, [(i, i ^ distance) for i in range(size)])  27.5 us
  transfers between devices with their start and end apart: 46, of which 16 were waited for; matrix products, arithmetic and copies ran while one was open for 2% of the time, Pallas kernels for 40%

profile of v8, /device:TPU:0, one launch (start us, length us, event | category | flops | bytes accessed | tf_op | source)
XLA Modules:
  0.0 168.8 jit_solution(14884072264053057472)
XLA Ops:
  0.6 2.3 %pack_projections.1.pa = bf16[16,2176]{1,0:T(8,128)(2,1)} custom-call(bf16[128]{0:T(256)(128)(2,1)} %g1.1, bf16[128]{0:T(256)(128)(2,1)} %b1.1, bf16[128]{0:T(256)(128)(2,1)} %g2.1, bf16[128]{0:T(256)(128)(2,1)} %b2.1, bf16[128]{0:T(256)(128)(2,1)} %bd.1, bf16[512]{0:T(512)(128)(2,1)} %bu.1, bf16[128,512]{1,0:T(8,128)(2,1)} %wq.1, bf16[128,512]{1,0:T(8,128)(2,1)} %wk.1, ...), custom_call_target="tpu_custom_call" | custom-call | flops 1000 | bytes 1000 | tf_op jit(solution)/shard_map/pack_projections/pallas_call | solution.py:670
  3.0 5.1 %collective-permute-start.2 = (bf16[16,2176]{1,0:T(8,128)(2,1)}, bf16[16,2176]{1,0:T(8,128)(2,1)S(1)}, u32[]{:S(2)}, u32[]{:S(2)}) collective-permute-start(bf16[16,2176]{1,0:T(8,128)(2,1)} %pack_projections.1.pa), channel_id=1, source_target_pairs={{0,3},{1,2},{2,1},{3,0},{4,7},{5,6},{6,5},{7,4},{8,11},{9,10},{10,... | collective-permute-start | bytes 208904 | tf_op jit(solution)/shard_map/ppermute | solution.py:687
  8.7 1.7 pack_feed.1
  10.4 1.5 collective-permute-start.6
  11.9 2.4 %collective-permute-done.1 = bf16[16,2176]{1,0:T(8,128)(2,1)S(1)} collective-permute-done((bf16[16,2176]{1,0:T(8,128)(2,1)}, bf16[16,2176]{1,0:T(8,128)(2,1)S(1)}, u32[]{:S(2)}, u32[]{:S(2)}) %collective-permute-start.1) | collective-permute-done | bytes 69664 | tf_op jit(solution)/shard_map/ppermute | solution.py:687
  14.4 2.5 %collective-permute-start.5 = (bf16[4,16,2048]{2,1,0:T(8,128)(2,1)S(1)}, bf16[4,16,2048]{2,1,0:T(8,128)(2,1)S(1)}, u32[]{:S(2)}, u32[]{:S(2)}) collective-permute-start(bf16[4,16,2048]{2,1,0:T(8,128)(2,1)S(1)} %pad_maximum_fusion.14), channel_id=1, source_target_pairs={{0,24},{4,28},{8,16},{12,20},{16,8},{20,12},{24,0},{28,4},{1,25},{... | collective-permute-start | bytes 786440 | tf_op jit(solution)/shard_map/ppermute | solution.py:687
  18.9 1.9 %collective-permute-start.7 = (bf16[2,16,2560]{2,1,0:T(8,128)(2,1)S(1)}, bf16[2,16,2560]{2,1,0:T(8,128)(2,1)S(1)}, u32[]{:S(2)}, u32[]{:S(2)}) collective-permute-start(bf16[2,16,2560]{2,1,0:T(8,128)(2,1)S(1)} %pad_maximum_fusion.15), channel_id=1, source_target_pairs={{0,2},{1,3},{2,0},{3,1},{4,6},{5,7},{6,4},{7,5},{8,10},{9,11},{10,... | collective-permute-start | bytes 491528 | tf_op jit(solution)/shard_map/ppermute | solution.py:687
  20.9 1.3 collective-permute-start.12
  22.2 1.8 %first_norm.1 = (bf16[1024,512]{1,0:T(8,128)(2,1)S(1)}, bf16[1040,1024]{1,0:T(8,128)(2,1)S(1)}) custom-call(s32[3]{0:T(128)S(1)} %pad_add_fusion.idx, bf16[4,16,128]{2,1,0:T(8,128)(2,1)S(1)} %pad_maximum_fusion.17.vec, bf16[1024,512]{1,0:T(8,128)(2,1)S(1)} %copy-done), custom_call_target="tpu_custom_call" | custom-call | flops 1000 | bytes 1000 | tf_op jit(solution)/shard_map/first_norm/pallas_call | solution.py:670
  24.1 3.6 %collective-permute-done.7 = bf16[2,16,2560]{2,1,0:T(8,128)(2,1)S(1)} collective-permute-done((bf16[2,16,2560]{2,1,0:T(8,128)(2,1)S(1)}, bf16[2,16,2560]{2,1,0:T(8,128)(2,1)S(1)}, u32[]{:S(2)}, u32[]{:S(2)}) %collective-permute-start.7) | collective-permute-done | bytes 163872 | tf_op jit(solution)/shard_map/ppermute | solution.py:687
  27.7 1.0 collective-permute-done.4
  30.0 1.6 collective-permute-start.11
  31.6 1.4 collective-permute-start.10
  33.6 8.6 %attend.2 = (bf16[1024,1024]{1,0:T(8,128)(2,1)S(1)}, f32[1024,1024]{1,0:T(8,128)}, bf16[1024,512]{1,0:T(8,128)(2,1)S(1)}, bf16[8,2,128,256]{3,2,1,0:T(8,128)(2,1)S(1)}, bf16[512,1024]{1,0:T(8,128)(2,1)S(1)}) custom-call(s32[3]{0:T(128)S(1)} %pad_add_fusion.idx, bf16[1024,512]{1,0:T(8,128)(2,1)S(1)} %get-tuple-element.173.a1, ...), custom_call_target="tpu_custom_call" | custom-call | flops 1000 | bytes 1000 | tf_op jit(solution)/shard_map/attend/pallas_call | solution.py:670
  42.1 5.9 %collective-permute-done.13 = bf16[2,2,16,2304]{3,2,0,1:T(8,128)(2,1)S(1)} collective-permute-done((bf16[2,2,16,2304]{3,2,0,1:T(8,128)(2,1)S(1)}, bf16[2,2,16,2304]{3,2,0,1:T(8,128)(2,1)S(1)}, u32[]{:S(2)}, u32[]{:S(2)}) %collective-permute-start.13) | collective-permute-done | bytes 294944 | tf_op jit(solution)/shard_map/ppermute | solution.py:687
  49.3 1.4 collective-permute-start.17
  51.6 8.3 %attend.3 = (bf16[1024,1024]{1,0:T(8,128)(2,1)S(1)}, f32[1024,1024]{1,0:T(8,128)}, bf16[1024,512]{1,0:T(8,128)(2,1)S(1)}, bf16[8,2,128,256]{3,2,1,0:T(8,128)(2,1)S(1)}, bf16[512,1024]{1,0:T(8,128)(2,1)S(1)}) custom-call(s32[3]{0:T(128)S(1)} %pad_add_fusion.idx, bf16[1024,512]{1,0:T(8,128)(2,1)S(1)} %get-tuple-element.173.a1, ...), custom_call_target="tpu_custom_call" | custom-call | flops 1000 | bytes 1000 | tf_op jit(solution)/shard_map/attend/pallas_call | solution.py:670
  59.9 1.2 copy-done.11
  61.2 1.2 pad_maximum_fusion.1.down_near_i
  63.2 16.2 %feed_forward.1 = (bf16[1024,512]{1,0:T(8,128)(2,1)}, f32[1024,512]{1,0:T(8,128)}, bf16[1024,2048]{1,0:T(8,128)(2,1)}, f32[1024,512]{1,0:T(8,128)}, f32[1,512]{1...) custom-call(s32[3]{0:T(128)S(1)} %pad_add_fusion.idx, ...), custom_call_target="tpu_custom_call" | custom-call | flops 1000 | bytes 1000 | tf_op jit(solution)/shard_map/feed_forward/pallas_call | solution.py:670
  79.6 13.1 %feed_backward.1 = (f32[1024,512]{1,0:T(8,128)}, bf16[1024,512]{1,0:T(8,128)(2,1)S(1)}, f32[1,512]{1,0:T(1,128)S(1)}, f32[1,512]{1,0:T(1,128)S(1)}, f32[1,2048]{...) custom-call(s32[3]{0:T(128)S(1)} %pad_add_fusion.idx, ...), custom_call_target="tpu_custom_call" | custom-call | flops 1000 | bytes 1000 | tf_op jit(solution)/shard_map/feed_backward/pallas_call | solution.py:670
  93.3 1.2 collective-permute-start.20
  94.5 1.1 collective-permute-start.21
  95.6 1.2 collective-permute-start.22
  96.9 13.0 %attend_backward.2 = (bf16[1024,1024]{1,0:T(8,128)(2,1)S(1)}, bf16[4,4,16,1024]{3,2,1,0:T(8,128)(2,1)S(1)}, bf16[4,4,16,1024]{3,2,1,0:T(8,128)(2,1)S(1)}, f32[8,512]{1,0:T(8,128)S(1)}) custom-call(s32[3]{0:T(128)S(1)} %pad_add_fusion.idx, bf16[1040,1024]{1,0:T(8,128)(2,1)} %copy-done.1, bf16[512,1024]{1,0:T(8,128)(2,1)S(1)} %get-tuple-element.207.w.w0, ...), custom_call_target="tpu_custom_call" | custom-call | flops 1000 | bytes 1000 | tf_op jit(solution)/shard_map/attend_backward/pallas_call | solution.py:670
  110.6 1.2 collective-permute-start.25
  111.9 1.1 collective-permute-start.26
  112.9 1.2 collective-permute-start.27
  114.2 13.4 %attend_backward.3 = (bf16[1024,1024]{1,0:T(8,128)(2,1)S(1)}, bf16[4,4,16,1152]{3,2,1,0:T(8,128)(2,1)S(1)}, bf16[4,4,16,1152]{3,2,1,0:T(8,128)(2,1)S(1)}) custom-call(s32[3]{0:T(128)S(1)} %pad_add_fusion.idx, bf16[1040,1024]{1,0:T(8,128)(2,1)} %copy-done.1, bf16[512,1024]{1,0:T(8,128)(2,1)S(1)} %get-tuple-element.225.w.w1, bf16[1024,1024]{1,0:T(8,128)(2,1)S(1)} %copy-done.4, ...), custom_call_target="tpu_custom_call" | custom-call | flops 1000 | bytes 1000 | tf_op jit(solution)/shard_map/attend_backward/pallas_call | solution.py:670
  127.6 1.1 collective-permute-done.26
  128.9 1.8 %collective-permute-done.29 = bf16[4,4,16,1152]{3,2,1,0:T(8,128)(2,1)S(1)} collective-permute-done((bf16[4,4,16,1152]{3,2,1,0:T(8,128)(2,1)S(1)}, bf16[4,4,16,1152]{3,2,1,0:T(8,128)(2,1)S(1)}, u32[]{:S(2)}, u32[]{:S(2)}) %collective-permute-start.29) | collective-permute-done | bytes 589856 | tf_op jit(solution)/shard_map/ppermute | solution.py:687
  131.2 1.7 %collective-permute-start.30 = (bf16[2,16,2560]{2,1,0:T(8,128)(2,1)S(1)}, bf16[2,16,2560]{2,1,0:T(8,128)(2,1)S(1)}, u32[]{:S(2)}, u32[]{:S(2)}) collective-permute-start(bf16[2,16,2560]{2,1,0:T(8,128)(2,1)S(1)} %slice.299), channel_id=1, source_target_pairs={{0,2},{1,3},{2,0},{3,1},{4,6},{5,7},{6,4},{7,5},{8,10},{9,11},{10,... | collective-permute-start | bytes 491528 | tf_op jit(solution)/shard_map/ppermute | solution.py:687
  133.9 1.0 collective-permute-start.32
  135.9 1.5 collective-permute-start.34
  137.3 5.0 %input_gradient.1 = f32[1024,512]{1,0:T(8,128)} custom-call(s32[3]{0:T(128)S(1)} %pad_add_fusion.idx, bf16[4,16,128]{2,1,0:T(8,128)(2,1)S(1)} %pad_maximum_fusion.17.vec, bf16[1024,512]{1,0:T(8,128)(2,1)S(1)} %copy-done, f32[1024,512]{1,0:T(8,128)S(1)} %copy-done.2, bf16[1024,1024]{1,0:T(8,128)(2,1)S(1)} %get-tuple-element.256.dx0, ...), custom_call_target="tpu_custom_call" | custom-call | flops 1000 | bytes 1000 | tf_op jit(solution)/shard_map/input_gradient/pallas_call | solution.py:670
  142.3 1.2 collective-permute-start.35
  143.6 3.3 %collective-permute-done.35 = bf16[16,2560]{1,0:T(8,128)(2,1)S(1)} collective-permute-done((bf16[16,2560]{1,0:T(8,128)(2,1)S(1)}, bf16[16,2560]{1,0:T(8,128)(2,1)S(1)}, u32[]{:S(2)}, u32[]{:S(2)}) %collective-permute-start.35) | collective-permute-done | bytes 81952 | tf_op jit(solution)/shard_map/ppermute | solution.py:687
  146.9 1.1 collective-permute-start.39
  148.9 1.7 %collective-permute-start.38 = (bf16[16,2176]{1,0:T(8,128)(2,1)S(1)}, bf16[16,2176]{1,0:T(8,128)(2,1)S(1)}, u32[]{:S(2)}, u32[]{:S(2)}) collective-permute-start(bf16[16,2176]{1,0:T(8,128)(2,1)S(1)} %get-tuple-element.303), channel_id=1, source_target_pairs={{0,3},{1,2},{2,1},{3,0},{4,7},{5,6},{6,5},{7,4},{8,11},{9,10},{10,... | collective-permute-start | bytes 208904 | tf_op jit(solution)/shard_map/ppermute | solution.py:687
  150.6 1.0 collective-permute-start.37
  151.7 1.7 %collective-permute-start.36 = (bf16[16,2176]{1,0:T(8,128)(2,1)S(1)}, bf16[16,2176]{1,0:T(8,128)(2,1)S(1)}, u32[]{:S(2)}, u32[]{:S(2)}) collective-permute-start(bf16[16,2176]{1,0:T(8,128)(2,1)S(1)} %get-tuple-element.305), channel_id=1, source_target_pairs={{0,1},{1,0},{2,3},{3,2},{4,5},{5,4},{6,7},{7,6},{8,9},{9,8},{10,11... | collective-permute-start | bytes 208904 | tf_op jit(solution)/shard_map/ppermute | solution.py:687
  153.4 1.1 collective-permute-start.44
  155.2 1.7 %collective-permute-done.37 = bf16[16,2176]{1,0:T(8,128)(2,1)S(1)} collective-permute-done((bf16[16,2176]{1,0:T(8,128)(2,1)S(1)}, bf16[16,2176]{1,0:T(8,128)(2,1)S(1)}, u32[]{:S(2)}, u32[]{:S(2)}) %collective-permute-start.37) | collective-permute-done | bytes 69664 | tf_op jit(solution)/shard_map/ppermute | solution.py:687
  157.0 1.0 collective-permute-start.40
  158.0 1.7 collective-permute-start.42
  160.6 2.1 %collective-permute-done.40 = bf16[16,2176]{1,0:T(8,128)(2,1)S(1)} collective-permute-done((bf16[16,2176]{1,0:T(8,128)(2,1)S(1)}, bf16[16,2176]{1,0:T(8,128)(2,1)S(1)}, u32[]{:S(2)}, u32[]{:S(2)}) %collective-permute-start.40) | collective-permute-done | bytes 69664 | tf_op jit(solution)/shard_map/ppermute | solution.py:687
  164.9 2.1 %unpack_feed.1 = (f32[128,512]{1,0:T(8,128)}, f32[128,2048]{1,0:T(8,128)}, f32[512,512]{1,0:T(8,128)}, f32[128,256]{1,0:T(8,128)}) custom-call(s32[3]{0:T(128)S(1)} %pad_add_fusion.idx, bf16[4,16,4864]{2,1,0:T(8,128)(2,1)S(1)} %bitcast.104, bf16[4,16,4864]{2,1,0:T(8,128)(2,1)S(1)} %collective-permute-done.45.far), custom_call_target="tpu_custom_call" | custom-call | flops 1000 | bytes 1000 | tf_op jit(solution)/shard_map/unpack_feed/pallas_call | solution.py:670
  167.0 1.6 unpack_proj.1
  (129 shorter events, 16.4 us)
Async XLA Ops:
  3.0 19.3 %copy-start = (bf16[1024,512]{1,0:T(8,128)(2,1)S(1)}, bf16[1024,512]{1,0:T(8,128)(2,1)}, u32[]{:S(2)}) copy-start(bf16[1024,512]{1,0:T(8,128)(2,1)} %x.4) | copy-start | bytes 3145732
  3.0 8.9 %collective-permute-start.2 = (bf16[16,2176]{1,0:T(8,128)(2,1)}, bf16[16,2176]{1,0:T(8,128)(2,1)S(1)}, u32[]{:S(2)}, u32[]{:S(2)}) collective-permute-start(bf16[16,2176]{1,0:T(8,128)(2,1)} %pack_projections.1.pa), channel_id=1, source_target_pairs={{0,3},{1,2},{2,1},{3,0},{4,7},{5,6},{6,5},{7,4},{8,11},{9,10},{10,... | collective-permute-start | bytes 208904 | tf_op jit(solution)/shard_map/ppermute | solution.py:687
  8.1 6.2 %collective-permute-start.1 = (bf16[16,2176]{1,0:T(8,128)(2,1)}, bf16[16,2176]{1,0:T(8,128)(2,1)S(1)}, u32[]{:S(2)}, u32[]{:S(2)}) collective-permute-start(bf16[16,2176]{1,0:T(8,128)(2,1)} %pack_projections.1.pa), channel_id=1, source_target_pairs={{0,2},{1,3},{2,0},{3,1},{4,6},{5,7},{6,4},{7,5},{8,10},{9,11},{10,... | collective-permute-start | bytes 208904 | tf_op jit(solution)/shard_map/ppermute | solution.py:687
  8.1 6.2 %collective-permute-start = (bf16[16,2176]{1,0:T(8,128)(2,1)}, bf16[16,2176]{1,0:T(8,128)(2,1)S(1)}, u32[]{:S(2)}, u32[]{:S(2)}) collective-permute-start(bf16[16,2176]{1,0:T(8,128)(2,1)} %pack_projections.1.pa), channel_id=1, source_target_pairs={{0,1},{1,0},{2,3},{3,2},{4,5},{5,4},{6,7},{7,6},{8,9},{9,8},{10,11... | collective-permute-start | bytes 208904 | tf_op jit(solution)/shard_map/ppermute | solution.py:687
  10.4 10.5 %copy-start.14 = (bf16[2,16,2304]{2,1,0:T(8,128)(2,1)S(1)}, bf16[2,16,2304]{2,1,0:T(8,128)(2,1)}, u32[]{:S(2)}) copy-start(bf16[2,16,2304]{2,1,0:T(8,128)(2,1)} %get-tuple-element.170) | copy-start | bytes 442372
  10.4 7.6 %collective-permute-start.6 = (bf16[16,2560]{1,0:T(8,128)(2,1)}, bf16[16,2560]{1,0:T(8,128)(2,1)S(1)}, u32[]{:S(2)}, u32[]{:S(2)}) collective-permute-start(bf16[16,2560]{1,0:T(8,128)(2,1)} %get-tuple-element.155), channel_id=1, source_target_pairs={{0,1},{1,0},{2,3},{3,2},{4,5},{5,4},{6,7},{7,6},{8,9},{9,8},{10,11... | collective-permute-start | bytes 245768 | tf_op jit(solution)/shard_map/ppermute | solution.py:687
  14.4 13.3 %collective-permute-start.5 = (bf16[4,16,2048]{2,1,0:T(8,128)(2,1)S(1)}, bf16[4,16,2048]{2,1,0:T(8,128)(2,1)S(1)}, u32[]{:S(2)}, u32[]{:S(2)}) collective-permute-start(bf16[4,16,2048]{2,1,0:T(8,128)(2,1)S(1)} %pad_maximum_fusion.14), channel_id=1, source_target_pairs={{0,24},{4,28},{8,16},{12,20},{16,8},{20,12},{24,0},{28,4},{1,25},{... | collective-permute-start | bytes 786440 | tf_op jit(solution)/shard_map/ppermute | solution.py:687
  16.9 11.8 %collective-permute-start.4 = (bf16[4,16,2048]{2,1,0:T(8,128)(2,1)S(1)}, bf16[4,16,2048]{2,1,0:T(8,128)(2,1)S(1)}, u32[]{:S(2)}, u32[]{:S(2)}) collective-permute-start(bf16[4,16,2048]{2,1,0:T(8,128)(2,1)S(1)} %pad_maximum_fusion.14), channel_id=1, source_target_pairs={{0,16},{4,20},{8,24},{12,28},{16,0},{20,4},{24,8},{28,12},{1,17},{... | collective-permute-start | bytes 786440 | tf_op jit(solution)/shard_map/ppermute | solution.py:687
  17.4 11.6 %collective-permute-start.3 = (bf16[4,16,2048]{2,1,0:T(8,128)(2,1)S(1)}, bf16[4,16,2048]{2,1,0:T(8,128)(2,1)S(1)}, u32[]{:S(2)}, u32[]{:S(2)}) collective-permute-start(bf16[4,16,2048]{2,1,0:T(8,128)(2,1)S(1)} %pad_maximum_fusion.14), channel_id=1, source_target_pairs={{0,8},{4,12},{8,0},{12,4},{16,24},{20,28},{24,16},{28,20},{1,9},{5... | collective-permute-start | bytes 786440 | tf_op jit(solution)/shard_map/ppermute | solution.py:687
  18.9 8.8 %collective-permute-start.7 = (bf16[2,16,2560]{2,1,0:T(8,128)(2,1)S(1)}, bf16[2,16,2560]{2,1,0:T(8,128)(2,1)S(1)}, u32[]{:S(2)}, u32[]{:S(2)}) collective-permute-start(bf16[2,16,2560]{2,1,0:T(8,128)(2,1)S(1)} %pad_maximum_fusion.15), channel_id=1, source_target_pairs={{0,2},{1,3},{2,0},{3,1},{4,6},{5,7},{6,4},{7,5},{8,10},{9,11},{10,... | collective-permute-start | bytes 491528 | tf_op jit(solution)/shard_map/ppermute | solution.py:687
  20.9 8.3 %collective-permute-start.12 = (bf16[2,16,2304]{2,1,0:T(8,128)(2,1)S(1)}, bf16[2,16,2304]{2,1,0:T(8,128)(2,1)S(1)}, u32[]{:S(2)}, u32[]{:S(2)}) collective-permute-start(bf16[2,16,2304]{2,1,0:T(8,128)(2,1)S(1)} %copy-done.14), channel_id=1, source_target_pairs={{0,1},{1,0},{2,3},{3,2},{4,5},{5,4},{6,7},{7,6},{8,9},{9,8},{10,11... | collective-permute-start | bytes 442376 | tf_op jit(solution)/shard_map/ppermute | solution.py:687
  29.2 4.4 %collective-permute-start.8 = (bf16[4,4,16,2048]{3,2,1,0:T(8,128)(2,1)S(1)}, bf16[4,4,16,2048]{3,2,1,0:T(8,128)(2,1)S(1)}, u32[]{:S(2)}, u32[]{:S(2)}) collective-permute-start(bf16[4,4,16,2048]{3,2,1,0:T(8,128)(2,1)S(1)} %pad_maximum_fusion.2.near), channel_id=1, source_target_pairs={{0,4},{4,0},{8,12},{12,8},{16,20},{20,16},{24,28},{28,24},{1,5},{5... | collective-permute-start | bytes 3145736 | tf_op jit(solution)/shard_map/ppermute | solution.py:687
  30.0 18.1 %collective-permute-start.11 = (bf16[4,16,2560]{2,1,0:T(8,128)(2,1)S(1)}, bf16[4,16,2560]{2,1,0:T(8,128)(2,1)S(1)}, u32[]{:S(2)}, u32[]{:S(2)}) collective-permute-start(bf16[4,16,2560]{2,1,0:T(8,128)(2,1)S(1)} %get-tuple-element.314), channel_id=1, source_target_pairs={{0,24},{4,28},{8,16},{12,20},{16,8},{20,12},{24,0},{28,4},{1,25},{... | collective-permute-start | bytes 983048 | tf_op jit(solution)/shard_map/ppermute | solution.py:687
  31.6 16.5 %collective-permute-start.10 = (bf16[4,16,2560]{2,1,0:T(8,128)(2,1)S(1)}, bf16[4,16,2560]{2,1,0:T(8,128)(2,1)S(1)}, u32[]{:S(2)}, u32[]{:S(2)}) collective-permute-start(bf16[4,16,2560]{2,1,0:T(8,128)(2,1)S(1)} %get-tuple-element.314), channel_id=1, source_target_pairs={{0,16},{4,20},{8,24},{12,28},{16,0},{20,4},{24,8},{28,12},{1,17},{... | collective-permute-start | bytes 983048 | tf_op jit(solution)/shard_map/ppermute | solution.py:687
  33.0 15.1 %collective-permute-start.9 = (bf16[4,16,2560]{2,1,0:T(8,128)(2,1)S(1)}, bf16[4,16,2560]{2,1,0:T(8,128)(2,1)S(1)}, u32[]{:S(2)}, u32[]{:S(2)}) collective-permute-start(bf16[4,16,2560]{2,1,0:T(8,128)(2,1)S(1)} %get-tuple-element.314), channel_id=1, source_target_pairs={{0,8},{4,12},{8,0},{12,4},{16,24},{20,28},{24,16},{28,20},{1,9},{5... | collective-permute-start | bytes 983048 | tf_op jit(solution)/shard_map/ppermute | solution.py:687
  33.5 14.5 %collective-permute-start.13 = (bf16[2,2,16,2304]{3,2,0,1:T(8,128)(2,1)S(1)}, bf16[2,2,16,2304]{3,2,0,1:T(8,128)(2,1)S(1)}, u32[]{:S(2)}, u32[]{:S(2)}) collective-permute-start(bf16[2,2,16,2304]{3,2,0,1:T(8,128)(2,1)S(1)} %pad_maximum_fusion.8), channel_id=1, source_target_pairs={{0,2},{1,3},{2,0},{3,1},{4,6},{5,7},{6,4},{7,5},{8,10},{9,11},{10,... | collective-permute-start | bytes 884744 | tf_op jit(solution)/shard_map/ppermute | solution.py:687
  48.3 11.6 %collective-permute-start.14 = (bf16[4,4,16,2560]{3,2,1,0:T(8,128)(2,1)S(1)}, bf16[4,4,16,2560]{3,2,1,0:T(8,128)(2,1)S(1)}, u32[]{:S(2)}, u32[]{:S(2)}) collective-permute-start(bf16[4,4,16,2560]{3,2,1,0:T(8,128)(2,1)S(1)} %pad_maximum_fusion.up_near_i), channel_id=1, source_target_pairs={{0,4},{4,0},{8,12},{12,8},{16,20},{20,16},{24,28},{28,24},{1,5},{5... | collective-permute-start | bytes 3932168 | tf_op jit(solution)/shard_map/ppermute | solution.py:687
  49.3 10.6 %collective-permute-start.15 = (bf16[2,4,16,2304]{3,2,1,0:T(8,128)(2,1)S(1)}, bf16[2,4,16,2304]{3,2,1,0:T(8,128)(2,1)S(1)}, u32[]{:S(2)}, u32[]{:S(2)}) collective-permute-start(bf16[2,4,16,2304]{3,2,1,0:T(8,128)(2,1)S(1)} %pad_maximum_fusion.4), channel_id=1, source_target_pairs={{0,4},{4,0},{8,12},{12,8},{16,20},{20,16},{24,28},{28,24},{1,5},{5... | collective-permute-start | bytes 1769480 | tf_op jit(solution)/shard_map/ppermute | solution.py:687
  49.3 10.5 %collective-permute-start.17 = (bf16[4,16,2304]{2,1,0:T(8,128)(2,1)S(1)}, bf16[4,16,2304]{2,1,0:T(8,128)(2,1)S(1)}, u32[]{:S(2)}, u32[]{:S(2)}) collective-permute-start(bf16[4,16,2304]{2,1,0:T(8,128)(2,1)S(1)} %get-tuple-element.310), channel_id=1, source_target_pairs={{0,16},{4,20},{8,24},{12,28},{16,0},{20,4},{24,8},{28,12},{1,17},{... | collective-permute-start | bytes 884744 | tf_op jit(solution)/shard_map/ppermute | solution.py:687
  50.8 9.1 %collective-permute-start.16 = (bf16[4,16,2304]{2,1,0:T(8,128)(2,1)S(1)}, bf16[4,16,2304]{2,1,0:T(8,128)(2,1)S(1)}, u32[]{:S(2)}, u32[]{:S(2)}) collective-permute-start(bf16[4,16,2304]{2,1,0:T(8,128)(2,1)S(1)} %get-tuple-element.310), channel_id=1, source_target_pairs={{0,8},{4,12},{8,0},{12,4},{16,24},{20,28},{24,16},{28,20},{1,9},{5... | collective-permute-start | bytes 884744 | tf_op jit(solution)/shard_map/ppermute | solution.py:687
  61.1 2.1 %collective-permute-start.18 = (bf16[2,4,16,2304]{3,2,1,0:T(8,128)(2,1)S(1)}, bf16[2,4,16,2304]{3,2,1,0:T(8,128)(2,1)S(1)}, u32[]{:S(2)}, u32[]{:S(2)}) collective-permute-start(bf16[2,4,16,2304]{3,2,1,0:T(8,128)(2,1)S(1)} %pad_maximum_fusion.5), channel_id=1, source_target_pairs={{0,4},{4,0},{8,12},{12,8},{16,20},{20,16},{24,28},{28,24},{1,5},{5... | collective-permute-start | bytes 1769480 | tf_op jit(solution)/shard_map/ppermute | solution.py:687
  79.4 13.3 %collective-permute-start.19 = (bf16[4,4,16,2304]{3,2,1,0:T(8,128)(2,1)S(1)}, bf16[4,4,16,2304]{3,2,1,0:T(8,128)(2,1)S(1)}, u32[]{:S(2)}, u32[]{:S(2)}) collective-permute-start(bf16[4,4,16,2304]{3,2,1,0:T(8,128)(2,1)S(1)} %get-tuple-element.197), channel_id=1, source_target_pairs={{0,4},{4,0},{8,12},{12,8},{16,20},{20,16},{24,28},{28,24},{1,5},{5... | collective-permute-start | bytes 3538952 | tf_op jit(solution)/shard_map/ppermute | solution.py:687
  92.7 17.2 %collective-permute-start.23 = (bf16[4,4,16,2560]{3,2,1,0:T(8,128)(2,1)S(1)}, bf16[4,4,16,2560]{3,2,1,0:T(8,128)(2,1)S(1)}, u32[]{:S(2)}, u32[]{:S(2)}) collective-permute-start(bf16[4,4,16,2560]{3,2,1,0:T(8,128)(2,1)S(1)} %get-tuple-element.205), channel_id=1, source_target_pairs={{0,4},{4,0},{8,12},{12,8},{16,20},{20,16},{24,28},{28,24},{1,5},{5... | collective-permute-start | bytes 3932168 | tf_op jit(solution)/shard_map/ppermute | solution.py:687
  93.3 16.6 %collective-permute-start.20 = (bf16[4,16,2304]{2,1,0:T(8,128)(2,1)S(1)}, bf16[4,16,2304]{2,1,0:T(8,128)(2,1)S(1)}, u32[]{:S(2)}, u32[]{:S(2)}) collective-permute-start(bf16[4,16,2304]{2,1,0:T(8,128)(2,1)S(1)} %get-tuple-element.202), channel_id=1, source_target_pairs={{0,8},{4,12},{8,0},{12,4},{16,24},{20,28},{24,16},{28,20},{1,9},{5... | collective-permute-start | bytes 884744 | tf_op jit(solution)/shard_map/ppermute | solution.py:687
  94.5 15.4 %collective-permute-start.21 = (bf16[4,16,2304]{2,1,0:T(8,128)(2,1)S(1)}, bf16[4,16,2304]{2,1,0:T(8,128)(2,1)S(1)}, u32[]{:S(2)}, u32[]{:S(2)}) collective-permute-start(bf16[4,16,2304]{2,1,0:T(8,128)(2,1)S(1)} %get-tuple-element.203), channel_id=1, source_target_pairs={{0,16},{4,20},{8,24},{12,28},{16,0},{20,4},{24,8},{28,12},{1,17},{... | collective-permute-start | bytes 884744 | tf_op jit(solution)/shard_map/ppermute | solution.py:687
  95.6 14.3 %collective-permute-start.22 = (bf16[4,16,2304]{2,1,0:T(8,128)(2,1)S(1)}, bf16[4,16,2304]{2,1,0:T(8,128)(2,1)S(1)}, u32[]{:S(2)}, u32[]{:S(2)}) collective-permute-start(bf16[4,16,2304]{2,1,0:T(8,128)(2,1)S(1)} %get-tuple-element.204), channel_id=1, source_target_pairs={{0,24},{4,28},{8,16},{12,20},{16,8},{20,12},{24,0},{28,4},{1,25},{... | collective-permute-start | bytes 884744 | tf_op jit(solution)/shard_map/ppermute | solution.py:687
  110.0 18.8 %collective-permute-start.28 = (bf16[4,4,16,1024]{3,2,1,0:T(8,128)(2,1)S(1)}, bf16[4,4,16,1024]{3,2,1,0:T(8,128)(2,1)S(1)}, u32[]{:S(2)}, u32[]{:S(2)}) collective-permute-start(bf16[4,4,16,1024]{3,2,1,0:T(8,128)(2,1)S(1)} %get-tuple-element.224), channel_id=1, source_target_pairs={{0,4},{4,0},{8,12},{12,8},{16,20},{20,16},{24,28},{28,24},{1,5},{5... | collective-permute-start | bytes 1572872 | tf_op jit(solution)/shard_map/ppermute | solution.py:687
  110.6 17.0 %collective-permute-start.25 = (bf16[4,16,2560]{2,1,0:T(8,128)(2,1)S(1)}, bf16[4,16,2560]{2,1,0:T(8,128)(2,1)S(1)}, u32[]{:S(2)}, u32[]{:S(2)}) collective-permute-start(bf16[4,16,2560]{2,1,0:T(8,128)(2,1)S(1)} %get-tuple-element.221), channel_id=1, source_target_pairs={{0,8},{4,12},{8,0},{12,4},{16,24},{20,28},{24,16},{28,20},{1,9},{5... | collective-permute-start | bytes 983048 | tf_op jit(solution)/shard_map/ppermute | solution.py:687
  111.9 16.8 %collective-permute-start.26 = (bf16[4,16,2560]{2,1,0:T(8,128)(2,1)S(1)}, bf16[4,16,2560]{2,1,0:T(8,128)(2,1)S(1)}, u32[]{:S(2)}, u32[]{:S(2)}) collective-permute-start(bf16[4,16,2560]{2,1,0:T(8,128)(2,1)S(1)} %get-tuple-element.222), channel_id=1, source_target_pairs={{0,16},{4,20},{8,24},{12,28},{16,0},{20,4},{24,8},{28,12},{1,17},{... | collective-permute-start | bytes 983048 | tf_op jit(solution)/shard_map/ppermute | solution.py:687
  112.9 15.8 %collective-permute-start.27 = (bf16[4,16,2560]{2,1,0:T(8,128)(2,1)S(1)}, bf16[4,16,2560]{2,1,0:T(8,128)(2,1)S(1)}, u32[]{:S(2)}, u32[]{:S(2)}) collective-permute-start(bf16[4,16,2560]{2,1,0:T(8,128)(2,1)S(1)} %get-tuple-element.223), channel_id=1, source_target_pairs={{0,24},{4,28},{8,16},{12,20},{16,8},{20,12},{24,0},{28,4},{1,25},{... | collective-permute-start | bytes 983048 | tf_op jit(solution)/shard_map/ppermute | solution.py:687
  114.2 13.4 %collective-permute-start.24 = (bf16[2,16,2304]{2,1,0:T(8,128)(2,1)S(1)}, bf16[2,16,2304]{2,1,0:T(8,128)(2,1)S(1)}, u32[]{:S(2)}, u32[]{:S(2)}) collective-permute-start(bf16[2,16,2304]{2,1,0:T(8,128)(2,1)S(1)} %get-tuple-element.220), channel_id=1, source_target_pairs={{0,2},{1,3},{2,0},{3,1},{4,6},{5,7},{6,4},{7,5},{8,10},{9,11},{10,... | collective-permute-start | bytes 442376 | tf_op jit(solution)/shard_map/ppermute | solution.py:687
  128.7 2.0 %collective-permute-start.29 = (bf16[4,4,16,1152]{3,2,1,0:T(8,128)(2,1)S(1)}, bf16[4,4,16,1152]{3,2,1,0:T(8,128)(2,1)S(1)}, u32[]{:S(2)}, u32[]{:S(2)}) collective-permute-start(bf16[4,4,16,1152]{3,2,1,0:T(8,128)(2,1)S(1)} %get-tuple-element.244), channel_id=1, source_target_pairs={{0,4},{4,0},{8,12},{12,8},{16,20},{20,16},{24,28},{28,24},{1,5},{5... | collective-permute-start | bytes 1769480 | tf_op jit(solution)/shard_map/ppermute | solution.py:687
  131.2 11.2 %collective-permute-start.30 = (bf16[2,16,2560]{2,1,0:T(8,128)(2,1)S(1)}, bf16[2,16,2560]{2,1,0:T(8,128)(2,1)S(1)}, u32[]{:S(2)}, u32[]{:S(2)}) collective-permute-start(bf16[2,16,2560]{2,1,0:T(8,128)(2,1)S(1)} %slice.299), channel_id=1, source_target_pairs={{0,2},{1,3},{2,0},{3,1},{4,6},{5,7},{6,4},{7,5},{8,10},{9,11},{10,... | collective-permute-start | bytes 491528 | tf_op jit(solution)/shard_map/ppermute | solution.py:687
  132.9 9.4 %collective-permute-start.31 = (bf16[16,2304]{1,0:T(8,128)(2,1)S(1)}, bf16[16,2304]{1,0:T(8,128)(2,1)S(1)}, u32[]{:S(2)}, u32[]{:S(2)}) collective-permute-start(bf16[16,2304]{1,0:T(8,128)(2,1)S(1)} %fusion.19), channel_id=1, source_target_pairs={{0,1},{1,0},{2,3},{3,2},{4,5},{5,4},{6,7},{7,6},{8,9},{9,8},{10,11... | collective-permute-start | bytes 221192 | tf_op jit(solution)/shard_map/ppermute | solution.py:687
  133.9 14.1 %collective-permute-start.32 = (bf16[4,16,2176]{2,1,0:T(8,128)(2,1)S(1)}, bf16[4,16,2176]{2,1,0:T(8,128)(2,1)S(1)}, u32[]{:S(2)}, u32[]{:S(2)}) collective-permute-start(bf16[4,16,2176]{2,1,0:T(8,128)(2,1)S(1)} %get-tuple-element.247), channel_id=1, source_target_pairs={{0,8},{4,12},{8,0},{12,4},{16,24},{20,28},{24,16},{28,20},{1,9},{5... | collective-permute-start | bytes 835592 | tf_op jit(solution)/shard_map/ppermute | solution.py:687
  134.9 13.9 %collective-permute-start.33 = (bf16[4,16,2176]{2,1,0:T(8,128)(2,1)S(1)}, bf16[4,16,2176]{2,1,0:T(8,128)(2,1)S(1)}, u32[]{:S(2)}, u32[]{:S(2)}) collective-permute-start(bf16[4,16,2176]{2,1,0:T(8,128)(2,1)S(1)} %get-tuple-element.248), channel_id=1, source_target_pairs={{0,16},{4,20},{8,24},{12,28},{16,0},{20,4},{24,8},{28,12},{1,17},{... | collective-permute-start | bytes 835592 | tf_op jit(solution)/shard_map/ppermute | solution.py:687
  135.9 12.9 %collective-permute-start.34 = (bf16[4,16,2176]{2,1,0:T(8,128)(2,1)S(1)}, bf16[4,16,2176]{2,1,0:T(8,128)(2,1)S(1)}, u32[]{:S(2)}, u32[]{:S(2)}) collective-permute-start(bf16[4,16,2176]{2,1,0:T(8,128)(2,1)S(1)} %get-tuple-element.249), channel_id=1, source_target_pairs={{0,24},{4,28},{8,16},{12,20},{16,8},{20,12},{24,0},{28,4},{1,25},{... | collective-permute-start | bytes 835592 | tf_op jit(solution)/shard_map/ppermute | solution.py:687
  142.3 4.5 %collective-permute-start.35 = (bf16[16,2560]{1,0:T(8,128)(2,1)S(1)}, bf16[16,2560]{1,0:T(8,128)(2,1)S(1)}, u32[]{:S(2)}, u32[]{:S(2)}) collective-permute-start(bf16[16,2560]{1,0:T(8,128)(2,1)S(1)} %fusion.18), channel_id=1, source_target_pairs={{0,1},{1,0},{2,3},{3,2},{4,5},{5,4},{6,7},{7,6},{8,9},{9,8},{10,11... | collective-permute-start | bytes 245768 | tf_op jit(solution)/shard_map/ppermute | solution.py:687
  146.9 6.5 %collective-permute-start.39 = (bf16[16,4864]{1,0:T(8,128)(2,1)S(1)}, bf16[16,4864]{1,0:T(8,128)(2,1)S(1)}, u32[]{:S(2)}, u32[]{:S(2)}) collective-permute-start(bf16[16,4864]{1,0:T(8,128)(2,1)S(1)} %get-tuple-element.320), channel_id=1, source_target_pairs={{0,16},{4,20},{8,24},{12,28},{16,0},{20,4},{24,8},{28,12},{1,17},{... | collective-permute-start | bytes 466952 | tf_op jit(solution)/shard_map/ppermute | solution.py:687
  148.9 6.3 %collective-permute-start.38 = (bf16[16,2176]{1,0:T(8,128)(2,1)S(1)}, bf16[16,2176]{1,0:T(8,128)(2,1)S(1)}, u32[]{:S(2)}, u32[]{:S(2)}) collective-permute-start(bf16[16,2176]{1,0:T(8,128)(2,1)S(1)} %get-tuple-element.303), channel_id=1, source_target_pairs={{0,3},{1,2},{2,1},{3,0},{4,7},{5,6},{6,5},{7,4},{8,11},{9,10},{10,... | collective-permute-start | bytes 208904 | tf_op jit(solution)/shard_map/ppermute | solution.py:687
  150.6 6.3 %collective-permute-start.37 = (bf16[16,2176]{1,0:T(8,128)(2,1)S(1)}, bf16[16,2176]{1,0:T(8,128)(2,1)S(1)}, u32[]{:S(2)}, u32[]{:S(2)}) collective-permute-start(bf16[16,2176]{1,0:T(8,128)(2,1)S(1)} %get-tuple-element.304), channel_id=1, source_target_pairs={{0,2},{1,3},{2,0},{3,1},{4,6},{5,7},{6,4},{7,5},{8,10},{9,11},{10,... | collective-permute-start | bytes 208904 | tf_op jit(solution)/shard_map/ppermute | solution.py:687
  151.7 5.3 %collective-permute-start.36 = (bf16[16,2176]{1,0:T(8,128)(2,1)S(1)}, bf16[16,2176]{1,0:T(8,128)(2,1)S(1)}, u32[]{:S(2)}, u32[]{:S(2)}) collective-permute-start(bf16[16,2176]{1,0:T(8,128)(2,1)S(1)} %get-tuple-element.305), channel_id=1, source_target_pairs={{0,1},{1,0},{2,3},{3,2},{4,5},{5,4},{6,7},{7,6},{8,9},{9,8},{10,11... | collective-permute-start | bytes 208904 | tf_op jit(solution)/shard_map/ppermute | solution.py:687
  153.4 9.2 %collective-permute-start.44 = (bf16[2,16,4864]{2,1,0:T(8,128)(2,1)S(1)}, bf16[2,16,4864]{2,1,0:T(8,128)(2,1)S(1)}, u32[]{:S(2)}, u32[]{:S(2)}) collective-permute-start(bf16[2,16,4864]{2,1,0:T(8,128)(2,1)S(1)} %get-tuple-element.316), channel_id=1, source_target_pairs={{0,8},{4,12},{8,0},{12,4},{16,24},{20,28},{24,16},{28,20},{1,9},{5... | collective-permute-start | bytes 933896 | tf_op jit(solution)/shard_map/ppermute | solution.py:687
  157.0 5.7 %collective-permute-start.40 = (bf16[16,2176]{1,0:T(8,128)(2,1)S(1)}, bf16[16,2176]{1,0:T(8,128)(2,1)S(1)}, u32[]{:S(2)}, u32[]{:S(2)}) collective-permute-start(bf16[16,2176]{1,0:T(8,128)(2,1)S(1)} %add_convert_fusion.23), channel_id=1, source_target_pairs={{0,8},{4,12},{8,0},{12,4},{16,24},{20,28},{24,16},{28,20},{1,9},{5... | collective-permute-start | bytes 208904 | tf_op jit(solution)/shard_map/ppermute | solution.py:687
  158.0 5.7 %collective-permute-start.42 = (bf16[16,2176]{1,0:T(8,128)(2,1)S(1)}, bf16[16,2176]{1,0:T(8,128)(2,1)S(1)}, u32[]{:S(2)}, u32[]{:S(2)}) collective-permute-start(bf16[16,2176]{1,0:T(8,128)(2,1)S(1)} %add_convert_fusion.23), channel_id=1, source_target_pairs={{0,24},{4,28},{8,16},{12,20},{16,8},{20,12},{24,0},{28,4},{1,25},{... | collective-permute-start | bytes 208904 | tf_op jit(solution)/shard_map/ppermute | solution.py:687
  159.7 4.7 %collective-permute-start.41 = (bf16[16,2176]{1,0:T(8,128)(2,1)S(1)}, bf16[16,2176]{1,0:T(8,128)(2,1)S(1)}, u32[]{:S(2)}, u32[]{:S(2)}) collective-permute-start(bf16[16,2176]{1,0:T(8,128)(2,1)S(1)} %add_convert_fusion.23), channel_id=1, source_target_pairs={{0,16},{4,20},{8,24},{12,28},{16,0},{20,4},{24,8},{28,12},{1,17},{... | collective-permute-start | bytes 208904 | tf_op jit(solution)/shard_map/ppermute | solution.py:687
  162.8 2.1 %collective-permute-start.45 = (bf16[4,16,4864]{2,1,0:T(8,128)(2,1)S(1)}, bf16[4,16,4864]{2,1,0:T(8,128)(2,1)S(1)}, u32[]{:S(2)}, u32[]{:S(2)}) collective-permute-start(bf16[4,16,4864]{2,1,0:T(8,128)(2,1)S(1)} %bitcast.103), channel_id=1, source_target_pairs={{0,4},{4,0},{8,12},{12,8},{16,20},{20,16},{24,28},{28,24},{1,5},{5... | collective-permute-start | bytes 1867784 | tf_op jit(solution)/shard_map/ppermute | solution.py:687
  164.5 2.5 %collective-permute-start.43 = (bf16[4,16,2176]{2,1,0:T(8,128)(2,1)S(1)}, bf16[4,16,2176]{2,1,0:T(8,128)(2,1)S(1)}, u32[]{:S(2)}, u32[]{:S(2)}) collective-permute-start(bf16[4,16,2176]{2,1,0:T(8,128)(2,1)S(1)} %pad_maximum_fusion.13.near), channel_id=1, source_target_pairs={{0,4},{4,0},{8,12},{12,8},{16,20},{20,16},{24,28},{28,24},{1,5},{5... | collective-permute-start | bytes 835592 | tf_op jit(solution)/shard_map/ppermute | solution.py:687
  (13 other events, 48.7 us)
